TPU v7x, 32 devices: a whole 2x2x4 slice. The times are simulated.
32 devices in a mesh: proof: 8 (over y, x, core), landmark: 4 (over z).
Axes of the slice: x: 2, y: 2, z: 4, core: 2. Of those that a mesh axis runs over, the one named last changes fastest.
Arguments:
- row_features: bfloat16 [3072, 7168], P('proof', 'landmark'), may hold values from -48 to 48
- landmark_features: bfloat16 [2048, 7168], P('landmark', 'proof'), may hold values from -48 to 48
- targets: float32 [3072, 64], P('proof'), may hold values from -6 to 6
Outputs:
- coefficient: float32 [2048, 64], P('landmark')
- residual: float32 [2048, 64], P('landmark')
All inputs are finite; a program needn't handle non-finite values.
Results may differ from a plain program's by a relative error of at most 0.0007.
Values may be sent and summed in bfloat16 or wider, within the bound.
No kernel may reach another device: no remote copies, remote signals or barrier semaphores. Data moves between devices by JAX's collectives and lax.ppermute only.
A program may use at most 64 MiB of HBM per device.

v0:
```python
import jax
import jax.numpy as jnp
from jax import lax
from jax.sharding import PartitionSpec as P

ITERS = 2
SPREAD = 10690


ridge_scale = 0.002


def times_kernel(kernel, columns):
    return jnp.dot(kernel, columns, precision=lax.Precision.HIGHEST)


def kernel_transposed(kernel, columns):
    return lax.dot_general(
        kernel, columns, (((0,), (0,)), ((), ())), precision=lax.Precision.HIGHEST
    )


def cross_piece(left, right):
    return lax.dot_general(
        left, right, (((1,), (1,)), ((), ())), preferred_element_type=jnp.float32
    )


def squares(block):
    return jnp.sum(jnp.square(block.astype(jnp.float32)), axis=1)


def shards(row_features, landmark_features, targets):
    rows = row_features.shape[0]
    whole_rows = lax.all_gather(row_features, "landmark", axis=1, tiled=True)
    row_norm = squares(whole_rows)
    piece = lax.all_gather(landmark_features, "proof", axis=1, tiled=True)
    cross = cross_piece(whole_rows, piece)
    landmark_norm = squares(piece)
    kernel = jnp.exp(-(row_norm[:, None] + landmark_norm[None, :] - 2.0 * cross) / SPREAD)
    lam = ridge_scale * rows * lax.axis_size("proof")
    projected, diagonal = lax.psum(
        (kernel_transposed(kernel, targets), jnp.sum(kernel * kernel, axis=0)), "proof"
    )
    precond = (lam + diagonal)[:, None]
    coefficient = jnp.zeros_like(projected)
    residual = projected
    scaled = residual / precond
    direction = scaled
    inner = lax.psum(jnp.sum(residual * scaled, axis=0), "landmark")
    for iteration in range(ITERS):
        image = lax.psum(times_kernel(kernel, direction), "landmark")
        gradient = lax.psum(kernel_transposed(kernel, image), "proof") + lam * direction
        curvature = lax.psum(jnp.sum(direction * gradient, axis=0), "landmark")
        step_size = inner / curvature
        coefficient = coefficient + step_size * direction
        residual = residual - step_size * gradient
        scaled = residual / precond
        inner_next = lax.psum(jnp.sum(residual * scaled, axis=0), "landmark")
        direction = scaled + inner_next / inner * direction
        inner = inner_next
    return (coefficient, residual)


def solution(mesh):
    placed = (P("proof", "landmark"), P("landmark", "proof"), P("proof", None))
    return jax.shard_map(
        shards,
        mesh=mesh,
        in_specs=placed,
        out_specs=(P("landmark", None), P("landmark", None)),
        check_vma=False,
    )
```

profile of v0, /device:TPU:0, one launch (start us, length us, event | category | flops | bytes accessed | tf_op | source)
XLA Modules:
  0.0 472.8 jit_solution(16752193414744917460)
XLA Ops:
  7.2 0.0 copy-start
  7.2 0.0 all-gather.3.cloned.1.call-start
  7.2 0.7 all-gather.3.cloned.1.call-update
  7.9 0.0 all-gather.5.cloned.1.call-start
  8.0 0.7 all-gather.5.cloned.1.call-update
  8.7 0.0 all-reduce.7.cloned.1.call-start
  8.7 106.0 %all-gather.3.cloned.1.call-done = bf16[384,7168]{1,0:T(8,128)(2,1)} async-done(((bf16[384,1792]{1,0:T(8,128)(2,1)}), bf16[384,7168]{1,0:T(8,128)(2,1)}) %all-gather.3.cloned.1.call-update) | async-done | bytes 5505040 | tf_op jit(solution)/shard_map/all_gather | solution.py:35
  114.7 3.7 multiply_reduce_fusion.1
  118.4 46.3 %all-gather.5.cloned.1.call-done = bf16[512,7168]{1,0:T(8,128)(2,1)} async-done(((bf16[512,896]{1,0:T(8,128)(2,1)}), bf16[512,7168]{1,0:T(8,128)(2,1)}) %all-gather.5.cloned.1.call-update) | async-done | bytes 7340048 | tf_op jit(solution)/shard_map/all_gather | solution.py:37
  164.7 0.0 copy-start.1
  164.7 4.7 %multiply_reduce_fusion = f32[512]{0:T(512)S(1)} fusion(bf16[512,7168]{1,0:T(8,128)(2,1)} %all-gather.5.cloned.1.call-done), kind=kLoop, calls=%fused_computation | loop fusion | flops 11009536 | bytes 7342080 | tf_op jit(solution)/shard_map/reduce_sum | solution.py:30
  169.4 0.4 copy-done.1
  169.9 7.1 %multiply_reduce_fusion.2 = (f32[512]{0:T(512)S(1)}, f32[384,512]{1,0:T(8,128)S(1)}) fusion(bf16[384,7168]{1,0:T(8,128)(2,1)} %all-gather.3.cloned.1.call-done, bf16[512,7168]{1,0:T(8,128)(2,1)S(1)} %copy-done.1, f32[512]{0:T(512)S(1)} %multiply_reduce_fusion, f32[384]{0:T(512)S(1)} %multiply_reduce_fusion.1), kind=kOutput, calls=%fused_computation.7 | convolution fusion | flops 2819948032 | bytes 13637120 | tf_op jit(solution)/shard_map/dot_general | solution.py:24
  176.9 13.1 %psum.71 = f32[512]{0:T(512)S(1)} all-reduce(f32[512]{0:T(512)S(1)} %get-tuple-element.10), channel_id=1, replica_groups=mesh['proof'=8,'landmark'=4] {'proof'}, use_global_device_ids=true, to_apply=%region_4.0 | all-reduce | flops 512 | bytes 4096 | tf_op jit(solution)/shard_map/psum | solution.py:42
  190.0 0.0 copy-done
  190.0 1.3 fusion.5
  191.3 0.0 all-reduce.7.cloned.1.call-update
  191.3 0.0 all-reduce.9.cloned.1.call-start
  191.4 53.0 %all-reduce.7.cloned.1.call-done = f32[512,64]{0,1:T(8,128)} async-done(((f32[512,64]{0,1:T(8,128)}), f32[512,64]{0,1:T(8,128)}) %all-reduce.7.cloned.1.call-update) | async-done | bytes 131088 | tf_op jit(solution)/shard_map/psum | solution.py:42
  244.4 2.4 fusion.4
  246.8 0.0 all-reduce.9.cloned.1.call-update
  246.8 0.0 all-reduce.11.cloned.1.call-start
  246.8 34.3 %all-reduce.9.cloned.1.call-done = f32[384,64]{1,0:T(8,128)} async-done(((f32[384,64]{1,0:T(8,128)}), f32[384,64]{1,0:T(8,128)}) %all-reduce.9.cloned.1.call-update) | async-done | bytes 98320 | tf_op jit(solution)/shard_map/psum | solution.py:52
  281.1 2.2 fusion.6
  283.3 0.0 all-reduce.11.cloned.1.call-update
  283.3 0.0 all-reduce.13.cloned.1.call-start
  283.4 53.9 %all-reduce.11.cloned.1.call-done = f32[512,64]{0,1:T(8,128)} async-done(((f32[512,64]{0,1:T(8,128)}), f32[512,64]{0,1:T(8,128)}) %all-reduce.11.cloned.1.call-update) | async-done | bytes 131088 | tf_op jit(solution)/shard_map/psum | solution.py:53
  337.3 1.1 multiply_reduce_fusion.5
  338.4 11.7 %all-reduce = (f32[64]{0:T(128)S(1)}, f32[64]{0:T(128)S(1)}) all-reduce(f32[64]{0:T(128)S(1)} %get-tuple-element.3, f32[64]{0:T(128)S(1)} %get-tuple-element.2), channel_id=1, replica_groups=mesh['proof'=8,'landmark'=4] {'landmark'}, use_global_device_ids=true, to_apply=%region_6.0 | all-reduce | flops 128 | bytes 1024 | tf_op jit(solution)/shard_map/psum | solution.py:50
  350.1 1.2 multiply_reduce_fusion.4
  351.2 8.4 %psum.76 = f32[64]{0:T(128)S(1)} all-reduce(f32[64]{0:T(128)S(1)} %get-tuple-element.6), channel_id=1, replica_groups=mesh['proof'=8,'landmark'=4] {'landmark'}, use_global_device_ids=true, to_apply=%region_12.0 | all-reduce | flops 64 | bytes 512 | tf_op jit(solution)/shard_map/psum | solution.py:59
  359.6 1.0 multiply_add_fusion.2
  360.6 1.4 fusion.7
  362.1 0.0 all-reduce.13.cloned.1.call-update
  362.1 0.0 all-reduce.15.cloned.1.call-start
  362.1 33.0 %all-reduce.13.cloned.1.call-done = f32[384,64]{1,0:T(8,128)} async-done(((f32[384,64]{1,0:T(8,128)}), f32[384,64]{1,0:T(8,128)}) %all-reduce.13.cloned.1.call-update) | async-done | bytes 98320 | tf_op jit(solution)/shard_map/psum | solution.py:52
  395.1 2.2 fusion.8
  397.3 0.0 all-reduce.15.cloned.1.call-update
  397.4 54.1 %all-reduce.15.cloned.1.call-done = f32[512,64]{0,1:T(8,128)} async-done(((f32[512,64]{0,1:T(8,128)}), f32[512,64]{0,1:T(8,128)}) %all-reduce.15.cloned.1.call-update) | async-done | bytes 131088 | tf_op jit(solution)/shard_map/psum | solution.py:53
  451.4 1.0 multiply_reduce_fusion.3
  452.5 11.7 %psum.79 = f32[64]{0:T(128)S(1)} all-reduce(f32[64]{0:T(128)S(1)} %multiply_reduce_fusion.3), channel_id=1, replica_groups=mesh['proof'=8,'landmark'=4] {'landmark'}, use_global_device_ids=true, to_apply=%region_16.0 | all-reduce | flops 64 | bytes 512 | tf_op jit(solution)/shard_map/psum | solution.py:54
  464.2 1.8 multiply_subtract_fusion
  (4 shorter events, 0.0 us)
Async XLA Ops:
  7.2 182.9 %copy-start = (f32[384,64]{0,1:T(8,128)S(1)}, f32[384,64]{0,1:T(8,128)}, u32[]{:S(2)}) copy-start(f32[384,64]{0,1:T(8,128)} %param.5) | copy-start | bytes 294916
  7.2 107.5 %all-gather.3.cloned.1.call-start = ((), (), s32[]{:S(2)}) async-start(), calls=%async_computation | async-start | bytes 6881280 | tf_op jit(solution)/shard_map/all_gather | solution.py:35
  7.9 156.8 %all-gather.5.cloned.1.call-start = ((), (), s32[]{:S(2)}) async-start(), calls=%async_computation.1 | async-start | bytes 8257536 | tf_op jit(solution)/shard_map/all_gather | solution.py:37
  8.7 235.8 %all-reduce.7.cloned.1.call-start = ((), (), s32[]{:S(2)}) async-start(), calls=%async_computation.2 | async-start | bytes 262144 | tf_op jit(solution)/shard_map/psum | solution.py:42
  164.7 5.2 %copy-start.1 = (bf16[512,7168]{1,0:T(8,128)(2,1)S(1)}, bf16[512,7168]{1,0:T(8,128)(2,1)}, u32[]{:S(2)}) copy-start(bf16[512,7168]{1,0:T(8,128)(2,1)} %all-gather.5.cloned.1.call-done) | copy-start | bytes 22020100
  191.3 89.8 %all-reduce.9.cloned.1.call-start = ((), (), s32[]{:S(2)}) async-start(), calls=%async_computation.3 | async-start | bytes 393216 | tf_op jit(solution)/shard_map/psum | solution.py:52
  246.8 90.5 %all-reduce.11.cloned.1.call-start = ((), (), s32[]{:S(2)}) async-start(), calls=%async_computation.4 | async-start | bytes 262144 | tf_op jit(solution)/shard_map/psum | solution.py:53
  283.3 111.8 %all-reduce.13.cloned.1.call-start = ((), (), s32[]{:S(2)}) async-start(), calls=%async_computation.5 | async-start | bytes 393216 | tf_op jit(solution)/shard_map/psum | solution.py:52
  362.1 89.3 %all-reduce.15.cloned.1.call-start = ((), (), s32[]{:S(2)}) async-start(), calls=%async_computation.6 | async-start | bytes 262144 | tf_op jit(solution)/shard_map/psum | solution.py:53
Sparse Core Ops, SparseCore 0:
  9.6 105.0 all-gather.2
  116.6 48.0 all-gather.4
  191.5 52.9 all-reduce.6
  246.9 34.1 all-reduce.8
  284.6 52.6 all-reduce.10
  362.2 32.8 all-reduce.12
  398.8 52.6 all-reduce.14
where the time goes:
time: 473 us
  waiting for transfers between devices  382 us (81%)
  blocking collectives  44.9 us (9%)
  matrix products  16.5 us (3%)
  other arithmetic  14.5 us (3%)
  between operations  14.2 us (3%)
    psum x2, waiting for transfers between devices, shards(): lax.psum(kernel_transposed(kernel, image), 'proof') + lam * direction  108 us
    all_gather x1, waiting for transfers between devices, shards(): whole_rows = lax.all_gather(row_features, 'landmark', axis=1, tiled=True)  106 us
    psum x2, waiting for transfers between devices, shards(): image = lax.psum(times_kernel(kernel, direction), 'landmark')  67.3 us
    psum x1, waiting for transfers between devices, shards(): lax.psum((kernel_transposed(kernel, targets), jnp.sum(kernel * kernel, ax...  53 us
    all_gather x1, waiting for transfers between devices, shards(): piece = lax.all_gather(landmark_features, 'proof', axis=1, tiled=True)  46.3 us
    psum x1, blocking collectives, shards(): lax.psum((kernel_transposed(kernel, targets), jnp.sum(kernel * kernel, ax...  13.1 us
    psum x1, blocking collectives, shards(): inner = lax.psum(jnp.sum(residual * scaled, axis=0), 'landmark')  11.7 us
    psum x1, blocking collectives, shards(): curvature = lax.psum(jnp.sum(direction * gradient, axis=0), 'landmark')  11.7 us
  transfers between devices with their start and end apart: 7, of which 7 were waited for; matrix products, arithmetic and copies ran while one was open for 1% of the time, Pallas kernels for 0%

commit v1 on v0

v1 whole, which is shorter than its diff:
```python
import jax
import jax.numpy as jnp
from jax import lax
from jax.sharding import PartitionSpec as P

ITERS = 2
SPREAD = 10690

ridge_scale = 0.002


def squares(block):
    return jnp.sum(jnp.square(block.astype(jnp.float32)), axis=1)


def cross_piece(left, right):
    return lax.dot_general(
        left, right, (((1,), (1,)), ((), ())), preferred_element_type=jnp.float32
    )


def times(left, right, contract):
    return lax.dot_general(
        left, right, ((contract[:1], contract[1:]), ((), ())), precision=lax.Precision.HIGHEST
    )


def flipped(block, axis, bits):
    size = lax.axis_size(axis)
    return lax.ppermute(block, axis, [(i, i ^ bits) for i in range(size)])


def sum_rows_axis(block):
    size = lax.axis_size("proof")
    if size != 8:
        return lax.psum(block, "proof")
    odd = lax.axis_index("proof") % 2
    half = block.shape[1] // 2
    low, high = block[:, :half], block[:, half:]
    mine, other = jnp.where(odd == 0, low, high), jnp.where(odd == 0, high, low)
    mine = mine + flipped(other, "proof", 1)
    mine = mine + flipped(mine, "proof", 2) + flipped(mine, "proof", 4) + flipped(mine, "proof", 6)
    other = flipped(mine, "proof", 1)
    low, high = jnp.where(odd == 0, mine, other), jnp.where(odd == 0, other, mine)
    return jnp.concatenate([low, high], axis=1)


def sum_landmark_axis(block):
    size = lax.axis_size("landmark")
    if size != 4:
        return lax.psum(block, "landmark")
    total = block
    for shift in range(1, size):
        pairs = [(i, (i + shift) % size) for i in range(size)]
        total = total + lax.ppermute(block, "landmark", pairs)
    return total


def packed(block, *vectors):
    rows = jnp.stack(vectors)
    rows = jnp.pad(rows, ((0, 8 - rows.shape[0]), (0, block.shape[1] - rows.shape[1])))
    return jnp.concatenate([block, rows], axis=0)


def gathered_landmarks(piece):
    size = lax.axis_size("proof")
    if size != 8:
        return lax.all_gather(piece, "proof", axis=1, tiled=True)
    me = lax.axis_index("proof")
    half = piece.shape[0] // 2
    pieces = {0: piece, 2: flipped(piece, "proof", 2), 4: flipped(piece, "proof", 4)}
    corner_low = flipped(pieces[2][:half], "proof", 4)
    corner_high = flipped(pieces[4][half:], "proof", 2)
    pieces[6] = jnp.concatenate([corner_low, corner_high], axis=0)
    for bits in (0, 2, 4, 6):
        pieces[bits + 1] = flipped(pieces[bits], "proof", 1)
    whole = jnp.zeros((piece.shape[0], piece.shape[1] * size), piece.dtype)
    for bits, part in pieces.items():
        whole = lax.dynamic_update_slice(whole, part, (0, (me ^ bits) * piece.shape[1]))
    return whole


def squared_distances(row_features, landmark_features):
    size = lax.axis_size("landmark")
    me = lax.axis_index("landmark")
    width = row_features.shape[1]
    whole = gathered_landmarks(landmark_features)
    landmark_norm = squares(whole)

    def term(block, owner):
        start = jnp.clip(owner, 0, size - 1) * width
        other = lax.dynamic_slice_in_dim(whole, start, width, axis=1)
        return cross_piece(block, other)

    if size != 4:
        rows = lax.all_gather(row_features, "landmark", axis=1, tiled=True)
        return squares(rows)[:, None] + landmark_norm[None, :] - 2.0 * cross_piece(rows, whole)
    cross = term(row_features, me)
    row_norm = squares(row_features)
    up = [(i, i + 1) for i in range(size - 1)]
    down = [(i + 1, i) for i in range(size - 1)]
    below = above = row_features
    for step in range(1, size):
        below, above = lax.ppermute(below, "landmark", up), lax.ppermute(above, "landmark", down)
        cross = cross + term(below, me - step) + term(above, me + step)
        row_norm = row_norm + squares(below) + squares(above)
    return row_norm[:, None] + landmark_norm[None, :] - 2.0 * cross


def shards(row_features, landmark_features, targets):
    kernel = jnp.exp(-squared_distances(row_features, landmark_features) / SPREAD)
    lam = ridge_scale * row_features.shape[0] * lax.axis_size("proof")
    count = targets.shape[1]
    columns = targets.T
    sums = sum_rows_axis(packed(times(columns, kernel, (1, 0)), jnp.sum(kernel * kernel, axis=0)))
    residual, precond = sums[:count], lam + sums[count]
    coefficient = jnp.zeros_like(residual)
    inner = None
    for iteration in range(ITERS):
        scaled = residual / precond
        part = times(scaled, kernel, (1, 1))
        dots = [jnp.sum(residual * scaled, axis=1), jnp.sum(scaled * scaled, axis=1)]
        if iteration > 0:
            dots.append(jnp.sum(scaled * direction, axis=1))
        sums = sum_landmark_axis(packed(part, *dots))
        inner_next, square = sums[count, :count], sums[count + 1, :count]
        if iteration == 0:
            direction, image, length = scaled, sums[:count], square
        else:
            beta = inner_next / inner
            length = square + beta * (2.0 * sums[count + 2, :count] + beta * length)
            direction = scaled + beta[:, None] * direction
            image = sums[:count] + beta[:, None] * image
        inner = inner_next
        sums = sum_rows_axis(packed(times(image, kernel, (1, 0)), jnp.sum(image * image, axis=1)))
        gradient = sums[:count] + lam * direction
        step_size = (inner / (sums[count, :count] + lam * length))[:, None]
        coefficient = coefficient + step_size * direction
        residual = residual - step_size * gradient
    return coefficient.T, residual.T


def solution(mesh):
    placed = (P("proof", "landmark"), P("landmark", "proof"), P("proof", None))
    return jax.shard_map(
        shards,
        mesh=mesh,
        in_specs=placed,
        out_specs=(P("landmark", None), P("landmark", None)),
        check_vma=False,
    )
```

time: 473 us -> 182 us (0.38)
  waiting for transfers between devices: 382 us -> 79.5 us
  starting transfers between devices: 0.28 us -> 50.4 us
  blocking collectives: 44.9 us -> 0 us
  local copies, waits for them, and re-layouts: 0.43 us -> 17.4 us
  between operations: 14.2 us -> 1.01 us
    psum x5 -> x0, waiting for transfers between devices: 228 us -> none  [the longest x2 108 us: shards(): lax.psum(kernel_transposed(kernel, image), 'proof') + lam * direction]
    all_gather x2 -> x0, waiting for transfers between devices: 152 us -> none  [the longest x1 106 us: shards(): whole_rows = lax.all_gather(row_features, 'landmark', axis=1, tiled=True)]
    ppermute x0 -> x35, waiting for transfers between devices: none -> 79.5 us  [the longest x23 33.1 us: flipped(): return lax.ppermute(block, axis, [(i, i ^ bits) for i in range(size)])]
    ppermute x0 -> x35, starting transfers between devices: none -> 50.4 us  [the longest x23 19.4 us: flipped(): return lax.ppermute(block, axis, [(i, i ^ bits) for i in range(size)])]
    psum x4 -> x0, blocking collectives: 44.9 us -> none  [the longest x1 13.1 us: shards(): lax.psum((kernel_transposed(kernel, targets), jnp.sum(kernel * kernel, ax...]
    dot_general x1 -> x7, matrix products: 7.06 us -> 17.4 us  [cross_piece(): lax.dot_general(left, right, (((1,), (1,)), ((), ())), preferred_element_...]
    dynamic_update_slice x0 -> x8, local copies, waits for them, and re-layouts: none -> 9.74 us  [gathered_landmarks(): lax.dynamic_update_slice(whole, part, (0, (me ^ bits) * piece.shape[1]))]
    dot_general x5, matrix products: 9.44 us -> 3.53 us  [times(): lax.dot_general(left, right, ((contract[:1], contract[1:]), ((), ())), pr...]
  transfers between devices with their start and end apart: 7 -> 35, of which waited for: 7 -> 24; matrix products, arithmetic and copies ran while one was open for 1% -> 22% of each run, Pallas kernels for 0% -> 0%
where the time goes in v1:
time: 182 us; the launch traced here: 181 us
  waiting for transfers between devices  79.5 us (44%)
  starting transfers between devices  50.4 us (28%)
  matrix products  21 us (12%)
  local copies, waits for them, and re-layouts  17.4 us (10%)
  other arithmetic  11.6 us (6%)
    ppermute x23, waiting for transfers between devices, flipped(): return lax.ppermute(block, axis, [(i, i ^ bits) for i in range(size)])  33.1 us
    ppermute x3, waiting for transfers between devices, squared_distances(): lax.ppermute(above, 'landmark', down)  30 us
    ppermute x23, starting transfers between devices, flipped(): return lax.ppermute(block, axis, [(i, i ^ bits) for i in range(size)])  19.4 us
    dot_general x7, matrix products, cross_piece(): lax.dot_general(left, right, (((1,), (1,)), ((), ())), preferred_element_...  17.4 us
    ppermute x3, starting transfers between devices, squared_distances(): lax.ppermute(below, 'landmark', up)  15.2 us
    ppermute x6, waiting for transfers between devices, sum_landmark_axis(): total = total + lax.ppermute(block, 'landmark', pairs)  13.1 us
    ppermute x6, starting transfers between devices, sum_landmark_axis(): total = total + lax.ppermute(block, 'landmark', pairs)  11.9 us
    dynamic_update_slice x8, local copies, waits for them, and re-layouts, gathered_landmarks(): lax.dynamic_update_slice(whole, part, (0, (me ^ bits) * piece.shape[1]))  9.74 us
  transfers between devices with their start and end apart: 35, of which 24 were waited for; matrix products, arithmetic and copies ran while one was open for 22% of the time, Pallas kernels for 0%

profile of v1, /device:TPU:0, one launch (start us, length us, event | category | flops | bytes accessed | tf_op | source)
XLA Modules:
  0.0 180.8 jit_solution(3129575858668428998)
XLA Ops:
  0.6 3.0 %collective-permute-start.6 = (bf16[512,896]{1,0:T(8,128)(2,1)}, bf16[512,896]{1,0:T(8,128)(2,1)S(1)}, u32[]{:S(2)}, u32[]{:S(2)}) collective-permute-start(bf16[512,896]{1,0:T(8,128)(2,1)} %param.4), channel_id=1, source_target_pairs={{0,8},{4,12},{8,0},{12,4},{16,24},{20,28},{24,16},{28,20},{1,9},{5... | collective-permute-start | bytes 2752520 | tf_op jit(solution)/shard_map/ppermute | solution.py:30
  3.6 1.5 collective-permute-start.7
  5.2 1.3 collective-permute-start.1
  6.5 5.7 %collective-permute-start = (bf16[384,1792]{1,0:T(8,128)(2,1)}, bf16[384,1792]{1,0:T(8,128)(2,1)}, u32[]{:S(2)}, u32[]{:S(2)}) collective-permute-start(bf16[384,1792]{1,0:T(8,128)(2,1)} %param.3), channel_id=1, source_target_pairs={{0,1},{1,2},{2,3},{4,5},{5,6},{6,7},{8,9},{9,10},{10,11},{12,13},{... | collective-permute-start | bytes 4128776 | tf_op jit(solution)/shard_map/ppermute | solution.py:104
  12.2 12.0 %collective-permute-done.6 = bf16[512,896]{1,0:T(8,128)(2,1)S(1)} collective-permute-done((bf16[512,896]{1,0:T(8,128)(2,1)}, bf16[512,896]{1,0:T(8,128)(2,1)S(1)}, u32[]{:S(2)}, u32[]{:S(2)}) %collective-permute-start.6) | collective-permute-done | bytes 917536 | tf_op jit(solution)/shard_map/ppermute | solution.py:30
  25.0 1.8 collective-permute-start.8
  26.8 1.7 multiply_reduce_fusion.7
  29.3 1.5 collective-permute-start.9
  30.8 3.9 %broadcast_in_dim.2 = bf16[512,7168]{1,0:T(8,128)(2,1)} broadcast(bf16[]{:T(256)} %constant.49.clone.1), dimensions={} | broadcast | bytes 7340034 | tf_op jit(solution)/shard_map/broadcast_in_dim | solution.py:77
  34.6 1.0 constant_dynamic-update-slice_fusion.9
  35.7 1.1 constant_dynamic-update-slice_fusion.8
  37.1 1.1 constant_dynamic-update-slice_fusion.7
  38.1 1.1 constant_dynamic-update-slice_fusion.1
  39.2 1.5 collective-permute-done.9
  40.7 1.1 constant_dynamic-update-slice_fusion
  42.4 1.1 constant_dynamic-update-slice_fusion.6
  43.8 1.3 collective-permute-start.3
  45.1 1.7 multiply_reduce_fusion.6
  46.8 4.6 %collective-permute-start.2 = (bf16[384,1792]{1,0:T(8,128)(2,1)}, bf16[384,1792]{1,0:T(8,128)(2,1)S(1)}, u32[]{:S(2)}, u32[]{:S(2)}) collective-permute-start(bf16[384,1792]{1,0:T(8,128)(2,1)} %collective-permute-done), channel_id=1, source_target_pairs={{0,1},{1,2},{2,3},{4,5},{5,6},{6,7},{8,9},{9,10},{10,11},{12,13},{... | collective-permute-start | bytes 4128776 | tf_op jit(solution)/shard_map/ppermute | solution.py:104
  51.4 2.3 %constant_dynamic-update-slice_fusion.5 = bf16[512,7168]{1,0:T(8,128)(2,1)} fusion(bf16[512,7168]{1,0:T(8,128)(2,1)} %constant_dynamic-update-slice_fusion.6, bf16[512,896]{1,0:T(8,128)(2,1)} %collective-permute-done.10, s32[]{:T(128)S(6)} %select_n.114), kind=kLoop, calls=%fused_computation.100 | loop fusion | bytes 1835012 | tf_op jit(solution)/shard_map/dynamic_update_slice | solution.py:79
  53.7 1.0 constant_dynamic-update-slice_fusion.4
  54.8 1.1 constant_dynamic-update-slice_fusion.3
  55.9 1.0 constant_dynamic-update-slice_fusion.2
  56.9 2.8 %fusion.10 = f32[512,384]{0,1:T(8,128)S(1)} fusion(bf16[384,1792]{1,0:T(8,128)(2,1)} %collective-permute-done, bf16[512,7168]{1,0:T(8,128)(2,1)} %constant_dynamic-update-slice_fusion.2, s32[]{:T(128)S(6)} %select_n.119), kind=kOutput, calls=%fused_computation.18 | convolution fusion | flops 704643072 | bytes 3997700 | tf_op jit(solution)/shard_map/dot_general | solution.py:17
  59.7 4.6 %multiply_reduce_fusion = f32[512]{0:T(512)S(1)} fusion(bf16[512,7168]{1,0:T(8,128)(2,1)} %constant_dynamic-update-slice_fusion.2), kind=kLoop, calls=%fused_computation | loop fusion | flops 11009536 | bytes 7342080 | tf_op jit(solution)/shard_map/reduce_sum | solution.py:13
  64.3 13.4 %collective-permute-done.3 = bf16[384,1792]{1,0:T(8,128)(2,1)S(1)} collective-permute-done((bf16[384,1792]{1,0:T(8,128)(2,1)S(1)}, bf16[384,1792]{1,0:T(8,128)(2,1)S(1)}, u32[]{:S(2)}, u32[]{:S(2)}) %collective-permute-start.3) | collective-permute-done | bytes 1376288 | tf_op jit(solution)/shard_map/ppermute | solution.py:104
  77.8 1.3 collective-permute-start.5
  79.0 2.4 %fusion.8 = f32[512,384]{0,1:T(8,128)S(1)} fusion(bf16[384,1792]{1,0:T(8,128)(2,1)S(1)} %collective-permute-done.1, bf16[512,7168]{1,0:T(8,128)(2,1)} %constant_dynamic-update-slice_fusion.2, s32[]{:T(128)S(6)} %select_n.120), kind=kOutput, calls=%fused_computation.16 | convolution fusion | flops 704643072 | bytes 3997700 | tf_op jit(solution)/shard_map/dot_general | solution.py:17
  81.5 4.8 %collective-permute-start.4 = (bf16[384,1792]{1,0:T(8,128)(2,1)S(1)}, bf16[384,1792]{1,0:T(8,128)(2,1)S(1)}, u32[]{:S(2)}, u32[]{:S(2)}) collective-permute-start(bf16[384,1792]{1,0:T(8,128)(2,1)S(1)} %collective-permute-done.2), channel_id=1, source_target_pairs={{0,1},{1,2},{2,3},{4,5},{5,6},{6,7},{8,9},{9,10},{10,11},{12,13},{... | collective-permute-start | bytes 4128776 | tf_op jit(solution)/shard_map/ppermute | solution.py:104
  86.3 2.4 %fusion.35 = f32[512,384]{0,1:T(8,128)S(1)} fusion(f32[512,384]{0,1:T(8,128)S(1)} %fusion.8, f32[512,384]{0,1:T(8,128)S(1)} %fusion.10, bf16[384,1792]{1,0:T(8,128)(2,1)S(1)} %copy-done.1, bf16[512,7168]{1,0:T(8,128)(2,1)} %constant_dynamic-update-slice_fusion.2, s32[]{:T(128)S(6)} %select_n.118), kind=kOutput, calls=%fused_computation.29 | convolution fusion | flops 705036288 | bytes 5570564 | tf_op jit(solution)/shard_map/dot_general | solution.py:17
  89.4 2.4 %fusion.4 = f32[512,384]{0,1:T(8,128)S(1)} fusion(bf16[384,1792]{1,0:T(8,128)(2,1)S(1)} %collective-permute-done.3, bf16[512,7168]{1,0:T(8,128)(2,1)} %constant_dynamic-update-slice_fusion.2, s32[]{:T(128)S(6)} %select_n.122), kind=kOutput, calls=%fused_computation.12 | convolution fusion | flops 704643072 | bytes 3997700 | tf_op jit(solution)/shard_map/dot_general | solution.py:17
  91.8 2.4 %fusion.32 = f32[512,384]{0,1:T(8,128)S(1)} fusion(f32[512,384]{0,1:T(8,128)S(1)} %fusion.4, f32[512,384]{0,1:T(8,128)S(1)} %fusion.35, bf16[384,1792]{1,0:T(8,128)(2,1)S(1)} %collective-permute-done.2, bf16[512,7168]{1,0:T(8,128)(2,1)} %constant_dynamic-update-slice_fusion.2, s32[]{:T(128)S(6)} %select_n.121), kind=kOutput, calls=%fused_computation.28 | convolution fusion | flops 705036288 | bytes 5570564 | tf_op jit(solution)/shard_map/dot_general | solution.py:17
  94.2 16.6 %collective-permute-done.5 = bf16[384,1792]{1,0:T(8,128)(2,1)S(1)} collective-permute-done((bf16[384,1792]{1,0:T(8,128)(2,1)S(1)}, bf16[384,1792]{1,0:T(8,128)(2,1)S(1)}, u32[]{:S(2)}, u32[]{:S(2)}) %collective-permute-start.5) | collective-permute-done | bytes 1376288 | tf_op jit(solution)/shard_map/ppermute | solution.py:104
  111.2 3.3 %collective-permute-done.4 = bf16[384,1792]{1,0:T(8,128)(2,1)S(1)} collective-permute-done((bf16[384,1792]{1,0:T(8,128)(2,1)S(1)}, bf16[384,1792]{1,0:T(8,128)(2,1)S(1)}, u32[]{:S(2)}, u32[]{:S(2)}) %collective-permute-start.4) | collective-permute-done | bytes 1376288 | tf_op jit(solution)/shard_map/ppermute | solution.py:104
  114.8 2.4 %fusion = f32[512,384]{0,1:T(8,128)S(1)} fusion(bf16[384,1792]{1,0:T(8,128)(2,1)S(1)} %collective-permute-done.5, bf16[512,7168]{1,0:T(8,128)(2,1)} %constant_dynamic-update-slice_fusion.2, s32[]{:T(128)S(6)} %select_n.124), kind=kOutput, calls=%fused_computation.8 | convolution fusion | flops 704643072 | bytes 3997700 | tf_op jit(solution)/shard_map/dot_general | solution.py:17
  117.2 2.6 %multiply_reduce_fusion.8 = (f32[512]{0:T(512)S(1)}, f32[384,512]{1,0:T(8,128)S(1)}) fusion(f32[512,384]{0,1:T(8,128)S(1)} %fusion, f32[512,384]{0,1:T(8,128)S(1)} %fusion.32, bf16[384,1792]{1,0:T(8,128)(2,1)S(1)} %collective-permute-done.4, bf16[512,7168]{1,0:T(8,128)(2,1)} %constant_dynamic-update-slice_fusion.2, s32[]{:T(128)S(6)} %select_n.123, ...), kind=kOutput, calls=%fused_computation.31 | convolution fusion | flops 706412032 | bytes 5576196 | tf_op jit(solution)/shard_map/dot_general | solution.py:17
  120.6 1.3 collective-permute-done.14
  121.9 1.7 collective-permute-start.15
  124.2 1.3 collective-permute-start.17
  125.4 0.9 collective-permute-done.15
  126.3 2.4 %collective-permute-done.16 = f32[72,256]{1,0:T(8,128)S(1)} collective-permute-done((f32[72,256]{1,0:T(8,128)S(1)}, f32[72,256]{1,0:T(8,128)S(1)}, u32[]{:S(2)}, u32[]{:S(2)}) %collective-permute-start.16) | collective-permute-done | bytes 73760 | tf_op jit(solution)/shard_map/ppermute | solution.py:30
  129.6 1.3 collective-permute-done.18
  131.9 2.5 %collective-permute-start.19 = (f32[72,384]{1,0:T(8,128)S(1)}, f32[72,384]{1,0:T(8,128)S(1)}, u32[]{:S(2)}, u32[]{:S(2)}) collective-permute-start(f32[72,384]{1,0:T(8,128)S(1)} %pad_maximum_fusion.2), channel_id=1, source_target_pairs={{0,1},{1,2},{2,3},{3,0},{4,5},{5,6},{6,7},{7,4},{8,9},{9,10},{10,1... | collective-permute-start | bytes 331784 | tf_op jit(solution)/shard_map/ppermute | solution.py:55
  134.5 2.8 %collective-permute-start.20 = (f32[72,384]{1,0:T(8,128)S(1)}, f32[72,384]{1,0:T(8,128)S(1)}, u32[]{:S(2)}, u32[]{:S(2)}) collective-permute-start(f32[72,384]{1,0:T(8,128)S(1)} %pad_maximum_fusion.2), channel_id=1, source_target_pairs={{0,2},{1,3},{2,0},{3,1},{4,6},{5,7},{6,4},{7,5},{8,10},{9,11},{10,... | collective-permute-start | bytes 331784 | tf_op jit(solution)/shard_map/ppermute | solution.py:55
  137.2 1.3 collective-permute-start.21
  138.5 2.1 %collective-permute-done.19 = f32[72,384]{1,0:T(8,128)S(1)} collective-permute-done((f32[72,384]{1,0:T(8,128)S(1)}, f32[72,384]{1,0:T(8,128)S(1)}, u32[]{:S(2)}, u32[]{:S(2)}) %collective-permute-start.19) | collective-permute-done | bytes 110624 | tf_op jit(solution)/shard_map/ppermute | solution.py:55
  140.6 4.3 %collective-permute-done.20 = f32[72,384]{1,0:T(8,128)S(1)} collective-permute-done((f32[72,384]{1,0:T(8,128)S(1)}, f32[72,384]{1,0:T(8,128)S(1)}, u32[]{:S(2)}, u32[]{:S(2)}) %collective-permute-start.20) | collective-permute-done | bytes 110624 | tf_op jit(solution)/shard_map/ppermute | solution.py:55
  145.8 1.3 collective-permute-done.22
  147.5 1.3 collective-permute-start.24
  148.8 1.8 collective-permute-start.25
  150.6 1.3 collective-permute-done.23
  151.8 2.2 %collective-permute-done.25 = f32[72,256]{1,0:T(8,128)S(1)} collective-permute-done((f32[72,256]{1,0:T(8,128)S(1)}, f32[72,256]{1,0:T(8,128)S(1)}, u32[]{:S(2)}, u32[]{:S(2)}) %collective-permute-start.25) | collective-permute-done | bytes 73760 | tf_op jit(solution)/shard_map/ppermute | solution.py:30
  154.2 1.3 collective-permute-done.26
  156.6 2.9 %collective-permute-start.27 = (f32[72,384]{1,0:T(8,128)S(1)}, f32[72,384]{1,0:T(8,128)S(1)}, u32[]{:S(2)}, u32[]{:S(2)}) collective-permute-start(f32[72,384]{1,0:T(8,128)S(1)} %pad_maximum_fusion.3), channel_id=1, source_target_pairs={{0,1},{1,2},{2,3},{3,0},{4,5},{5,6},{6,7},{7,4},{8,9},{9,10},{10,1... | collective-permute-start | bytes 331784 | tf_op jit(solution)/shard_map/ppermute | solution.py:55
  159.5 1.6 collective-permute-start.28
  161.0 0.9 collective-permute-start.29
  161.9 2.5 %collective-permute-done.27 = f32[72,384]{1,0:T(8,128)S(1)} collective-permute-done((f32[72,384]{1,0:T(8,128)S(1)}, f32[72,384]{1,0:T(8,128)S(1)}, u32[]{:S(2)}, u32[]{:S(2)}) %collective-permute-start.27) | collective-permute-done | bytes 110624 | tf_op jit(solution)/shard_map/ppermute | solution.py:55
  164.4 4.3 %collective-permute-done.28 = f32[72,384]{1,0:T(8,128)S(1)} collective-permute-done((f32[72,384]{1,0:T(8,128)S(1)}, f32[72,384]{1,0:T(8,128)S(1)}, u32[]{:S(2)}, u32[]{:S(2)}) %collective-permute-start.28) | collective-permute-done | bytes 110624 | tf_op jit(solution)/shard_map/ppermute | solution.py:55
  169.7 1.3 collective-permute-done.30
  170.9 1.7 collective-permute-start.31
  173.3 1.1 collective-permute-start.33
  174.5 0.9 collective-permute-done.31
  175.3 2.4 %collective-permute-done.32 = f32[72,256]{1,0:T(8,128)S(1)} collective-permute-done((f32[72,256]{1,0:T(8,128)S(1)}, f32[72,256]{1,0:T(8,128)S(1)}, u32[]{:S(2)}, u32[]{:S(2)}) %collective-permute-start.32) | collective-permute-done | bytes 73760 | tf_op jit(solution)/shard_map/ppermute | solution.py:30
  178.7 1.3 collective-permute-done.34
  (76 shorter events, 13.4 us)
Async XLA Ops:
  0.6 119.2 %copy-start = (f32[384,64]{0,1:T(8,128)S(1)}, f32[384,64]{0,1:T(8,128)}, u32[]{:S(2)}) copy-start(f32[384,64]{0,1:T(8,128)} %param.5) | copy-start | bytes 294916
  0.6 23.6 %collective-permute-start.6 = (bf16[512,896]{1,0:T(8,128)(2,1)}, bf16[512,896]{1,0:T(8,128)(2,1)S(1)}, u32[]{:S(2)}, u32[]{:S(2)}) collective-permute-start(bf16[512,896]{1,0:T(8,128)(2,1)} %param.4), channel_id=1, source_target_pairs={{0,8},{4,12},{8,0},{12,4},{16,24},{20,28},{24,16},{28,20},{1,9},{5... | collective-permute-start | bytes 2752520 | tf_op jit(solution)/shard_map/ppermute | solution.py:30
  3.6 24.8 %collective-permute-start.7 = (bf16[512,896]{1,0:T(8,128)(2,1)}, bf16[512,896]{1,0:T(8,128)(2,1)S(1)}, u32[]{:S(2)}, u32[]{:S(2)}) collective-permute-start(bf16[512,896]{1,0:T(8,128)(2,1)} %param.4), channel_id=1, source_target_pairs={{0,16},{4,20},{8,24},{12,28},{16,0},{20,4},{24,8},{28,12},{1,17},{... | collective-permute-start | bytes 2752520 | tf_op jit(solution)/shard_map/ppermute | solution.py:30
  5.2 36.6 %collective-permute-start.1 = (bf16[384,1792]{1,0:T(8,128)(2,1)}, bf16[384,1792]{1,0:T(8,128)(2,1)S(1)}, u32[]{:S(2)}, u32[]{:S(2)}) collective-permute-start(bf16[384,1792]{1,0:T(8,128)(2,1)} %param.3), channel_id=1, source_target_pairs={{1,0},{2,1},{3,2},{5,4},{6,5},{7,6},{9,8},{10,9},{11,10},{13,12},{... | collective-permute-start | bytes 4128776 | tf_op jit(solution)/shard_map/ppermute | solution.py:104
  6.5 37.3 %collective-permute-start = (bf16[384,1792]{1,0:T(8,128)(2,1)}, bf16[384,1792]{1,0:T(8,128)(2,1)}, u32[]{:S(2)}, u32[]{:S(2)}) collective-permute-start(bf16[384,1792]{1,0:T(8,128)(2,1)} %param.3), channel_id=1, source_target_pairs={{0,1},{1,2},{2,3},{4,5},{5,6},{6,7},{8,9},{9,10},{10,11},{12,13},{... | collective-permute-start | bytes 4128776 | tf_op jit(solution)/shard_map/ppermute | solution.py:104
  12.2 34.6 %collective-permute-start.10 = (bf16[512,896]{1,0:T(8,128)(2,1)}, bf16[512,896]{1,0:T(8,128)(2,1)}, u32[]{:S(2)}, u32[]{:S(2)}) collective-permute-start(bf16[512,896]{1,0:T(8,128)(2,1)} %param.4), channel_id=1, source_target_pairs={{0,4},{4,0},{8,12},{12,8},{16,20},{20,16},{24,28},{28,24},{1,5},{5... | collective-permute-start | bytes 2752520 | tf_op jit(solution)/shard_map/ppermute | solution.py:30
  25.0 12.0 %collective-permute-start.8 = (bf16[256,896]{1,0:T(8,128)(2,1)}, bf16[256,896]{1,0:T(8,128)(2,1)}, u32[]{:S(2)}, u32[]{:S(2)}) collective-permute-start(bf16[256,896]{1,0:T(8,128)(2,1)} %slice.84), channel_id=1, source_target_pairs={{0,16},{4,20},{8,24},{12,28},{16,0},{20,4},{24,8},{28,12},{1,17},{... | collective-permute-start | bytes 1376264 | tf_op jit(solution)/shard_map/ppermute | solution.py:30
  29.3 5.4 %copy-start.2 = (bf16[512,896]{1,0:T(8,128)(2,1)S(1)}, bf16[512,896]{1,0:T(8,128)(2,1)}, u32[]{:S(2)}) copy-start(bf16[512,896]{1,0:T(8,128)(2,1)} %param.4) | copy-start | bytes 2752516
  29.3 11.4 %collective-permute-start.9 = (bf16[256,896]{1,0:T(8,128)(2,1)}, bf16[256,896]{1,0:T(8,128)(2,1)}, u32[]{:S(2)}, u32[]{:S(2)}) collective-permute-start(bf16[256,896]{1,0:T(8,128)(2,1)} %slice.85), channel_id=1, source_target_pairs={{0,8},{4,12},{8,0},{12,4},{16,24},{20,28},{24,16},{28,20},{1,9},{5... | collective-permute-start | bytes 1376264 | tf_op jit(solution)/shard_map/ppermute | solution.py:30
  37.1 16.7 %collective-permute-start.11 = (bf16[512,896]{1,0:T(8,128)(2,1)S(1)}, bf16[512,896]{1,0:T(8,128)(2,1)S(1)}, u32[]{:S(2)}, u32[]{:S(2)}) collective-permute-start(bf16[512,896]{1,0:T(8,128)(2,1)S(1)} %collective-permute-done.6), channel_id=1, source_target_pairs={{0,4},{4,0},{8,12},{12,8},{16,20},{20,16},{24,28},{28,24},{1,5},{5... | collective-permute-start | bytes 2752520 | tf_op jit(solution)/shard_map/ppermute | solution.py:30
  40.7 14.1 %collective-permute-start.12 = (bf16[512,896]{1,0:T(8,128)(2,1)S(1)}, bf16[512,896]{1,0:T(8,128)(2,1)S(1)}, u32[]{:S(2)}, u32[]{:S(2)}) collective-permute-start(bf16[512,896]{1,0:T(8,128)(2,1)S(1)} %collective-permute-done.7), channel_id=1, source_target_pairs={{0,4},{4,0},{8,12},{12,8},{16,20},{20,16},{24,28},{28,24},{1,5},{5... | collective-permute-start | bytes 2752520 | tf_op jit(solution)/shard_map/ppermute | solution.py:30
  41.8 14.1 %collective-permute-start.13 = (bf16[512,896]{1,0:T(8,128)(2,1)S(1)}, bf16[512,896]{1,0:T(8,128)(2,1)S(1)}, u32[]{:S(2)}, u32[]{:S(2)}) collective-permute-start(bf16[512,896]{1,0:T(8,128)(2,1)S(1)} %constant_dynamic-update-slice_fusion), channel_id=1, source_target_pairs={{0,4},{4,0},{8,12},{12,8},{16,20},{20,16},{24,28},{28,24},{1,5},{5... | collective-permute-start | bytes 2752520 | tf_op jit(solution)/shard_map/ppermute | solution.py:30
  43.8 34.0 %collective-permute-start.3 = (bf16[384,1792]{1,0:T(8,128)(2,1)S(1)}, bf16[384,1792]{1,0:T(8,128)(2,1)S(1)}, u32[]{:S(2)}, u32[]{:S(2)}) collective-permute-start(bf16[384,1792]{1,0:T(8,128)(2,1)S(1)} %collective-permute-done.1), channel_id=1, source_target_pairs={{1,0},{2,1},{3,2},{5,4},{6,5},{7,6},{9,8},{10,9},{11,10},{13,12},{... | collective-permute-start | bytes 4128776 | tf_op jit(solution)/shard_map/ppermute | solution.py:104
  46.8 34.7 %collective-permute-start.2 = (bf16[384,1792]{1,0:T(8,128)(2,1)}, bf16[384,1792]{1,0:T(8,128)(2,1)S(1)}, u32[]{:S(2)}, u32[]{:S(2)}) collective-permute-start(bf16[384,1792]{1,0:T(8,128)(2,1)} %collective-permute-done), channel_id=1, source_target_pairs={{0,1},{1,2},{2,3},{4,5},{5,6},{6,7},{8,9},{9,10},{10,11},{12,13},{... | collective-permute-start | bytes 4128776 | tf_op jit(solution)/shard_map/ppermute | solution.py:104
  64.3 22.0 %copy-start.1 = (bf16[384,1792]{1,0:T(8,128)(2,1)S(1)}, bf16[384,1792]{1,0:T(8,128)(2,1)}, u32[]{:S(2)}) copy-start(bf16[384,1792]{1,0:T(8,128)(2,1)} %param.3) | copy-start | bytes 4128772
  77.8 33.1 %collective-permute-start.5 = (bf16[384,1792]{1,0:T(8,128)(2,1)S(1)}, bf16[384,1792]{1,0:T(8,128)(2,1)S(1)}, u32[]{:S(2)}, u32[]{:S(2)}) collective-permute-start(bf16[384,1792]{1,0:T(8,128)(2,1)S(1)} %collective-permute-done.3), channel_id=1, source_target_pairs={{1,0},{2,1},{3,2},{5,4},{6,5},{7,6},{9,8},{10,9},{11,10},{13,12},{... | collective-permute-start | bytes 4128776 | tf_op jit(solution)/shard_map/ppermute | solution.py:104
  81.5 33.0 %collective-permute-start.4 = (bf16[384,1792]{1,0:T(8,128)(2,1)S(1)}, bf16[384,1792]{1,0:T(8,128)(2,1)S(1)}, u32[]{:S(2)}, u32[]{:S(2)}) collective-permute-start(bf16[384,1792]{1,0:T(8,128)(2,1)S(1)} %collective-permute-done.2), channel_id=1, source_target_pairs={{0,1},{1,2},{2,3},{4,5},{5,6},{6,7},{8,9},{9,10},{10,11},{12,13},{... | collective-permute-start | bytes 4128776 | tf_op jit(solution)/shard_map/ppermute | solution.py:104
  120.5 1.3 collective-permute-start.14
  121.9 4.4 %collective-permute-start.15 = (f32[72,256]{1,0:T(8,128)S(1)}, f32[72,256]{1,0:T(8,128)S(1)}, u32[]{:S(2)}, u32[]{:S(2)}) collective-permute-start(f32[72,256]{1,0:T(8,128)S(1)} %select_add_fusion.2), channel_id=1, source_target_pairs={{0,8},{4,12},{8,0},{12,4},{16,24},{20,28},{24,16},{28,20},{1,9},{5... | collective-permute-start | bytes 221192 | tf_op jit(solution)/shard_map/ppermute | solution.py:30
  123.6 5.2 %collective-permute-start.16 = (f32[72,256]{1,0:T(8,128)S(1)}, f32[72,256]{1,0:T(8,128)S(1)}, u32[]{:S(2)}, u32[]{:S(2)}) collective-permute-start(f32[72,256]{1,0:T(8,128)S(1)} %select_add_fusion.2), channel_id=1, source_target_pairs={{0,16},{4,20},{8,24},{12,28},{16,0},{20,4},{24,8},{28,12},{1,17},{... | collective-permute-start | bytes 221192 | tf_op jit(solution)/shard_map/ppermute | solution.py:30
  124.2 5.3 %collective-permute-start.17 = (f32[72,256]{1,0:T(8,128)S(1)}, f32[72,256]{1,0:T(8,128)S(1)}, u32[]{:S(2)}, u32[]{:S(2)}) collective-permute-start(f32[72,256]{1,0:T(8,128)S(1)} %select_add_fusion.2), channel_id=1, source_target_pairs={{0,24},{4,28},{8,16},{12,20},{16,8},{20,12},{24,0},{28,4},{1,25},{... | collective-permute-start | bytes 221192 | tf_op jit(solution)/shard_map/ppermute | solution.py:30
  129.5 1.3 collective-permute-start.18
  131.9 8.7 %collective-permute-start.19 = (f32[72,384]{1,0:T(8,128)S(1)}, f32[72,384]{1,0:T(8,128)S(1)}, u32[]{:S(2)}, u32[]{:S(2)}) collective-permute-start(f32[72,384]{1,0:T(8,128)S(1)} %pad_maximum_fusion.2), channel_id=1, source_target_pairs={{0,1},{1,2},{2,3},{3,0},{4,5},{5,6},{6,7},{7,4},{8,9},{9,10},{10,1... | collective-permute-start | bytes 331784 | tf_op jit(solution)/shard_map/ppermute | solution.py:55
  134.5 10.4 %collective-permute-start.20 = (f32[72,384]{1,0:T(8,128)S(1)}, f32[72,384]{1,0:T(8,128)S(1)}, u32[]{:S(2)}, u32[]{:S(2)}) collective-permute-start(f32[72,384]{1,0:T(8,128)S(1)} %pad_maximum_fusion.2), channel_id=1, source_target_pairs={{0,2},{1,3},{2,0},{3,1},{4,6},{5,7},{6,4},{7,5},{8,10},{9,11},{10,... | collective-permute-start | bytes 331784 | tf_op jit(solution)/shard_map/ppermute | solution.py:55
  137.2 7.6 %collective-permute-start.21 = (f32[72,384]{1,0:T(8,128)S(1)}, f32[72,384]{1,0:T(8,128)S(1)}, u32[]{:S(2)}, u32[]{:S(2)}) collective-permute-start(f32[72,384]{1,0:T(8,128)S(1)} %pad_maximum_fusion.2), channel_id=1, source_target_pairs={{0,3},{1,0},{2,1},{3,2},{4,7},{5,4},{6,5},{7,6},{8,11},{9,8},{10,9... | collective-permute-start | bytes 331784 | tf_op jit(solution)/shard_map/ppermute | solution.py:55
  145.7 1.3 collective-permute-start.22
  147.0 4.8 %collective-permute-start.23 = (f32[72,256]{1,0:T(8,128)S(1)}, f32[72,256]{1,0:T(8,128)S(1)}, u32[]{:S(2)}, u32[]{:S(2)}) collective-permute-start(f32[72,256]{1,0:T(8,128)S(1)} %select_add_fusion.1), channel_id=1, source_target_pairs={{0,8},{4,12},{8,0},{12,4},{16,24},{20,28},{24,16},{28,20},{1,9},{5... | collective-permute-start | bytes 221192 | tf_op jit(solution)/shard_map/ppermute | solution.py:30
  147.5 4.4 %collective-permute-start.24 = (f32[72,256]{1,0:T(8,128)S(1)}, f32[72,256]{1,0:T(8,128)S(1)}, u32[]{:S(2)}, u32[]{:S(2)}) collective-permute-start(f32[72,256]{1,0:T(8,128)S(1)} %select_add_fusion.1), channel_id=1, source_target_pairs={{0,16},{4,20},{8,24},{12,28},{16,0},{20,4},{24,8},{28,12},{1,17},{... | collective-permute-start | bytes 221192 | tf_op jit(solution)/shard_map/ppermute | solution.py:30
  148.8 5.3 %collective-permute-start.25 = (f32[72,256]{1,0:T(8,128)S(1)}, f32[72,256]{1,0:T(8,128)S(1)}, u32[]{:S(2)}, u32[]{:S(2)}) collective-permute-start(f32[72,256]{1,0:T(8,128)S(1)} %select_add_fusion.1), channel_id=1, source_target_pairs={{0,24},{4,28},{8,16},{12,20},{16,8},{20,12},{24,0},{28,4},{1,25},{... | collective-permute-start | bytes 221192 | tf_op jit(solution)/shard_map/ppermute | solution.py:30
  154.1 1.3 collective-permute-start.26
  156.6 7.8 %collective-permute-start.27 = (f32[72,384]{1,0:T(8,128)S(1)}, f32[72,384]{1,0:T(8,128)S(1)}, u32[]{:S(2)}, u32[]{:S(2)}) collective-permute-start(f32[72,384]{1,0:T(8,128)S(1)} %pad_maximum_fusion.3), channel_id=1, source_target_pairs={{0,1},{1,2},{2,3},{3,0},{4,5},{5,6},{6,7},{7,4},{8,9},{9,10},{10,1... | collective-permute-start | bytes 331784 | tf_op jit(solution)/shard_map/ppermute | solution.py:55
  159.5 9.2 %collective-permute-start.28 = (f32[72,384]{1,0:T(8,128)S(1)}, f32[72,384]{1,0:T(8,128)S(1)}, u32[]{:S(2)}, u32[]{:S(2)}) collective-permute-start(f32[72,384]{1,0:T(8,128)S(1)} %pad_maximum_fusion.3), channel_id=1, source_target_pairs={{0,2},{1,3},{2,0},{3,1},{4,6},{5,7},{6,4},{7,5},{8,10},{9,11},{10,... | collective-permute-start | bytes 331784 | tf_op jit(solution)/shard_map/ppermute | solution.py:55
  161.0 7.7 %collective-permute-start.29 = (f32[72,384]{1,0:T(8,128)S(1)}, f32[72,384]{1,0:T(8,128)S(1)}, u32[]{:S(2)}, u32[]{:S(2)}) collective-permute-start(f32[72,384]{1,0:T(8,128)S(1)} %pad_maximum_fusion.3), channel_id=1, source_target_pairs={{0,3},{1,0},{2,1},{3,2},{4,7},{5,4},{6,5},{7,6},{8,11},{9,8},{10,9... | collective-permute-start | bytes 331784 | tf_op jit(solution)/shard_map/ppermute | solution.py:55
  169.6 1.3 collective-permute-start.30
  170.9 4.4 %collective-permute-start.31 = (f32[72,256]{1,0:T(8,128)S(1)}, f32[72,256]{1,0:T(8,128)S(1)}, u32[]{:S(2)}, u32[]{:S(2)}) collective-permute-start(f32[72,256]{1,0:T(8,128)S(1)} %select_add_fusion), channel_id=1, source_target_pairs={{0,8},{4,12},{8,0},{12,4},{16,24},{20,28},{24,16},{28,20},{1,9},{5... | collective-permute-start | bytes 221192 | tf_op jit(solution)/shard_map/ppermute | solution.py:30
  172.6 5.1 %collective-permute-start.32 = (f32[72,256]{1,0:T(8,128)S(1)}, f32[72,256]{1,0:T(8,128)S(1)}, u32[]{:S(2)}, u32[]{:S(2)}) collective-permute-start(f32[72,256]{1,0:T(8,128)S(1)} %select_add_fusion), channel_id=1, source_target_pairs={{0,16},{4,20},{8,24},{12,28},{16,0},{20,4},{24,8},{28,12},{1,17},{... | collective-permute-start | bytes 221192 | tf_op jit(solution)/shard_map/ppermute | solution.py:30
  173.3 5.3 %collective-permute-start.33 = (f32[72,256]{1,0:T(8,128)S(1)}, f32[72,256]{1,0:T(8,128)S(1)}, u32[]{:S(2)}, u32[]{:S(2)}) collective-permute-start(f32[72,256]{1,0:T(8,128)S(1)} %select_add_fusion), channel_id=1, source_target_pairs={{0,24},{4,28},{8,16},{12,20},{16,8},{20,12},{24,0},{28,4},{1,25},{... | collective-permute-start | bytes 221192 | tf_op jit(solution)/shard_map/ppermute | solution.py:30
  178.6 1.3 collective-permute-start.34

commit v2 on v1

v2 whole, which is shorter than its diff:
```python
import jax
import jax.numpy as jnp
from jax import lax
from jax.experimental import pallas as pl
from jax.experimental.pallas import tpu as pltpu
from jax.sharding import PartitionSpec as P

ITERS = 2
SPREAD = 10690

ridge_scale = 0.002


def squares(block):
    return jnp.sum(jnp.square(block.astype(jnp.float32)), axis=1)


def cross_piece(left, right):
    return lax.dot_general(
        left, right, (((1,), (1,)), ((), ())), preferred_element_type=jnp.float32
    )


def times(left, right, contract):
    return lax.dot_general(
        left, right, ((contract[:1], contract[1:]), ((), ())), precision=lax.Precision.HIGHEST
    )


TO_MIDDLE = [(0, 1), (3, 2)]
ACROSS = [(1, 2), (2, 1)]
TO_END = [(1, 0), (2, 3)]


def flipped(block, bits):
    return lax.ppermute(block, "proof", [(i, i ^ bits) for i in range(8)])


def sum_rows_axis(block):
    odd = lax.axis_index("proof") % 2
    half = block.shape[1] // 2
    low, high = block[:, :half], block[:, half:]
    mine, other = jnp.where(odd == 0, low, high), jnp.where(odd == 0, high, low)
    mine = mine + flipped(other, 1)
    mine = mine + flipped(mine, 2) + flipped(mine, 4) + flipped(mine, 6)
    other = flipped(mine, 1)
    low, high = jnp.where(odd == 0, mine, other), jnp.where(odd == 0, other, mine)
    return jnp.concatenate([low, high], axis=1)


def sum_middle(block):
    return block + lax.ppermute(block, "landmark", ACROSS)


def packed(block, *vectors):
    rows = jnp.stack(vectors)
    rows = jnp.pad(rows, ((0, 8 - rows.shape[0]), (0, block.shape[1] - rows.shape[1])))
    return jnp.concatenate([block, rows], axis=0)


def plane_pieces(piece):
    half = piece.shape[0] // 2
    across_x, across_y = flipped(piece, 2), flipped(piece, 4)
    corner_low, corner_high = flipped(across_x[:half], 4), flipped(across_y[half:], 2)
    found = [(0, 0, piece), (2, 0, across_x), (4, 0, across_y), (6, 0, corner_low), (6, half, corner_high)]
    return found + [(bits + 1, row, flipped(block, 1)) for bits, row, block in found]


def kernel_block(rows, landmarks, columns):
    n, count = columns.shape[1], columns.shape[0]
    m = max(row + block.shape[0] for _, row, block in landmarks)
    width = rows[0][2].shape[1]
    part = landmarks[0][2].shape[1]
    tile = 256
    place = jnp.stack([lax.axis_index("proof"), lax.axis_index("landmark")]).astype(jnp.int32)

    def body(place_ref, columns_ref, *refs):
        row_refs, landmark_refs = refs[: len(rows)], refs[len(rows) : len(rows) + len(landmarks)]
        kernel_ref, sums_ref, rows_s, land_s, cross_s, norm_s, row_sem, land_sem = refs[len(rows) + len(landmarks) :]
        p, z = place_ref[0], place_ref[1]
        for (bits, row, block), ref in zip(rows, row_refs):
            slot = z ^ bits
            pltpu.make_async_copy(ref, rows_s.at[slot, pl.ds(row, block.shape[0])], row_sem.at[slot]).start()
        for (bits, row, block), ref in zip(landmarks, landmark_refs):
            f = p ^ bits
            lane = pl.multiple_of((f % 2) * part, 128)
            target = land_s.at[f // 2, pl.ds(row, block.shape[0]), pl.ds(lane, part)]
            pltpu.make_async_copy(ref, target, land_sem.at[f // 2]).start()
        cross_s[...] = jnp.zeros_like(cross_s)
        norm_s[...] = jnp.zeros_like(norm_s)
        row_norm = jnp.zeros((n, 128), jnp.float32)
        for b in range(4):
            pltpu.make_async_copy(rows_s.at[b], rows_s.at[b], row_sem.at[b]).wait()
            pltpu.make_async_copy(land_s.at[b], land_s.at[b], land_sem.at[b]).wait()
            for j in range(width // 128):
                x = rows_s[b, :, j * 128 : (j + 1) * 128].astype(jnp.float32)
                row_norm = row_norm + x * x

            @pl.loop(0, m // tile)
            def _(t):
                start = pl.multiple_of(t * tile, tile)
                cross_s[t] += lax.dot_general(
                    rows_s[b], land_s[b, pl.ds(start, tile)], (((1,), (1,)), ((), ())),
                    preferred_element_type=jnp.float32,
                )
                total = norm_s[pl.ds(start, tile)]
                for j in range(width // 128):
                    x = land_s[b, pl.ds(start, tile), j * 128 : (j + 1) * 128].astype(jnp.float32)
                    total = total + x * x
                norm_s[pl.ds(start, tile)] = total

        row_norm = jnp.sum(row_norm, axis=1, keepdims=True)
        for t in range(m // tile):
            inside = slice(t * tile, (t + 1) * tile)
            landmark_norm = lax.dot_general(
                jnp.ones((8, 128), jnp.float32), norm_s[inside], (((1,), (1,)), ((), ())),
                precision=lax.Precision.HIGHEST,
            )[:1]
            k = jnp.exp(-(row_norm + landmark_norm - 2.0 * cross_s[t]) / SPREAD)
            kernel_ref[:, inside] = k
            sums_ref[:count, inside] = jnp.dot(columns_ref[...], k, precision=lax.Precision.HIGHEST)
            sums_ref[count:, inside] = jnp.broadcast_to(jnp.sum(k * k, axis=0, keepdims=True), (8, tile))

    any_spec = pl.BlockSpec(memory_space=pl.ANY)
    vmem = pl.BlockSpec(memory_space=pltpu.VMEM)
    blocks = [block for _, _, block in rows] + [block for _, _, block in landmarks]
    return pl.pallas_call(
        body,
        out_shape=(
            jax.ShapeDtypeStruct((n, m), jnp.float32),
            jax.ShapeDtypeStruct((count + 8, m), jnp.float32),
        ),
        in_specs=[pl.BlockSpec(memory_space=pltpu.SMEM), vmem] + [any_spec] * len(blocks),
        out_specs=(vmem, vmem),
        scratch_shapes=[
            pltpu.VMEM((4, n, width), jnp.bfloat16),
            pltpu.VMEM((4, m, width), jnp.bfloat16),
            pltpu.VMEM((m // tile, n, tile), jnp.float32),
            pltpu.VMEM((m, 128), jnp.float32),
            pltpu.SemaphoreType.DMA((4,)),
            pltpu.SemaphoreType.DMA((4,)),
        ],
        compiler_params=pltpu.CompilerParams(vmem_limit_bytes=48 << 20),
        name="kernel_block",
    )(place, columns, *blocks)


def middle_kernel(row_features, landmark_features, columns):
    half = row_features.shape[0] // 2
    end_landmarks = lax.ppermute(landmark_features, "landmark", TO_MIDDLE)
    end_top = lax.ppermute(row_features[:half], "landmark", TO_MIDDLE)
    middle_rows = lax.ppermute(row_features, "landmark", ACROSS)
    bottom, end_top = lax.optimization_barrier((row_features[half:], end_top))
    end_bottom = lax.ppermute(bottom, "landmark", TO_MIDDLE)
    far_top = lax.ppermute(end_top, "landmark", ACROSS)
    far_bottom = lax.ppermute(end_bottom, "landmark", ACROSS)
    rows = [
        (0, 0, row_features), (3, 0, middle_rows), (1, 0, end_top), (1, half, end_bottom),
        (2, 0, far_top), (2, half, far_bottom),
    ]
    landmarks = plane_pieces(landmark_features)
    shift = landmark_features.shape[0]
    landmarks += [(bits, row + shift, block) for bits, row, block in plane_pieces(end_landmarks)]
    return kernel_block(rows, landmarks, columns)


def conjugate_gradients(kernel, sums, columns, lam, sum_rows, sum_landmarks):
    count = columns.shape[0]
    residual, precond = sums[:count], lam + sums[count]
    coefficient = jnp.zeros_like(residual)
    inner = None
    for iteration in range(ITERS):
        scaled = residual / precond
        part = times(scaled, kernel, (1, 1))
        dots = [jnp.sum(residual * scaled, axis=1), jnp.sum(scaled * scaled, axis=1)]
        if iteration > 0:
            dots.append(jnp.sum(scaled * direction, axis=1))
        sums = sum_landmarks(packed(part, *dots))
        inner_next, square = sums[count, :count], sums[count + 1, :count]
        if iteration == 0:
            direction, image, length = scaled, sums[:count], square
        else:
            beta = inner_next / inner
            length = square + beta * (2.0 * sums[count + 2, :count] + beta * length)
            direction = scaled + beta[:, None] * direction
            image = sums[:count] + beta[:, None] * image
        inner = inner_next
        sums = sum_rows(packed(times(image, kernel, (1, 0)), jnp.sum(image * image, axis=1)))
        gradient = sums[:count] + lam * direction
        step_size = (inner / (sums[count, :count] + lam * length))[:, None]
        coefficient = coefficient + step_size * direction
        residual = residual - step_size * gradient
    return coefficient, residual


def folded(row_features, landmark_features, targets):
    lam = ridge_scale * row_features.shape[0] * lax.axis_size("proof")
    columns = targets.T
    kernel, sums = middle_kernel(row_features, landmark_features, columns)
    sums = sum_rows_axis(sums)
    coefficient, residual = conjugate_gradients(kernel, sums, columns, lam, sum_rows_axis, sum_middle)
    both = jnp.concatenate([coefficient, residual], axis=0)
    half = both.shape[1] // 2
    received = lax.ppermute(both[:, half:], "landmark", TO_END)
    z = lax.axis_index("landmark")
    both = jnp.where((z == 1) | (z == 2), both[:, :half], received)
    return both[: columns.shape[0]].T, both[columns.shape[0] :].T


def plain(row_features, landmark_features, targets):
    lam = ridge_scale * row_features.shape[0] * lax.axis_size("proof")
    columns = targets.T
    rows = lax.all_gather(row_features, "landmark", axis=1, tiled=True)
    whole = lax.all_gather(landmark_features, "proof", axis=1, tiled=True)
    kernel = jnp.exp(-(squares(rows)[:, None] + squares(whole)[None, :] - 2.0 * cross_piece(rows, whole)) / SPREAD)
    sum_rows = lambda block: lax.psum(block, "proof")
    sums = sum_rows(packed(times(columns, kernel, (1, 0)), jnp.sum(kernel * kernel, axis=0)))
    sum_landmarks = lambda block: lax.psum(block, "landmark")
    coefficient, residual = conjugate_gradients(kernel, sums, columns, lam, sum_rows, sum_landmarks)
    return coefficient.T, residual.T


def solution(mesh):
    placed = (P("proof", "landmark"), P("landmark", "proof"), P("proof", None))
    four_planes = mesh.shape["proof"] == 8 and mesh.shape["landmark"] == 4
    return jax.shard_map(
        folded if four_planes else plain,
        mesh=mesh,
        in_specs=placed,
        out_specs=(P("landmark", None), P("landmark", None)),
        check_vma=False,
    )
```

time: 182 us -> 193 us (1.060)
  waiting for transfers between devices: 79.5 us -> 118 us
  Pallas kernels: 0 us -> 20.1 us
  matrix products: 21 us -> 5.36 us
  local copies, waits for them, and re-layouts: 17.4 us -> 6.13 us
  starting transfers between devices: 50.4 us -> 40.3 us
  other arithmetic: 11.6 us -> 1.52 us
    ppermute x35 -> x42, waiting for transfers between devices: 79.5 us -> 118 us  [the longest x33 59.5 us: flipped(): return lax.ppermute(block, 'proof', [(i, i ^ bits) for i in range(8)])]
    pallas_call x0 -> x1, Pallas kernels: none -> 20.1 us  [kernel_block(): pl.pallas_call(body, out_shape=(jax.ShapeDtypeStruct((n, m), jnp.float32)...]
    dot_general x7 -> x0, matrix products: 17.4 us -> none  [cross_piece(): lax.dot_general(left, right, (((1,), (1,)), ((), ())), preferred_element_...]
    ppermute x35 -> x42, starting transfers between devices: 50.4 us -> 40.3 us  [the longest x33 23.5 us: flipped(): return lax.ppermute(block, 'proof', [(i, i ^ bits) for i in range(8)])]
    dynamic_update_slice x8 -> x0, local copies, waits for them, and re-layouts: 9.74 us -> none  [gathered_landmarks(): lax.dynamic_update_slice(whole, part, (0, (me ^ bits) * piece.shape[1]))]
    reduce_sum x12 -> x4, other arithmetic: 10.4 us -> 0.71 us  [the longest x2 0.42 us: conjugate_gradients(): jnp.sum(residual * scaled, axis=1)]
    broadcast_in_dim x1 -> x0, local copies, waits for them, and re-layouts: 3.86 us -> none  [gathered_landmarks(): whole = jnp.zeros((piece.shape[0], piece.shape[1] * size), piece.dtype)]
    slice x2 -> x5, local copies, waits for them, and re-layouts: 1.62 us -> 3.58 us  [the longest x1 1.4 us: middle_kernel(): end_top = lax.ppermute(row_features[:half], 'landmark', TO_MIDDLE)]
  transfers between devices with their start and end apart: 35 -> 42, of which waited for: 24 -> 24; matrix products, arithmetic and copies ran while one was open for 22% -> 2% of each run, Pallas kernels for 0% -> 0%
where the time goes in v2:
time: 193 us
  waiting for transfers between devices  118 us (61%)
  starting transfers between devices  40.3 us (21%)
  Pallas kernels  20.1 us (10%)
  local copies, waits for them, and re-layouts  6.13 us (3%)
  matrix products  5.36 us (3%)
    ppermute x33, waiting for transfers between devices, flipped(): return lax.ppermute(block, 'proof', [(i, i ^ bits) for i in range(8)])  59.5 us
    ppermute x1, waiting for transfers between devices, folded(): received = lax.ppermute(both[:, half:], 'landmark', TO_END)  36.7 us
    ppermute x33, starting transfers between devices, flipped(): return lax.ppermute(block, 'proof', [(i, i ^ bits) for i in range(8)])  23.5 us
    pallas_call x1, Pallas kernels, kernel_block(): pl.pallas_call(body, out_shape=(jax.ShapeDtypeStruct((n, m), jnp.float32)...  20.1 us
    ppermute x1, waiting for transfers between devices, middle_kernel(): end_bottom = lax.ppermute(bottom, 'landmark', TO_MIDDLE)  11.8 us
    ppermute x1, waiting for transfers between devices, middle_kernel(): end_landmarks = lax.ppermute(landmark_features, 'landmark', TO_MIDDLE)  10.2 us
    ppermute x1, starting transfers between devices, middle_kernel(): end_bottom = lax.ppermute(bottom, 'landmark', TO_MIDDLE)  6.25 us
    dot_general x4, matrix products, times(): lax.dot_general(left, right, ((contract[:1], contract[1:]), ((), ())), pr...  5.36 us
  transfers between devices with their start and end apart: 42, of which 24 were waited for; matrix products, arithmetic and copies ran while one was open for 2% of the time, Pallas kernels for 0%

profile of v2, /device:TPU:0, one launch (start us, length us, event | category | flops | bytes accessed | tf_op | source)
XLA Modules:
  0.0 192.8 jit_solution(12648524526977433957)
XLA Ops:
  0.7 0.5 collective-permute-start.9
  1.2 2.6 %collective-permute-start.6 = (bf16[512,896]{1,0:T(8,128)(2,1)}, bf16[512,896]{1,0:T(8,128)(2,1)S(1)}, u32[]{:S(2)}, u32[]{:S(2)}) collective-permute-start(bf16[512,896]{1,0:T(8,128)(2,1)} %refs_6_.1), channel_id=1, source_target_pairs={{0,16},{4,20},{8,24},{12,28},{16,0},{20,4},{24,8},{28,12},{1,17},{... | collective-permute-start | bytes 2752520 | tf_op jit(solution)/shard_map/ppermute | solution.py:36
  3.8 1.5 collective-permute-start.5
  5.3 1.4 fusion.27
  6.7 3.5 %collective-permute-start.1 = (bf16[192,1792]{1,0:T(8,128)(2,1)S(1)}, bf16[192,1792]{1,0:T(8,128)(2,1)S(1)}, u32[]{:S(2)}, u32[]{:S(2)}) collective-permute-start(bf16[192,1792]{1,0:T(8,128)(2,1)S(1)} %get-tuple-element.17), channel_id=1, source_target_pairs={{0,1},{3,2},{4,5},{7,6},{8,9},{11,10},{12,13},{15,14},{16,17},{19,... | collective-permute-start | bytes 2064392 | tf_op jit(solution)/shard_map/ppermute | solution.py:151
  10.2 1.3 collective-permute-start.14
  11.6 13.4 %collective-permute-done.6.refs_8_ = bf16[512,896]{1,0:T(8,128)(2,1)S(1)} collective-permute-done((bf16[512,896]{1,0:T(8,128)(2,1)}, bf16[512,896]{1,0:T(8,128)(2,1)S(1)}, u32[]{:S(2)}, u32[]{:S(2)}) %collective-permute-start.6) | collective-permute-done | bytes 917536 | tf_op jit(solution)/shard_map/ppermute | solution.py:36
  24.9 0.7 collective-permute-start
  25.7 0.7 collective-permute-done.5.refs_7_
  26.4 1.5 collective-permute-start.8
  27.9 1.2 collective-permute-start.7
  29.2 6.2 %collective-permute-start.2 = (bf16[192,1792]{1,0:T(8,128)(2,1)S(1)}, bf16[192,1792]{1,0:T(8,128)(2,1)S(1)}, u32[]{:S(2)}, u32[]{:S(2)}) collective-permute-start(bf16[192,1792]{1,0:T(8,128)(2,1)S(1)} %get-tuple-element.7), channel_id=1, source_target_pairs={{0,1},{3,2},{4,5},{7,6},{8,9},{11,10},{12,13},{15,14},{16,17},{19,... | collective-permute-start | bytes 2064392 | tf_op jit(solution)/shard_map/ppermute | solution.py:154
  35.4 10.2 %collective-permute-done.14.refs_16_ = bf16[512,896]{1,0:T(8,128)(2,1)S(1)} collective-permute-done((bf16[512,896]{1,0:T(8,128)(2,1)S(1)}, bf16[512,896]{1,0:T(8,128)(2,1)S(1)}, u32[]{:S(2)}, u32[]{:S(2)}) %collective-permute-start.14) | collective-permute-done | bytes 917536 | tf_op jit(solution)/shard_map/ppermute | solution.py:150
  45.6 0.7 collective-permute-start.3
  46.3 0.6 collective-permute-start.16
  46.9 0.5 collective-permute-start.15
  47.4 11.8 %collective-permute-done.2.refs_3_ = bf16[192,1792]{1,0:T(8,128)(2,1)S(1)} collective-permute-done((bf16[192,1792]{1,0:T(8,128)(2,1)S(1)}, bf16[192,1792]{1,0:T(8,128)(2,1)S(1)}, u32[]{:S(2)}, u32[]{:S(2)}) %collective-permute-start.2) | collective-permute-done | bytes 688160 | tf_op jit(solution)/shard_map/ppermute | solution.py:154
  59.3 0.5 collective-permute-start.10
  59.9 6.8 %collective-permute-done.16.refs_18_ = bf16[512,896]{1,0:T(8,128)(2,1)} collective-permute-done((bf16[512,896]{1,0:T(8,128)(2,1)S(1)}, bf16[512,896]{1,0:T(8,128)(2,1)}, u32[]{:S(2)}, u32[]{:S(2)}) %collective-permute-start.16) | collective-permute-done | bytes 917536 | tf_op jit(solution)/shard_map/ppermute | solution.py:36
  66.9 0.3 collective-permute-start.12
  67.2 1.1 slice.119
  68.3 1.1 slice.118
  69.3 0.6 collective-permute-start.18
  70.0 1.2 collective-permute-start.17
  71.2 0.8 copy-done
  72.0 0.5 collective-permute-start.20
  72.5 1.5 collective-permute-start.4
  74.0 8.1 %collective-permute-done.18.refs_20_ = bf16[256,896]{1,0:T(8,128)(2,1)} collective-permute-done((bf16[256,896]{1,0:T(8,128)(2,1)S(1)}, bf16[256,896]{1,0:T(8,128)(2,1)}, u32[]{:S(2)}, u32[]{:S(2)}) %collective-permute-start.18) | collective-permute-done | bytes 458784 | tf_op jit(solution)/shard_map/ppermute | solution.py:36
  82.4 0.3 collective-permute-start.22
  82.8 1.6 collective-permute-done.23.refs_25_
  84.3 0.7 collective-permute-done.22.refs_24_
  85.0 1.0 copy-done.1
  86.0 20.1 %kernel_block.1 = (f32[384,1024]{1,0:T(8,128)}, f32[72,1024]{1,0:T(8,128)S(1)}) custom-call(s32[2]{0:T(128)S(1)} %pad_add_fusion.place_ref, f32[64,384]{1,0:T(8,128)S(1)} %bitcast.70, bf16[384,1792]{1,0:T(8,128)(2,1)} %refs_0_.1, bf16[384,1792]{1,0:T(8,128)(2,1)} %copy-done.7, bf16[192,1792]{1,0:T(8,128)(2,1)S(1)} %collective-permute-done.1.refs_2_, ...), custom_call_target="tpu_custom_call" | custom-call | tf_op jit(solution)/shard_map/kernel_block/pallas_call | solution.py:127
  106.4 1.2 collective-permute-done.24
  107.6 2.9 %collective-permute-start.27 = (f32[72,512]{1,0:T(8,128)S(1)}, f32[72,512]{1,0:T(8,128)S(1)}, u32[]{:S(2)}, u32[]{:S(2)}) collective-permute-start(f32[72,512]{1,0:T(8,128)S(1)} %select_add_fusion.2), channel_id=1, source_target_pairs={{0,24},{4,28},{8,16},{12,20},{16,8},{20,12},{24,0},{28,4},{1,25},{... | collective-permute-start | bytes 442376 | tf_op jit(solution)/shard_map/ppermute | solution.py:36
  110.5 0.7 collective-permute-start.25
  111.2 3.9 %collective-permute-done.27 = f32[72,512]{1,0:T(8,128)S(1)} collective-permute-done((f32[72,512]{1,0:T(8,128)S(1)}, f32[72,512]{1,0:T(8,128)S(1)}, u32[]{:S(2)}, u32[]{:S(2)}) %collective-permute-start.27) | collective-permute-done | bytes 147488 | tf_op jit(solution)/shard_map/ppermute | solution.py:36
  115.1 2.7 %collective-permute-done.26 = f32[72,512]{1,0:T(8,128)S(1)} collective-permute-done((f32[72,512]{1,0:T(8,128)S(1)}, f32[72,512]{1,0:T(8,128)S(1)}, u32[]{:S(2)}, u32[]{:S(2)}) %collective-permute-start.26) | collective-permute-done | bytes 147488 | tf_op jit(solution)/shard_map/ppermute | solution.py:36
  117.8 0.5 collective-permute-done.25
  118.4 1.4 collective-permute-done.28
  120.0 1.6 fusion.28
  121.6 0.8 collective-permute-start.29
  122.6 1.1 fusion.9
  123.9 1.2 collective-permute-done.30
  125.2 1.5 collective-permute-start.33
  126.7 1.4 collective-permute-start.32
  128.0 0.7 collective-permute-start.31
  128.8 4.1 %collective-permute-done.33 = f32[72,512]{1,0:T(8,128)S(1)} collective-permute-done((f32[72,512]{1,0:T(8,128)S(1)}, f32[72,512]{1,0:T(8,128)S(1)}, u32[]{:S(2)}, u32[]{:S(2)}) %collective-permute-start.33) | collective-permute-done | bytes 147488 | tf_op jit(solution)/shard_map/ppermute | solution.py:36
  132.9 2.3 %collective-permute-done.32 = f32[72,512]{1,0:T(8,128)S(1)} collective-permute-done((f32[72,512]{1,0:T(8,128)S(1)}, f32[72,512]{1,0:T(8,128)S(1)}, u32[]{:S(2)}, u32[]{:S(2)}) %collective-permute-start.32) | collective-permute-done | bytes 147488 | tf_op jit(solution)/shard_map/ppermute | solution.py:36
  135.4 1.4 collective-permute-done.34
  136.8 0.3 multiply_reduce_fusion.2
  137.0 1.6 fusion.25
  138.7 0.7 collective-permute-start.35
  139.4 1.1 fusion.12
  140.9 1.2 collective-permute-done.36
  142.2 1.5 collective-permute-start.39
  143.7 1.4 collective-permute-start.38
  145.1 0.7 collective-permute-start.37
  145.8 4.1 %collective-permute-done.39 = f32[72,512]{1,0:T(8,128)S(1)} collective-permute-done((f32[72,512]{1,0:T(8,128)S(1)}, f32[72,512]{1,0:T(8,128)S(1)}, u32[]{:S(2)}, u32[]{:S(2)}) %collective-permute-start.39) | collective-permute-done | bytes 147488 | tf_op jit(solution)/shard_map/ppermute | solution.py:36
  149.9 2.3 %collective-permute-done.38 = f32[72,512]{1,0:T(8,128)S(1)} collective-permute-done((f32[72,512]{1,0:T(8,128)S(1)}, f32[72,512]{1,0:T(8,128)S(1)}, u32[]{:S(2)}, u32[]{:S(2)}) %collective-permute-start.38) | collective-permute-done | bytes 147488 | tf_op jit(solution)/shard_map/ppermute | solution.py:36
  152.4 1.4 collective-permute-done.40
  154.0 1.3 collective-permute-start.41
  155.3 36.7 %collective-permute-done.41 = f32[128,512]{1,0:T(8,128)S(1)} collective-permute-done((f32[128,512]{1,0:T(8,128)S(1)}, f32[128,512]{1,0:T(8,128)S(1)}, u32[]{:S(2)}, u32[]{:S(2)}) %collective-permute-start.41) | collective-permute-done | bytes 262176 | tf_op jit(solution)/shard_map/ppermute | solution.py:204
  192.1 0.7 slice_bitcast_fusion
  (89 shorter events, 2.9 us)
Async XLA Ops:
  0.6 9.6 %copy-start.8 = (bf16[512,896]{1,0:T(8,128)(2,1)S(1)}, bf16[512,896]{1,0:T(8,128)(2,1)}, u32[]{:S(2)}) copy-start(bf16[512,896]{1,0:T(8,128)(2,1)} %refs_6_.1) | copy-start | bytes 2752516
  0.6 24.3 %copy-start.4 = (bf16[384,1792]{1,0:T(8,128)(2,1)S(1)}, bf16[384,1792]{1,0:T(8,128)(2,1)}, u32[]{:S(2)}) copy-start(bf16[384,1792]{1,0:T(8,128)(2,1)} %refs_0_.1) | copy-start | bytes 4128772
  0.7 28.5 %collective-permute-start.9 = (bf16[512,896]{1,0:T(8,128)(2,1)}, bf16[512,896]{1,0:T(8,128)(2,1)}, u32[]{:S(2)}, u32[]{:S(2)}) collective-permute-start(bf16[512,896]{1,0:T(8,128)(2,1)} %refs_6_.1), channel_id=1, source_target_pairs={{0,4},{4,0},{8,12},{12,8},{16,20},{20,16},{24,28},{28,24},{1,5},{5... | collective-permute-start | bytes 2752520 | tf_op jit(solution)/shard_map/ppermute | solution.py:36
  1.2 23.7 %collective-permute-start.6 = (bf16[512,896]{1,0:T(8,128)(2,1)}, bf16[512,896]{1,0:T(8,128)(2,1)S(1)}, u32[]{:S(2)}, u32[]{:S(2)}) collective-permute-start(bf16[512,896]{1,0:T(8,128)(2,1)} %refs_6_.1), channel_id=1, source_target_pairs={{0,16},{4,20},{8,24},{12,28},{16,0},{20,4},{24,8},{28,12},{1,17},{... | collective-permute-start | bytes 2752520 | tf_op jit(solution)/shard_map/ppermute | solution.py:36
  3.8 22.6 %collective-permute-start.5 = (bf16[512,896]{1,0:T(8,128)(2,1)}, bf16[512,896]{1,0:T(8,128)(2,1)S(1)}, u32[]{:S(2)}, u32[]{:S(2)}) collective-permute-start(bf16[512,896]{1,0:T(8,128)(2,1)} %refs_6_.1), channel_id=1, source_target_pairs={{0,8},{4,12},{8,0},{12,4},{16,24},{20,28},{24,16},{28,20},{1,9},{5... | collective-permute-start | bytes 2752520 | tf_op jit(solution)/shard_map/ppermute | solution.py:36
  6.7 21.3 %collective-permute-start.1 = (bf16[192,1792]{1,0:T(8,128)(2,1)S(1)}, bf16[192,1792]{1,0:T(8,128)(2,1)S(1)}, u32[]{:S(2)}, u32[]{:S(2)}) collective-permute-start(bf16[192,1792]{1,0:T(8,128)(2,1)S(1)} %get-tuple-element.17), channel_id=1, source_target_pairs={{0,1},{3,2},{4,5},{7,6},{8,9},{11,10},{12,13},{15,14},{16,17},{19,... | collective-permute-start | bytes 2064392 | tf_op jit(solution)/shard_map/ppermute | solution.py:151
  10.2 35.4 %collective-permute-start.14 = (bf16[512,896]{1,0:T(8,128)(2,1)S(1)}, bf16[512,896]{1,0:T(8,128)(2,1)S(1)}, u32[]{:S(2)}, u32[]{:S(2)}) collective-permute-start(bf16[512,896]{1,0:T(8,128)(2,1)S(1)} %copy-done.8), channel_id=1, source_target_pairs={{0,1},{3,2},{4,5},{7,6},{8,9},{11,10},{12,13},{15,14},{16,17},{19,... | collective-permute-start | bytes 2752520 | tf_op jit(solution)/shard_map/ppermute | solution.py:150
  24.9 44.4 %copy-start.5 = (bf16[512,896]{1,0:T(8,128)(2,1)}, bf16[512,896]{1,0:T(8,128)(2,1)S(1)}, u32[]{:S(2)}) copy-start(bf16[512,896]{1,0:T(8,128)(2,1)S(1)} %collective-permute-done.6.refs_8_) | copy-start | bytes 2752516
  24.9 34.9 %collective-permute-start = (bf16[384,1792]{1,0:T(8,128)(2,1)S(1)}, bf16[384,1792]{1,0:T(8,128)(2,1)S(1)}, u32[]{:S(2)}, u32[]{:S(2)}) collective-permute-start(bf16[384,1792]{1,0:T(8,128)(2,1)S(1)} %copy-done.4), channel_id=1, source_target_pairs={{1,2},{2,1},{5,6},{6,5},{9,10},{10,9},{13,14},{14,13},{17,18},{18,... | collective-permute-start | bytes 4128776 | tf_op jit(solution)/shard_map/ppermute | solution.py:152
  25.7 59.3 %copy-start.2 = (f32[384,64]{0,1:T(8,128)S(1)}, f32[384,64]{0,1:T(8,128)}, u32[]{:S(2)}) copy-start(f32[384,64]{0,1:T(8,128)} %param.5) | copy-start | bytes 294916
  26.4 46.1 %copy-start.6 = (bf16[512,896]{1,0:T(8,128)(2,1)}, bf16[512,896]{1,0:T(8,128)(2,1)S(1)}, u32[]{:S(2)}) copy-start(bf16[512,896]{1,0:T(8,128)(2,1)S(1)} %collective-permute-done.5.refs_7_) | copy-start | bytes 2752516
  26.4 19.9 %collective-permute-start.8 = (bf16[256,896]{1,0:T(8,128)(2,1)S(1)}, bf16[256,896]{1,0:T(8,128)(2,1)S(1)}, u32[]{:S(2)}, u32[]{:S(2)}) collective-permute-start(bf16[256,896]{1,0:T(8,128)(2,1)S(1)} %slice.117), channel_id=1, source_target_pairs={{0,8},{4,12},{8,0},{12,4},{16,24},{20,28},{24,16},{28,20},{1,9},{5... | collective-permute-start | bytes 1376264 | tf_op jit(solution)/shard_map/ppermute | solution.py:36
  27.9 19.0 %collective-permute-start.7 = (bf16[256,896]{1,0:T(8,128)(2,1)S(1)}, bf16[256,896]{1,0:T(8,128)(2,1)S(1)}, u32[]{:S(2)}, u32[]{:S(2)}) collective-permute-start(bf16[256,896]{1,0:T(8,128)(2,1)S(1)} %slice.116), channel_id=1, source_target_pairs={{0,16},{4,20},{8,24},{12,28},{16,0},{20,4},{24,8},{28,12},{1,17},{... | collective-permute-start | bytes 1376264 | tf_op jit(solution)/shard_map/ppermute | solution.py:36
  29.2 30.1 %collective-permute-start.2 = (bf16[192,1792]{1,0:T(8,128)(2,1)S(1)}, bf16[192,1792]{1,0:T(8,128)(2,1)S(1)}, u32[]{:S(2)}, u32[]{:S(2)}) collective-permute-start(bf16[192,1792]{1,0:T(8,128)(2,1)S(1)} %get-tuple-element.7), channel_id=1, source_target_pairs={{0,1},{3,2},{4,5},{7,6},{8,9},{11,10},{12,13},{15,14},{16,17},{19,... | collective-permute-start | bytes 2064392 | tf_op jit(solution)/shard_map/ppermute | solution.py:154
  45.6 26.9 %copy-start.9 = (bf16[512,896]{1,0:T(8,128)(2,1)}, bf16[512,896]{1,0:T(8,128)(2,1)S(1)}, u32[]{:S(2)}) copy-start(bf16[512,896]{1,0:T(8,128)(2,1)S(1)} %collective-permute-done.14.refs_16_) | copy-start | bytes 2752516
  45.6 13.7 %collective-permute-start.3 = (bf16[192,1792]{1,0:T(8,128)(2,1)S(1)}, bf16[192,1792]{1,0:T(8,128)(2,1)S(1)}, u32[]{:S(2)}, u32[]{:S(2)}) collective-permute-start(bf16[192,1792]{1,0:T(8,128)(2,1)S(1)} %collective-permute-done.1.refs_2_), channel_id=1, source_target_pairs={{1,2},{2,1},{5,6},{6,5},{9,10},{10,9},{13,14},{14,13},{17,18},{18,... | collective-permute-start | bytes 2064392 | tf_op jit(solution)/shard_map/ppermute | solution.py:155
  46.3 20.4 %collective-permute-start.16 = (bf16[512,896]{1,0:T(8,128)(2,1)S(1)}, bf16[512,896]{1,0:T(8,128)(2,1)}, u32[]{:S(2)}, u32[]{:S(2)}) collective-permute-start(bf16[512,896]{1,0:T(8,128)(2,1)S(1)} %collective-permute-done.14.refs_16_), channel_id=1, source_target_pairs={{0,16},{4,20},{8,24},{12,28},{16,0},{20,4},{24,8},{28,12},{1,17},{... | collective-permute-start | bytes 2752520 | tf_op jit(solution)/shard_map/ppermute | solution.py:36
  46.9 20.0 %collective-permute-start.15 = (bf16[512,896]{1,0:T(8,128)(2,1)S(1)}, bf16[512,896]{1,0:T(8,128)(2,1)}, u32[]{:S(2)}, u32[]{:S(2)}) collective-permute-start(bf16[512,896]{1,0:T(8,128)(2,1)S(1)} %collective-permute-done.14.refs_16_), channel_id=1, source_target_pairs={{0,8},{4,12},{8,0},{12,4},{16,24},{20,28},{24,16},{28,20},{1,9},{5... | collective-permute-start | bytes 2752520 | tf_op jit(solution)/shard_map/ppermute | solution.py:36
  59.3 10.7 %collective-permute-start.11 = (bf16[512,896]{1,0:T(8,128)(2,1)S(1)}, bf16[512,896]{1,0:T(8,128)(2,1)S(1)}, u32[]{:S(2)}, u32[]{:S(2)}) collective-permute-start(bf16[512,896]{1,0:T(8,128)(2,1)S(1)} %collective-permute-done.6.refs_8_), channel_id=1, source_target_pairs={{0,4},{4,0},{8,12},{12,8},{16,20},{20,16},{24,28},{28,24},{1,5},{5... | collective-permute-start | bytes 2752520 | tf_op jit(solution)/shard_map/ppermute | solution.py:36
  59.3 12.7 %collective-permute-start.10 = (bf16[512,896]{1,0:T(8,128)(2,1)S(1)}, bf16[512,896]{1,0:T(8,128)(2,1)S(1)}, u32[]{:S(2)}, u32[]{:S(2)}) collective-permute-start(bf16[512,896]{1,0:T(8,128)(2,1)S(1)} %collective-permute-done.5.refs_7_), channel_id=1, source_target_pairs={{0,4},{4,0},{8,12},{12,8},{16,20},{20,16},{24,28},{28,24},{1,5},{5... | collective-permute-start | bytes 2752520 | tf_op jit(solution)/shard_map/ppermute | solution.py:36
  59.8 6.9 %copy-start.7 = (bf16[384,1792]{1,0:T(8,128)(2,1)}, bf16[384,1792]{1,0:T(8,128)(2,1)S(1)}, u32[]{:S(2)}) copy-start(bf16[384,1792]{1,0:T(8,128)(2,1)S(1)} %collective-permute-done.refs_1_) | copy-start | bytes 4128772
  59.8 12.7 %collective-permute-start.19 = (bf16[512,896]{1,0:T(8,128)(2,1)S(1)}, bf16[512,896]{1,0:T(8,128)(2,1)S(1)}, u32[]{:S(2)}, u32[]{:S(2)}) collective-permute-start(bf16[512,896]{1,0:T(8,128)(2,1)S(1)} %collective-permute-done.14.refs_16_), channel_id=1, source_target_pairs={{0,4},{4,0},{8,12},{12,8},{16,20},{20,16},{24,28},{28,24},{1,5},{5... | collective-permute-start | bytes 2752520 | tf_op jit(solution)/shard_map/ppermute | solution.py:36
  66.7 2.6 %collective-permute-start.13 = (bf16[256,896]{1,0:T(8,128)(2,1)S(1)}, bf16[256,896]{1,0:T(8,128)(2,1)S(1)}, u32[]{:S(2)}, u32[]{:S(2)}) collective-permute-start(bf16[256,896]{1,0:T(8,128)(2,1)S(1)} %collective-permute-done.8.refs_10_), channel_id=1, source_target_pairs={{0,4},{4,0},{8,12},{12,8},{16,20},{20,16},{24,28},{28,24},{1,5},{5... | collective-permute-start | bytes 1376264 | tf_op jit(solution)/shard_map/ppermute | solution.py:36
  66.9 4.3 %collective-permute-start.12 = (bf16[256,896]{1,0:T(8,128)(2,1)S(1)}, bf16[256,896]{1,0:T(8,128)(2,1)S(1)}, u32[]{:S(2)}, u32[]{:S(2)}) collective-permute-start(bf16[256,896]{1,0:T(8,128)(2,1)S(1)} %collective-permute-done.7.refs_9_), channel_id=1, source_target_pairs={{0,4},{4,0},{8,12},{12,8},{16,20},{20,16},{24,28},{28,24},{1,5},{5... | collective-permute-start | bytes 1376264 | tf_op jit(solution)/shard_map/ppermute | solution.py:36
  69.3 12.8 %collective-permute-start.18 = (bf16[256,896]{1,0:T(8,128)(2,1)S(1)}, bf16[256,896]{1,0:T(8,128)(2,1)}, u32[]{:S(2)}, u32[]{:S(2)}) collective-permute-start(bf16[256,896]{1,0:T(8,128)(2,1)S(1)} %slice.119), channel_id=1, source_target_pairs={{0,8},{4,12},{8,0},{12,4},{16,24},{20,28},{24,16},{28,20},{1,9},{5... | collective-permute-start | bytes 1376264 | tf_op jit(solution)/shard_map/ppermute | solution.py:36
  69.9 4.1 %copy-start.10 = (bf16[512,896]{1,0:T(8,128)(2,1)}, bf16[512,896]{1,0:T(8,128)(2,1)S(1)}, u32[]{:S(2)}) copy-start(bf16[512,896]{1,0:T(8,128)(2,1)S(1)} %collective-permute-done.11.refs_13_) | copy-start | bytes 2752516
  70.0 12.5 %collective-permute-start.17 = (bf16[256,896]{1,0:T(8,128)(2,1)S(1)}, bf16[256,896]{1,0:T(8,128)(2,1)}, u32[]{:S(2)}, u32[]{:S(2)}) collective-permute-start(bf16[256,896]{1,0:T(8,128)(2,1)S(1)} %slice.118), channel_id=1, source_target_pairs={{0,16},{4,20},{8,24},{12,28},{16,0},{20,4},{24,8},{28,12},{1,17},{... | collective-permute-start | bytes 1376264 | tf_op jit(solution)/shard_map/ppermute | solution.py:36
  71.2 0.8 copy-start
  72.0 12.4 %collective-permute-start.21 = (bf16[512,896]{1,0:T(8,128)(2,1)}, bf16[512,896]{1,0:T(8,128)(2,1)}, u32[]{:S(2)}, u32[]{:S(2)}) collective-permute-start(bf16[512,896]{1,0:T(8,128)(2,1)} %collective-permute-done.16.refs_18_), channel_id=1, source_target_pairs={{0,4},{4,0},{8,12},{12,8},{16,20},{20,16},{24,28},{28,24},{1,5},{5... | collective-permute-start | bytes 2752520 | tf_op jit(solution)/shard_map/ppermute | solution.py:36
  72.0 10.2 %copy-start.11 = (bf16[512,896]{1,0:T(8,128)(2,1)}, bf16[512,896]{1,0:T(8,128)(2,1)S(1)}, u32[]{:S(2)}) copy-start(bf16[512,896]{1,0:T(8,128)(2,1)S(1)} %collective-permute-done.10.refs_12_) | copy-start | bytes 2752516
  72.0 13.0 %collective-permute-start.20 = (bf16[512,896]{1,0:T(8,128)(2,1)}, bf16[512,896]{1,0:T(8,128)(2,1)}, u32[]{:S(2)}, u32[]{:S(2)}) collective-permute-start(bf16[512,896]{1,0:T(8,128)(2,1)} %collective-permute-done.15.refs_17_), channel_id=1, source_target_pairs={{0,4},{4,0},{8,12},{12,8},{16,20},{20,16},{24,28},{28,24},{1,5},{5... | collective-permute-start | bytes 2752520 | tf_op jit(solution)/shard_map/ppermute | solution.py:36
  72.5 9.7 %copy-start.12 = (bf16[512,896]{1,0:T(8,128)(2,1)}, bf16[512,896]{1,0:T(8,128)(2,1)S(1)}, u32[]{:S(2)}) copy-start(bf16[512,896]{1,0:T(8,128)(2,1)S(1)} %collective-permute-done.19.refs_21_) | copy-start | bytes 2752516
  72.5 10.3 %collective-permute-start.4 = (bf16[192,1792]{1,0:T(8,128)(2,1)S(1)}, bf16[192,1792]{1,0:T(8,128)(2,1)}, u32[]{:S(2)}, u32[]{:S(2)}) collective-permute-start(bf16[192,1792]{1,0:T(8,128)(2,1)S(1)} %collective-permute-done.2.refs_3_), channel_id=1, source_target_pairs={{1,2},{2,1},{5,6},{6,5},{9,10},{10,9},{13,14},{14,13},{17,18},{18,... | collective-permute-start | bytes 2064392 | tf_op jit(solution)/shard_map/ppermute | solution.py:156
  82.2 2.2 %collective-permute-start.23 = (bf16[256,896]{1,0:T(8,128)(2,1)}, bf16[256,896]{1,0:T(8,128)(2,1)}, u32[]{:S(2)}, u32[]{:S(2)}) collective-permute-start(bf16[256,896]{1,0:T(8,128)(2,1)} %collective-permute-done.18.refs_20_), channel_id=1, source_target_pairs={{0,4},{4,0},{8,12},{12,8},{16,20},{20,16},{24,28},{28,24},{1,5},{5... | collective-permute-start | bytes 1376264 | tf_op jit(solution)/shard_map/ppermute | solution.py:36
  82.4 2.6 %collective-permute-start.22 = (bf16[256,896]{1,0:T(8,128)(2,1)}, bf16[256,896]{1,0:T(8,128)(2,1)}, u32[]{:S(2)}, u32[]{:S(2)}) collective-permute-start(bf16[256,896]{1,0:T(8,128)(2,1)} %collective-permute-done.17.refs_19_), channel_id=1, source_target_pairs={{0,4},{4,0},{8,12},{12,8},{16,20},{20,16},{24,28},{28,24},{1,5},{5... | collective-permute-start | bytes 1376264 | tf_op jit(solution)/shard_map/ppermute | solution.py:36
  85.0 1.0 copy-start.1
  106.1 13.8 %copy-start.3 = (f32[384,1024]{1,0:T(8,128)S(1)}, f32[384,1024]{1,0:T(8,128)}, u32[]{:S(2)}) copy-start(f32[384,1024]{1,0:T(8,128)} %get-tuple-element.9) | copy-start | bytes 4718596
  106.2 1.4 collective-permute-start.24
  107.6 7.5 %collective-permute-start.27 = (f32[72,512]{1,0:T(8,128)S(1)}, f32[72,512]{1,0:T(8,128)S(1)}, u32[]{:S(2)}, u32[]{:S(2)}) collective-permute-start(f32[72,512]{1,0:T(8,128)S(1)} %select_add_fusion.2), channel_id=1, source_target_pairs={{0,24},{4,28},{8,16},{12,20},{16,8},{20,12},{24,0},{28,4},{1,25},{... | collective-permute-start | bytes 442376 | tf_op jit(solution)/shard_map/ppermute | solution.py:36
  110.5 7.3 %collective-permute-start.26 = (f32[72,512]{1,0:T(8,128)S(1)}, f32[72,512]{1,0:T(8,128)S(1)}, u32[]{:S(2)}, u32[]{:S(2)}) collective-permute-start(f32[72,512]{1,0:T(8,128)S(1)} %select_add_fusion.2), channel_id=1, source_target_pairs={{0,16},{4,20},{8,24},{12,28},{16,0},{20,4},{24,8},{28,12},{1,17},{... | collective-permute-start | bytes 442376 | tf_op jit(solution)/shard_map/ppermute | solution.py:36
  110.5 7.8 %collective-permute-start.25 = (f32[72,512]{1,0:T(8,128)S(1)}, f32[72,512]{1,0:T(8,128)S(1)}, u32[]{:S(2)}, u32[]{:S(2)}) collective-permute-start(f32[72,512]{1,0:T(8,128)S(1)} %select_add_fusion.2), channel_id=1, source_target_pairs={{0,8},{4,12},{8,0},{12,4},{16,24},{20,28},{24,16},{28,20},{1,9},{5... | collective-permute-start | bytes 442376 | tf_op jit(solution)/shard_map/ppermute | solution.py:36
  118.3 1.4 collective-permute-start.28
  121.6 0.9 collective-permute-start.29
  123.7 1.4 collective-permute-start.30
  125.2 7.7 %collective-permute-start.33 = (f32[72,512]{1,0:T(8,128)S(1)}, f32[72,512]{1,0:T(8,128)S(1)}, u32[]{:S(2)}, u32[]{:S(2)}) collective-permute-start(f32[72,512]{1,0:T(8,128)S(1)} %select_add_fusion.1), channel_id=1, source_target_pairs={{0,24},{4,28},{8,16},{12,20},{16,8},{20,12},{24,0},{28,4},{1,25},{... | collective-permute-start | bytes 442376 | tf_op jit(solution)/shard_map/ppermute | solution.py:36
  126.7 8.5 %collective-permute-start.32 = (f32[72,512]{1,0:T(8,128)S(1)}, f32[72,512]{1,0:T(8,128)S(1)}, u32[]{:S(2)}, u32[]{:S(2)}) collective-permute-start(f32[72,512]{1,0:T(8,128)S(1)} %select_add_fusion.1), channel_id=1, source_target_pairs={{0,16},{4,20},{8,24},{12,28},{16,0},{20,4},{24,8},{28,12},{1,17},{... | collective-permute-start | bytes 442376 | tf_op jit(solution)/shard_map/ppermute | solution.py:36
  128.0 7.2 %collective-permute-start.31 = (f32[72,512]{1,0:T(8,128)S(1)}, f32[72,512]{1,0:T(8,128)S(1)}, u32[]{:S(2)}, u32[]{:S(2)}) collective-permute-start(f32[72,512]{1,0:T(8,128)S(1)} %select_add_fusion.1), channel_id=1, source_target_pairs={{0,8},{4,12},{8,0},{12,4},{16,24},{20,28},{24,16},{28,20},{1,9},{5... | collective-permute-start | bytes 442376 | tf_op jit(solution)/shard_map/ppermute | solution.py:36
  135.3 1.4 collective-permute-start.34
  138.7 0.7 collective-permute-start.35
  140.7 1.4 collective-permute-start.36
  142.2 7.7 %collective-permute-start.39 = (f32[72,512]{1,0:T(8,128)S(1)}, f32[72,512]{1,0:T(8,128)S(1)}, u32[]{:S(2)}, u32[]{:S(2)}) collective-permute-start(f32[72,512]{1,0:T(8,128)S(1)} %select_add_fusion), channel_id=1, source_target_pairs={{0,24},{4,28},{8,16},{12,20},{16,8},{20,12},{24,0},{28,4},{1,25},{... | collective-permute-start | bytes 442376 | tf_op jit(solution)/shard_map/ppermute | solution.py:36
  143.7 8.5 %collective-permute-start.38 = (f32[72,512]{1,0:T(8,128)S(1)}, f32[72,512]{1,0:T(8,128)S(1)}, u32[]{:S(2)}, u32[]{:S(2)}) collective-permute-start(f32[72,512]{1,0:T(8,128)S(1)} %select_add_fusion), channel_id=1, source_target_pairs={{0,16},{4,20},{8,24},{12,28},{16,0},{20,4},{24,8},{28,12},{1,17},{... | collective-permute-start | bytes 442376 | tf_op jit(solution)/shard_map/ppermute | solution.py:36
  145.1 7.2 %collective-permute-start.37 = (f32[72,512]{1,0:T(8,128)S(1)}, f32[72,512]{1,0:T(8,128)S(1)}, u32[]{:S(2)}, u32[]{:S(2)}) collective-permute-start(f32[72,512]{1,0:T(8,128)S(1)} %select_add_fusion), channel_id=1, source_target_pairs={{0,8},{4,12},{8,0},{12,4},{16,24},{20,28},{24,16},{28,20},{1,9},{5... | collective-permute-start | bytes 442376 | tf_op jit(solution)/shard_map/ppermute | solution.py:36
  152.3 1.4 collective-permute-start.40
  154.0 38.0 %collective-permute-start.41 = (f32[128,512]{1,0:T(8,128)S(1)}, f32[128,512]{1,0:T(8,128)S(1)}, u32[]{:S(2)}, u32[]{:S(2)}) collective-permute-start(f32[128,512]{1,0:T(8,128)S(1)} %pad_maximum_fusion), channel_id=1, source_target_pairs={{1,0},{2,3},{5,4},{6,7},{9,8},{10,11},{13,12},{14,15},{17,16},{18,... | collective-permute-start | bytes 786440 | tf_op jit(solution)/shard_map/ppermute | solution.py:204

commit v3 on v2

v3 whole, which is shorter than its diff:
```python
import jax
import jax.numpy as jnp
from jax import lax
from jax.experimental import pallas as pl
from jax.experimental.pallas import tpu as pltpu
from jax.sharding import PartitionSpec as P

ITERS = 2
SPREAD = 10690

ridge_scale = 0.002


def squares(block):
    return jnp.sum(jnp.square(block.astype(jnp.float32)), axis=1)


def cross_piece(left, right):
    return lax.dot_general(
        left, right, (((1,), (1,)), ((), ())), preferred_element_type=jnp.float32
    )


def times(left, right, contract):
    return lax.dot_general(
        left, right, ((contract[:1], contract[1:]), ((), ())), precision=lax.Precision.HIGHEST
    )


TO_MIDDLE = [(0, 1), (3, 2)]
ACROSS = [(1, 2), (2, 1)]
TO_END = [(1, 0), (2, 3)]


def flipped(block, bits):
    return lax.ppermute(block, "proof", [(i, i ^ bits) for i in range(8)])


def sum_rows_axis(block):
    odd = lax.axis_index("proof") % 2
    half = block.shape[1] // 2
    low, high = block[:, :half], block[:, half:]
    mine, other = jnp.where(odd == 0, low, high), jnp.where(odd == 0, high, low)
    mine = mine + flipped(other, 1)
    mine = mine + flipped(mine, 2) + flipped(mine, 4) + flipped(mine, 6)
    other = flipped(mine, 1)
    low, high = jnp.where(odd == 0, mine, other), jnp.where(odd == 0, other, mine)
    return jnp.concatenate([low, high], axis=1)


def sum_middle(block):
    return block + lax.ppermute(block, "landmark", ACROSS)


def packed(block, *vectors):
    rows = jnp.stack(vectors)
    rows = jnp.pad(rows, ((0, 8 - rows.shape[0]), (0, block.shape[1] - rows.shape[1])))
    return jnp.concatenate([block, rows], axis=0)


def after(block, *earlier):
    return lax.optimization_barrier((block, *earlier))[0]


ANY = pl.BlockSpec(memory_space=pl.ANY)
VMEM = pl.BlockSpec(memory_space=pltpu.VMEM)
SMEM = pl.BlockSpec(memory_space=pltpu.SMEM)


def place():
    return jnp.stack([lax.axis_index("proof"), lax.axis_index("landmark")]).astype(jnp.int32)


def lane_squares(block):
    total = None
    for j in range(block.shape[1] // 128):
        x = block[:, j * 128 : (j + 1) * 128].astype(jnp.float32)
        total = x * x if total is None else total + x * x
    return total


def product(left, right):
    return lax.dot_general(left, right, (((1,), (1,)), ((), ())), preferred_element_type=jnp.float32)


def tiled_product(cross_ref, left, right_ref):
    for t in range(cross_ref.shape[0]):
        cross_ref[t] += product(left[...], right_ref[t * 256 : (t + 1) * 256])


def feature_block(z, zbits, side):
    return 2 * (z ^ zbits) + side


class Rows:
    def __init__(self, blocks):
        self.keys, self.blocks = list(blocks), list(blocks.values())

    def source(self, refs, zbits, side, width):
        if (zbits, None) in self.keys:
            return refs[self.keys.index((zbits, None))].at[:, pl.ds(side * width, width)]
        return refs[self.keys.index((zbits, side))]


class Landmarks:
    def __init__(self, parts):
        self.keys = [(bits, row) for bits, row, _ in parts]
        self.blocks = [block for _, _, block in parts]

    def start(self, refs, bits, target, sem):
        for (found, row), ref in zip(self.keys, refs):
            if found == bits:
                pltpu.make_async_copy(ref, target.at[pl.ds(row, ref.shape[0])], sem).start()

    def start_any(self, refs, bits, target, sem):
        for one in sorted({found for found, _ in self.keys}):
            @pl.when(bits == one)
            def _():
                self.start(refs, one, target, sem)


def wait(target, sem):
    pltpu.make_async_copy(target, target, sem).wait()


def call(body, inputs, specs, shapes, scratch, name):
    return pl.pallas_call(
        body,
        out_shape=tuple(jax.ShapeDtypeStruct(shape, jnp.float32) for shape in shapes),
        in_specs=specs,
        out_specs=tuple(VMEM for _ in shapes),
        scratch_shapes=scratch,
        compiler_params=pltpu.CompilerParams(vmem_limit_bytes=60 << 20),
        cost_estimate=pl.CostEstimate(flops=1000, bytes_accessed=1000, transcendentals=0),
        name=name,
    )(*inputs)


def own_block(rows, landmarks, n, m, width):
    rows, landmarks = Rows(rows), Landmarks(landmarks)
    sources = [(0, 0), (0, 1), (3, 0), (3, 1), (1, 0)]

    def body(place_ref, *refs):
        row_refs, refs = refs[: len(rows.keys)], refs[len(rows.keys) :]
        landmark_refs, refs = refs[: len(landmarks.keys)], refs[len(landmarks.keys) :]
        cross_ref, row_norm_ref, norm_ref, rows_s, land_s, row_sem, land_sem = refs
        p, z = place_ref[0], place_ref[1]
        wanted = [feature_block(z, zbits, side) ^ p for zbits, side in sources]
        for i, (zbits, side) in enumerate(sources):
            pltpu.make_async_copy(rows.source(row_refs, zbits, side, width), rows_s.at[i], row_sem.at[i]).start()
        for bits in range(8):
            landmarks.start(landmark_refs, bits, land_s.at[bits], land_sem.at[bits])
        cross_ref[...] = jnp.zeros_like(cross_ref)
        for bits in range(8):
            wait(land_s.at[bits], land_sem.at[bits])
            squares_here = lane_squares(land_s[bits])
            norm_ref[...] = squares_here if bits == 0 else norm_ref[...] + squares_here
        for i in range(len(sources)):
            wait(rows_s.at[i], row_sem.at[i])
            tiled_product(cross_ref, rows_s.at[i], land_s.at[wanted[i]])
            squares_here = lane_squares(rows_s[i])
            row_norm_ref[...] = squares_here if i == 0 else row_norm_ref[...] + squares_here

    return call(
        body,
        [place()] + rows.blocks + landmarks.blocks,
        [SMEM] + [ANY] * (len(rows.keys) + len(landmarks.keys)),
        [(m // 256, n, 256), (n, 128), (m, 128)],
        [
            pltpu.VMEM((len(sources), n, width), jnp.bfloat16),
            pltpu.VMEM((8, m, width), jnp.bfloat16),
            pltpu.SemaphoreType.DMA((len(sources),)),
            pltpu.SemaphoreType.DMA((8,)),
        ],
        "own_block",
    )


def end_block(rows, own, end, cross_own, row_norm, n, m, width):
    rows, own, end = Rows(rows), Landmarks(own), Landmarks(end)
    late = 2 * 2 + 1

    def body(place_ref, cross_in, norm_in, *refs):
        row_refs, refs = refs[: len(rows.keys)], refs[len(rows.keys) :]
        own_refs, refs = refs[: len(own.keys)], refs[len(own.keys) :]
        end_refs, refs = refs[: len(end.keys)], refs[len(end.keys) :]
        cross_own_ref, cross_ref, row_norm_ref, norm_ref, rows_s, own_s, end_s, row_sem, own_sem, end_sem = refs
        p, z = place_ref[0], place_ref[1]
        more = [(1, 1), (2, 0)]
        for zbits, side in more:
            slot = 2 * zbits + side
            pltpu.make_async_copy(rows.source(row_refs, zbits, side, width), rows_s.at[slot], row_sem.at[slot]).start()
        for i, (zbits, side) in enumerate(more):
            own.start_any(own_refs, feature_block(z, zbits, side) ^ p, own_s.at[i], own_sem.at[i])
        for slot in range(8):
            if slot != late and (slot // 2, slot % 2) not in more:
                source = rows.source(row_refs, slot // 2, slot % 2, width)
                pltpu.make_async_copy(source, rows_s.at[slot], row_sem.at[slot]).start()
        for bits in range(6):
            end.start(end_refs, bits, end_s.at[bits], end_sem.at[bits])
        cross_own_ref[...] = cross_in[...]
        cross_ref[...] = jnp.zeros_like(cross_ref)
        row_total = norm_in[...]
        for i, (zbits, side) in enumerate(more):
            slot = 2 * zbits + side
            wait(rows_s.at[slot], row_sem.at[slot])
            wait(own_s.at[i], own_sem.at[i])
            tiled_product(cross_own_ref, rows_s.at[slot], own_s.at[i])
            row_total = row_total + lane_squares(rows_s[slot])
        row_norm_ref[...] = row_total
        for slot in range(8):
            if slot != late and (slot // 2, slot % 2) not in more:
                wait(rows_s.at[slot], row_sem.at[slot])
        for bits in range(6):
            wait(end_s.at[bits], end_sem.at[bits])
            f = p ^ bits
            slot = 2 * (z ^ (f // 2)) + f % 2

            @pl.when(slot != late)
            def _():
                tiled_product(cross_ref, rows_s.at[slot], end_s.at[bits])

            squares_here = lane_squares(end_s[bits])
            norm_ref[...] = squares_here if bits == 0 else norm_ref[...] + squares_here

    return call(
        body,
        [place(), cross_own, row_norm] + rows.blocks + own.blocks + end.blocks,
        [SMEM, VMEM, VMEM] + [ANY] * (len(rows.keys) + len(own.keys) + len(end.keys)),
        [(m // 256, n, 256), (m // 256, n, 256), (n, 128), (m, 128)],
        [
            pltpu.VMEM((8, n, width), jnp.bfloat16),
            pltpu.VMEM((2, m, width), jnp.bfloat16),
            pltpu.VMEM((6, m, width), jnp.bfloat16),
            pltpu.SemaphoreType.DMA((8,)),
            pltpu.SemaphoreType.DMA((2,)),
            pltpu.SemaphoreType.DMA((6,)),
        ],
        "end_block",
    )


def last_block(rows, own, end, cross_own, cross_end, row_norm, norm_own, norm_end, columns, width):
    rows, own, end = Rows(rows), Landmarks(own), Landmarks(end)
    n, m, count = columns.shape[1], norm_own.shape[0], columns.shape[0]

    def body(place_ref, cross_own_in, cross_end_in, row_norm_in, norm_own_in, norm_end_in, columns_ref, *refs):
        row_refs, refs = refs[: len(rows.keys)], refs[len(rows.keys) :]
        own_refs, refs = refs[: len(own.keys)], refs[len(own.keys) :]
        end_refs, refs = refs[: len(end.keys)], refs[len(end.keys) :]
        kernel_ref, sums_ref, cross_s, rows_s, own_s, end_s, row_sem, own_sem, end_sem = refs
        p, z = place_ref[0], place_ref[1]
        far = feature_block(z, 2, 1) ^ p
        pltpu.make_async_copy(rows.source(row_refs, 2, 1, width), rows_s.at[2], row_sem.at[2]).start()
        own.start_any(own_refs, far, own_s, own_sem)
        for i in range(2):
            f = p ^ (6 + i)
            for zbits in range(4):
                for side in range(2):
                    @pl.when((z ^ (f // 2) == zbits) & (f % 2 == side))
                    def _():
                        source = rows.source(row_refs, zbits, side, width)
                        pltpu.make_async_copy(source, rows_s.at[i], row_sem.at[i]).start()
            end.start(end_refs, 6 + i, end_s.at[i], end_sem.at[i])

        @pl.when(far < 6)
        def _():
            end.start_any(end_refs, far, end_s.at[2], end_sem.at[2])

        half = m // 256
        cross_s[:half] = cross_own_in[...]
        cross_s[half:] = cross_end_in[...]
        wait(rows_s.at[2], row_sem.at[2])
        wait(own_s, own_sem)
        tiled_product(cross_s.at[:half], rows_s.at[2], own_s)
        row_norm = jnp.sum(row_norm_in[...] + lane_squares(rows_s[2]), axis=1, keepdims=True)
        norm_end = norm_end_in[...]
        for i in range(2):
            wait(rows_s.at[i], row_sem.at[i])
            wait(end_s.at[i], end_sem.at[i])
            tiled_product(cross_s.at[half:], rows_s.at[i], end_s.at[i])
            norm_end = norm_end + lane_squares(end_s[i])

        @pl.when(far < 6)
        def _():
            wait(end_s.at[2], end_sem.at[2])
            tiled_product(cross_s.at[half:], rows_s.at[2], end_s.at[2])

        ones = jnp.ones((8, 128), jnp.float32)
        for t in range(2 * half):
            inside = slice(t * 256, (t + 1) * 256)
            lanes = norm_own_in[inside] if t < half else norm_end[(t - half) * 256 : (t - half + 1) * 256]
            norm = lax.dot_general(ones, lanes, (((1,), (1,)), ((), ())), precision=lax.Precision.HIGHEST)[:1]
            k = jnp.exp(-(row_norm + norm - 2.0 * cross_s[t]) / SPREAD)
            kernel_ref[:, inside] = k
            sums_ref[:count, inside] = jnp.dot(columns_ref[...], k, precision=lax.Precision.HIGHEST)
            sums_ref[count:, inside] = jnp.broadcast_to(jnp.sum(k * k, axis=0, keepdims=True), (8, 256))

    return call(
        body,
        [place(), cross_own, cross_end, row_norm, norm_own, norm_end, columns]
        + rows.blocks + own.blocks + end.blocks,
        [SMEM] + [VMEM] * 6 + [ANY] * (len(rows.keys) + len(own.keys) + len(end.keys)),
        [(n, 2 * m), (count + 8, 2 * m)],
        [
            pltpu.VMEM((2 * m // 256, n, 256), jnp.float32),
            pltpu.VMEM((3, n, width), jnp.bfloat16),
            pltpu.VMEM((m, width), jnp.bfloat16),
            pltpu.VMEM((3, m, width), jnp.bfloat16),
            pltpu.SemaphoreType.DMA((3,)),
            pltpu.SemaphoreType.DMA,
            pltpu.SemaphoreType.DMA((3,)),
        ],
        "last_block",
    )


def middle_kernel(row_features, landmark_features, columns):
    own = landmark_features
    m, half = own.shape
    n, middle = row_features.shape[0], m // 2
    left, right = row_features[:, :half], row_features[:, half:]
    end = lax.ppermute(own, "landmark", TO_MIDDLE)
    own_x, own_y = flipped(own, 2), flipped(own, 4)
    middle_rows = lax.ppermute(row_features, "landmark", ACROSS)
    own_x, own_y, end, left = lax.optimization_barrier((own_x, own_y, end, left))
    end_left = lax.ppermute(left, "landmark", TO_MIDDLE)
    own_low, own_high = flipped(own_x[:middle], 4), flipped(own_y[middle:], 2)
    other_own, other_x, other_y = flipped(after(own, own_x), 1), flipped(own_x, 1), flipped(own_y, 1)
    own_low, own_high, end = lax.optimization_barrier((own_low, own_high, end))
    end_x, end_y = flipped(end, 2), flipped(end, 4)
    other_low, other_high = flipped(own_low, 1), flipped(own_high, 1)
    end_bottom = end[middle:]
    end_left, right, middle_rows = lax.optimization_barrier((end_left, right, middle_rows))
    far_left = lax.ppermute(end_left, "landmark", ACROSS)
    end_right = lax.ppermute(right, "landmark", TO_MIDDLE)
    own_parts = [
        (0, 0, own), (2, 0, own_x), (4, 0, own_y), (6, 0, own_low), (6, middle, own_high),
        (1, 0, other_own), (3, 0, other_x), (5, 0, other_y), (7, 0, other_low), (7, middle, other_high),
    ]
    rows = {(0, None): row_features, (3, None): middle_rows, (1, 0): end_left}
    cross_own, row_norm, norm_own = own_block(rows, own_parts, n, m, half)
    end_x, end_y, end_bottom, far_left, _ = lax.optimization_barrier((end_x, end_y, end_bottom, far_left, cross_own))
    end_high = flipped(end_bottom, 6)
    end_right = after(end_right, end_x, end_y)
    far_right = lax.ppermute(end_right, "landmark", ACROSS)
    end_low = lax.ppermute(after(own_low, end_right), "landmark", TO_MIDDLE)
    end_parts = [(0, 0, end), (2, 0, end_x), (4, 0, end_y)]
    end_parts += [(bits + 1, row, flipped(block, 1)) for bits, row, block in end_parts]
    rows |= {(1, 1): end_right, (2, 0): far_left}
    cross_own, cross_end, row_norm, norm_end = end_block(
        rows, own_parts, end_parts, cross_own, row_norm, n, m, half
    )
    corner = [(6, 0, after(end_low, cross_end)), (6, middle, after(end_high, cross_end))]
    end_parts += corner + [(bits + 1, row, flipped(block, 1)) for bits, row, block in corner]
    rows |= {(2, 1): far_right}
    return last_block(
        rows, own_parts, end_parts, cross_own, cross_end, row_norm, norm_own, norm_end, columns, half
    )


def conjugate_gradients(kernel, sums, columns, lam, sum_rows, sum_landmarks):
    count = columns.shape[0]
    residual, precond = sums[:count], lam + sums[count]
    coefficient = jnp.zeros_like(residual)
    inner = None
    for iteration in range(ITERS):
        scaled = residual / precond
        part = times(scaled, kernel, (1, 1))
        dots = [jnp.sum(residual * scaled, axis=1), jnp.sum(scaled * scaled, axis=1)]
        if iteration > 0:
            dots.append(jnp.sum(scaled * direction, axis=1))
        sums = sum_landmarks(packed(part, *dots))
        inner_next, square = sums[count, :count], sums[count + 1, :count]
        if iteration == 0:
            direction, image, length = scaled, sums[:count], square
        else:
            beta = inner_next / inner
            length = square + beta * (2.0 * sums[count + 2, :count] + beta * length)
            direction = scaled + beta[:, None] * direction
            image = sums[:count] + beta[:, None] * image
        inner = inner_next
        sums = sum_rows(packed(times(image, kernel, (1, 0)), jnp.sum(image * image, axis=1)))
        gradient = sums[:count] + lam * direction
        step_size = (inner / (sums[count, :count] + lam * length))[:, None]
        coefficient = coefficient + step_size * direction
        residual = residual - step_size * gradient
    return coefficient, residual


def folded(row_features, landmark_features, targets):
    lam = ridge_scale * row_features.shape[0] * lax.axis_size("proof")
    columns = targets.T
    kernel, sums = middle_kernel(row_features, landmark_features, columns)
    sums = sum_rows_axis(sums)
    coefficient, residual = conjugate_gradients(kernel, sums, columns, lam, sum_rows_axis, sum_middle)
    both = jnp.concatenate([coefficient, residual], axis=0)
    half = both.shape[1] // 2
    received = lax.ppermute(both[:, half:], "landmark", TO_END)
    z = lax.axis_index("landmark")
    both = jnp.where((z == 1) | (z == 2), both[:, :half], received)
    return both[: columns.shape[0]].T, both[columns.shape[0] :].T


def plain(row_features, landmark_features, targets):
    lam = ridge_scale * row_features.shape[0] * lax.axis_size("proof")
    columns = targets.T
    rows = lax.all_gather(row_features, "landmark", axis=1, tiled=True)
    whole = lax.all_gather(landmark_features, "proof", axis=1, tiled=True)
    kernel = jnp.exp(-(squares(rows)[:, None] + squares(whole)[None, :] - 2.0 * cross_piece(rows, whole)) / SPREAD)
    sum_rows = lambda block: lax.psum(block, "proof")
    sums = sum_rows(packed(times(columns, kernel, (1, 0)), jnp.sum(kernel * kernel, axis=0)))
    sum_landmarks = lambda block: lax.psum(block, "landmark")
    coefficient, residual = conjugate_gradients(kernel, sums, columns, lam, sum_rows, sum_landmarks)
    return coefficient.T, residual.T


def solution(mesh):
    placed = (P("proof", "landmark"), P("landmark", "proof"), P("proof", None))
    four_planes = mesh.shape["proof"] == 8 and mesh.shape["landmark"] == 4
    return jax.shard_map(
        folded if four_planes else plain,
        mesh=mesh,
        in_specs=placed,
        out_specs=(P("landmark", None), P("landmark", None)),
        check_vma=False,
    )
```

time: 193 us -> 176 us (0.912)
  waiting for transfers between devices: 118 us -> 80.4 us
  Pallas kernels: 20.1 us -> 29.7 us
  starting transfers between devices: 40.3 us -> 47.2 us
  other arithmetic: 1.52 us -> 4.2 us
    ppermute x33 -> x32, waiting for transfers between devices: 59.5 us -> 40.9 us  [flipped(): return lax.ppermute(block, 'proof', [(i, i ^ bits) for i in range(8)])]
    ppermute x1, waiting for transfers between devices: 36.7 us -> 21.8 us  [folded(): received = lax.ppermute(both[:, half:], 'landmark', TO_END)]
    pallas_call x1 -> x3, Pallas kernels: 20.1 us -> 29.7 us  [call(): pl.pallas_call(body, out_shape=tuple((jax.ShapeDtypeStruct(shape, jnp.flo...]
    ppermute x5 -> x6, starting transfers between devices: 13.3 us -> 22 us  [the longest x1 7.35 us: middle_kernel(): end_right = lax.ppermute(right, 'landmark', TO_MIDDLE)]
    ppermute x5 -> x6, waiting for transfers between devices: 22 us -> 17.7 us  [the longest x1 12.9 us: middle_kernel(): end = lax.ppermute(own, 'landmark', TO_MIDDLE)]
    ppermute x33 -> x32, starting transfers between devices: 23.5 us -> 21.8 us  [flipped(): return lax.ppermute(block, 'proof', [(i, i ^ bits) for i in range(8)])]
    slice x5 -> x4, local copies, waits for them, and re-layouts: 3.58 us -> 4.16 us  [the longest x1 2.27 us: middle_kernel(): left, right = (row_features[:, :half], row_features[:, half:])]
  transfers between devices with their start and end apart: 42 -> 42, of which waited for: 24 -> 23; matrix products, arithmetic and copies ran while one was open for 2% -> 3% of each run, Pallas kernels for 0% -> 11%
where the time goes in v3:
time: 176 us
  waiting for transfers between devices  80.4 us (46%)
  starting transfers between devices  47.2 us (27%)
  Pallas kernels  29.7 us (17%)
  local copies, waits for them, and re-layouts  7.89 us (4%)
  matrix products  5.36 us (3%)
  other arithmetic  4.2 us (2%)
    ppermute x32, waiting for transfers between devices, flipped(): return lax.ppermute(block, 'proof', [(i, i ^ bits) for i in range(8)])  40.9 us
    pallas_call x3, Pallas kernels, call(): pl.pallas_call(body, out_shape=tuple((jax.ShapeDtypeStruct(shape, jnp.flo...  29.7 us
    ppermute x32, starting transfers between devices, flipped(): return lax.ppermute(block, 'proof', [(i, i ^ bits) for i in range(8)])  21.8 us
    ppermute x1, waiting for transfers between devices, folded(): received = lax.ppermute(both[:, half:], 'landmark', TO_END)  21.8 us
    ppermute x1, waiting for transfers between devices, middle_kernel(): end = lax.ppermute(own, 'landmark', TO_MIDDLE)  12.9 us
    ppermute x1, starting transfers between devices, middle_kernel(): end_right = lax.ppermute(right, 'landmark', TO_MIDDLE)  7.35 us
    ppermute x1, starting transfers between devices, middle_kernel(): end = lax.ppermute(own, 'landmark', TO_MIDDLE)  5.87 us
    dot_general x4, matrix products, times(): lax.dot_general(left, right, ((contract[:1], contract[1:]), ((), ())), pr...  5.36 us
  transfers between devices with their start and end apart: 42, of which 23 were waited for; matrix products, arithmetic and copies ran while one was open for 3% of the time, Pallas kernels for 11%

profile of v3, /device:TPU:0, one launch (start us, length us, event | category | flops | bytes accessed | tf_op | source)
XLA Modules:
  0.0 175.9 jit_solution(15310891723301866509)
XLA Ops:
  0.6 5.9 %collective-permute-start.2 = (bf16[512,896]{1,0:T(8,128)(2,1)}, bf16[512,896]{1,0:T(8,128)(2,1)}, u32[]{:S(2)}, u32[]{:S(2)}) collective-permute-start(bf16[512,896]{1,0:T(8,128)(2,1)} %refs_6_.1), channel_id=1, source_target_pairs={{0,1},{3,2},{4,5},{7,6},{8,9},{11,10},{12,13},{15,14},{16,17},{19,... | collective-permute-start | bytes 2752520 | tf_op jit(solution)/shard_map/ppermute | solution.py:323
  6.5 1.5 collective-permute-start.1
  8.0 1.5 collective-permute-start
  9.5 0.7 collective-permute-start.4
  10.3 2.3 %fusion.27 = (bf16[384,896]{1,0:T(8,128)(2,1)}, bf16[384,896]{1,0:T(8,128)(2,1)S(1)}) fusion(bf16[384,1792]{1,0:T(8,128)(2,1)} %refs_0_.5), kind=kLoop, calls=%fused_computation.82 | loop fusion | bytes 2752512 | tf_op jit(solution)/shard_map/slice | solution.py:322
  12.5 12.9 %collective-permute-done.2.refs_15_.refs_16_ = bf16[512,896]{1,0:T(8,128)(2,1)} collective-permute-done((bf16[512,896]{1,0:T(8,128)(2,1)}, bf16[512,896]{1,0:T(8,128)(2,1)}, u32[]{:S(2)}, u32[]{:S(2)}) %collective-permute-start.2) | collective-permute-done | bytes 917536 | tf_op jit(solution)/shard_map/ppermute | solution.py:323
  25.5 3.0 %collective-permute-done.1.refs_5_.refs_7_.refs_8_ = bf16[512,896]{1,0:T(8,128)(2,1)S(1)} collective-permute-done((bf16[512,896]{1,0:T(8,128)(2,1)}, bf16[512,896]{1,0:T(8,128)(2,1)S(1)}, u32[]{:S(2)}, u32[]{:S(2)}) %collective-permute-start.1) | collective-permute-done | bytes 917536 | tf_op jit(solution)/shard_map/ppermute | solution.py:36
  28.5 1.2 collective-permute-done.refs_4_.refs_6_.refs_7_
  29.9 0.6 collective-permute-start.5
  30.4 1.5 collective-permute-start.6
  31.9 2.2 %collective-permute-start.3 = (bf16[384,896]{1,0:T(8,128)(2,1)S(1)}, bf16[384,896]{1,0:T(8,128)(2,1)}, u32[]{:S(2)}, u32[]{:S(2)}) collective-permute-start(bf16[384,896]{1,0:T(8,128)(2,1)S(1)} %get-tuple-element.30), channel_id=1, source_target_pairs={{0,1},{3,2},{4,5},{7,6},{8,9},{11,10},{12,13},{15,14},{16,17},{19,... | collective-permute-start | bytes 2064392 | tf_op jit(solution)/shard_map/ppermute | solution.py:327
  34.1 6.6 %collective-permute-done.5.refs_6_.refs_8_.refs_9_ = bf16[256,896]{1,0:T(8,128)(2,1)S(1)} collective-permute-done((bf16[256,896]{1,0:T(8,128)(2,1)S(1)}, bf16[256,896]{1,0:T(8,128)(2,1)S(1)}, u32[]{:S(2)}, u32[]{:S(2)}) %collective-permute-start.5) | collective-permute-done | bytes 458784 | tf_op jit(solution)/shard_map/ppermute | solution.py:36
  41.0 0.5 collective-permute-start.10
  41.6 4.7 %collective-permute-done.3.refs_2_ = bf16[384,896]{1,0:T(8,128)(2,1)} collective-permute-done((bf16[384,896]{1,0:T(8,128)(2,1)S(1)}, bf16[384,896]{1,0:T(8,128)(2,1)}, u32[]{:S(2)}, u32[]{:S(2)}) %collective-permute-start.3) | collective-permute-done | bytes 688160 | tf_op jit(solution)/shard_map/ppermute | solution.py:327
  46.3 1.4 collective-permute-start.14
  47.7 0.5 collective-permute-start.13
  48.2 1.5 collective-permute-start.15
  49.8 7.3 %collective-permute-start.12 = (bf16[384,896]{1,0:T(8,128)(2,1)}, bf16[384,896]{1,0:T(8,128)(2,1)}, u32[]{:S(2)}, u32[]{:S(2)}) collective-permute-start(bf16[384,896]{1,0:T(8,128)(2,1)} %get-tuple-element.41), channel_id=1, source_target_pairs={{0,1},{3,2},{4,5},{7,6},{8,9},{11,10},{12,13},{15,14},{16,17},{19,... | collective-permute-start | bytes 2064392 | tf_op jit(solution)/shard_map/ppermute | solution.py:336
  57.2 0.9 copy-done.7
  58.1 0.7 pad_add_fusion.place_ref
  58.7 1.8 %slice.88 = bf16[256,896]{1,0:T(8,128)(2,1)} slice(bf16[512,896]{1,0:T(8,128)(2,1)} %collective-permute-done.2.refs_15_.refs_16_), slice={[256:512], [0:896]} | slice | bytes 917504 | tf_op jit(solution)/shard_map/slice | solution.py:333
  60.6 9.3 %own_block.1 = (f32[2,384,256]{2,1,0:T(8,128)}, f32[384,128]{1,0:T(8,128)}, f32[512,128]{1,0:T(8,128)}) custom-call(s32[2]{0:T(128)} %pad_add_fusion.place_ref, bf16[384,1792]{1,0:T(8,128)(2,1)} %refs_0_.5, bf16[384,1792]{1,0:T(8,128)(2,1)} %copy-done.1, bf16[384,896]{1,0:T(8,128)(2,1)} %collective-permute-done.3.refs_2_, bf16[512,896]{1,0:T(8,128)(2,1)} %refs_6_.1, ...), custom_call_target="tpu_custom_call" | custom-call | flops 1000 | bytes 1000 | tf_op jit(solution)/shard_map/own_block/pallas_call | solution.py:127
  69.9 0.6 collective-permute-done.13.refs_16_.refs_17_
  70.5 0.5 collective-permute-start.18
  71.0 1.6 collective-permute-start.21
  72.6 4.4 %collective-permute-start.20 = (bf16[256,896]{1,0:T(8,128)(2,1)S(1)}, bf16[256,896]{1,0:T(8,128)(2,1)S(1)}, u32[]{:S(2)}, u32[]{:S(2)}) collective-permute-start(bf16[256,896]{1,0:T(8,128)(2,1)S(1)} %copy-done.9), channel_id=1, source_target_pairs={{0,1},{3,2},{4,5},{7,6},{8,9},{11,10},{12,13},{15,14},{16,17},{19,... | collective-permute-start | bytes 1376264 | tf_op jit(solution)/shard_map/ppermute | solution.py:347
  77.1 0.7 collective-permute-start.19
  77.8 0.9 copy-done.13
  79.1 10.9 %end_block.1 = (f32[2,384,256]{2,1,0:T(8,128)}, f32[2,384,256]{2,1,0:T(8,128)}, f32[384,128]{1,0:T(8,128)}, f32[512,128]{1,0:T(8,128)}) custom-call(s32[2]{0:T(128)} %pad_add_fusion.place_ref, f32[2,384,256]{2,1,0:T(8,128)} %get-tuple-element.39.cross_in, f32[384,128]{1,0:T(8,128)} %get-tuple-element.40.norm_in, bf16[384,1792]{1,0:T(8,128)(2,1)} %refs_0_.5, ...), custom_call_target="tpu_custom_call" | custom-call | flops 1000 | bytes 1000 | tf_op jit(solution)/shard_map/end_block/pallas_call | solution.py:127
  90.6 1.3 collective-permute-done.22.refs_24_
  92.0 0.7 collective-permute-done.23.refs_25_
  92.7 0.7 copy-done.19
  93.4 9.5 %last_block.1 = (f32[384,1024]{1,0:T(8,128)}, f32[72,1024]{1,0:T(8,128)}) custom-call(s32[2]{0:T(128)} %pad_add_fusion.place_ref, f32[2,384,256]{2,1,0:T(8,128)} %get-tuple-element.47.cross_own_in, f32[2,384,256]{2,1,0:T(8,128)} %get-tuple-element.48.cross_end_in, f32[384,128]{1,0:T(8,128)} %get-tuple-element.49.row_norm_in, ...), custom_call_target="tpu_custom_call" | custom-call | flops 1000 | bytes 1000 | tf_op jit(solution)/shard_map/last_block/pallas_call | solution.py:127
  102.9 1.1 slice_select_fusion.2
  104.2 1.2 collective-permute-done.24
  105.5 1.0 select_add_fusion.2
  106.5 1.8 %collective-permute-start.27 = (f32[72,512]{1,0:T(8,128)S(1)}, f32[72,512]{1,0:T(8,128)S(1)}, u32[]{:S(2)}, u32[]{:S(2)}) collective-permute-start(f32[72,512]{1,0:T(8,128)S(1)} %select_add_fusion.2), channel_id=1, source_target_pairs={{0,24},{4,28},{8,16},{12,20},{16,8},{20,12},{24,0},{28,4},{1,25},{... | collective-permute-start | bytes 442376 | tf_op jit(solution)/shard_map/ppermute | solution.py:36
  108.8 1.3 collective-permute-start.25
  110.0 4.1 %collective-permute-done.27 = f32[72,512]{1,0:T(8,128)S(1)} collective-permute-done((f32[72,512]{1,0:T(8,128)S(1)}, f32[72,512]{1,0:T(8,128)S(1)}, u32[]{:S(2)}, u32[]{:S(2)}) %collective-permute-start.27) | collective-permute-done | bytes 147488 | tf_op jit(solution)/shard_map/ppermute | solution.py:36
  114.2 2.3 %collective-permute-done.26 = f32[72,512]{1,0:T(8,128)S(1)} collective-permute-done((f32[72,512]{1,0:T(8,128)S(1)}, f32[72,512]{1,0:T(8,128)S(1)}, u32[]{:S(2)}, u32[]{:S(2)}) %collective-permute-start.26) | collective-permute-done | bytes 147488 | tf_op jit(solution)/shard_map/ppermute | solution.py:36
  116.6 1.4 collective-permute-done.28
  118.2 1.6 fusion.28
  119.8 0.7 collective-permute-start.29
  120.7 1.1 fusion.9
  122.0 1.2 collective-permute-done.30
  123.3 1.8 %collective-permute-start.33 = (f32[72,512]{1,0:T(8,128)S(1)}, f32[72,512]{1,0:T(8,128)S(1)}, u32[]{:S(2)}, u32[]{:S(2)}) collective-permute-start(f32[72,512]{1,0:T(8,128)S(1)} %select_add_fusion.1), channel_id=1, source_target_pairs={{0,24},{4,28},{8,16},{12,20},{16,8},{20,12},{24,0},{28,4},{1,25},{... | collective-permute-start | bytes 442376 | tf_op jit(solution)/shard_map/ppermute | solution.py:36
  125.1 0.6 collective-permute-start.32
  125.7 1.1 collective-permute-start.31
  126.8 4.1 %collective-permute-done.33 = f32[72,512]{1,0:T(8,128)S(1)} collective-permute-done((f32[72,512]{1,0:T(8,128)S(1)}, f32[72,512]{1,0:T(8,128)S(1)}, u32[]{:S(2)}, u32[]{:S(2)}) %collective-permute-start.33) | collective-permute-done | bytes 147488 | tf_op jit(solution)/shard_map/ppermute | solution.py:36
  130.9 2.3 %collective-permute-done.32 = f32[72,512]{1,0:T(8,128)S(1)} collective-permute-done((f32[72,512]{1,0:T(8,128)S(1)}, f32[72,512]{1,0:T(8,128)S(1)}, u32[]{:S(2)}, u32[]{:S(2)}) %collective-permute-start.32) | collective-permute-done | bytes 147488 | tf_op jit(solution)/shard_map/ppermute | solution.py:36
  133.4 1.4 collective-permute-done.34
  135.1 1.6 fusion.25
  136.7 0.7 collective-permute-start.35
  137.4 1.1 fusion.12
  139.0 1.2 collective-permute-done.36
  140.3 1.8 %collective-permute-start.39 = (f32[72,512]{1,0:T(8,128)S(1)}, f32[72,512]{1,0:T(8,128)S(1)}, u32[]{:S(2)}, u32[]{:S(2)}) collective-permute-start(f32[72,512]{1,0:T(8,128)S(1)} %select_add_fusion), channel_id=1, source_target_pairs={{0,24},{4,28},{8,16},{12,20},{16,8},{20,12},{24,0},{28,4},{1,25},{... | collective-permute-start | bytes 442376 | tf_op jit(solution)/shard_map/ppermute | solution.py:36
  142.1 0.6 collective-permute-start.38
  142.7 1.1 collective-permute-start.37
  143.8 4.1 %collective-permute-done.39 = f32[72,512]{1,0:T(8,128)S(1)} collective-permute-done((f32[72,512]{1,0:T(8,128)S(1)}, f32[72,512]{1,0:T(8,128)S(1)}, u32[]{:S(2)}, u32[]{:S(2)}) %collective-permute-start.39) | collective-permute-done | bytes 147488 | tf_op jit(solution)/shard_map/ppermute | solution.py:36
  148.0 2.3 %collective-permute-done.38 = f32[72,512]{1,0:T(8,128)S(1)} collective-permute-done((f32[72,512]{1,0:T(8,128)S(1)}, f32[72,512]{1,0:T(8,128)S(1)}, u32[]{:S(2)}, u32[]{:S(2)}) %collective-permute-start.38) | collective-permute-done | bytes 147488 | tf_op jit(solution)/shard_map/ppermute | solution.py:36
  150.4 1.4 collective-permute-done.40
  152.0 1.3 collective-permute-start.41
  153.3 21.8 %collective-permute-done.41 = f32[128,512]{1,0:T(8,128)S(1)} collective-permute-done((f32[128,512]{1,0:T(8,128)S(1)}, f32[128,512]{1,0:T(8,128)S(1)}, u32[]{:S(2)}, u32[]{:S(2)}) %collective-permute-start.41) | collective-permute-done | bytes 262176 | tf_op jit(solution)/shard_map/ppermute | solution.py:399
  175.2 0.7 slice_bitcast_fusion
  (104 shorter events, 4.4 us)
Async XLA Ops:
  0.6 24.8 %collective-permute-start.2 = (bf16[512,896]{1,0:T(8,128)(2,1)}, bf16[512,896]{1,0:T(8,128)(2,1)}, u32[]{:S(2)}, u32[]{:S(2)}) collective-permute-start(bf16[512,896]{1,0:T(8,128)(2,1)} %refs_6_.1), channel_id=1, source_target_pairs={{0,1},{3,2},{4,5},{7,6},{8,9},{11,10},{12,13},{15,14},{16,17},{19,... | collective-permute-start | bytes 2752520 | tf_op jit(solution)/shard_map/ppermute | solution.py:323
  6.5 22.0 %collective-permute-start.1 = (bf16[512,896]{1,0:T(8,128)(2,1)}, bf16[512,896]{1,0:T(8,128)(2,1)S(1)}, u32[]{:S(2)}, u32[]{:S(2)}) collective-permute-start(bf16[512,896]{1,0:T(8,128)(2,1)} %refs_6_.1), channel_id=1, source_target_pairs={{0,16},{4,20},{8,24},{12,28},{16,0},{20,4},{24,8},{28,12},{1,17},{... | collective-permute-start | bytes 2752520 | tf_op jit(solution)/shard_map/ppermute | solution.py:36
  8.0 21.7 %collective-permute-start = (bf16[512,896]{1,0:T(8,128)(2,1)}, bf16[512,896]{1,0:T(8,128)(2,1)S(1)}, u32[]{:S(2)}, u32[]{:S(2)}) collective-permute-start(bf16[512,896]{1,0:T(8,128)(2,1)} %refs_6_.1), channel_id=1, source_target_pairs={{0,8},{4,12},{8,0},{12,4},{16,24},{20,28},{24,16},{28,20},{1,9},{5... | collective-permute-start | bytes 2752520 | tf_op jit(solution)/shard_map/ppermute | solution.py:36
  9.5 32.0 %collective-permute-start.4 = (bf16[384,1792]{1,0:T(8,128)(2,1)}, bf16[384,1792]{1,0:T(8,128)(2,1)S(1)}, u32[]{:S(2)}, u32[]{:S(2)}) collective-permute-start(bf16[384,1792]{1,0:T(8,128)(2,1)} %refs_0_.5), channel_id=1, source_target_pairs={{1,2},{2,1},{5,6},{6,5},{9,10},{10,9},{13,14},{14,13},{17,18},{18,... | collective-permute-start | bytes 4128776 | tf_op jit(solution)/shard_map/ppermute | solution.py:325
  12.5 21.6 %copy-start.4 = (bf16[512,896]{1,0:T(8,128)(2,1)S(1)}, bf16[512,896]{1,0:T(8,128)(2,1)}, u32[]{:S(2)}) copy-start(bf16[512,896]{1,0:T(8,128)(2,1)} %refs_6_.1) | copy-start | bytes 2752516
  28.5 32.0 %copy-start.2 = (bf16[512,896]{1,0:T(8,128)(2,1)}, bf16[512,896]{1,0:T(8,128)(2,1)S(1)}, u32[]{:S(2)}) copy-start(bf16[512,896]{1,0:T(8,128)(2,1)S(1)} %collective-permute-done.1.refs_5_.refs_7_.refs_8_) | copy-start | bytes 2752516
  29.8 30.8 %copy-start.3 = (bf16[512,896]{1,0:T(8,128)(2,1)}, bf16[512,896]{1,0:T(8,128)(2,1)S(1)}, u32[]{:S(2)}) copy-start(bf16[512,896]{1,0:T(8,128)(2,1)S(1)} %collective-permute-done.refs_4_.refs_6_.refs_7_) | copy-start | bytes 2752516
  29.9 10.8 %collective-permute-start.5 = (bf16[256,896]{1,0:T(8,128)(2,1)S(1)}, bf16[256,896]{1,0:T(8,128)(2,1)S(1)}, u32[]{:S(2)}, u32[]{:S(2)}) collective-permute-start(bf16[256,896]{1,0:T(8,128)(2,1)S(1)} %slice.86), channel_id=1, source_target_pairs={{0,16},{4,20},{8,24},{12,28},{16,0},{20,4},{24,8},{28,12},{1,17},{... | collective-permute-start | bytes 1376264 | tf_op jit(solution)/shard_map/ppermute | solution.py:36
  30.4 10.6 %collective-permute-start.6 = (bf16[256,896]{1,0:T(8,128)(2,1)S(1)}, bf16[256,896]{1,0:T(8,128)(2,1)S(1)}, u32[]{:S(2)}, u32[]{:S(2)}) collective-permute-start(bf16[256,896]{1,0:T(8,128)(2,1)S(1)} %slice.87), channel_id=1, source_target_pairs={{0,8},{4,12},{8,0},{12,4},{16,24},{20,28},{24,16},{28,20},{1,9},{5... | collective-permute-start | bytes 1376264 | tf_op jit(solution)/shard_map/ppermute | solution.py:36
  31.9 14.4 %collective-permute-start.3 = (bf16[384,896]{1,0:T(8,128)(2,1)S(1)}, bf16[384,896]{1,0:T(8,128)(2,1)}, u32[]{:S(2)}, u32[]{:S(2)}) collective-permute-start(bf16[384,896]{1,0:T(8,128)(2,1)S(1)} %get-tuple-element.30), channel_id=1, source_target_pairs={{0,1},{3,2},{4,5},{7,6},{8,9},{11,10},{12,13},{15,14},{16,17},{19,... | collective-permute-start | bytes 2064392 | tf_op jit(solution)/shard_map/ppermute | solution.py:327
  34.1 14.2 %collective-permute-start.7 = (bf16[512,896]{1,0:T(8,128)(2,1)S(1)}, bf16[512,896]{1,0:T(8,128)(2,1)S(1)}, u32[]{:S(2)}, u32[]{:S(2)}) collective-permute-start(bf16[512,896]{1,0:T(8,128)(2,1)S(1)} %copy-done.4), channel_id=1, source_target_pairs={{0,4},{4,0},{8,12},{12,8},{16,20},{20,16},{24,28},{28,24},{1,5},{5... | collective-permute-start | bytes 2752520 | tf_op jit(solution)/shard_map/ppermute | solution.py:36
  40.7 16.4 %copy-start.8 = (bf16[256,896]{1,0:T(8,128)(2,1)}, bf16[256,896]{1,0:T(8,128)(2,1)S(1)}, u32[]{:S(2)}) copy-start(bf16[256,896]{1,0:T(8,128)(2,1)S(1)} %collective-permute-done.5.refs_6_.refs_8_.refs_9_) | copy-start | bytes 1376260
  41.0 16.2 %copy-start.10 = (bf16[256,896]{1,0:T(8,128)(2,1)}, bf16[256,896]{1,0:T(8,128)(2,1)S(1)}, u32[]{:S(2)}) copy-start(bf16[256,896]{1,0:T(8,128)(2,1)S(1)} %collective-permute-done.6.refs_7_.refs_9_.refs_10_) | copy-start | bytes 1376260
  41.0 5.3 %collective-permute-start.11 = (bf16[256,896]{1,0:T(8,128)(2,1)S(1)}, bf16[256,896]{1,0:T(8,128)(2,1)S(1)}, u32[]{:S(2)}, u32[]{:S(2)}) collective-permute-start(bf16[256,896]{1,0:T(8,128)(2,1)S(1)} %collective-permute-done.6.refs_7_.refs_9_.refs_10_), channel_id=1, source_target_pairs={{0,4},{4,0},{8,12},{12,8},{16,20},{20,16},{24,28},{28,24},{1,5},{5... | collective-permute-start | bytes 1376264 | tf_op jit(solution)/shard_map/ppermute | solution.py:36
  41.0 6.7 %collective-permute-start.10 = (bf16[256,896]{1,0:T(8,128)(2,1)S(1)}, bf16[256,896]{1,0:T(8,128)(2,1)S(1)}, u32[]{:S(2)}, u32[]{:S(2)}) collective-permute-start(bf16[256,896]{1,0:T(8,128)(2,1)S(1)} %collective-permute-done.5.refs_6_.refs_8_.refs_9_), channel_id=1, source_target_pairs={{0,4},{4,0},{8,12},{12,8},{16,20},{20,16},{24,28},{28,24},{1,5},{5... | collective-permute-start | bytes 1376264 | tf_op jit(solution)/shard_map/ppermute | solution.py:36
  41.5 19.0 %copy-start.1 = (bf16[384,1792]{1,0:T(8,128)(2,1)}, bf16[384,1792]{1,0:T(8,128)(2,1)S(1)}, u32[]{:S(2)}) copy-start(bf16[384,1792]{1,0:T(8,128)(2,1)S(1)} %collective-permute-done.4.refs_1_) | copy-start | bytes 4128772
  41.5 8.3 %collective-permute-start.9 = (bf16[512,896]{1,0:T(8,128)(2,1)S(1)}, bf16[512,896]{1,0:T(8,128)(2,1)S(1)}, u32[]{:S(2)}, u32[]{:S(2)}) collective-permute-start(bf16[512,896]{1,0:T(8,128)(2,1)S(1)} %collective-permute-done.1.refs_5_.refs_7_.refs_8_), channel_id=1, source_target_pairs={{0,4},{4,0},{8,12},{12,8},{16,20},{20,16},{24,28},{28,24},{1,5},{5... | collective-permute-start | bytes 2752520 | tf_op jit(solution)/shard_map/ppermute | solution.py:36
  46.3 10.8 %collective-permute-start.8 = (bf16[512,896]{1,0:T(8,128)(2,1)S(1)}, bf16[512,896]{1,0:T(8,128)(2,1)S(1)}, u32[]{:S(2)}, u32[]{:S(2)}) collective-permute-start(bf16[512,896]{1,0:T(8,128)(2,1)S(1)} %collective-permute-done.refs_4_.refs_6_.refs_7_), channel_id=1, source_target_pairs={{0,4},{4,0},{8,12},{12,8},{16,20},{20,16},{24,28},{28,24},{1,5},{5... | collective-permute-start | bytes 2752520 | tf_op jit(solution)/shard_map/ppermute | solution.py:36
  46.3 10.9 %copy-start.11 = (bf16[256,896]{1,0:T(8,128)(2,1)}, bf16[256,896]{1,0:T(8,128)(2,1)S(1)}, u32[]{:S(2)}) copy-start(bf16[256,896]{1,0:T(8,128)(2,1)S(1)} %collective-permute-done.11.refs_12_.refs_14_.refs_15_) | copy-start | bytes 1376260
  46.3 23.6 %collective-permute-start.14 = (bf16[512,896]{1,0:T(8,128)(2,1)}, bf16[512,896]{1,0:T(8,128)(2,1)}, u32[]{:S(2)}, u32[]{:S(2)}) collective-permute-start(bf16[512,896]{1,0:T(8,128)(2,1)} %collective-permute-done.2.refs_15_.refs_16_), channel_id=1, source_target_pairs={{0,16},{4,20},{8,24},{12,28},{16,0},{20,4},{24,8},{28,12},{1,17},{... | collective-permute-start | bytes 2752520 | tf_op jit(solution)/shard_map/ppermute | solution.py:36
  47.7 9.5 %copy-start.12 = (bf16[256,896]{1,0:T(8,128)(2,1)}, bf16[256,896]{1,0:T(8,128)(2,1)S(1)}, u32[]{:S(2)}) copy-start(bf16[256,896]{1,0:T(8,128)(2,1)S(1)} %collective-permute-done.10.refs_11_.refs_13_.refs_14_) | copy-start | bytes 1376260
  47.7 22.7 %collective-permute-start.13 = (bf16[512,896]{1,0:T(8,128)(2,1)}, bf16[512,896]{1,0:T(8,128)(2,1)}, u32[]{:S(2)}, u32[]{:S(2)}) collective-permute-start(bf16[512,896]{1,0:T(8,128)(2,1)} %collective-permute-done.2.refs_15_.refs_16_), channel_id=1, source_target_pairs={{0,8},{4,12},{8,0},{12,4},{16,24},{20,28},{24,16},{28,20},{1,9},{5... | collective-permute-start | bytes 2752520 | tf_op jit(solution)/shard_map/ppermute | solution.py:36
  48.2 8.9 %copy-start.5 = (bf16[512,896]{1,0:T(8,128)(2,1)}, bf16[512,896]{1,0:T(8,128)(2,1)S(1)}, u32[]{:S(2)}) copy-start(bf16[512,896]{1,0:T(8,128)(2,1)S(1)} %collective-permute-done.7.refs_8_.refs_10_.refs_11_) | copy-start | bytes 2752516
  48.2 22.2 %collective-permute-start.15 = (bf16[384,896]{1,0:T(8,128)(2,1)}, bf16[384,896]{1,0:T(8,128)(2,1)}, u32[]{:S(2)}, u32[]{:S(2)}) collective-permute-start(bf16[384,896]{1,0:T(8,128)(2,1)} %collective-permute-done.3.refs_2_), channel_id=1, source_target_pairs={{1,2},{2,1},{5,6},{6,5},{9,10},{10,9},{13,14},{14,13},{17,18},{18,... | collective-permute-start | bytes 2064392 | tf_op jit(solution)/shard_map/ppermute | solution.py:335
  49.8 7.4 %copy-start.6 = (bf16[512,896]{1,0:T(8,128)(2,1)}, bf16[512,896]{1,0:T(8,128)(2,1)S(1)}, u32[]{:S(2)}) copy-start(bf16[512,896]{1,0:T(8,128)(2,1)S(1)} %collective-permute-done.9.refs_10_.refs_12_.refs_13_) | copy-start | bytes 2752516
  49.8 21.2 %collective-permute-start.12 = (bf16[384,896]{1,0:T(8,128)(2,1)}, bf16[384,896]{1,0:T(8,128)(2,1)}, u32[]{:S(2)}, u32[]{:S(2)}) collective-permute-start(bf16[384,896]{1,0:T(8,128)(2,1)} %get-tuple-element.41), channel_id=1, source_target_pairs={{0,1},{3,2},{4,5},{7,6},{8,9},{11,10},{12,13},{15,14},{16,17},{19,... | collective-permute-start | bytes 2064392 | tf_op jit(solution)/shard_map/ppermute | solution.py:336
  57.1 0.9 copy-start.7
  57.1 19.9 %collective-permute-start.16 = (bf16[512,896]{1,0:T(8,128)(2,1)}, bf16[512,896]{1,0:T(8,128)(2,1)}, u32[]{:S(2)}, u32[]{:S(2)}) collective-permute-start(bf16[512,896]{1,0:T(8,128)(2,1)} %collective-permute-done.2.refs_15_.refs_16_), channel_id=1, source_target_pairs={{0,4},{4,0},{8,12},{12,8},{16,20},{20,16},{24,28},{28,24},{1,5},{5... | collective-permute-start | bytes 2752520 | tf_op jit(solution)/shard_map/ppermute | solution.py:36
  60.6 12.1 %copy-start.9 = (bf16[256,896]{1,0:T(8,128)(2,1)S(1)}, bf16[256,896]{1,0:T(8,128)(2,1)}, u32[]{:S(2)}) copy-start(bf16[256,896]{1,0:T(8,128)(2,1)} %copy-done.8) | copy-start | bytes 1376260
  70.5 7.3 %collective-permute-start.17 = (bf16[512,896]{1,0:T(8,128)(2,1)}, bf16[512,896]{1,0:T(8,128)(2,1)S(1)}, u32[]{:S(2)}, u32[]{:S(2)}) collective-permute-start(bf16[512,896]{1,0:T(8,128)(2,1)} %collective-permute-done.13.refs_16_.refs_17_), channel_id=1, source_target_pairs={{0,4},{4,0},{8,12},{12,8},{16,20},{20,16},{24,28},{28,24},{1,5},{5... | collective-permute-start | bytes 2752520 | tf_op jit(solution)/shard_map/ppermute | solution.py:36
  70.5 7.3 %collective-permute-start.18 = (bf16[512,896]{1,0:T(8,128)(2,1)}, bf16[512,896]{1,0:T(8,128)(2,1)S(1)}, u32[]{:S(2)}, u32[]{:S(2)}) collective-permute-start(bf16[512,896]{1,0:T(8,128)(2,1)} %collective-permute-done.14.refs_17_.refs_18_), channel_id=1, source_target_pairs={{0,4},{4,0},{8,12},{12,8},{16,20},{20,16},{24,28},{28,24},{1,5},{5... | collective-permute-start | bytes 2752520 | tf_op jit(solution)/shard_map/ppermute | solution.py:36
  71.0 19.0 %collective-permute-start.21 = (bf16[256,896]{1,0:T(8,128)(2,1)}, bf16[256,896]{1,0:T(8,128)(2,1)S(1)}, u32[]{:S(2)}, u32[]{:S(2)}) collective-permute-start(bf16[256,896]{1,0:T(8,128)(2,1)} %slice.88), channel_id=1, source_target_pairs={{0,24},{4,28},{8,16},{12,20},{16,8},{20,12},{24,0},{28,4},{1,25},{... | collective-permute-start | bytes 1376264 | tf_op jit(solution)/shard_map/ppermute | solution.py:36
  72.6 17.4 %collective-permute-start.20 = (bf16[256,896]{1,0:T(8,128)(2,1)S(1)}, bf16[256,896]{1,0:T(8,128)(2,1)S(1)}, u32[]{:S(2)}, u32[]{:S(2)}) collective-permute-start(bf16[256,896]{1,0:T(8,128)(2,1)S(1)} %copy-done.9), channel_id=1, source_target_pairs={{0,1},{3,2},{4,5},{7,6},{8,9},{11,10},{12,13},{15,14},{16,17},{19,... | collective-permute-start | bytes 1376264 | tf_op jit(solution)/shard_map/ppermute | solution.py:347
  77.1 13.6 %collective-permute-start.19 = (bf16[384,896]{1,0:T(8,128)(2,1)}, bf16[384,896]{1,0:T(8,128)(2,1)S(1)}, u32[]{:S(2)}, u32[]{:S(2)}) collective-permute-start(bf16[384,896]{1,0:T(8,128)(2,1)} %collective-permute-done.12.refs_3_), channel_id=1, source_target_pairs={{1,2},{2,1},{5,6},{6,5},{9,10},{10,9},{13,14},{14,13},{17,18},{18,... | collective-permute-start | bytes 2064392 | tf_op jit(solution)/shard_map/ppermute | solution.py:346
  77.8 0.9 copy-start.13
  77.8 1.3 copy-start.14
  90.0 2.6 %copy-start.16 = (bf16[256,896]{1,0:T(8,128)(2,1)}, bf16[256,896]{1,0:T(8,128)(2,1)S(1)}, u32[]{:S(2)}) copy-start(bf16[256,896]{1,0:T(8,128)(2,1)S(1)} %collective-permute-done.21.refs_23_) | copy-start | bytes 1376260
  90.1 2.6 %copy-start.17 = (bf16[256,896]{1,0:T(8,128)(2,1)}, bf16[256,896]{1,0:T(8,128)(2,1)S(1)}, u32[]{:S(2)}) copy-start(bf16[256,896]{1,0:T(8,128)(2,1)S(1)} %collective-permute-done.20.refs_22_) | copy-start | bytes 1376260
  90.1 1.9 %collective-permute-start.22 = (bf16[256,896]{1,0:T(8,128)(2,1)S(1)}, bf16[256,896]{1,0:T(8,128)(2,1)S(1)}, u32[]{:S(2)}, u32[]{:S(2)}) collective-permute-start(bf16[256,896]{1,0:T(8,128)(2,1)S(1)} %collective-permute-done.20.refs_22_), channel_id=1, source_target_pairs={{0,4},{4,0},{8,12},{12,8},{16,20},{20,16},{24,28},{28,24},{1,5},{5... | collective-permute-start | bytes 1376264 | tf_op jit(solution)/shard_map/ppermute | solution.py:36
  90.1 2.5 %collective-permute-start.23 = (bf16[256,896]{1,0:T(8,128)(2,1)S(1)}, bf16[256,896]{1,0:T(8,128)(2,1)S(1)}, u32[]{:S(2)}, u32[]{:S(2)}) collective-permute-start(bf16[256,896]{1,0:T(8,128)(2,1)S(1)} %collective-permute-done.21.refs_23_), channel_id=1, source_target_pairs={{0,4},{4,0},{8,12},{12,8},{16,20},{20,16},{24,28},{28,24},{1,5},{5... | collective-permute-start | bytes 1376264 | tf_op jit(solution)/shard_map/ppermute | solution.py:36
  90.6 2.0 %copy-start.15 = (bf16[384,896]{1,0:T(8,128)(2,1)}, bf16[384,896]{1,0:T(8,128)(2,1)S(1)}, u32[]{:S(2)}) copy-start(bf16[384,896]{1,0:T(8,128)(2,1)S(1)} %collective-permute-done.19.refs_5_) | copy-start | bytes 2064388
  92.0 0.8 copy-start.18
  92.6 0.8 copy-start.19
  102.9 15.3 %copy-start = (f32[384,1024]{1,0:T(8,128)S(1)}, f32[384,1024]{1,0:T(8,128)}, u32[]{:S(2)}) copy-start(f32[384,1024]{1,0:T(8,128)} %get-tuple-element.57) | copy-start | bytes 4718596
  104.0 1.4 collective-permute-start.24
  106.5 7.7 %collective-permute-start.27 = (f32[72,512]{1,0:T(8,128)S(1)}, f32[72,512]{1,0:T(8,128)S(1)}, u32[]{:S(2)}, u32[]{:S(2)}) collective-permute-start(f32[72,512]{1,0:T(8,128)S(1)} %select_add_fusion.2), channel_id=1, source_target_pairs={{0,24},{4,28},{8,16},{12,20},{16,8},{20,12},{24,0},{28,4},{1,25},{... | collective-permute-start | bytes 442376 | tf_op jit(solution)/shard_map/ppermute | solution.py:36
  108.3 8.2 %collective-permute-start.26 = (f32[72,512]{1,0:T(8,128)S(1)}, f32[72,512]{1,0:T(8,128)S(1)}, u32[]{:S(2)}, u32[]{:S(2)}) collective-permute-start(f32[72,512]{1,0:T(8,128)S(1)} %select_add_fusion.2), channel_id=1, source_target_pairs={{0,16},{4,20},{8,24},{12,28},{16,0},{20,4},{24,8},{28,12},{1,17},{... | collective-permute-start | bytes 442376 | tf_op jit(solution)/shard_map/ppermute | solution.py:36
  108.8 7.7 %collective-permute-start.25 = (f32[72,512]{1,0:T(8,128)S(1)}, f32[72,512]{1,0:T(8,128)S(1)}, u32[]{:S(2)}, u32[]{:S(2)}) collective-permute-start(f32[72,512]{1,0:T(8,128)S(1)} %select_add_fusion.2), channel_id=1, source_target_pairs={{0,8},{4,12},{8,0},{12,4},{16,24},{20,28},{24,16},{28,20},{1,9},{5... | collective-permute-start | bytes 442376 | tf_op jit(solution)/shard_map/ppermute | solution.py:36
  116.6 1.4 collective-permute-start.28
  119.8 0.7 collective-permute-start.29
  121.8 1.4 collective-permute-start.30
  123.3 7.7 %collective-permute-start.33 = (f32[72,512]{1,0:T(8,128)S(1)}, f32[72,512]{1,0:T(8,128)S(1)}, u32[]{:S(2)}, u32[]{:S(2)}) collective-permute-start(f32[72,512]{1,0:T(8,128)S(1)} %select_add_fusion.1), channel_id=1, source_target_pairs={{0,24},{4,28},{8,16},{12,20},{16,8},{20,12},{24,0},{28,4},{1,25},{... | collective-permute-start | bytes 442376 | tf_op jit(solution)/shard_map/ppermute | solution.py:36
  125.1 8.2 %collective-permute-start.32 = (f32[72,512]{1,0:T(8,128)S(1)}, f32[72,512]{1,0:T(8,128)S(1)}, u32[]{:S(2)}, u32[]{:S(2)}) collective-permute-start(f32[72,512]{1,0:T(8,128)S(1)} %select_add_fusion.1), channel_id=1, source_target_pairs={{0,16},{4,20},{8,24},{12,28},{16,0},{20,4},{24,8},{28,12},{1,17},{... | collective-permute-start | bytes 442376 | tf_op jit(solution)/shard_map/ppermute | solution.py:36
  125.7 7.6 %collective-permute-start.31 = (f32[72,512]{1,0:T(8,128)S(1)}, f32[72,512]{1,0:T(8,128)S(1)}, u32[]{:S(2)}, u32[]{:S(2)}) collective-permute-start(f32[72,512]{1,0:T(8,128)S(1)} %select_add_fusion.1), channel_id=1, source_target_pairs={{0,8},{4,12},{8,0},{12,4},{16,24},{20,28},{24,16},{28,20},{1,9},{5... | collective-permute-start | bytes 442376 | tf_op jit(solution)/shard_map/ppermute | solution.py:36
  133.3 1.4 collective-permute-start.34
  136.7 0.7 collective-permute-start.35
  138.8 1.4 collective-permute-start.36
  140.3 7.7 %collective-permute-start.39 = (f32[72,512]{1,0:T(8,128)S(1)}, f32[72,512]{1,0:T(8,128)S(1)}, u32[]{:S(2)}, u32[]{:S(2)}) collective-permute-start(f32[72,512]{1,0:T(8,128)S(1)} %select_add_fusion), channel_id=1, source_target_pairs={{0,24},{4,28},{8,16},{12,20},{16,8},{20,12},{24,0},{28,4},{1,25},{... | collective-permute-start | bytes 442376 | tf_op jit(solution)/shard_map/ppermute | solution.py:36
  142.1 8.2 %collective-permute-start.38 = (f32[72,512]{1,0:T(8,128)S(1)}, f32[72,512]{1,0:T(8,128)S(1)}, u32[]{:S(2)}, u32[]{:S(2)}) collective-permute-start(f32[72,512]{1,0:T(8,128)S(1)} %select_add_fusion), channel_id=1, source_target_pairs={{0,16},{4,20},{8,24},{12,28},{16,0},{20,4},{24,8},{28,12},{1,17},{... | collective-permute-start | bytes 442376 | tf_op jit(solution)/shard_map/ppermute | solution.py:36
  142.7 7.6 %collective-permute-start.37 = (f32[72,512]{1,0:T(8,128)S(1)}, f32[72,512]{1,0:T(8,128)S(1)}, u32[]{:S(2)}, u32[]{:S(2)}) collective-permute-start(f32[72,512]{1,0:T(8,128)S(1)} %select_add_fusion), channel_id=1, source_target_pairs={{0,8},{4,12},{8,0},{12,4},{16,24},{20,28},{24,16},{28,20},{1,9},{5... | collective-permute-start | bytes 442376 | tf_op jit(solution)/shard_map/ppermute | solution.py:36
  150.3 1.4 collective-permute-start.40
  152.0 23.1 %collective-permute-start.41 = (f32[128,512]{1,0:T(8,128)S(1)}, f32[128,512]{1,0:T(8,128)S(1)}, u32[]{:S(2)}, u32[]{:S(2)}) collective-permute-start(f32[128,512]{1,0:T(8,128)S(1)} %pad_maximum_fusion), channel_id=1, source_target_pairs={{1,0},{2,3},{5,4},{6,7},{9,8},{10,11},{13,12},{14,15},{17,16},{18,... | collective-permute-start | bytes 786440 | tf_op jit(solution)/shard_map/ppermute | solution.py:399

commit v4 on v3

--- a/solution.py
+++ b/solution.py
@@ -27,9 +27,16 @@
     )
 
 
-TO_MIDDLE = [(0, 1), (3, 2)]
-ACROSS = [(1, 2), (2, 1)]
-TO_END = [(1, 0), (2, 3)]
+NEIGHBOURS = [(0, 1), (1, 0), (2, 3), (3, 2)]
+
+
+def handed(block):
+    return lax.ppermute(block, "landmark", NEIGHBOURS)
+
+
+def across(block):
+    pairs = [(4 * p + z, 4 * p + 3 - z if z in (1, 2) else 4 * (p ^ 1) + z) for p in range(8) for z in range(4)]
+    return lax.ppermute(block, ("proof", "landmark"), pairs)
 
 
 def flipped(block, bits):
@@ -49,7 +56,7 @@
 
 
 def sum_middle(block):
-    return block + lax.ppermute(block, "landmark", ACROSS)
+    return block + across(block)
 
 
 def packed(block, *vectors):
@@ -320,11 +327,11 @@
     m, half = own.shape
     n, middle = row_features.shape[0], m // 2
     left, right = row_features[:, :half], row_features[:, half:]
-    end = lax.ppermute(own, "landmark", TO_MIDDLE)
+    end = handed(own)
     own_x, own_y = flipped(own, 2), flipped(own, 4)
-    middle_rows = lax.ppermute(row_features, "landmark", ACROSS)
+    middle_rows = across(row_features)
     own_x, own_y, end, left = lax.optimization_barrier((own_x, own_y, end, left))
-    end_left = lax.ppermute(left, "landmark", TO_MIDDLE)
+    end_left = handed(left)
     own_low, own_high = flipped(own_x[:middle], 4), flipped(own_y[middle:], 2)
     other_own, other_x, other_y = flipped(after(own, own_x), 1), flipped(own_x, 1), flipped(own_y, 1)
     own_low, own_high, end = lax.optimization_barrier((own_low, own_high, end))
@@ -332,8 +339,8 @@
     other_low, other_high = flipped(own_low, 1), flipped(own_high, 1)
     end_bottom = end[middle:]
     end_left, right, middle_rows = lax.optimization_barrier((end_left, right, middle_rows))
-    far_left = lax.ppermute(end_left, "landmark", ACROSS)
-    end_right = lax.ppermute(right, "landmark", TO_MIDDLE)
+    far_left = across(end_left)
+    end_right = handed(right)
     own_parts = [
         (0, 0, own), (2, 0, own_x), (4, 0, own_y), (6, 0, own_low), (6, middle, own_high),
         (1, 0, other_own), (3, 0, other_x), (5, 0, other_y), (7, 0, other_low), (7, middle, other_high),
@@ -343,8 +350,8 @@
     end_x, end_y, end_bottom, far_left, _ = lax.optimization_barrier((end_x, end_y, end_bottom, far_left, cross_own))
     end_high = flipped(end_bottom, 6)
     end_right = after(end_right, end_x, end_y)
-    far_right = lax.ppermute(end_right, "landmark", ACROSS)
-    end_low = lax.ppermute(after(own_low, end_right), "landmark", TO_MIDDLE)
+    far_right = across(end_right)
+    end_low = handed(after(own_low, end_right))
     end_parts = [(0, 0, end), (2, 0, end_x), (4, 0, end_y)]
     end_parts += [(bits + 1, row, flipped(block, 1)) for bits, row, block in end_parts]
     rows |= {(1, 1): end_right, (2, 0): far_left}
@@ -396,7 +403,7 @@
     coefficient, residual = conjugate_gradients(kernel, sums, columns, lam, sum_rows_axis, sum_middle)
     both = jnp.concatenate([coefficient, residual], axis=0)
     half = both.shape[1] // 2
-    received = lax.ppermute(both[:, half:], "landmark", TO_END)
+    received = handed(both[:, half:])
     z = lax.axis_index("landmark")
     both = jnp.where((z == 1) | (z == 2), both[:, :half], received)
     return both[: columns.shape[0]].T, both[columns.shape[0] :].T

time: 176 us -> 166 us (0.943)
  starting transfers between devices: 47.2 us -> 38.8 us
  waiting for transfers between devices: 80.4 us -> 78.6 us
    ppermute x10, waiting for transfers between devices: 39.5 us -> 30 us  [the longest x5 27.7 us: handed(): return lax.ppermute(block, 'landmark', NEIGHBOURS)]
    ppermute x32, waiting for transfers between devices: 40.9 us -> 48.6 us  [flipped(): return lax.ppermute(block, 'proof', [(i, i ^ bits) for i in range(8)])]
    ppermute x10, starting transfers between devices: 25.4 us -> 17.7 us  [the longest x5 17.3 us: handed(): return lax.ppermute(block, 'landmark', NEIGHBOURS)]
  transfers between devices with their start and end apart: 42 -> 42, of which waited for: 23 -> 27; matrix products, arithmetic and copies ran while one was open for 3% -> 3% of each run, Pallas kernels for 11% -> 12%
where the time goes in v4:
time: 166 us; the launch traced here: 165 us
  waiting for transfers between devices  78.6 us (47%)
  starting transfers between devices  38.8 us (23%)
  Pallas kernels  29.7 us (18%)
  local copies, waits for them, and re-layouts  7.51 us (5%)
  matrix products  5.35 us (3%)
  other arithmetic  4.19 us (3%)
    ppermute x32, waiting for transfers between devices, flipped(): return lax.ppermute(block, 'proof', [(i, i ^ bits) for i in range(8)])  48.6 us
    pallas_call x3, Pallas kernels, call(): pl.pallas_call(body, out_shape=tuple((jax.ShapeDtypeStruct(shape, jnp.flo...  29.7 us
    ppermute x5, waiting for transfers between devices, handed(): return lax.ppermute(block, 'landmark', NEIGHBOURS)  27.7 us
    ppermute x32, starting transfers between devices, flipped(): return lax.ppermute(block, 'proof', [(i, i ^ bits) for i in range(8)])  21.1 us
    ppermute x5, starting transfers between devices, handed(): return lax.ppermute(block, 'landmark', NEIGHBOURS)  17.3 us
    dot_general x4, matrix products, times(): lax.dot_general(left, right, ((contract[:1], contract[1:]), ((), ())), pr...  5.35 us
  transfers between devices with their start and end apart: 42, of which 27 were waited for; matrix products, arithmetic and copies ran while one was open for 3% of the time, Pallas kernels for 12%

profile of v4, /device:TPU:0, one launch (start us, length us, event | category | flops | bytes accessed | tf_op | source)
XLA Modules:
  0.0 165.2 jit_solution(6488033304377423037)
XLA Ops:
  0.6 3.1 %collective-permute-start.2 = (bf16[512,896]{1,0:T(8,128)(2,1)}, bf16[512,896]{1,0:T(8,128)(2,1)}, u32[]{:S(2)}, u32[]{:S(2)}) collective-permute-start(bf16[512,896]{1,0:T(8,128)(2,1)} %refs_6_.1), channel_id=1, source_target_pairs={{0,1},{1,0},{2,3},{3,2},{4,5},{5,4},{6,7},{7,6},{8,9},{9,8},{10,11... | collective-permute-start | bytes 2752520 | tf_op jit(solution)/shard_map/ppermute | solution.py:34
  3.7 1.5 collective-permute-start.1
  5.2 1.5 collective-permute-start
  6.7 2.3 %fusion.27 = (bf16[384,896]{1,0:T(8,128)(2,1)}, bf16[384,896]{1,0:T(8,128)(2,1)S(1)}) fusion(bf16[384,1792]{1,0:T(8,128)(2,1)} %refs_0_.5), kind=kLoop, calls=%fused_computation.82 | loop fusion | bytes 2752512 | tf_op jit(solution)/shard_map/slice | solution.py:329
  9.0 15.4 %collective-permute-done.2.refs_15_.refs_16_ = bf16[512,896]{1,0:T(8,128)(2,1)} collective-permute-done((bf16[512,896]{1,0:T(8,128)(2,1)}, bf16[512,896]{1,0:T(8,128)(2,1)}, u32[]{:S(2)}, u32[]{:S(2)}) %collective-permute-start.2) | collective-permute-done | bytes 917536 | tf_op jit(solution)/shard_map/ppermute | solution.py:34
  24.4 1.4 collective-permute-done.1.refs_5_.refs_7_.refs_8_
  25.7 1.2 collective-permute-done.refs_4_.refs_6_.refs_7_
  27.1 0.6 collective-permute-start.5
  27.6 1.5 collective-permute-start.6
  29.6 8.3 %collective-permute-done.5.refs_6_.refs_8_.refs_9_ = bf16[256,896]{1,0:T(8,128)(2,1)S(1)} collective-permute-done((bf16[256,896]{1,0:T(8,128)(2,1)S(1)}, bf16[256,896]{1,0:T(8,128)(2,1)S(1)}, u32[]{:S(2)}, u32[]{:S(2)}) %collective-permute-start.5) | collective-permute-done | bytes 458784 | tf_op jit(solution)/shard_map/ppermute | solution.py:43
  38.3 0.5 collective-permute-start.10
  38.9 5.6 %collective-permute-done.3.refs_2_ = bf16[384,896]{1,0:T(8,128)(2,1)} collective-permute-done((bf16[384,896]{1,0:T(8,128)(2,1)S(1)}, bf16[384,896]{1,0:T(8,128)(2,1)}, u32[]{:S(2)}, u32[]{:S(2)}) %collective-permute-start.3) | collective-permute-done | bytes 688160 | tf_op jit(solution)/shard_map/ppermute | solution.py:34
  44.6 1.4 collective-permute-start.14
  46.0 0.5 collective-permute-start.13
  46.5 3.1 %collective-permute-start.12 = (bf16[384,896]{1,0:T(8,128)(2,1)}, bf16[384,896]{1,0:T(8,128)(2,1)}, u32[]{:S(2)}, u32[]{:S(2)}) collective-permute-start(bf16[384,896]{1,0:T(8,128)(2,1)} %get-tuple-element.41), channel_id=1, source_target_pairs={{0,1},{1,0},{2,3},{3,2},{4,5},{5,4},{6,7},{7,6},{8,9},{9,8},{10,11... | collective-permute-start | bytes 2064392 | tf_op jit(solution)/shard_map/ppermute | solution.py:34
  49.8 0.8 copy-done.7
  50.6 0.7 pad_add_fusion.place_ref
  51.3 1.8 %slice.88 = bf16[256,896]{1,0:T(8,128)(2,1)} slice(bf16[512,896]{1,0:T(8,128)(2,1)} %collective-permute-done.2.refs_15_.refs_16_), slice={[256:512], [0:896]} | slice | bytes 917504 | tf_op jit(solution)/shard_map/slice | solution.py:340
  53.1 9.3 %own_block.1 = (f32[2,384,256]{2,1,0:T(8,128)}, f32[384,128]{1,0:T(8,128)}, f32[512,128]{1,0:T(8,128)}) custom-call(s32[2]{0:T(128)} %pad_add_fusion.place_ref, bf16[384,1792]{1,0:T(8,128)(2,1)} %refs_0_.5, bf16[384,1792]{1,0:T(8,128)(2,1)} %copy-done.1, bf16[384,896]{1,0:T(8,128)(2,1)} %collective-permute-done.3.refs_2_, bf16[512,896]{1,0:T(8,128)(2,1)} %refs_6_.1, ...), custom_call_target="tpu_custom_call" | custom-call | flops 1000 | bytes 1000 | tf_op jit(solution)/shard_map/own_block/pallas_call | solution.py:134
  62.4 5.2 %collective-permute-done.14.refs_17_.refs_18_ = bf16[512,896]{1,0:T(8,128)(2,1)} collective-permute-done((bf16[512,896]{1,0:T(8,128)(2,1)}, bf16[512,896]{1,0:T(8,128)(2,1)}, u32[]{:S(2)}, u32[]{:S(2)}) %collective-permute-start.14) | collective-permute-done | bytes 917536 | tf_op jit(solution)/shard_map/ppermute | solution.py:43
  67.6 1.1 collective-permute-done.13.refs_16_.refs_17_
  68.7 0.5 collective-permute-start.18
  69.2 0.7 collective-permute-start.21
  69.9 0.6 collective-permute-start.20
  70.5 0.9 collective-permute-done.17.refs_19_.refs_20_
  71.4 1.3 collective-permute-done.18.refs_20_.refs_21_
  72.7 1.0 copy-done.14
  73.7 10.9 %end_block.1 = (f32[2,384,256]{2,1,0:T(8,128)}, f32[2,384,256]{2,1,0:T(8,128)}, f32[384,128]{1,0:T(8,128)}, f32[512,128]{1,0:T(8,128)}) custom-call(s32[2]{0:T(128)} %pad_add_fusion.place_ref, f32[2,384,256]{2,1,0:T(8,128)} %get-tuple-element.39.cross_in, f32[384,128]{1,0:T(8,128)} %get-tuple-element.40.norm_in, bf16[384,1792]{1,0:T(8,128)(2,1)} %refs_0_.5, ...), custom_call_target="tpu_custom_call" | custom-call | flops 1000 | bytes 1000 | tf_op jit(solution)/shard_map/end_block/pallas_call | solution.py:134
  85.2 1.3 collective-permute-done.22.refs_24_
  86.5 0.7 collective-permute-done.23.refs_25_
  87.3 0.7 copy-done.19
  88.0 9.5 %last_block.1 = (f32[384,1024]{1,0:T(8,128)}, f32[72,1024]{1,0:T(8,128)}) custom-call(s32[2]{0:T(128)} %pad_add_fusion.place_ref, f32[2,384,256]{2,1,0:T(8,128)} %get-tuple-element.47.cross_own_in, f32[2,384,256]{2,1,0:T(8,128)} %get-tuple-element.48.cross_end_in, f32[384,128]{1,0:T(8,128)} %get-tuple-element.49.row_norm_in, ...), custom_call_target="tpu_custom_call" | custom-call | flops 1000 | bytes 1000 | tf_op jit(solution)/shard_map/last_block/pallas_call | solution.py:134
  97.5 1.1 slice_select_fusion.2
  99.0 1.0 collective-permute-done.24
  100.1 1.0 select_add_fusion.2
  101.1 1.1 collective-permute-start.27
  102.2 1.2 collective-permute-start.26
  103.4 1.3 collective-permute-start.25
  104.6 4.1 %collective-permute-done.27 = f32[72,512]{1,0:T(8,128)S(1)} collective-permute-done((f32[72,512]{1,0:T(8,128)S(1)}, f32[72,512]{1,0:T(8,128)S(1)}, u32[]{:S(2)}, u32[]{:S(2)}) %collective-permute-start.27) | collective-permute-done | bytes 147488 | tf_op jit(solution)/shard_map/ppermute | solution.py:43
  108.8 2.2 %collective-permute-done.26 = f32[72,512]{1,0:T(8,128)S(1)} collective-permute-done((f32[72,512]{1,0:T(8,128)S(1)}, f32[72,512]{1,0:T(8,128)S(1)}, u32[]{:S(2)}, u32[]{:S(2)}) %collective-permute-start.26) | collective-permute-done | bytes 147488 | tf_op jit(solution)/shard_map/ppermute | solution.py:43
  111.1 1.4 collective-permute-done.28
  112.7 1.6 fusion.28
  114.5 1.2 collective-permute-done.29
  115.8 1.1 fusion.9
  117.1 1.2 collective-permute-done.30
  118.4 1.3 collective-permute-start.33
  119.6 1.4 collective-permute-start.32
  121.0 0.9 collective-permute-start.31
  121.9 4.1 %collective-permute-done.33 = f32[72,512]{1,0:T(8,128)S(1)} collective-permute-done((f32[72,512]{1,0:T(8,128)S(1)}, f32[72,512]{1,0:T(8,128)S(1)}, u32[]{:S(2)}, u32[]{:S(2)}) %collective-permute-start.33) | collective-permute-done | bytes 147488 | tf_op jit(solution)/shard_map/ppermute | solution.py:43
  126.1 2.3 %collective-permute-done.32 = f32[72,512]{1,0:T(8,128)S(1)} collective-permute-done((f32[72,512]{1,0:T(8,128)S(1)}, f32[72,512]{1,0:T(8,128)S(1)}, u32[]{:S(2)}, u32[]{:S(2)}) %collective-permute-start.32) | collective-permute-done | bytes 147488 | tf_op jit(solution)/shard_map/ppermute | solution.py:43
  128.5 1.4 collective-permute-done.34
  130.2 1.6 fusion.25
  132.1 1.2 collective-permute-done.35
  133.3 1.1 fusion.12
  134.8 1.2 collective-permute-done.36
  136.1 1.2 collective-permute-start.39
  137.3 1.4 collective-permute-start.38
  138.7 0.9 collective-permute-start.37
  139.7 4.1 %collective-permute-done.39 = f32[72,512]{1,0:T(8,128)S(1)} collective-permute-done((f32[72,512]{1,0:T(8,128)S(1)}, f32[72,512]{1,0:T(8,128)S(1)}, u32[]{:S(2)}, u32[]{:S(2)}) %collective-permute-start.39) | collective-permute-done | bytes 147488 | tf_op jit(solution)/shard_map/ppermute | solution.py:43
  143.8 2.3 %collective-permute-done.38 = f32[72,512]{1,0:T(8,128)S(1)} collective-permute-done((f32[72,512]{1,0:T(8,128)S(1)}, f32[72,512]{1,0:T(8,128)S(1)}, u32[]{:S(2)}, u32[]{:S(2)}) %collective-permute-start.38) | collective-permute-done | bytes 147488 | tf_op jit(solution)/shard_map/ppermute | solution.py:43
  146.3 1.4 collective-permute-done.40
  147.9 10.0 %collective-permute-start.41 = (f32[128,512]{1,0:T(8,128)S(1)}, f32[128,512]{1,0:T(8,128)S(1)}, u32[]{:S(2)}, u32[]{:S(2)}) collective-permute-start(f32[128,512]{1,0:T(8,128)S(1)} %pad_maximum_fusion), channel_id=1, source_target_pairs={{0,1},{1,0},{2,3},{3,2},{4,5},{5,4},{6,7},{7,6},{8,9},{9,8},{10,11... | collective-permute-start | bytes 786440 | tf_op jit(solution)/shard_map/ppermute | solution.py:34
  157.9 6.6 %collective-permute-done.41 = f32[128,512]{1,0:T(8,128)S(1)} collective-permute-done((f32[128,512]{1,0:T(8,128)S(1)}, f32[128,512]{1,0:T(8,128)S(1)}, u32[]{:S(2)}, u32[]{:S(2)}) %collective-permute-start.41) | collective-permute-done | bytes 262176 | tf_op jit(solution)/shard_map/ppermute | solution.py:34
  164.5 0.7 slice_bitcast_fusion
  (104 shorter events, 4.7 us)
Async XLA Ops:
  0.6 23.8 %collective-permute-start.2 = (bf16[512,896]{1,0:T(8,128)(2,1)}, bf16[512,896]{1,0:T(8,128)(2,1)}, u32[]{:S(2)}, u32[]{:S(2)}) collective-permute-start(bf16[512,896]{1,0:T(8,128)(2,1)} %refs_6_.1), channel_id=1, source_target_pairs={{0,1},{1,0},{2,3},{3,2},{4,5},{5,4},{6,7},{7,6},{8,9},{9,8},{10,11... | collective-permute-start | bytes 2752520 | tf_op jit(solution)/shard_map/ppermute | solution.py:34
  3.7 22.0 %collective-permute-start.1 = (bf16[512,896]{1,0:T(8,128)(2,1)}, bf16[512,896]{1,0:T(8,128)(2,1)S(1)}, u32[]{:S(2)}, u32[]{:S(2)}) collective-permute-start(bf16[512,896]{1,0:T(8,128)(2,1)} %refs_6_.1), channel_id=1, source_target_pairs={{0,16},{4,20},{8,24},{12,28},{16,0},{20,4},{24,8},{28,12},{1,17},{... | collective-permute-start | bytes 2752520 | tf_op jit(solution)/shard_map/ppermute | solution.py:43
  5.2 21.7 %collective-permute-start = (bf16[512,896]{1,0:T(8,128)(2,1)}, bf16[512,896]{1,0:T(8,128)(2,1)S(1)}, u32[]{:S(2)}, u32[]{:S(2)}) collective-permute-start(bf16[512,896]{1,0:T(8,128)(2,1)} %refs_6_.1), channel_id=1, source_target_pairs={{0,8},{4,12},{8,0},{12,4},{16,24},{20,28},{24,16},{28,20},{1,9},{5... | collective-permute-start | bytes 2752520 | tf_op jit(solution)/shard_map/ppermute | solution.py:43
  6.7 32.1 %collective-permute-start.4 = (bf16[384,1792]{1,0:T(8,128)(2,1)}, bf16[384,1792]{1,0:T(8,128)(2,1)S(1)}, u32[]{:S(2)}, u32[]{:S(2)}) collective-permute-start(bf16[384,1792]{1,0:T(8,128)(2,1)} %refs_0_.5), channel_id=1, source_target_pairs={{0,4},{1,2},{2,1},{3,7},{4,0},{5,6},{6,5},{7,3},{8,12},{9,10},{10,... | collective-permute-start | bytes 4128776 | tf_op jit(solution)/shard_map/ppermute | solution.py:39
  9.0 20.6 %copy-start.4 = (bf16[512,896]{1,0:T(8,128)(2,1)S(1)}, bf16[512,896]{1,0:T(8,128)(2,1)}, u32[]{:S(2)}) copy-start(bf16[512,896]{1,0:T(8,128)(2,1)} %refs_6_.1) | copy-start | bytes 2752516
  25.7 27.4 %copy-start.2 = (bf16[512,896]{1,0:T(8,128)(2,1)}, bf16[512,896]{1,0:T(8,128)(2,1)S(1)}, u32[]{:S(2)}) copy-start(bf16[512,896]{1,0:T(8,128)(2,1)S(1)} %collective-permute-done.1.refs_5_.refs_7_.refs_8_) | copy-start | bytes 2752516
  27.0 26.1 %copy-start.3 = (bf16[512,896]{1,0:T(8,128)(2,1)}, bf16[512,896]{1,0:T(8,128)(2,1)S(1)}, u32[]{:S(2)}) copy-start(bf16[512,896]{1,0:T(8,128)(2,1)S(1)} %collective-permute-done.refs_4_.refs_6_.refs_7_) | copy-start | bytes 2752516
  27.1 10.8 %collective-permute-start.5 = (bf16[256,896]{1,0:T(8,128)(2,1)S(1)}, bf16[256,896]{1,0:T(8,128)(2,1)S(1)}, u32[]{:S(2)}, u32[]{:S(2)}) collective-permute-start(bf16[256,896]{1,0:T(8,128)(2,1)S(1)} %slice.86), channel_id=1, source_target_pairs={{0,16},{4,20},{8,24},{12,28},{16,0},{20,4},{24,8},{28,12},{1,17},{... | collective-permute-start | bytes 1376264 | tf_op jit(solution)/shard_map/ppermute | solution.py:43
  27.6 10.7 %collective-permute-start.6 = (bf16[256,896]{1,0:T(8,128)(2,1)S(1)}, bf16[256,896]{1,0:T(8,128)(2,1)S(1)}, u32[]{:S(2)}, u32[]{:S(2)}) collective-permute-start(bf16[256,896]{1,0:T(8,128)(2,1)S(1)} %slice.87), channel_id=1, source_target_pairs={{0,8},{4,12},{8,0},{12,4},{16,24},{20,28},{24,16},{28,20},{1,9},{5... | collective-permute-start | bytes 1376264 | tf_op jit(solution)/shard_map/ppermute | solution.py:43
  29.1 15.4 %collective-permute-start.3 = (bf16[384,896]{1,0:T(8,128)(2,1)S(1)}, bf16[384,896]{1,0:T(8,128)(2,1)}, u32[]{:S(2)}, u32[]{:S(2)}) collective-permute-start(bf16[384,896]{1,0:T(8,128)(2,1)S(1)} %get-tuple-element.30), channel_id=1, source_target_pairs={{0,1},{1,0},{2,3},{3,2},{4,5},{5,4},{6,7},{7,6},{8,9},{9,8},{10,11... | collective-permute-start | bytes 2064392 | tf_op jit(solution)/shard_map/ppermute | solution.py:34
  29.6 16.9 %collective-permute-start.7 = (bf16[512,896]{1,0:T(8,128)(2,1)S(1)}, bf16[512,896]{1,0:T(8,128)(2,1)S(1)}, u32[]{:S(2)}, u32[]{:S(2)}) collective-permute-start(bf16[512,896]{1,0:T(8,128)(2,1)S(1)} %copy-done.4), channel_id=1, source_target_pairs={{0,4},{4,0},{8,12},{12,8},{16,20},{20,16},{24,28},{28,24},{1,5},{5... | collective-permute-start | bytes 2752520 | tf_op jit(solution)/shard_map/ppermute | solution.py:43
  37.9 11.8 %copy-start.8 = (bf16[256,896]{1,0:T(8,128)(2,1)}, bf16[256,896]{1,0:T(8,128)(2,1)S(1)}, u32[]{:S(2)}) copy-start(bf16[256,896]{1,0:T(8,128)(2,1)S(1)} %collective-permute-done.5.refs_6_.refs_8_.refs_9_) | copy-start | bytes 1376260
  38.3 11.4 %copy-start.10 = (bf16[256,896]{1,0:T(8,128)(2,1)}, bf16[256,896]{1,0:T(8,128)(2,1)S(1)}, u32[]{:S(2)}) copy-start(bf16[256,896]{1,0:T(8,128)(2,1)S(1)} %collective-permute-done.6.refs_7_.refs_9_.refs_10_) | copy-start | bytes 1376260
  38.3 6.2 %collective-permute-start.11 = (bf16[256,896]{1,0:T(8,128)(2,1)S(1)}, bf16[256,896]{1,0:T(8,128)(2,1)S(1)}, u32[]{:S(2)}, u32[]{:S(2)}) collective-permute-start(bf16[256,896]{1,0:T(8,128)(2,1)S(1)} %collective-permute-done.6.refs_7_.refs_9_.refs_10_), channel_id=1, source_target_pairs={{0,4},{4,0},{8,12},{12,8},{16,20},{20,16},{24,28},{28,24},{1,5},{5... | collective-permute-start | bytes 1376264 | tf_op jit(solution)/shard_map/ppermute | solution.py:43
  38.3 7.6 %collective-permute-start.10 = (bf16[256,896]{1,0:T(8,128)(2,1)S(1)}, bf16[256,896]{1,0:T(8,128)(2,1)S(1)}, u32[]{:S(2)}, u32[]{:S(2)}) collective-permute-start(bf16[256,896]{1,0:T(8,128)(2,1)S(1)} %collective-permute-done.5.refs_6_.refs_8_.refs_9_), channel_id=1, source_target_pairs={{0,4},{4,0},{8,12},{12,8},{16,20},{20,16},{24,28},{28,24},{1,5},{5... | collective-permute-start | bytes 1376264 | tf_op jit(solution)/shard_map/ppermute | solution.py:43
  38.8 14.3 %copy-start.1 = (bf16[384,1792]{1,0:T(8,128)(2,1)}, bf16[384,1792]{1,0:T(8,128)(2,1)S(1)}, u32[]{:S(2)}) copy-start(bf16[384,1792]{1,0:T(8,128)(2,1)S(1)} %collective-permute-done.4.refs_1_) | copy-start | bytes 4128772
  38.8 7.7 %collective-permute-start.9 = (bf16[512,896]{1,0:T(8,128)(2,1)S(1)}, bf16[512,896]{1,0:T(8,128)(2,1)S(1)}, u32[]{:S(2)}, u32[]{:S(2)}) collective-permute-start(bf16[512,896]{1,0:T(8,128)(2,1)S(1)} %collective-permute-done.1.refs_5_.refs_7_.refs_8_), channel_id=1, source_target_pairs={{0,4},{4,0},{8,12},{12,8},{16,20},{20,16},{24,28},{28,24},{1,5},{5... | collective-permute-start | bytes 2752520 | tf_op jit(solution)/shard_map/ppermute | solution.py:43
  44.5 5.1 %collective-permute-start.8 = (bf16[512,896]{1,0:T(8,128)(2,1)S(1)}, bf16[512,896]{1,0:T(8,128)(2,1)S(1)}, u32[]{:S(2)}, u32[]{:S(2)}) collective-permute-start(bf16[512,896]{1,0:T(8,128)(2,1)S(1)} %collective-permute-done.refs_4_.refs_6_.refs_7_), channel_id=1, source_target_pairs={{0,4},{4,0},{8,12},{12,8},{16,20},{20,16},{24,28},{28,24},{1,5},{5... | collective-permute-start | bytes 2752520 | tf_op jit(solution)/shard_map/ppermute | solution.py:43
  44.6 5.2 %copy-start.11 = (bf16[256,896]{1,0:T(8,128)(2,1)}, bf16[256,896]{1,0:T(8,128)(2,1)S(1)}, u32[]{:S(2)}) copy-start(bf16[256,896]{1,0:T(8,128)(2,1)S(1)} %collective-permute-done.11.refs_12_.refs_14_.refs_15_) | copy-start | bytes 1376260
  44.6 23.1 %collective-permute-start.14 = (bf16[512,896]{1,0:T(8,128)(2,1)}, bf16[512,896]{1,0:T(8,128)(2,1)}, u32[]{:S(2)}, u32[]{:S(2)}) collective-permute-start(bf16[512,896]{1,0:T(8,128)(2,1)} %collective-permute-done.2.refs_15_.refs_16_), channel_id=1, source_target_pairs={{0,16},{4,20},{8,24},{12,28},{16,0},{20,4},{24,8},{28,12},{1,17},{... | collective-permute-start | bytes 2752520 | tf_op jit(solution)/shard_map/ppermute | solution.py:43
  46.0 3.8 %copy-start.12 = (bf16[256,896]{1,0:T(8,128)(2,1)}, bf16[256,896]{1,0:T(8,128)(2,1)S(1)}, u32[]{:S(2)}) copy-start(bf16[256,896]{1,0:T(8,128)(2,1)S(1)} %collective-permute-done.10.refs_11_.refs_13_.refs_14_) | copy-start | bytes 1376260
  46.0 22.7 %collective-permute-start.13 = (bf16[512,896]{1,0:T(8,128)(2,1)}, bf16[512,896]{1,0:T(8,128)(2,1)}, u32[]{:S(2)}, u32[]{:S(2)}) collective-permute-start(bf16[512,896]{1,0:T(8,128)(2,1)} %collective-permute-done.2.refs_15_.refs_16_), channel_id=1, source_target_pairs={{0,8},{4,12},{8,0},{12,4},{16,24},{20,28},{24,16},{28,20},{1,9},{5... | collective-permute-start | bytes 2752520 | tf_op jit(solution)/shard_map/ppermute | solution.py:43
  46.5 3.2 %copy-start.5 = (bf16[512,896]{1,0:T(8,128)(2,1)}, bf16[512,896]{1,0:T(8,128)(2,1)S(1)}, u32[]{:S(2)}) copy-start(bf16[512,896]{1,0:T(8,128)(2,1)S(1)} %collective-permute-done.7.refs_8_.refs_10_.refs_11_) | copy-start | bytes 2752516
  46.5 22.2 %collective-permute-start.15 = (bf16[384,896]{1,0:T(8,128)(2,1)}, bf16[384,896]{1,0:T(8,128)(2,1)}, u32[]{:S(2)}, u32[]{:S(2)}) collective-permute-start(bf16[384,896]{1,0:T(8,128)(2,1)} %collective-permute-done.3.refs_2_), channel_id=1, source_target_pairs={{0,4},{1,2},{2,1},{3,7},{4,0},{5,6},{6,5},{7,3},{8,12},{9,10},{10,... | collective-permute-start | bytes 2064392 | tf_op jit(solution)/shard_map/ppermute | solution.py:39
  46.5 3.3 %copy-start.6 = (bf16[512,896]{1,0:T(8,128)(2,1)}, bf16[512,896]{1,0:T(8,128)(2,1)S(1)}, u32[]{:S(2)}) copy-start(bf16[512,896]{1,0:T(8,128)(2,1)S(1)} %collective-permute-done.9.refs_10_.refs_12_.refs_13_) | copy-start | bytes 2752516
  46.5 22.7 %collective-permute-start.12 = (bf16[384,896]{1,0:T(8,128)(2,1)}, bf16[384,896]{1,0:T(8,128)(2,1)}, u32[]{:S(2)}, u32[]{:S(2)}) collective-permute-start(bf16[384,896]{1,0:T(8,128)(2,1)} %get-tuple-element.41), channel_id=1, source_target_pairs={{0,1},{1,0},{2,3},{3,2},{4,5},{5,4},{6,7},{7,6},{8,9},{9,8},{10,11... | collective-permute-start | bytes 2064392 | tf_op jit(solution)/shard_map/ppermute | solution.py:34
  49.7 0.9 copy-start.7
  49.7 20.8 %collective-permute-start.16 = (bf16[512,896]{1,0:T(8,128)(2,1)}, bf16[512,896]{1,0:T(8,128)(2,1)}, u32[]{:S(2)}, u32[]{:S(2)}) collective-permute-start(bf16[512,896]{1,0:T(8,128)(2,1)} %collective-permute-done.2.refs_15_.refs_16_), channel_id=1, source_target_pairs={{0,4},{4,0},{8,12},{12,8},{16,20},{20,16},{24,28},{28,24},{1,5},{5... | collective-permute-start | bytes 2752520 | tf_op jit(solution)/shard_map/ppermute | solution.py:43
  53.1 16.8 %copy-start.9 = (bf16[256,896]{1,0:T(8,128)(2,1)S(1)}, bf16[256,896]{1,0:T(8,128)(2,1)}, u32[]{:S(2)}) copy-start(bf16[256,896]{1,0:T(8,128)(2,1)} %copy-done.8) | copy-start | bytes 1376260
  68.7 2.7 %collective-permute-start.17 = (bf16[512,896]{1,0:T(8,128)(2,1)}, bf16[512,896]{1,0:T(8,128)(2,1)S(1)}, u32[]{:S(2)}, u32[]{:S(2)}) collective-permute-start(bf16[512,896]{1,0:T(8,128)(2,1)} %collective-permute-done.13.refs_16_.refs_17_), channel_id=1, source_target_pairs={{0,4},{4,0},{8,12},{12,8},{16,20},{20,16},{24,28},{28,24},{1,5},{5... | collective-permute-start | bytes 2752520 | tf_op jit(solution)/shard_map/ppermute | solution.py:43
  68.7 4.0 %collective-permute-start.18 = (bf16[512,896]{1,0:T(8,128)(2,1)}, bf16[512,896]{1,0:T(8,128)(2,1)S(1)}, u32[]{:S(2)}, u32[]{:S(2)}) collective-permute-start(bf16[512,896]{1,0:T(8,128)(2,1)} %collective-permute-done.14.refs_17_.refs_18_), channel_id=1, source_target_pairs={{0,4},{4,0},{8,12},{12,8},{16,20},{20,16},{24,28},{28,24},{1,5},{5... | collective-permute-start | bytes 2752520 | tf_op jit(solution)/shard_map/ppermute | solution.py:43
  69.2 15.4 %collective-permute-start.21 = (bf16[256,896]{1,0:T(8,128)(2,1)}, bf16[256,896]{1,0:T(8,128)(2,1)S(1)}, u32[]{:S(2)}, u32[]{:S(2)}) collective-permute-start(bf16[256,896]{1,0:T(8,128)(2,1)} %slice.88), channel_id=1, source_target_pairs={{0,24},{4,28},{8,16},{12,20},{16,8},{20,12},{24,0},{28,4},{1,25},{... | collective-permute-start | bytes 1376264 | tf_op jit(solution)/shard_map/ppermute | solution.py:43
  69.9 14.8 %collective-permute-start.20 = (bf16[256,896]{1,0:T(8,128)(2,1)S(1)}, bf16[256,896]{1,0:T(8,128)(2,1)S(1)}, u32[]{:S(2)}, u32[]{:S(2)}) collective-permute-start(bf16[256,896]{1,0:T(8,128)(2,1)S(1)} %copy-done.9), channel_id=1, source_target_pairs={{0,1},{1,0},{2,3},{3,2},{4,5},{5,4},{6,7},{7,6},{8,9},{9,8},{10,11... | collective-permute-start | bytes 1376264 | tf_op jit(solution)/shard_map/ppermute | solution.py:34
  70.5 14.7 %collective-permute-start.19 = (bf16[384,896]{1,0:T(8,128)(2,1)}, bf16[384,896]{1,0:T(8,128)(2,1)S(1)}, u32[]{:S(2)}, u32[]{:S(2)}) collective-permute-start(bf16[384,896]{1,0:T(8,128)(2,1)} %collective-permute-done.12.refs_3_), channel_id=1, source_target_pairs={{0,4},{1,2},{2,1},{3,7},{4,0},{5,6},{6,5},{7,3},{8,12},{9,10},{10,... | collective-permute-start | bytes 2064392 | tf_op jit(solution)/shard_map/ppermute | solution.py:39
  71.4 1.3 copy-start.13
  72.7 1.0 copy-start.14
  84.6 2.6 %copy-start.16 = (bf16[256,896]{1,0:T(8,128)(2,1)}, bf16[256,896]{1,0:T(8,128)(2,1)S(1)}, u32[]{:S(2)}) copy-start(bf16[256,896]{1,0:T(8,128)(2,1)S(1)} %collective-permute-done.21.refs_23_) | copy-start | bytes 1376260
  84.6 2.6 %copy-start.17 = (bf16[256,896]{1,0:T(8,128)(2,1)}, bf16[256,896]{1,0:T(8,128)(2,1)S(1)}, u32[]{:S(2)}) copy-start(bf16[256,896]{1,0:T(8,128)(2,1)S(1)} %collective-permute-done.20.refs_22_) | copy-start | bytes 1376260
  84.7 1.9 %collective-permute-start.22 = (bf16[256,896]{1,0:T(8,128)(2,1)S(1)}, bf16[256,896]{1,0:T(8,128)(2,1)S(1)}, u32[]{:S(2)}, u32[]{:S(2)}) collective-permute-start(bf16[256,896]{1,0:T(8,128)(2,1)S(1)} %collective-permute-done.20.refs_22_), channel_id=1, source_target_pairs={{0,4},{4,0},{8,12},{12,8},{16,20},{20,16},{24,28},{28,24},{1,5},{5... | collective-permute-start | bytes 1376264 | tf_op jit(solution)/shard_map/ppermute | solution.py:43
  85.0 2.1 %collective-permute-start.23 = (bf16[256,896]{1,0:T(8,128)(2,1)S(1)}, bf16[256,896]{1,0:T(8,128)(2,1)S(1)}, u32[]{:S(2)}, u32[]{:S(2)}) collective-permute-start(bf16[256,896]{1,0:T(8,128)(2,1)S(1)} %collective-permute-done.21.refs_23_), channel_id=1, source_target_pairs={{0,4},{4,0},{8,12},{12,8},{16,20},{20,16},{24,28},{28,24},{1,5},{5... | collective-permute-start | bytes 1376264 | tf_op jit(solution)/shard_map/ppermute | solution.py:43
  85.2 2.0 %copy-start.15 = (bf16[384,896]{1,0:T(8,128)(2,1)}, bf16[384,896]{1,0:T(8,128)(2,1)S(1)}, u32[]{:S(2)}) copy-start(bf16[384,896]{1,0:T(8,128)(2,1)S(1)} %collective-permute-done.19.refs_5_) | copy-start | bytes 2064388
  86.5 0.8 copy-start.18
  87.2 0.8 copy-start.19
  97.5 15.2 %copy-start = (f32[384,1024]{1,0:T(8,128)S(1)}, f32[384,1024]{1,0:T(8,128)}, u32[]{:S(2)}) copy-start(f32[384,1024]{1,0:T(8,128)} %get-tuple-element.57) | copy-start | bytes 4718596
  98.6 1.4 collective-permute-start.24
  101.1 7.7 %collective-permute-start.27 = (f32[72,512]{1,0:T(8,128)S(1)}, f32[72,512]{1,0:T(8,128)S(1)}, u32[]{:S(2)}, u32[]{:S(2)}) collective-permute-start(f32[72,512]{1,0:T(8,128)S(1)} %select_add_fusion.2), channel_id=1, source_target_pairs={{0,24},{4,28},{8,16},{12,20},{16,8},{20,12},{24,0},{28,4},{1,25},{... | collective-permute-start | bytes 442376 | tf_op jit(solution)/shard_map/ppermute | solution.py:43
  102.2 8.8 %collective-permute-start.26 = (f32[72,512]{1,0:T(8,128)S(1)}, f32[72,512]{1,0:T(8,128)S(1)}, u32[]{:S(2)}, u32[]{:S(2)}) collective-permute-start(f32[72,512]{1,0:T(8,128)S(1)} %select_add_fusion.2), channel_id=1, source_target_pairs={{0,16},{4,20},{8,24},{12,28},{16,0},{20,4},{24,8},{28,12},{1,17},{... | collective-permute-start | bytes 442376 | tf_op jit(solution)/shard_map/ppermute | solution.py:43
  103.4 7.6 %collective-permute-start.25 = (f32[72,512]{1,0:T(8,128)S(1)}, f32[72,512]{1,0:T(8,128)S(1)}, u32[]{:S(2)}, u32[]{:S(2)}) collective-permute-start(f32[72,512]{1,0:T(8,128)S(1)} %select_add_fusion.2), channel_id=1, source_target_pairs={{0,8},{4,12},{8,0},{12,4},{16,24},{20,28},{24,16},{28,20},{1,9},{5... | collective-permute-start | bytes 442376 | tf_op jit(solution)/shard_map/ppermute | solution.py:43
  111.0 1.4 collective-permute-start.28
  114.3 1.4 collective-permute-start.29
  116.9 1.4 collective-permute-start.30
  118.4 7.7 %collective-permute-start.33 = (f32[72,512]{1,0:T(8,128)S(1)}, f32[72,512]{1,0:T(8,128)S(1)}, u32[]{:S(2)}, u32[]{:S(2)}) collective-permute-start(f32[72,512]{1,0:T(8,128)S(1)} %select_add_fusion.1), channel_id=1, source_target_pairs={{0,24},{4,28},{8,16},{12,20},{16,8},{20,12},{24,0},{28,4},{1,25},{... | collective-permute-start | bytes 442376 | tf_op jit(solution)/shard_map/ppermute | solution.py:43
  119.6 8.8 %collective-permute-start.32 = (f32[72,512]{1,0:T(8,128)S(1)}, f32[72,512]{1,0:T(8,128)S(1)}, u32[]{:S(2)}, u32[]{:S(2)}) collective-permute-start(f32[72,512]{1,0:T(8,128)S(1)} %select_add_fusion.1), channel_id=1, source_target_pairs={{0,16},{4,20},{8,24},{12,28},{16,0},{20,4},{24,8},{28,12},{1,17},{... | collective-permute-start | bytes 442376 | tf_op jit(solution)/shard_map/ppermute | solution.py:43
  121.0 7.4 %collective-permute-start.31 = (f32[72,512]{1,0:T(8,128)S(1)}, f32[72,512]{1,0:T(8,128)S(1)}, u32[]{:S(2)}, u32[]{:S(2)}) collective-permute-start(f32[72,512]{1,0:T(8,128)S(1)} %select_add_fusion.1), channel_id=1, source_target_pairs={{0,8},{4,12},{8,0},{12,4},{16,24},{20,28},{24,16},{28,20},{1,9},{5... | collective-permute-start | bytes 442376 | tf_op jit(solution)/shard_map/ppermute | solution.py:43
  128.5 1.4 collective-permute-start.34
  131.9 1.4 collective-permute-start.35
  134.6 1.4 collective-permute-start.36
  136.1 7.7 %collective-permute-start.39 = (f32[72,512]{1,0:T(8,128)S(1)}, f32[72,512]{1,0:T(8,128)S(1)}, u32[]{:S(2)}, u32[]{:S(2)}) collective-permute-start(f32[72,512]{1,0:T(8,128)S(1)} %select_add_fusion), channel_id=1, source_target_pairs={{0,24},{4,28},{8,16},{12,20},{16,8},{20,12},{24,0},{28,4},{1,25},{... | collective-permute-start | bytes 442376 | tf_op jit(solution)/shard_map/ppermute | solution.py:43
  137.3 8.8 %collective-permute-start.38 = (f32[72,512]{1,0:T(8,128)S(1)}, f32[72,512]{1,0:T(8,128)S(1)}, u32[]{:S(2)}, u32[]{:S(2)}) collective-permute-start(f32[72,512]{1,0:T(8,128)S(1)} %select_add_fusion), channel_id=1, source_target_pairs={{0,16},{4,20},{8,24},{12,28},{16,0},{20,4},{24,8},{28,12},{1,17},{... | collective-permute-start | bytes 442376 | tf_op jit(solution)/shard_map/ppermute | solution.py:43
  138.7 7.4 %collective-permute-start.37 = (f32[72,512]{1,0:T(8,128)S(1)}, f32[72,512]{1,0:T(8,128)S(1)}, u32[]{:S(2)}, u32[]{:S(2)}) collective-permute-start(f32[72,512]{1,0:T(8,128)S(1)} %select_add_fusion), channel_id=1, source_target_pairs={{0,8},{4,12},{8,0},{12,4},{16,24},{20,28},{24,16},{28,20},{1,9},{5... | collective-permute-start | bytes 442376 | tf_op jit(solution)/shard_map/ppermute | solution.py:43
  146.2 1.4 collective-permute-start.40
  147.9 16.6 %collective-permute-start.41 = (f32[128,512]{1,0:T(8,128)S(1)}, f32[128,512]{1,0:T(8,128)S(1)}, u32[]{:S(2)}, u32[]{:S(2)}) collective-permute-start(f32[128,512]{1,0:T(8,128)S(1)} %pad_maximum_fusion), channel_id=1, source_target_pairs={{0,1},{1,0},{2,3},{3,2},{4,5},{5,4},{6,7},{7,6},{8,9},{9,8},{10,11... | collective-permute-start | bytes 786440 | tf_op jit(solution)/shard_map/ppermute | solution.py:34

commit v5 on v4

--- a/solution.py
+++ b/solution.py
@@ -47,7 +47,11 @@
     odd = lax.axis_index("proof") % 2
     half = block.shape[1] // 2
     low, high = block[:, :half], block[:, half:]
-    mine, other = jnp.where(odd == 0, low, high), jnp.where(odd == 0, high, low)
+    return sum_halves(jnp.where(odd == 0, low, high), jnp.where(odd == 0, high, low))
+
+
+def sum_halves(mine, other):
+    odd = lax.axis_index("proof") % 2
     mine = mine + flipped(other, 1)
     mine = mine + flipped(mine, 2) + flipped(mine, 4) + flipped(mine, 6)
     other = flipped(mine, 1)
@@ -69,7 +73,7 @@
     return lax.optimization_barrier((block, *earlier))[0]
 
 
-ANY = pl.BlockSpec(memory_space=pl.ANY)
+ANY = pl.BlockSpec(memory_space=pltpu.HBM)
 VMEM = pl.BlockSpec(memory_space=pltpu.VMEM)
 SMEM = pl.BlockSpec(memory_space=pltpu.SMEM)
 
@@ -78,12 +82,19 @@
     return jnp.stack([lax.axis_index("proof"), lax.axis_index("landmark")]).astype(jnp.int32)
 
 
-def lane_squares(block):
-    total = None
-    for j in range(block.shape[1] // 128):
-        x = block[:, j * 128 : (j + 1) * 128].astype(jnp.float32)
-        total = x * x if total is None else total + x * x
-    return total
+def add_squares(total_ref, block_ref, first=False):
+    for r in range(0, block_ref.shape[0], 32):
+        rows = slice(r, r + 32)
+        total = None if first else total_ref[rows]
+        for j in range(block_ref.shape[1] // 128):
+            x = block_ref[rows, j * 128 : (j + 1) * 128].astype(jnp.float32)
+            total = x * x if total is None else total + x * x
+        total_ref[rows] = total
+
+
+def across_lanes(norm_ref, inside):
+    ones = jnp.ones((8, 128), jnp.float32)
+    return lax.dot_general(ones, norm_ref[inside], (((1,), (1,)), ((), ())), precision=lax.Precision.HIGHEST)
 
 
 def product(left, right):
@@ -150,7 +161,7 @@
     def body(place_ref, *refs):
         row_refs, refs = refs[: len(rows.keys)], refs[len(rows.keys) :]
         landmark_refs, refs = refs[: len(landmarks.keys)], refs[len(landmarks.keys) :]
-        cross_ref, row_norm_ref, norm_ref, rows_s, land_s, row_sem, land_sem = refs
+        cross_ref, row_norm_ref, norm_ref, rows_s, land_s, norm_s, row_sem, land_sem = refs
         p, z = place_ref[0], place_ref[1]
         wanted = [feature_block(z, zbits, side) ^ p for zbits, side in sources]
         for i, (zbits, side) in enumerate(sources):
@@ -160,22 +171,24 @@
         cross_ref[...] = jnp.zeros_like(cross_ref)
         for bits in range(8):
             wait(land_s.at[bits], land_sem.at[bits])
-            squares_here = lane_squares(land_s[bits])
-            norm_ref[...] = squares_here if bits == 0 else norm_ref[...] + squares_here
         for i in range(len(sources)):
             wait(rows_s.at[i], row_sem.at[i])
             tiled_product(cross_ref, rows_s.at[i], land_s.at[wanted[i]])
-            squares_here = lane_squares(rows_s[i])
-            row_norm_ref[...] = squares_here if i == 0 else row_norm_ref[...] + squares_here
+            add_squares(row_norm_ref, rows_s.at[i], first=i == 0)
+            for bits in (2 * i, 2 * i + 1):
+                if bits < 8:
+                    add_squares(norm_s, land_s.at[bits], first=bits == 0)
+        norm_ref[...] = across_lanes(norm_s, slice(None))
 
     return call(
         body,
         [place()] + rows.blocks + landmarks.blocks,
         [SMEM] + [ANY] * (len(rows.keys) + len(landmarks.keys)),
-        [(m // 256, n, 256), (n, 128), (m, 128)],
+        [(m // 256, n, 256), (n, 128), (8, m)],
         [
             pltpu.VMEM((len(sources), n, width), jnp.bfloat16),
             pltpu.VMEM((8, m, width), jnp.bfloat16),
+            pltpu.VMEM((m, 128), jnp.float32),
             pltpu.SemaphoreType.DMA((len(sources),)),
             pltpu.SemaphoreType.DMA((8,)),
         ],
@@ -191,9 +204,11 @@
         row_refs, refs = refs[: len(rows.keys)], refs[len(rows.keys) :]
         own_refs, refs = refs[: len(own.keys)], refs[len(own.keys) :]
         end_refs, refs = refs[: len(end.keys)], refs[len(end.keys) :]
-        cross_own_ref, cross_ref, row_norm_ref, norm_ref, rows_s, own_s, end_s, row_sem, own_sem, end_sem = refs
+        cross_own_ref, cross_ref, row_norm_ref, norm_ref, rows_s, own_s, end_s, norm_s, row_sem, own_sem, end_sem, in_sem = refs
         p, z = place_ref[0], place_ref[1]
         more = [(1, 1), (2, 0)]
+        carry = pltpu.make_async_copy(cross_in, cross_own_ref, in_sem)
+        carry.start()
         for zbits, side in more:
             slot = 2 * zbits + side
             pltpu.make_async_copy(rows.source(row_refs, zbits, side, width), rows_s.at[slot], row_sem.at[slot]).start()
@@ -205,16 +220,16 @@
                 pltpu.make_async_copy(source, rows_s.at[slot], row_sem.at[slot]).start()
         for bits in range(6):
             end.start(end_refs, bits, end_s.at[bits], end_sem.at[bits])
-        cross_own_ref[...] = cross_in[...]
         cross_ref[...] = jnp.zeros_like(cross_ref)
-        row_total = norm_in[...]
+        rows_s[late] = jnp.zeros(rows_s.shape[1:], rows_s.dtype)
+        row_norm_ref[...] = norm_in[...]
+        carry.wait()
         for i, (zbits, side) in enumerate(more):
             slot = 2 * zbits + side
             wait(rows_s.at[slot], row_sem.at[slot])
             wait(own_s.at[i], own_sem.at[i])
             tiled_product(cross_own_ref, rows_s.at[slot], own_s.at[i])
-            row_total = row_total + lane_squares(rows_s[slot])
-        row_norm_ref[...] = row_total
+            add_squares(row_norm_ref, rows_s.at[slot])
         for slot in range(8):
             if slot != late and (slot // 2, slot % 2) not in more:
                 wait(rows_s.at[slot], row_sem.at[slot])
@@ -222,26 +237,24 @@
             wait(end_s.at[bits], end_sem.at[bits])
             f = p ^ bits
             slot = 2 * (z ^ (f // 2)) + f % 2
-
-            @pl.when(slot != late)
-            def _():
-                tiled_product(cross_ref, rows_s.at[slot], end_s.at[bits])
-
-            squares_here = lane_squares(end_s[bits])
-            norm_ref[...] = squares_here if bits == 0 else norm_ref[...] + squares_here
+            tiled_product(cross_ref, rows_s.at[slot], end_s.at[bits])
+            add_squares(norm_s, end_s.at[bits], first=bits == 0)
+        norm_ref[...] = across_lanes(norm_s, slice(None))
 
     return call(
         body,
         [place(), cross_own, row_norm] + rows.blocks + own.blocks + end.blocks,
-        [SMEM, VMEM, VMEM] + [ANY] * (len(rows.keys) + len(own.keys) + len(end.keys)),
-        [(m // 256, n, 256), (m // 256, n, 256), (n, 128), (m, 128)],
+        [SMEM, ANY, VMEM] + [ANY] * (len(rows.keys) + len(own.keys) + len(end.keys)),
+        [(m // 256, n, 256), (m // 256, n, 256), (n, 128), (8, m)],
         [
             pltpu.VMEM((8, n, width), jnp.bfloat16),
             pltpu.VMEM((2, m, width), jnp.bfloat16),
             pltpu.VMEM((6, m, width), jnp.bfloat16),
+            pltpu.VMEM((m, 128), jnp.float32),
             pltpu.SemaphoreType.DMA((8,)),
             pltpu.SemaphoreType.DMA((2,)),
             pltpu.SemaphoreType.DMA((6,)),
+            pltpu.SemaphoreType.DMA,
         ],
         "end_block",
     )
@@ -249,14 +262,20 @@
 
 def last_block(rows, own, end, cross_own, cross_end, row_norm, norm_own, norm_end, columns, width):
     rows, own, end = Rows(rows), Landmarks(own), Landmarks(end)
-    n, m, count = columns.shape[1], norm_own.shape[0], columns.shape[0]
+    n, m, count = columns.shape[1], norm_own.shape[1], columns.shape[0]
 
     def body(place_ref, cross_own_in, cross_end_in, row_norm_in, norm_own_in, norm_end_in, columns_ref, *refs):
         row_refs, refs = refs[: len(rows.keys)], refs[len(rows.keys) :]
         own_refs, refs = refs[: len(own.keys)], refs[len(own.keys) :]
         end_refs, refs = refs[: len(end.keys)], refs[len(end.keys) :]
-        kernel_ref, sums_ref, cross_s, rows_s, own_s, end_s, row_sem, own_sem, end_sem = refs
+        kernel_ref, mine_ref, other_ref, *refs = refs
+        cross_s, rows_s, own_s, end_s, row_norm_s, norm_s, sums_s, row_sem, own_sem, end_sem, in_sem = refs
         p, z = place_ref[0], place_ref[1]
+        half = m // 256
+        carry_own = pltpu.make_async_copy(cross_own_in, cross_s.at[:half], in_sem.at[0])
+        carry_end = pltpu.make_async_copy(cross_end_in, cross_s.at[half:], in_sem.at[1])
+        carry_own.start()
+        carry_end.start()
         far = feature_block(z, 2, 1) ^ p
         pltpu.make_async_copy(rows.source(row_refs, 2, 1, width), rows_s.at[2], row_sem.at[2]).start()
         own.start_any(own_refs, far, own_s, own_sem)
@@ -274,49 +293,58 @@
         def _():
             end.start_any(end_refs, far, end_s.at[2], end_sem.at[2])
 
-        half = m // 256
-        cross_s[:half] = cross_own_in[...]
-        cross_s[half:] = cross_end_in[...]
+        carry_own.wait()
         wait(rows_s.at[2], row_sem.at[2])
         wait(own_s, own_sem)
         tiled_product(cross_s.at[:half], rows_s.at[2], own_s)
-        row_norm = jnp.sum(row_norm_in[...] + lane_squares(rows_s[2]), axis=1, keepdims=True)
-        norm_end = norm_end_in[...]
+        row_norm_s[...] = row_norm_in[...]
+        add_squares(row_norm_s, rows_s.at[2])
+        carry_end.wait()
         for i in range(2):
             wait(rows_s.at[i], row_sem.at[i])
             wait(end_s.at[i], end_sem.at[i])
             tiled_product(cross_s.at[half:], rows_s.at[i], end_s.at[i])
-            norm_end = norm_end + lane_squares(end_s[i])
+            add_squares(norm_s, end_s.at[i], first=i == 0)
 
         @pl.when(far < 6)
         def _():
             wait(end_s.at[2], end_sem.at[2])
             tiled_product(cross_s.at[half:], rows_s.at[2], end_s.at[2])
 
-        ones = jnp.ones((8, 128), jnp.float32)
+        row_norm = jnp.sum(row_norm_s[...], axis=1, keepdims=True)
         for t in range(2 * half):
             inside = slice(t * 256, (t + 1) * 256)
-            lanes = norm_own_in[inside] if t < half else norm_end[(t - half) * 256 : (t - half + 1) * 256]
-            norm = lax.dot_general(ones, lanes, (((1,), (1,)), ((), ())), precision=lax.Precision.HIGHEST)[:1]
+            if t < half:
+                norm = norm_own_in[:1, inside]
+            else:
+                here = slice((t - half) * 256, (t - half + 1) * 256)
+                norm = norm_end_in[:1, here] + across_lanes(norm_s, here)[:1]
             k = jnp.exp(-(row_norm + norm - 2.0 * cross_s[t]) / SPREAD)
             kernel_ref[:, inside] = k
-            sums_ref[:count, inside] = jnp.dot(columns_ref[...], k, precision=lax.Precision.HIGHEST)
-            sums_ref[count:, inside] = jnp.broadcast_to(jnp.sum(k * k, axis=0, keepdims=True), (8, 256))
+            sums_s[:count, inside] = jnp.dot(columns_ref[...], k, precision=lax.Precision.HIGHEST)
+            sums_s[count:, inside] = jnp.broadcast_to(jnp.sum(k * k, axis=0, keepdims=True), (8, 256))
+        odd = p % 2 == 1
+        mine_ref[...] = jnp.where(odd, sums_s[:, m:], sums_s[:, :m])
+        other_ref[...] = jnp.where(odd, sums_s[:, :m], sums_s[:, m:])
 
     return call(
         body,
         [place(), cross_own, cross_end, row_norm, norm_own, norm_end, columns]
         + rows.blocks + own.blocks + end.blocks,
-        [SMEM] + [VMEM] * 6 + [ANY] * (len(rows.keys) + len(own.keys) + len(end.keys)),
-        [(n, 2 * m), (count + 8, 2 * m)],
+        [SMEM] + [ANY] * 2 + [VMEM] * 4 + [ANY] * (len(rows.keys) + len(own.keys) + len(end.keys)),
+        [(n, 2 * m), (count + 8, m), (count + 8, m)],
         [
             pltpu.VMEM((2 * m // 256, n, 256), jnp.float32),
             pltpu.VMEM((3, n, width), jnp.bfloat16),
             pltpu.VMEM((m, width), jnp.bfloat16),
             pltpu.VMEM((3, m, width), jnp.bfloat16),
+            pltpu.VMEM((n, 128), jnp.float32),
+            pltpu.VMEM((m, 128), jnp.float32),
+            pltpu.VMEM((count + 8, 2 * m), jnp.float32),
             pltpu.SemaphoreType.DMA((3,)),
             pltpu.SemaphoreType.DMA,
             pltpu.SemaphoreType.DMA((3,)),
+            pltpu.SemaphoreType.DMA((2,)),
         ],
         "last_block",
     )
@@ -358,7 +386,7 @@
     cross_own, cross_end, row_norm, norm_end = end_block(
         rows, own_parts, end_parts, cross_own, row_norm, n, m, half
     )
-    corner = [(6, 0, after(end_low, cross_end)), (6, middle, after(end_high, cross_end))]
+    corner = [(6, 0, after(end_low, cross_end)), (6, middle, after(end_high, cross_end, far_right))]
     end_parts += corner + [(bits + 1, row, flipped(block, 1)) for bits, row, block in corner]
     rows |= {(2, 1): far_right}
     return last_block(
@@ -398,8 +426,8 @@
 def folded(row_features, landmark_features, targets):
     lam = ridge_scale * row_features.shape[0] * lax.axis_size("proof")
     columns = targets.T
-    kernel, sums = middle_kernel(row_features, landmark_features, columns)
-    sums = sum_rows_axis(sums)
+    kernel, mine, other = middle_kernel(row_features, landmark_features, columns)
+    sums = sum_halves(mine, other)
     coefficient, residual = conjugate_gradients(kernel, sums, columns, lam, sum_rows_axis, sum_middle)
     both = jnp.concatenate([coefficient, residual], axis=0)
     half = both.shape[1] // 2

time: 166 us -> 163 us (0.982)
  waiting for transfers between devices: 78.6 us -> 74.5 us
  starting transfers between devices: 38.8 us -> 42.3 us
    ppermute x5, waiting for transfers between devices: 27.7 us -> 25.5 us  [handed(): return lax.ppermute(block, 'landmark', NEIGHBOURS)]
    ppermute x32, waiting for transfers between devices: 48.6 us -> 46.7 us  [flipped(): return lax.ppermute(block, 'proof', [(i, i ^ bits) for i in range(8)])]
    ppermute x32, starting transfers between devices: 21.1 us -> 22.8 us  [flipped(): return lax.ppermute(block, 'proof', [(i, i ^ bits) for i in range(8)])]
    ppermute x5, starting transfers between devices: 17.3 us -> 19 us  [handed(): return lax.ppermute(block, 'landmark', NEIGHBOURS)]
  transfers between devices with their start and end apart: 42 -> 42, of which waited for: 27 -> 25; matrix products, arithmetic and copies ran while one was open for 3% -> 3% of each run, Pallas kernels for 12% -> 12%
where the time goes in v5:
time: 163 us
  waiting for transfers between devices  74.5 us (46%)
  starting transfers between devices  42.3 us (26%)
  Pallas kernels  29.1 us (18%)
  local copies, waits for them, and re-layouts  7.83 us (5%)
  matrix products  5.36 us (3%)
  other arithmetic  2.98 us (2%)
    ppermute x32, waiting for transfers between devices, flipped(): return lax.ppermute(block, 'proof', [(i, i ^ bits) for i in range(8)])  46.7 us
    pallas_call x3, Pallas kernels, call(): pl.pallas_call(body, out_shape=tuple((jax.ShapeDtypeStruct(shape, jnp.flo...  29.1 us
    ppermute x5, waiting for transfers between devices, handed(): return lax.ppermute(block, 'landmark', NEIGHBOURS)  25.5 us
    ppermute x32, starting transfers between devices, flipped(): return lax.ppermute(block, 'proof', [(i, i ^ bits) for i in range(8)])  22.8 us
    ppermute x5, starting transfers between devices, handed(): return lax.ppermute(block, 'landmark', NEIGHBOURS)  19 us
    dot_general x4, matrix products, times(): lax.dot_general(left, right, ((contract[:1], contract[1:]), ((), ())), pr...  5.36 us
  transfers between devices with their start and end apart: 42, of which 25 were waited for; matrix products, arithmetic and copies ran while one was open for 3% of the time, Pallas kernels for 12%

profile of v5, /device:TPU:0, one launch (start us, length us, event | category | flops | bytes accessed | tf_op | source)
XLA Modules:
  0.0 163.1 jit_solution(8149741899998878180)
XLA Ops:
  0.6 3.1 %collective-permute-start.2 = (bf16[512,896]{1,0:T(8,128)(2,1)}, bf16[512,896]{1,0:T(8,128)(2,1)}, u32[]{:S(2)}, u32[]{:S(2)}) collective-permute-start(bf16[512,896]{1,0:T(8,128)(2,1)} %refs_6_.1), channel_id=1, source_target_pairs={{0,1},{1,0},{2,3},{3,2},{4,5},{5,4},{6,7},{7,6},{8,9},{9,8},{10,11... | collective-permute-start | bytes 2752520 | tf_op jit(solution)/shard_map/ppermute | solution.py:34
  3.7 1.5 collective-permute-start.1
  5.2 1.5 collective-permute-start
  6.7 2.3 %fusion.27 = (bf16[384,896]{1,0:T(8,128)(2,1)}, bf16[384,896]{1,0:T(8,128)(2,1)S(1)}) fusion(bf16[384,1792]{1,0:T(8,128)(2,1)} %refs_0_.5), kind=kLoop, calls=%fused_computation.80 | loop fusion | bytes 2752512 | tf_op jit(solution)/shard_map/slice | solution.py:357
  9.0 15.4 %collective-permute-done.2.refs_15_.refs_16_ = bf16[512,896]{1,0:T(8,128)(2,1)} collective-permute-done((bf16[512,896]{1,0:T(8,128)(2,1)}, bf16[512,896]{1,0:T(8,128)(2,1)}, u32[]{:S(2)}, u32[]{:S(2)}) %collective-permute-start.2) | collective-permute-done | bytes 917536 | tf_op jit(solution)/shard_map/ppermute | solution.py:34
  24.4 1.4 collective-permute-done.1.refs_5_.refs_7_.refs_8_
  25.7 1.2 collective-permute-done.refs_4_.refs_6_.refs_7_
  27.0 0.4 collective-permute-start.3
  27.5 0.5 collective-permute-start.5
  28.0 1.6 collective-permute-start.6
  29.6 8.6 %collective-permute-done.5.refs_6_.refs_8_.refs_9_ = bf16[256,896]{1,0:T(8,128)(2,1)S(1)} collective-permute-done((bf16[256,896]{1,0:T(8,128)(2,1)S(1)}, bf16[256,896]{1,0:T(8,128)(2,1)S(1)}, u32[]{:S(2)}, u32[]{:S(2)}) %collective-permute-start.5) | collective-permute-done | bytes 458784 | tf_op jit(solution)/shard_map/ppermute | solution.py:43
  38.2 0.5 collective-permute-done.6.refs_7_.refs_9_.refs_10_
  38.7 0.5 collective-permute-start.10
  39.3 3.5 %collective-permute-done.3.refs_2_ = bf16[384,896]{1,0:T(8,128)(2,1)} collective-permute-done((bf16[384,896]{1,0:T(8,128)(2,1)S(1)}, bf16[384,896]{1,0:T(8,128)(2,1)}, u32[]{:S(2)}, u32[]{:S(2)}) %collective-permute-start.3) | collective-permute-done | bytes 688160 | tf_op jit(solution)/shard_map/ppermute | solution.py:34
  42.8 0.8 collective-permute-start.14
  43.6 1.5 collective-permute-start.13
  45.1 3.1 %collective-permute-start.12 = (bf16[384,896]{1,0:T(8,128)(2,1)}, bf16[384,896]{1,0:T(8,128)(2,1)}, u32[]{:S(2)}, u32[]{:S(2)}) collective-permute-start(bf16[384,896]{1,0:T(8,128)(2,1)} %get-tuple-element.42), channel_id=1, source_target_pairs={{0,1},{1,0},{2,3},{3,2},{4,5},{5,4},{6,7},{7,6},{8,9},{9,8},{10,11... | collective-permute-start | bytes 2064392 | tf_op jit(solution)/shard_map/ppermute | solution.py:34
  48.4 0.8 copy-done.7
  49.2 0.7 pad_add_fusion.place_ref
  49.9 1.8 %slice.82 = bf16[256,896]{1,0:T(8,128)(2,1)} slice(bf16[512,896]{1,0:T(8,128)(2,1)} %collective-permute-done.2.refs_15_.refs_16_), slice={[256:512], [0:896]} | slice | bytes 917504 | tf_op jit(solution)/shard_map/slice | solution.py:368
  51.7 8.7 %own_block.1 = (f32[2,384,256]{2,1,0:T(8,128)}, f32[384,128]{1,0:T(8,128)}, f32[8,512]{1,0:T(8,128)}) custom-call(s32[2]{0:T(128)} %pad_add_fusion.place_ref, bf16[384,1792]{1,0:T(8,128)(2,1)} %refs_0_.5, bf16[384,1792]{1,0:T(8,128)(2,1)} %copy-done.1, bf16[384,896]{1,0:T(8,128)(2,1)} %collective-permute-done.3.refs_2_, bf16[512,896]{1,0:T(8,128)(2,1)} %refs_6_.1, ...), custom_call_target="tpu_custom_call" | custom-call | flops 1000 | bytes 1000 | tf_op jit(solution)/shard_map/own_block/pallas_call | solution.py:145
  60.5 5.4 %collective-permute-done.14.refs_17_.refs_18_ = bf16[512,896]{1,0:T(8,128)(2,1)} collective-permute-done((bf16[512,896]{1,0:T(8,128)(2,1)}, bf16[512,896]{1,0:T(8,128)(2,1)}, u32[]{:S(2)}, u32[]{:S(2)}) %collective-permute-start.14) | collective-permute-done | bytes 917536 | tf_op jit(solution)/shard_map/ppermute | solution.py:43
  65.9 0.5 collective-permute-done.13.refs_16_.refs_17_
  66.3 0.5 collective-permute-start.18
  66.9 2.2 %collective-permute-start.21 = (bf16[256,896]{1,0:T(8,128)(2,1)}, bf16[256,896]{1,0:T(8,128)(2,1)S(1)}, u32[]{:S(2)}, u32[]{:S(2)}) collective-permute-start(bf16[256,896]{1,0:T(8,128)(2,1)} %slice.82), channel_id=1, source_target_pairs={{0,24},{4,28},{8,16},{12,20},{16,8},{20,12},{24,0},{28,4},{1,25},{... | collective-permute-start | bytes 1376264 | tf_op jit(solution)/shard_map/ppermute | solution.py:43
  69.1 3.2 %collective-permute-start.20 = (bf16[256,896]{1,0:T(8,128)(2,1)S(1)}, bf16[256,896]{1,0:T(8,128)(2,1)S(1)}, u32[]{:S(2)}, u32[]{:S(2)}) collective-permute-start(bf16[256,896]{1,0:T(8,128)(2,1)S(1)} %copy-done.9), channel_id=1, source_target_pairs={{0,1},{1,0},{2,3},{3,2},{4,5},{5,4},{6,7},{7,6},{8,9},{9,8},{10,11... | collective-permute-start | bytes 1376264 | tf_op jit(solution)/shard_map/ppermute | solution.py:34
  72.2 0.9 copy-done.13
  73.6 11.2 %end_block.1 = (f32[2,384,256]{2,1,0:T(8,128)}, f32[2,384,256]{2,1,0:T(8,128)}, f32[384,128]{1,0:T(8,128)}, f32[8,512]{1,0:T(8,128)}) custom-call(s32[2]{0:T(128)} %pad_add_fusion.place_ref, f32[2,384,256]{2,1,0:T(8,128)} %get-tuple-element.40.cross_in, f32[384,128]{1,0:T(8,128)} %get-tuple-element.41.norm_in, bf16[384,1792]{1,0:T(8,128)(2,1)} %refs_0_.5, ...), custom_call_target="tpu_custom_call" | custom-call | flops 1000 | bytes 1000 | tf_op jit(solution)/shard_map/end_block/pallas_call | solution.py:145
  84.9 0.5 collective-permute-start.23
  85.4 1.3 collective-permute-done.22.refs_24_
  86.7 0.7 collective-permute-done.23.refs_25_
  87.4 0.7 copy-done.19
  88.1 9.2 %last_block.1 = (f32[384,1024]{1,0:T(8,128)}, f32[72,512]{1,0:T(8,128)}, f32[72,512]{1,0:T(8,128)}) custom-call(s32[2]{0:T(128)} %pad_add_fusion.place_ref, f32[2,384,256]{2,1,0:T(8,128)} %get-tuple-element.48.cross_own_in, f32[2,384,256]{2,1,0:T(8,128)} %get-tuple-element.49.cross_end_in, f32[384,128]{1,0:T(8,128)} %get-tuple-element.50.row_norm_in, ...), custom_call_target="tpu_custom_call" | custom-call | flops 1000 | bytes 1000 | tf_op jit(solution)/shard_map/last_block/pallas_call | solution.py:145
  97.5 1.4 collective-permute-done.24
  99.0 0.9 add.109
  99.9 1.0 collective-permute-start.27
  100.9 0.6 collective-permute-start.26
  101.5 2.0 %collective-permute-start.25 = (f32[72,512]{1,0:T(8,128)S(1)}, f32[72,512]{1,0:T(8,128)S(1)}, u32[]{:S(2)}, u32[]{:S(2)}) collective-permute-start(f32[72,512]{1,0:T(8,128)S(1)} %add.109), channel_id=1, source_target_pairs={{0,8},{4,12},{8,0},{12,4},{16,24},{20,28},{24,16},{28,20},{1,9},{5... | collective-permute-start | bytes 442376 | tf_op jit(solution)/shard_map/ppermute | solution.py:43
  103.5 4.1 %collective-permute-done.27 = f32[72,512]{1,0:T(8,128)S(1)} collective-permute-done((f32[72,512]{1,0:T(8,128)S(1)}, f32[72,512]{1,0:T(8,128)S(1)}, u32[]{:S(2)}, u32[]{:S(2)}) %collective-permute-start.27) | collective-permute-done | bytes 147488 | tf_op jit(solution)/shard_map/ppermute | solution.py:43
  107.6 2.1 %collective-permute-done.26 = f32[72,512]{1,0:T(8,128)S(1)} collective-permute-done((f32[72,512]{1,0:T(8,128)S(1)}, f32[72,512]{1,0:T(8,128)S(1)}, u32[]{:S(2)}, u32[]{:S(2)}) %collective-permute-start.26) | collective-permute-done | bytes 147488 | tf_op jit(solution)/shard_map/ppermute | solution.py:43
  109.8 1.3 collective-permute-done.28
  111.4 1.6 fusion.28
  113.2 1.2 collective-permute-done.29
  114.5 1.1 fusion.9
  115.8 1.2 collective-permute-done.30
  117.1 1.2 collective-permute-start.33
  118.4 0.6 collective-permute-start.32
  119.0 1.7 %collective-permute-start.31 = (f32[72,512]{1,0:T(8,128)S(1)}, f32[72,512]{1,0:T(8,128)S(1)}, u32[]{:S(2)}, u32[]{:S(2)}) collective-permute-start(f32[72,512]{1,0:T(8,128)S(1)} %select_add_fusion.1), channel_id=1, source_target_pairs={{0,8},{4,12},{8,0},{12,4},{16,24},{20,28},{24,16},{28,20},{1,9},{5... | collective-permute-start | bytes 442376 | tf_op jit(solution)/shard_map/ppermute | solution.py:43
  120.7 4.1 %collective-permute-done.33 = f32[72,512]{1,0:T(8,128)S(1)} collective-permute-done((f32[72,512]{1,0:T(8,128)S(1)}, f32[72,512]{1,0:T(8,128)S(1)}, u32[]{:S(2)}, u32[]{:S(2)}) %collective-permute-start.33) | collective-permute-done | bytes 147488 | tf_op jit(solution)/shard_map/ppermute | solution.py:43
  124.8 2.3 %collective-permute-done.32 = f32[72,512]{1,0:T(8,128)S(1)} collective-permute-done((f32[72,512]{1,0:T(8,128)S(1)}, f32[72,512]{1,0:T(8,128)S(1)}, u32[]{:S(2)}, u32[]{:S(2)}) %collective-permute-start.32) | collective-permute-done | bytes 147488 | tf_op jit(solution)/shard_map/ppermute | solution.py:43
  127.3 1.4 collective-permute-done.34
  128.9 1.6 fusion.25
  130.8 1.2 collective-permute-done.35
  132.0 1.1 fusion.12
  133.6 1.2 collective-permute-done.36
  134.8 1.2 collective-permute-start.39
  136.1 0.6 collective-permute-start.38
  136.7 1.7 %collective-permute-start.37 = (f32[72,512]{1,0:T(8,128)S(1)}, f32[72,512]{1,0:T(8,128)S(1)}, u32[]{:S(2)}, u32[]{:S(2)}) collective-permute-start(f32[72,512]{1,0:T(8,128)S(1)} %select_add_fusion), channel_id=1, source_target_pairs={{0,8},{4,12},{8,0},{12,4},{16,24},{20,28},{24,16},{28,20},{1,9},{5... | collective-permute-start | bytes 442376 | tf_op jit(solution)/shard_map/ppermute | solution.py:43
  138.4 4.1 %collective-permute-done.39 = f32[72,512]{1,0:T(8,128)S(1)} collective-permute-done((f32[72,512]{1,0:T(8,128)S(1)}, f32[72,512]{1,0:T(8,128)S(1)}, u32[]{:S(2)}, u32[]{:S(2)}) %collective-permute-start.39) | collective-permute-done | bytes 147488 | tf_op jit(solution)/shard_map/ppermute | solution.py:43
  142.5 2.3 %collective-permute-done.38 = f32[72,512]{1,0:T(8,128)S(1)} collective-permute-done((f32[72,512]{1,0:T(8,128)S(1)}, f32[72,512]{1,0:T(8,128)S(1)}, u32[]{:S(2)}, u32[]{:S(2)}) %collective-permute-start.38) | collective-permute-done | bytes 147488 | tf_op jit(solution)/shard_map/ppermute | solution.py:43
  145.0 1.4 collective-permute-done.40
  146.6 9.2 %collective-permute-start.41 = (f32[128,512]{1,0:T(8,128)S(1)}, f32[128,512]{1,0:T(8,128)S(1)}, u32[]{:S(2)}, u32[]{:S(2)}) collective-permute-start(f32[128,512]{1,0:T(8,128)S(1)} %pad_maximum_fusion), channel_id=1, source_target_pairs={{0,1},{1,0},{2,3},{3,2},{4,5},{5,4},{6,7},{7,6},{8,9},{9,8},{10,11... | collective-permute-start | bytes 786440 | tf_op jit(solution)/shard_map/ppermute | solution.py:34
  155.7 6.6 %collective-permute-done.41 = f32[128,512]{1,0:T(8,128)S(1)} collective-permute-done((f32[128,512]{1,0:T(8,128)S(1)}, f32[128,512]{1,0:T(8,128)S(1)}, u32[]{:S(2)}, u32[]{:S(2)}) %collective-permute-start.41) | collective-permute-done | bytes 262176 | tf_op jit(solution)/shard_map/ppermute | solution.py:34
  162.4 0.7 slice_bitcast_fusion
  (103 shorter events, 3.6 us)
Async XLA Ops:
  0.6 23.8 %collective-permute-start.2 = (bf16[512,896]{1,0:T(8,128)(2,1)}, bf16[512,896]{1,0:T(8,128)(2,1)}, u32[]{:S(2)}, u32[]{:S(2)}) collective-permute-start(bf16[512,896]{1,0:T(8,128)(2,1)} %refs_6_.1), channel_id=1, source_target_pairs={{0,1},{1,0},{2,3},{3,2},{4,5},{5,4},{6,7},{7,6},{8,9},{9,8},{10,11... | collective-permute-start | bytes 2752520 | tf_op jit(solution)/shard_map/ppermute | solution.py:34
  3.7 22.0 %collective-permute-start.1 = (bf16[512,896]{1,0:T(8,128)(2,1)}, bf16[512,896]{1,0:T(8,128)(2,1)S(1)}, u32[]{:S(2)}, u32[]{:S(2)}) collective-permute-start(bf16[512,896]{1,0:T(8,128)(2,1)} %refs_6_.1), channel_id=1, source_target_pairs={{0,16},{4,20},{8,24},{12,28},{16,0},{20,4},{24,8},{28,12},{1,17},{... | collective-permute-start | bytes 2752520 | tf_op jit(solution)/shard_map/ppermute | solution.py:43
  5.2 21.7 %collective-permute-start = (bf16[512,896]{1,0:T(8,128)(2,1)}, bf16[512,896]{1,0:T(8,128)(2,1)S(1)}, u32[]{:S(2)}, u32[]{:S(2)}) collective-permute-start(bf16[512,896]{1,0:T(8,128)(2,1)} %refs_6_.1), channel_id=1, source_target_pairs={{0,8},{4,12},{8,0},{12,4},{16,24},{20,28},{24,16},{28,20},{1,9},{5... | collective-permute-start | bytes 2752520 | tf_op jit(solution)/shard_map/ppermute | solution.py:43
  6.7 32.5 %collective-permute-start.4 = (bf16[384,1792]{1,0:T(8,128)(2,1)}, bf16[384,1792]{1,0:T(8,128)(2,1)S(1)}, u32[]{:S(2)}, u32[]{:S(2)}) collective-permute-start(bf16[384,1792]{1,0:T(8,128)(2,1)} %refs_0_.5), channel_id=1, source_target_pairs={{0,4},{1,2},{2,1},{3,7},{4,0},{5,6},{6,5},{7,3},{8,12},{9,10},{10,... | collective-permute-start | bytes 4128776 | tf_op jit(solution)/shard_map/ppermute | solution.py:39
  9.0 20.6 %copy-start.4 = (bf16[512,896]{1,0:T(8,128)(2,1)S(1)}, bf16[512,896]{1,0:T(8,128)(2,1)}, u32[]{:S(2)}) copy-start(bf16[512,896]{1,0:T(8,128)(2,1)} %refs_6_.1) | copy-start | bytes 2752516
  25.7 25.9 %copy-start.2 = (bf16[512,896]{1,0:T(8,128)(2,1)}, bf16[512,896]{1,0:T(8,128)(2,1)S(1)}, u32[]{:S(2)}) copy-start(bf16[512,896]{1,0:T(8,128)(2,1)S(1)} %collective-permute-done.1.refs_5_.refs_7_.refs_8_) | copy-start | bytes 2752516
  27.0 24.7 %copy-start.3 = (bf16[512,896]{1,0:T(8,128)(2,1)}, bf16[512,896]{1,0:T(8,128)(2,1)S(1)}, u32[]{:S(2)}) copy-start(bf16[512,896]{1,0:T(8,128)(2,1)S(1)} %collective-permute-done.refs_4_.refs_6_.refs_7_) | copy-start | bytes 2752516
  27.0 15.8 %collective-permute-start.3 = (bf16[384,896]{1,0:T(8,128)(2,1)S(1)}, bf16[384,896]{1,0:T(8,128)(2,1)}, u32[]{:S(2)}, u32[]{:S(2)}) collective-permute-start(bf16[384,896]{1,0:T(8,128)(2,1)S(1)} %get-tuple-element.31), channel_id=1, source_target_pairs={{0,1},{1,0},{2,3},{3,2},{4,5},{5,4},{6,7},{7,6},{8,9},{9,8},{10,11... | collective-permute-start | bytes 2064392 | tf_op jit(solution)/shard_map/ppermute | solution.py:34
  27.5 10.7 %collective-permute-start.5 = (bf16[256,896]{1,0:T(8,128)(2,1)S(1)}, bf16[256,896]{1,0:T(8,128)(2,1)S(1)}, u32[]{:S(2)}, u32[]{:S(2)}) collective-permute-start(bf16[256,896]{1,0:T(8,128)(2,1)S(1)} %slice.80), channel_id=1, source_target_pairs={{0,16},{4,20},{8,24},{12,28},{16,0},{20,4},{24,8},{28,12},{1,17},{... | collective-permute-start | bytes 1376264 | tf_op jit(solution)/shard_map/ppermute | solution.py:43
  28.0 10.7 %collective-permute-start.6 = (bf16[256,896]{1,0:T(8,128)(2,1)S(1)}, bf16[256,896]{1,0:T(8,128)(2,1)S(1)}, u32[]{:S(2)}, u32[]{:S(2)}) collective-permute-start(bf16[256,896]{1,0:T(8,128)(2,1)S(1)} %slice.81), channel_id=1, source_target_pairs={{0,8},{4,12},{8,0},{12,4},{16,24},{20,28},{24,16},{28,20},{1,9},{5... | collective-permute-start | bytes 1376264 | tf_op jit(solution)/shard_map/ppermute | solution.py:43
  29.6 15.5 %collective-permute-start.7 = (bf16[512,896]{1,0:T(8,128)(2,1)S(1)}, bf16[512,896]{1,0:T(8,128)(2,1)S(1)}, u32[]{:S(2)}, u32[]{:S(2)}) collective-permute-start(bf16[512,896]{1,0:T(8,128)(2,1)S(1)} %copy-done.4), channel_id=1, source_target_pairs={{0,4},{4,0},{8,12},{12,8},{16,20},{20,16},{24,28},{28,24},{1,5},{5... | collective-permute-start | bytes 2752520 | tf_op jit(solution)/shard_map/ppermute | solution.py:43
  38.2 10.2 %copy-start.8 = (bf16[256,896]{1,0:T(8,128)(2,1)}, bf16[256,896]{1,0:T(8,128)(2,1)S(1)}, u32[]{:S(2)}) copy-start(bf16[256,896]{1,0:T(8,128)(2,1)S(1)} %collective-permute-done.5.refs_6_.refs_8_.refs_9_) | copy-start | bytes 1376260
  38.7 9.6 %copy-start.10 = (bf16[256,896]{1,0:T(8,128)(2,1)}, bf16[256,896]{1,0:T(8,128)(2,1)S(1)}, u32[]{:S(2)}) copy-start(bf16[256,896]{1,0:T(8,128)(2,1)S(1)} %collective-permute-done.6.refs_7_.refs_9_.refs_10_) | copy-start | bytes 1376260
  38.7 4.1 %collective-permute-start.11 = (bf16[256,896]{1,0:T(8,128)(2,1)S(1)}, bf16[256,896]{1,0:T(8,128)(2,1)S(1)}, u32[]{:S(2)}, u32[]{:S(2)}) collective-permute-start(bf16[256,896]{1,0:T(8,128)(2,1)S(1)} %collective-permute-done.6.refs_7_.refs_9_.refs_10_), channel_id=1, source_target_pairs={{0,4},{4,0},{8,12},{12,8},{16,20},{20,16},{24,28},{28,24},{1,5},{5... | collective-permute-start | bytes 1376264 | tf_op jit(solution)/shard_map/ppermute | solution.py:43
  38.7 4.9 %collective-permute-start.10 = (bf16[256,896]{1,0:T(8,128)(2,1)S(1)}, bf16[256,896]{1,0:T(8,128)(2,1)S(1)}, u32[]{:S(2)}, u32[]{:S(2)}) collective-permute-start(bf16[256,896]{1,0:T(8,128)(2,1)S(1)} %collective-permute-done.5.refs_6_.refs_8_.refs_9_), channel_id=1, source_target_pairs={{0,4},{4,0},{8,12},{12,8},{16,20},{20,16},{24,28},{28,24},{1,5},{5... | collective-permute-start | bytes 1376264 | tf_op jit(solution)/shard_map/ppermute | solution.py:43
  39.2 12.5 %copy-start.1 = (bf16[384,1792]{1,0:T(8,128)(2,1)}, bf16[384,1792]{1,0:T(8,128)(2,1)S(1)}, u32[]{:S(2)}) copy-start(bf16[384,1792]{1,0:T(8,128)(2,1)S(1)} %collective-permute-done.4.refs_1_) | copy-start | bytes 4128772
  39.2 5.9 %collective-permute-start.9 = (bf16[512,896]{1,0:T(8,128)(2,1)S(1)}, bf16[512,896]{1,0:T(8,128)(2,1)S(1)}, u32[]{:S(2)}, u32[]{:S(2)}) collective-permute-start(bf16[512,896]{1,0:T(8,128)(2,1)S(1)} %collective-permute-done.1.refs_5_.refs_7_.refs_8_), channel_id=1, source_target_pairs={{0,4},{4,0},{8,12},{12,8},{16,20},{20,16},{24,28},{28,24},{1,5},{5... | collective-permute-start | bytes 2752520 | tf_op jit(solution)/shard_map/ppermute | solution.py:43
  42.8 5.5 %collective-permute-start.8 = (bf16[512,896]{1,0:T(8,128)(2,1)S(1)}, bf16[512,896]{1,0:T(8,128)(2,1)S(1)}, u32[]{:S(2)}, u32[]{:S(2)}) collective-permute-start(bf16[512,896]{1,0:T(8,128)(2,1)S(1)} %collective-permute-done.refs_4_.refs_6_.refs_7_), channel_id=1, source_target_pairs={{0,4},{4,0},{8,12},{12,8},{16,20},{20,16},{24,28},{28,24},{1,5},{5... | collective-permute-start | bytes 2752520 | tf_op jit(solution)/shard_map/ppermute | solution.py:43
  42.8 5.6 %copy-start.11 = (bf16[256,896]{1,0:T(8,128)(2,1)}, bf16[256,896]{1,0:T(8,128)(2,1)S(1)}, u32[]{:S(2)}) copy-start(bf16[256,896]{1,0:T(8,128)(2,1)S(1)} %collective-permute-done.11.refs_12_.refs_14_.refs_15_) | copy-start | bytes 1376260
  42.8 23.1 %collective-permute-start.14 = (bf16[512,896]{1,0:T(8,128)(2,1)}, bf16[512,896]{1,0:T(8,128)(2,1)}, u32[]{:S(2)}, u32[]{:S(2)}) collective-permute-start(bf16[512,896]{1,0:T(8,128)(2,1)} %collective-permute-done.2.refs_15_.refs_16_), channel_id=1, source_target_pairs={{0,16},{4,20},{8,24},{12,28},{16,0},{20,4},{24,8},{28,12},{1,17},{... | collective-permute-start | bytes 2752520 | tf_op jit(solution)/shard_map/ppermute | solution.py:43
  43.6 4.8 %copy-start.12 = (bf16[256,896]{1,0:T(8,128)(2,1)}, bf16[256,896]{1,0:T(8,128)(2,1)S(1)}, u32[]{:S(2)}) copy-start(bf16[256,896]{1,0:T(8,128)(2,1)S(1)} %collective-permute-done.10.refs_11_.refs_13_.refs_14_) | copy-start | bytes 1376260
  43.6 22.7 %collective-permute-start.13 = (bf16[512,896]{1,0:T(8,128)(2,1)}, bf16[512,896]{1,0:T(8,128)(2,1)}, u32[]{:S(2)}, u32[]{:S(2)}) collective-permute-start(bf16[512,896]{1,0:T(8,128)(2,1)} %collective-permute-done.2.refs_15_.refs_16_), channel_id=1, source_target_pairs={{0,8},{4,12},{8,0},{12,4},{16,24},{20,28},{24,16},{28,20},{1,9},{5... | collective-permute-start | bytes 2752520 | tf_op jit(solution)/shard_map/ppermute | solution.py:43
  45.1 3.2 %copy-start.5 = (bf16[512,896]{1,0:T(8,128)(2,1)}, bf16[512,896]{1,0:T(8,128)(2,1)S(1)}, u32[]{:S(2)}) copy-start(bf16[512,896]{1,0:T(8,128)(2,1)S(1)} %collective-permute-done.7.refs_8_.refs_10_.refs_11_) | copy-start | bytes 2752516
  45.1 21.2 %collective-permute-start.15 = (bf16[384,896]{1,0:T(8,128)(2,1)}, bf16[384,896]{1,0:T(8,128)(2,1)}, u32[]{:S(2)}, u32[]{:S(2)}) collective-permute-start(bf16[384,896]{1,0:T(8,128)(2,1)} %collective-permute-done.3.refs_2_), channel_id=1, source_target_pairs={{0,4},{1,2},{2,1},{3,7},{4,0},{5,6},{6,5},{7,3},{8,12},{9,10},{10,... | collective-permute-start | bytes 2064392 | tf_op jit(solution)/shard_map/ppermute | solution.py:39
  45.1 3.3 %copy-start.6 = (bf16[512,896]{1,0:T(8,128)(2,1)}, bf16[512,896]{1,0:T(8,128)(2,1)S(1)}, u32[]{:S(2)}) copy-start(bf16[512,896]{1,0:T(8,128)(2,1)S(1)} %collective-permute-done.9.refs_10_.refs_12_.refs_13_) | copy-start | bytes 2752516
  45.1 21.7 %collective-permute-start.12 = (bf16[384,896]{1,0:T(8,128)(2,1)}, bf16[384,896]{1,0:T(8,128)(2,1)}, u32[]{:S(2)}, u32[]{:S(2)}) collective-permute-start(bf16[384,896]{1,0:T(8,128)(2,1)} %get-tuple-element.42), channel_id=1, source_target_pairs={{0,1},{1,0},{2,3},{3,2},{4,5},{5,4},{6,7},{7,6},{8,9},{9,8},{10,11... | collective-permute-start | bytes 2064392 | tf_op jit(solution)/shard_map/ppermute | solution.py:34
  48.3 0.9 copy-start.7
  48.3 20.8 %collective-permute-start.16 = (bf16[512,896]{1,0:T(8,128)(2,1)}, bf16[512,896]{1,0:T(8,128)(2,1)}, u32[]{:S(2)}, u32[]{:S(2)}) collective-permute-start(bf16[512,896]{1,0:T(8,128)(2,1)} %collective-permute-done.2.refs_15_.refs_16_), channel_id=1, source_target_pairs={{0,4},{4,0},{8,12},{12,8},{16,20},{20,16},{24,28},{28,24},{1,5},{5... | collective-permute-start | bytes 2752520 | tf_op jit(solution)/shard_map/ppermute | solution.py:43
  51.7 17.4 %copy-start.9 = (bf16[256,896]{1,0:T(8,128)(2,1)S(1)}, bf16[256,896]{1,0:T(8,128)(2,1)}, u32[]{:S(2)}) copy-start(bf16[256,896]{1,0:T(8,128)(2,1)} %copy-done.8) | copy-start | bytes 1376260
  66.3 5.9 %collective-permute-start.17 = (bf16[512,896]{1,0:T(8,128)(2,1)}, bf16[512,896]{1,0:T(8,128)(2,1)S(1)}, u32[]{:S(2)}, u32[]{:S(2)}) collective-permute-start(bf16[512,896]{1,0:T(8,128)(2,1)} %collective-permute-done.13.refs_16_.refs_17_), channel_id=1, source_target_pairs={{0,4},{4,0},{8,12},{12,8},{16,20},{20,16},{24,28},{28,24},{1,5},{5... | collective-permute-start | bytes 2752520 | tf_op jit(solution)/shard_map/ppermute | solution.py:43
  66.3 5.9 %collective-permute-start.18 = (bf16[512,896]{1,0:T(8,128)(2,1)}, bf16[512,896]{1,0:T(8,128)(2,1)S(1)}, u32[]{:S(2)}, u32[]{:S(2)}) collective-permute-start(bf16[512,896]{1,0:T(8,128)(2,1)} %collective-permute-done.14.refs_17_.refs_18_), channel_id=1, source_target_pairs={{0,4},{4,0},{8,12},{12,8},{16,20},{20,16},{24,28},{28,24},{1,5},{5... | collective-permute-start | bytes 2752520 | tf_op jit(solution)/shard_map/ppermute | solution.py:43
  66.9 17.9 %collective-permute-start.19 = (bf16[384,896]{1,0:T(8,128)(2,1)}, bf16[384,896]{1,0:T(8,128)(2,1)S(1)}, u32[]{:S(2)}, u32[]{:S(2)}) collective-permute-start(bf16[384,896]{1,0:T(8,128)(2,1)} %collective-permute-done.12.refs_3_), channel_id=1, source_target_pairs={{0,4},{1,2},{2,1},{3,7},{4,0},{5,6},{6,5},{7,3},{8,12},{9,10},{10,... | collective-permute-start | bytes 2064392 | tf_op jit(solution)/shard_map/ppermute | solution.py:39
  66.9 17.9 %collective-permute-start.21 = (bf16[256,896]{1,0:T(8,128)(2,1)}, bf16[256,896]{1,0:T(8,128)(2,1)S(1)}, u32[]{:S(2)}, u32[]{:S(2)}) collective-permute-start(bf16[256,896]{1,0:T(8,128)(2,1)} %slice.82), channel_id=1, source_target_pairs={{0,24},{4,28},{8,16},{12,20},{16,8},{20,12},{24,0},{28,4},{1,25},{... | collective-permute-start | bytes 1376264 | tf_op jit(solution)/shard_map/ppermute | solution.py:43
  69.1 15.7 %collective-permute-start.20 = (bf16[256,896]{1,0:T(8,128)(2,1)S(1)}, bf16[256,896]{1,0:T(8,128)(2,1)S(1)}, u32[]{:S(2)}, u32[]{:S(2)}) collective-permute-start(bf16[256,896]{1,0:T(8,128)(2,1)S(1)} %copy-done.9), channel_id=1, source_target_pairs={{0,1},{1,0},{2,3},{3,2},{4,5},{5,4},{6,7},{7,6},{8,9},{9,8},{10,11... | collective-permute-start | bytes 1376264 | tf_op jit(solution)/shard_map/ppermute | solution.py:34
  72.2 0.9 copy-start.13
  72.2 1.3 copy-start.14
  84.7 2.6 %copy-start.16 = (bf16[256,896]{1,0:T(8,128)(2,1)}, bf16[256,896]{1,0:T(8,128)(2,1)S(1)}, u32[]{:S(2)}) copy-start(bf16[256,896]{1,0:T(8,128)(2,1)S(1)} %collective-permute-done.21.refs_23_) | copy-start | bytes 1376260
  84.7 2.6 %copy-start.15 = (bf16[384,896]{1,0:T(8,128)(2,1)}, bf16[384,896]{1,0:T(8,128)(2,1)S(1)}, u32[]{:S(2)}) copy-start(bf16[384,896]{1,0:T(8,128)(2,1)S(1)} %collective-permute-done.19.refs_5_) | copy-start | bytes 2064388
  84.8 2.6 %copy-start.17 = (bf16[256,896]{1,0:T(8,128)(2,1)}, bf16[256,896]{1,0:T(8,128)(2,1)S(1)}, u32[]{:S(2)}) copy-start(bf16[256,896]{1,0:T(8,128)(2,1)S(1)} %collective-permute-done.20.refs_22_) | copy-start | bytes 1376260
  84.8 1.9 %collective-permute-start.22 = (bf16[256,896]{1,0:T(8,128)(2,1)S(1)}, bf16[256,896]{1,0:T(8,128)(2,1)S(1)}, u32[]{:S(2)}, u32[]{:S(2)}) collective-permute-start(bf16[256,896]{1,0:T(8,128)(2,1)S(1)} %collective-permute-done.20.refs_22_), channel_id=1, source_target_pairs={{0,4},{4,0},{8,12},{12,8},{16,20},{20,16},{24,28},{28,24},{1,5},{5... | collective-permute-start | bytes 1376264 | tf_op jit(solution)/shard_map/ppermute | solution.py:43
  84.9 2.5 %collective-permute-start.23 = (bf16[256,896]{1,0:T(8,128)(2,1)S(1)}, bf16[256,896]{1,0:T(8,128)(2,1)S(1)}, u32[]{:S(2)}, u32[]{:S(2)}) collective-permute-start(bf16[256,896]{1,0:T(8,128)(2,1)S(1)} %collective-permute-done.21.refs_23_), channel_id=1, source_target_pairs={{0,4},{4,0},{8,12},{12,8},{16,20},{20,16},{24,28},{28,24},{1,5},{5... | collective-permute-start | bytes 1376264 | tf_op jit(solution)/shard_map/ppermute | solution.py:43
  86.7 0.8 copy-start.18
  87.3 0.8 copy-start.19
  97.3 14.1 %copy-start = (f32[384,1024]{1,0:T(8,128)S(1)}, f32[384,1024]{1,0:T(8,128)}, u32[]{:S(2)}) copy-start(f32[384,1024]{1,0:T(8,128)} %get-tuple-element.59) | copy-start | bytes 4718596
  97.3 1.6 %collective-permute-start.24 = (f32[72,512]{1,0:T(8,128)}, f32[72,512]{1,0:T(8,128)S(1)}, u32[]{:S(2)}, u32[]{:S(2)}) collective-permute-start(f32[72,512]{1,0:T(8,128)} %get-tuple-element.58), channel_id=1, source_target_pairs={{0,4},{4,0},{8,12},{12,8},{16,20},{20,16},{24,28},{28,24},{1,5},{5... | collective-permute-start | bytes 442376 | tf_op jit(solution)/shard_map/ppermute | solution.py:43
  99.9 7.7 %collective-permute-start.27 = (f32[72,512]{1,0:T(8,128)S(1)}, f32[72,512]{1,0:T(8,128)S(1)}, u32[]{:S(2)}, u32[]{:S(2)}) collective-permute-start(f32[72,512]{1,0:T(8,128)S(1)} %add.109), channel_id=1, source_target_pairs={{0,24},{4,28},{8,16},{12,20},{16,8},{20,12},{24,0},{28,4},{1,25},{... | collective-permute-start | bytes 442376 | tf_op jit(solution)/shard_map/ppermute | solution.py:43
  100.9 8.8 %collective-permute-start.26 = (f32[72,512]{1,0:T(8,128)S(1)}, f32[72,512]{1,0:T(8,128)S(1)}, u32[]{:S(2)}, u32[]{:S(2)}) collective-permute-start(f32[72,512]{1,0:T(8,128)S(1)} %add.109), channel_id=1, source_target_pairs={{0,16},{4,20},{8,24},{12,28},{16,0},{20,4},{24,8},{28,12},{1,17},{... | collective-permute-start | bytes 442376 | tf_op jit(solution)/shard_map/ppermute | solution.py:43
  101.5 8.2 %collective-permute-start.25 = (f32[72,512]{1,0:T(8,128)S(1)}, f32[72,512]{1,0:T(8,128)S(1)}, u32[]{:S(2)}, u32[]{:S(2)}) collective-permute-start(f32[72,512]{1,0:T(8,128)S(1)} %add.109), channel_id=1, source_target_pairs={{0,8},{4,12},{8,0},{12,4},{16,24},{20,28},{24,16},{28,20},{1,9},{5... | collective-permute-start | bytes 442376 | tf_op jit(solution)/shard_map/ppermute | solution.py:43
  109.7 1.4 collective-permute-start.28
  113.0 1.4 collective-permute-start.29
  115.6 1.4 collective-permute-start.30
  117.1 7.7 %collective-permute-start.33 = (f32[72,512]{1,0:T(8,128)S(1)}, f32[72,512]{1,0:T(8,128)S(1)}, u32[]{:S(2)}, u32[]{:S(2)}) collective-permute-start(f32[72,512]{1,0:T(8,128)S(1)} %select_add_fusion.1), channel_id=1, source_target_pairs={{0,24},{4,28},{8,16},{12,20},{16,8},{20,12},{24,0},{28,4},{1,25},{... | collective-permute-start | bytes 442376 | tf_op jit(solution)/shard_map/ppermute | solution.py:43
  118.4 8.8 %collective-permute-start.32 = (f32[72,512]{1,0:T(8,128)S(1)}, f32[72,512]{1,0:T(8,128)S(1)}, u32[]{:S(2)}, u32[]{:S(2)}) collective-permute-start(f32[72,512]{1,0:T(8,128)S(1)} %select_add_fusion.1), channel_id=1, source_target_pairs={{0,16},{4,20},{8,24},{12,28},{16,0},{20,4},{24,8},{28,12},{1,17},{... | collective-permute-start | bytes 442376 | tf_op jit(solution)/shard_map/ppermute | solution.py:43
  119.0 8.2 %collective-permute-start.31 = (f32[72,512]{1,0:T(8,128)S(1)}, f32[72,512]{1,0:T(8,128)S(1)}, u32[]{:S(2)}, u32[]{:S(2)}) collective-permute-start(f32[72,512]{1,0:T(8,128)S(1)} %select_add_fusion.1), channel_id=1, source_target_pairs={{0,8},{4,12},{8,0},{12,4},{16,24},{20,28},{24,16},{28,20},{1,9},{5... | collective-permute-start | bytes 442376 | tf_op jit(solution)/shard_map/ppermute | solution.py:43
  127.2 1.4 collective-permute-start.34
  130.6 1.4 collective-permute-start.35
  133.3 1.4 collective-permute-start.36
  134.8 7.7 %collective-permute-start.39 = (f32[72,512]{1,0:T(8,128)S(1)}, f32[72,512]{1,0:T(8,128)S(1)}, u32[]{:S(2)}, u32[]{:S(2)}) collective-permute-start(f32[72,512]{1,0:T(8,128)S(1)} %select_add_fusion), channel_id=1, source_target_pairs={{0,24},{4,28},{8,16},{12,20},{16,8},{20,12},{24,0},{28,4},{1,25},{... | collective-permute-start | bytes 442376 | tf_op jit(solution)/shard_map/ppermute | solution.py:43
  136.1 8.8 %collective-permute-start.38 = (f32[72,512]{1,0:T(8,128)S(1)}, f32[72,512]{1,0:T(8,128)S(1)}, u32[]{:S(2)}, u32[]{:S(2)}) collective-permute-start(f32[72,512]{1,0:T(8,128)S(1)} %select_add_fusion), channel_id=1, source_target_pairs={{0,16},{4,20},{8,24},{12,28},{16,0},{20,4},{24,8},{28,12},{1,17},{... | collective-permute-start | bytes 442376 | tf_op jit(solution)/shard_map/ppermute | solution.py:43
  136.7 8.2 %collective-permute-start.37 = (f32[72,512]{1,0:T(8,128)S(1)}, f32[72,512]{1,0:T(8,128)S(1)}, u32[]{:S(2)}, u32[]{:S(2)}) collective-permute-start(f32[72,512]{1,0:T(8,128)S(1)} %select_add_fusion), channel_id=1, source_target_pairs={{0,8},{4,12},{8,0},{12,4},{16,24},{20,28},{24,16},{28,20},{1,9},{5... | collective-permute-start | bytes 442376 | tf_op jit(solution)/shard_map/ppermute | solution.py:43
  144.9 1.4 collective-permute-start.40
  146.6 15.8 %collective-permute-start.41 = (f32[128,512]{1,0:T(8,128)S(1)}, f32[128,512]{1,0:T(8,128)S(1)}, u32[]{:S(2)}, u32[]{:S(2)}) collective-permute-start(f32[128,512]{1,0:T(8,128)S(1)} %pad_maximum_fusion), channel_id=1, source_target_pairs={{0,1},{1,0},{2,3},{3,2},{4,5},{5,4},{6,7},{7,6},{8,9},{9,8},{10,11... | collective-permute-start | bytes 786440 | tf_op jit(solution)/shard_map/ppermute | solution.py:34

commit v6 on v5

--- a/solution.py
+++ b/solution.py
@@ -394,7 +394,7 @@
     )
 
 
-def conjugate_gradients(kernel, sums, columns, lam, sum_rows, sum_landmarks):
+def conjugate_gradients(kernel, sums, columns, lam, sum_rows, sum_landmarks, settle=None):
     count = columns.shape[0]
     residual, precond = sums[:count], lam + sums[count]
     coefficient = jnp.zeros_like(residual)
@@ -415,12 +415,39 @@
             direction = scaled + beta[:, None] * direction
             image = sums[:count] + beta[:, None] * image
         inner = inner_next
-        sums = sum_rows(packed(times(image, kernel, (1, 0)), jnp.sum(image * image, axis=1)))
+        last = packed(times(image, kernel, (1, 0)), jnp.sum(image * image, axis=1))
+        if settle is not None and iteration == ITERS - 1:
+            state, finish = settle((coefficient, residual, direction), packed_twice((inner, lam * length), last.shape[1]))
+            sums = finish(sum_rows(last.at[count:].set(packed_twice((jnp.sum(image * image, axis=1),), last.shape[1]))))
+            coefficient, residual, direction = (state[i * count : (i + 1) * count] for i in range(3))
+            inner, ridge = state[3 * count, :count], state[3 * count + 1, :count]
+        else:
+            sums = sum_rows(last)
+            ridge = lam * length
         gradient = sums[:count] + lam * direction
-        step_size = (inner / (sums[count, :count] + lam * length))[:, None]
+        step_size = (inner / (sums[count, :count] + ridge))[:, None]
         coefficient = coefficient + step_size * direction
         residual = residual - step_size * gradient
     return coefficient, residual
+
+
+def packed_twice(vectors, width):
+    rows = jnp.stack(vectors)
+    rows = jnp.pad(rows, ((0, 8 - rows.shape[0]), (0, width // 2 - rows.shape[1])))
+    return jnp.concatenate([rows, rows], axis=1)
+
+
+def settled(state, vectors):
+    z = lax.axis_index("landmark")
+    middle = (z == 1) | (z == 2)
+    whole = jnp.concatenate([*state, vectors], axis=0)
+    half = whole.shape[1] // 2
+    taken = jnp.where(middle, whole[:, :half], handed(whole[:, half:]))
+
+    def finish(sums):
+        return jnp.where(middle, sums[:, :half], handed(sums[:, half:]))
+
+    return taken, finish
 
 
 def folded(row_features, landmark_features, targets):
@@ -428,13 +455,8 @@
     columns = targets.T
     kernel, mine, other = middle_kernel(row_features, landmark_features, columns)
     sums = sum_halves(mine, other)
-    coefficient, residual = conjugate_gradients(kernel, sums, columns, lam, sum_rows_axis, sum_middle)
-    both = jnp.concatenate([coefficient, residual], axis=0)
-    half = both.shape[1] // 2
-    received = handed(both[:, half:])
-    z = lax.axis_index("landmark")
-    both = jnp.where((z == 1) | (z == 2), both[:, :half], received)
-    return both[: columns.shape[0]].T, both[columns.shape[0] :].T
+    coefficient, residual = conjugate_gradients(kernel, sums, columns, lam, sum_rows_axis, sum_middle, settled)
+    return coefficient.T, residual.T
 
 
 def plain(row_features, landmark_features, targets):

time: 163 us -> 161 us (0.988)
  waiting for transfers between devices: 74.5 us -> 65.5 us
  starting transfers between devices: 42.3 us -> 48.6 us
    ppermute x32, waiting for transfers between devices: 46.7 us -> 40.1 us  [flipped(): return lax.ppermute(block, 'proof', [(i, i ^ bits) for i in range(8)])]
    ppermute x5 -> x6, starting transfers between devices: 19 us -> 25.3 us  [handed(): return lax.ppermute(block, 'landmark', NEIGHBOURS)]
    ppermute x5 -> x6, waiting for transfers between devices: 25.5 us -> 23.1 us  [handed(): return lax.ppermute(block, 'landmark', NEIGHBOURS)]
  transfers between devices with their start and end apart: 42 -> 43, of which waited for: 25 -> 24; matrix products, arithmetic and copies ran while one was open for 3% -> 3% of each run, Pallas kernels for 12% -> 12%
where the time goes in v6:
time: 161 us
  waiting for transfers between devices  65.5 us (41%)
  starting transfers between devices  48.6 us (30%)
  Pallas kernels  29.1 us (18%)
  local copies, waits for them, and re-layouts  7.16 us (4%)
  matrix products  5.35 us (3%)
  other arithmetic  3.82 us (2%)
    ppermute x32, waiting for transfers between devices, flipped(): return lax.ppermute(block, 'proof', [(i, i ^ bits) for i in range(8)])  40.1 us
    pallas_call x3, Pallas kernels, call(): pl.pallas_call(body, out_shape=tuple((jax.ShapeDtypeStruct(shape, jnp.flo...  29.1 us
    ppermute x6, starting transfers between devices, handed(): return lax.ppermute(block, 'landmark', NEIGHBOURS)  25.3 us
    ppermute x6, waiting for transfers between devices, handed(): return lax.ppermute(block, 'landmark', NEIGHBOURS)  23.1 us
    ppermute x32, starting transfers between devices, flipped(): return lax.ppermute(block, 'proof', [(i, i ^ bits) for i in range(8)])  22.8 us
    dot_general x4, matrix products, times(): lax.dot_general(left, right, ((contract[:1], contract[1:]), ((), ())), pr...  5.35 us
  transfers between devices with their start and end apart: 43, of which 24 were waited for; matrix products, arithmetic and copies ran while one was open for 3% of the time, Pallas kernels for 12%

profile of v6, /device:TPU:0, one launch (start us, length us, event | category | flops | bytes accessed | tf_op | source)
XLA Modules:
  0.0 160.6 jit_solution(6872579268876320431)
XLA Ops:
  0.6 3.1 %collective-permute-start.2 = (bf16[512,896]{1,0:T(8,128)(2,1)}, bf16[512,896]{1,0:T(8,128)(2,1)}, u32[]{:S(2)}, u32[]{:S(2)}) collective-permute-start(bf16[512,896]{1,0:T(8,128)(2,1)} %refs_6_.1), channel_id=1, source_target_pairs={{0,1},{1,0},{2,3},{3,2},{4,5},{5,4},{6,7},{7,6},{8,9},{9,8},{10,11... | collective-permute-start | bytes 2752520 | tf_op jit(solution)/shard_map/ppermute | solution.py:34
  3.7 1.5 collective-permute-start.1
  5.2 1.5 collective-permute-start
  6.7 2.3 %fusion.23 = (bf16[384,896]{1,0:T(8,128)(2,1)}, bf16[384,896]{1,0:T(8,128)(2,1)S(1)}) fusion(bf16[384,1792]{1,0:T(8,128)(2,1)} %refs_0_.5), kind=kLoop, calls=%fused_computation.76 | loop fusion | bytes 2752512 | tf_op jit(solution)/shard_map/slice | solution.py:357
  9.0 15.4 %collective-permute-done.2.refs_15_.refs_16_ = bf16[512,896]{1,0:T(8,128)(2,1)} collective-permute-done((bf16[512,896]{1,0:T(8,128)(2,1)}, bf16[512,896]{1,0:T(8,128)(2,1)}, u32[]{:S(2)}, u32[]{:S(2)}) %collective-permute-start.2) | collective-permute-done | bytes 917536 | tf_op jit(solution)/shard_map/ppermute | solution.py:34
  24.4 1.4 collective-permute-done.1.refs_5_.refs_7_.refs_8_
  25.7 1.2 collective-permute-done.refs_4_.refs_6_.refs_7_
  27.0 0.4 collective-permute-start.3
  27.5 0.5 collective-permute-start.5
  28.0 1.6 collective-permute-start.6
  29.6 8.6 %collective-permute-done.5.refs_6_.refs_8_.refs_9_ = bf16[256,896]{1,0:T(8,128)(2,1)S(1)} collective-permute-done((bf16[256,896]{1,0:T(8,128)(2,1)S(1)}, bf16[256,896]{1,0:T(8,128)(2,1)S(1)}, u32[]{:S(2)}, u32[]{:S(2)}) %collective-permute-start.5) | collective-permute-done | bytes 458784 | tf_op jit(solution)/shard_map/ppermute | solution.py:43
  38.2 0.5 collective-permute-done.6.refs_7_.refs_9_.refs_10_
  38.7 0.5 collective-permute-start.10
  39.3 3.5 %collective-permute-done.3.refs_2_ = bf16[384,896]{1,0:T(8,128)(2,1)} collective-permute-done((bf16[384,896]{1,0:T(8,128)(2,1)S(1)}, bf16[384,896]{1,0:T(8,128)(2,1)}, u32[]{:S(2)}, u32[]{:S(2)}) %collective-permute-start.3) | collective-permute-done | bytes 688160 | tf_op jit(solution)/shard_map/ppermute | solution.py:34
  42.8 0.8 collective-permute-start.14
  43.6 1.5 collective-permute-start.13
  45.1 3.1 %collective-permute-start.12 = (bf16[384,896]{1,0:T(8,128)(2,1)}, bf16[384,896]{1,0:T(8,128)(2,1)}, u32[]{:S(2)}, u32[]{:S(2)}) collective-permute-start(bf16[384,896]{1,0:T(8,128)(2,1)} %get-tuple-element.54), channel_id=1, source_target_pairs={{0,1},{1,0},{2,3},{3,2},{4,5},{5,4},{6,7},{7,6},{8,9},{9,8},{10,11... | collective-permute-start | bytes 2064392 | tf_op jit(solution)/shard_map/ppermute | solution.py:34
  48.4 0.8 copy-done.7
  49.2 0.7 pad_add_fusion.place_ref
  49.9 1.8 %slice.108 = bf16[256,896]{1,0:T(8,128)(2,1)} slice(bf16[512,896]{1,0:T(8,128)(2,1)} %collective-permute-done.2.refs_15_.refs_16_), slice={[256:512], [0:896]} | slice | bytes 917504 | tf_op jit(solution)/shard_map/slice | solution.py:368
  51.7 8.7 %own_block.1 = (f32[2,384,256]{2,1,0:T(8,128)}, f32[384,128]{1,0:T(8,128)}, f32[8,512]{1,0:T(8,128)}) custom-call(s32[2]{0:T(128)} %pad_add_fusion.place_ref, bf16[384,1792]{1,0:T(8,128)(2,1)} %refs_0_.5, bf16[384,1792]{1,0:T(8,128)(2,1)} %copy-done.1, bf16[384,896]{1,0:T(8,128)(2,1)} %collective-permute-done.3.refs_2_, bf16[512,896]{1,0:T(8,128)(2,1)} %refs_6_.1, ...), custom_call_target="tpu_custom_call" | custom-call | flops 1000 | bytes 1000 | tf_op jit(solution)/shard_map/own_block/pallas_call | solution.py:145
  60.5 5.4 %collective-permute-done.14.refs_17_.refs_18_ = bf16[512,896]{1,0:T(8,128)(2,1)} collective-permute-done((bf16[512,896]{1,0:T(8,128)(2,1)}, bf16[512,896]{1,0:T(8,128)(2,1)}, u32[]{:S(2)}, u32[]{:S(2)}) %collective-permute-start.14) | collective-permute-done | bytes 917536 | tf_op jit(solution)/shard_map/ppermute | solution.py:43
  65.9 0.5 collective-permute-done.13.refs_16_.refs_17_
  66.3 0.5 collective-permute-start.18
  66.9 2.2 %collective-permute-start.21 = (bf16[256,896]{1,0:T(8,128)(2,1)}, bf16[256,896]{1,0:T(8,128)(2,1)S(1)}, u32[]{:S(2)}, u32[]{:S(2)}) collective-permute-start(bf16[256,896]{1,0:T(8,128)(2,1)} %slice.108), channel_id=1, source_target_pairs={{0,24},{4,28},{8,16},{12,20},{16,8},{20,12},{24,0},{28,4},{1,25},{... | collective-permute-start | bytes 1376264 | tf_op jit(solution)/shard_map/ppermute | solution.py:43
  69.1 3.2 %collective-permute-start.20 = (bf16[256,896]{1,0:T(8,128)(2,1)S(1)}, bf16[256,896]{1,0:T(8,128)(2,1)S(1)}, u32[]{:S(2)}, u32[]{:S(2)}) collective-permute-start(bf16[256,896]{1,0:T(8,128)(2,1)S(1)} %copy-done.9), channel_id=1, source_target_pairs={{0,1},{1,0},{2,3},{3,2},{4,5},{5,4},{6,7},{7,6},{8,9},{9,8},{10,11... | collective-permute-start | bytes 1376264 | tf_op jit(solution)/shard_map/ppermute | solution.py:34
  72.2 0.9 copy-done.13
  73.6 11.2 %end_block.1 = (f32[2,384,256]{2,1,0:T(8,128)}, f32[2,384,256]{2,1,0:T(8,128)}, f32[384,128]{1,0:T(8,128)}, f32[8,512]{1,0:T(8,128)}) custom-call(s32[2]{0:T(128)} %pad_add_fusion.place_ref, f32[2,384,256]{2,1,0:T(8,128)} %get-tuple-element.52.cross_in, f32[384,128]{1,0:T(8,128)} %get-tuple-element.53.norm_in, bf16[384,1792]{1,0:T(8,128)(2,1)} %refs_0_.5, ...), custom_call_target="tpu_custom_call" | custom-call | flops 1000 | bytes 1000 | tf_op jit(solution)/shard_map/end_block/pallas_call | solution.py:145
  84.9 0.5 collective-permute-start.23
  85.4 1.3 collective-permute-done.22.refs_24_
  86.7 0.7 collective-permute-done.23.refs_25_
  87.4 0.7 copy-done.19
  88.1 9.2 %last_block.1 = (f32[384,1024]{1,0:T(8,128)}, f32[72,512]{1,0:T(8,128)}, f32[72,512]{1,0:T(8,128)}) custom-call(s32[2]{0:T(128)} %pad_add_fusion.place_ref, f32[2,384,256]{2,1,0:T(8,128)} %get-tuple-element.60.cross_own_in, f32[2,384,256]{2,1,0:T(8,128)} %get-tuple-element.61.cross_end_in, f32[384,128]{1,0:T(8,128)} %get-tuple-element.62.row_norm_in, ...), custom_call_target="tpu_custom_call" | custom-call | flops 1000 | bytes 1000 | tf_op jit(solution)/shard_map/last_block/pallas_call | solution.py:145
  97.5 1.4 collective-permute-done.24
  99.0 0.9 add.111
  99.9 1.0 collective-permute-start.27
  100.9 0.6 collective-permute-start.26
  101.5 2.0 %collective-permute-start.25 = (f32[72,512]{1,0:T(8,128)S(1)}, f32[72,512]{1,0:T(8,128)S(1)}, u32[]{:S(2)}, u32[]{:S(2)}) collective-permute-start(f32[72,512]{1,0:T(8,128)S(1)} %add.111), channel_id=1, source_target_pairs={{0,8},{4,12},{8,0},{12,4},{16,24},{20,28},{24,16},{28,20},{1,9},{5... | collective-permute-start | bytes 442376 | tf_op jit(solution)/shard_map/ppermute | solution.py:43
  103.5 4.1 %collective-permute-done.27 = f32[72,512]{1,0:T(8,128)S(1)} collective-permute-done((f32[72,512]{1,0:T(8,128)S(1)}, f32[72,512]{1,0:T(8,128)S(1)}, u32[]{:S(2)}, u32[]{:S(2)}) %collective-permute-start.27) | collective-permute-done | bytes 147488 | tf_op jit(solution)/shard_map/ppermute | solution.py:43
  107.6 2.1 %collective-permute-done.26 = f32[72,512]{1,0:T(8,128)S(1)} collective-permute-done((f32[72,512]{1,0:T(8,128)S(1)}, f32[72,512]{1,0:T(8,128)S(1)}, u32[]{:S(2)}, u32[]{:S(2)}) %collective-permute-start.26) | collective-permute-done | bytes 147488 | tf_op jit(solution)/shard_map/ppermute | solution.py:43
  109.8 1.3 collective-permute-done.28
  111.4 1.6 fusion.24
  113.2 1.2 collective-permute-done.29
  114.5 1.1 fusion.8
  115.9 1.2 collective-permute-done.30
  117.1 1.2 collective-permute-start.33
  118.3 0.6 collective-permute-start.32
  119.0 1.7 %collective-permute-start.31 = (f32[72,512]{1,0:T(8,128)S(1)}, f32[72,512]{1,0:T(8,128)S(1)}, u32[]{:S(2)}, u32[]{:S(2)}) collective-permute-start(f32[72,512]{1,0:T(8,128)S(1)} %select_add_fusion.1), channel_id=1, source_target_pairs={{0,8},{4,12},{8,0},{12,4},{16,24},{20,28},{24,16},{28,20},{1,9},{5... | collective-permute-start | bytes 442376 | tf_op jit(solution)/shard_map/ppermute | solution.py:43
  120.7 4.2 %collective-permute-done.33 = f32[72,512]{1,0:T(8,128)S(1)} collective-permute-done((f32[72,512]{1,0:T(8,128)S(1)}, f32[72,512]{1,0:T(8,128)S(1)}, u32[]{:S(2)}, u32[]{:S(2)}) %collective-permute-start.33) | collective-permute-done | bytes 147488 | tf_op jit(solution)/shard_map/ppermute | solution.py:43
  124.8 2.3 %collective-permute-done.32 = f32[72,512]{1,0:T(8,128)S(1)} collective-permute-done((f32[72,512]{1,0:T(8,128)S(1)}, f32[72,512]{1,0:T(8,128)S(1)}, u32[]{:S(2)}, u32[]{:S(2)}) %collective-permute-start.32) | collective-permute-done | bytes 147488 | tf_op jit(solution)/shard_map/ppermute | solution.py:43
  127.3 1.4 collective-permute-done.34
  128.9 1.6 fusion.21
  130.8 1.2 collective-permute-done.35
  132.0 1.1 fusion.11
  133.7 1.1 collective-permute-done.37
  134.8 1.2 collective-permute-start.40
  136.1 0.6 collective-permute-start.39
  136.7 1.7 %collective-permute-start.38 = (f32[72,512]{1,0:T(8,128)S(1)}, f32[72,512]{1,0:T(8,128)S(1)}, u32[]{:S(2)}, u32[]{:S(2)}) collective-permute-start(f32[72,512]{1,0:T(8,128)S(1)} %select_add_fusion), channel_id=1, source_target_pairs={{0,8},{4,12},{8,0},{12,4},{16,24},{20,28},{24,16},{28,20},{1,9},{5... | collective-permute-start | bytes 442376 | tf_op jit(solution)/shard_map/ppermute | solution.py:43
  138.5 9.2 %collective-permute-start.36 = (f32[200,512]{1,0:T(8,128)S(1)}, f32[200,512]{1,0:T(8,128)S(1)}, u32[]{:S(2)}, u32[]{:S(2)}) collective-permute-start(f32[200,512]{1,0:T(8,128)S(1)} %slice.145), channel_id=1, source_target_pairs={{0,1},{1,0},{2,3},{3,2},{4,5},{5,4},{6,7},{7,6},{8,9},{9,8},{10,11... | collective-permute-start | bytes 1228808 | tf_op jit(solution)/shard_map/ppermute | solution.py:34
  147.8 1.3 collective-permute-done.41
  149.2 6.3 %collective-permute-start.42 = (f32[72,512]{1,0:T(8,128)S(1)}, f32[72,512]{1,0:T(8,128)S(1)}, u32[]{:S(2)}, u32[]{:S(2)}) collective-permute-start(f32[72,512]{1,0:T(8,128)S(1)} %broadcast_select_fusion), channel_id=1, source_target_pairs={{0,1},{1,0},{2,3},{3,2},{4,5},{5,4},{6,7},{7,6},{8,9},{9,8},{10,11... | collective-permute-start | bytes 442376 | tf_op jit(solution)/shard_map/ppermute | solution.py:34
  155.5 1.1 collective-permute-done.36
  156.7 3.1 %collective-permute-done.42 = f32[72,512]{1,0:T(8,128)S(1)} collective-permute-done((f32[72,512]{1,0:T(8,128)S(1)}, f32[72,512]{1,0:T(8,128)S(1)}, u32[]{:S(2)}, u32[]{:S(2)}) %collective-permute-start.42) | collective-permute-done | bytes 147488 | tf_op jit(solution)/shard_map/ppermute | solution.py:34
  159.8 0.8 fusion.6
  (110 shorter events, 3.7 us)
Async XLA Ops:
  0.6 23.8 %collective-permute-start.2 = (bf16[512,896]{1,0:T(8,128)(2,1)}, bf16[512,896]{1,0:T(8,128)(2,1)}, u32[]{:S(2)}, u32[]{:S(2)}) collective-permute-start(bf16[512,896]{1,0:T(8,128)(2,1)} %refs_6_.1), channel_id=1, source_target_pairs={{0,1},{1,0},{2,3},{3,2},{4,5},{5,4},{6,7},{7,6},{8,9},{9,8},{10,11... | collective-permute-start | bytes 2752520 | tf_op jit(solution)/shard_map/ppermute | solution.py:34
  3.7 22.0 %collective-permute-start.1 = (bf16[512,896]{1,0:T(8,128)(2,1)}, bf16[512,896]{1,0:T(8,128)(2,1)S(1)}, u32[]{:S(2)}, u32[]{:S(2)}) collective-permute-start(bf16[512,896]{1,0:T(8,128)(2,1)} %refs_6_.1), channel_id=1, source_target_pairs={{0,16},{4,20},{8,24},{12,28},{16,0},{20,4},{24,8},{28,12},{1,17},{... | collective-permute-start | bytes 2752520 | tf_op jit(solution)/shard_map/ppermute | solution.py:43
  5.2 21.7 %collective-permute-start = (bf16[512,896]{1,0:T(8,128)(2,1)}, bf16[512,896]{1,0:T(8,128)(2,1)S(1)}, u32[]{:S(2)}, u32[]{:S(2)}) collective-permute-start(bf16[512,896]{1,0:T(8,128)(2,1)} %refs_6_.1), channel_id=1, source_target_pairs={{0,8},{4,12},{8,0},{12,4},{16,24},{20,28},{24,16},{28,20},{1,9},{5... | collective-permute-start | bytes 2752520 | tf_op jit(solution)/shard_map/ppermute | solution.py:43
  6.7 32.5 %collective-permute-start.4 = (bf16[384,1792]{1,0:T(8,128)(2,1)}, bf16[384,1792]{1,0:T(8,128)(2,1)S(1)}, u32[]{:S(2)}, u32[]{:S(2)}) collective-permute-start(bf16[384,1792]{1,0:T(8,128)(2,1)} %refs_0_.5), channel_id=1, source_target_pairs={{0,4},{1,2},{2,1},{3,7},{4,0},{5,6},{6,5},{7,3},{8,12},{9,10},{10,... | collective-permute-start | bytes 4128776 | tf_op jit(solution)/shard_map/ppermute | solution.py:39
  9.0 20.6 %copy-start.4 = (bf16[512,896]{1,0:T(8,128)(2,1)S(1)}, bf16[512,896]{1,0:T(8,128)(2,1)}, u32[]{:S(2)}) copy-start(bf16[512,896]{1,0:T(8,128)(2,1)} %refs_6_.1) | copy-start | bytes 2752516
  25.7 25.9 %copy-start.2 = (bf16[512,896]{1,0:T(8,128)(2,1)}, bf16[512,896]{1,0:T(8,128)(2,1)S(1)}, u32[]{:S(2)}) copy-start(bf16[512,896]{1,0:T(8,128)(2,1)S(1)} %collective-permute-done.1.refs_5_.refs_7_.refs_8_) | copy-start | bytes 2752516
  27.0 24.7 %copy-start.3 = (bf16[512,896]{1,0:T(8,128)(2,1)}, bf16[512,896]{1,0:T(8,128)(2,1)S(1)}, u32[]{:S(2)}) copy-start(bf16[512,896]{1,0:T(8,128)(2,1)S(1)} %collective-permute-done.refs_4_.refs_6_.refs_7_) | copy-start | bytes 2752516
  27.0 15.8 %collective-permute-start.3 = (bf16[384,896]{1,0:T(8,128)(2,1)S(1)}, bf16[384,896]{1,0:T(8,128)(2,1)}, u32[]{:S(2)}, u32[]{:S(2)}) collective-permute-start(bf16[384,896]{1,0:T(8,128)(2,1)S(1)} %get-tuple-element.43), channel_id=1, source_target_pairs={{0,1},{1,0},{2,3},{3,2},{4,5},{5,4},{6,7},{7,6},{8,9},{9,8},{10,11... | collective-permute-start | bytes 2064392 | tf_op jit(solution)/shard_map/ppermute | solution.py:34
  27.5 10.7 %collective-permute-start.5 = (bf16[256,896]{1,0:T(8,128)(2,1)S(1)}, bf16[256,896]{1,0:T(8,128)(2,1)S(1)}, u32[]{:S(2)}, u32[]{:S(2)}) collective-permute-start(bf16[256,896]{1,0:T(8,128)(2,1)S(1)} %slice.106), channel_id=1, source_target_pairs={{0,16},{4,20},{8,24},{12,28},{16,0},{20,4},{24,8},{28,12},{1,17},{... | collective-permute-start | bytes 1376264 | tf_op jit(solution)/shard_map/ppermute | solution.py:43
  28.0 10.7 %collective-permute-start.6 = (bf16[256,896]{1,0:T(8,128)(2,1)S(1)}, bf16[256,896]{1,0:T(8,128)(2,1)S(1)}, u32[]{:S(2)}, u32[]{:S(2)}) collective-permute-start(bf16[256,896]{1,0:T(8,128)(2,1)S(1)} %slice.107), channel_id=1, source_target_pairs={{0,8},{4,12},{8,0},{12,4},{16,24},{20,28},{24,16},{28,20},{1,9},{5... | collective-permute-start | bytes 1376264 | tf_op jit(solution)/shard_map/ppermute | solution.py:43
  29.6 15.5 %collective-permute-start.7 = (bf16[512,896]{1,0:T(8,128)(2,1)S(1)}, bf16[512,896]{1,0:T(8,128)(2,1)S(1)}, u32[]{:S(2)}, u32[]{:S(2)}) collective-permute-start(bf16[512,896]{1,0:T(8,128)(2,1)S(1)} %copy-done.4), channel_id=1, source_target_pairs={{0,4},{4,0},{8,12},{12,8},{16,20},{20,16},{24,28},{28,24},{1,5},{5... | collective-permute-start | bytes 2752520 | tf_op jit(solution)/shard_map/ppermute | solution.py:43
  38.2 10.2 %copy-start.8 = (bf16[256,896]{1,0:T(8,128)(2,1)}, bf16[256,896]{1,0:T(8,128)(2,1)S(1)}, u32[]{:S(2)}) copy-start(bf16[256,896]{1,0:T(8,128)(2,1)S(1)} %collective-permute-done.5.refs_6_.refs_8_.refs_9_) | copy-start | bytes 1376260
  38.7 9.6 %copy-start.10 = (bf16[256,896]{1,0:T(8,128)(2,1)}, bf16[256,896]{1,0:T(8,128)(2,1)S(1)}, u32[]{:S(2)}) copy-start(bf16[256,896]{1,0:T(8,128)(2,1)S(1)} %collective-permute-done.6.refs_7_.refs_9_.refs_10_) | copy-start | bytes 1376260
  38.7 4.1 %collective-permute-start.11 = (bf16[256,896]{1,0:T(8,128)(2,1)S(1)}, bf16[256,896]{1,0:T(8,128)(2,1)S(1)}, u32[]{:S(2)}, u32[]{:S(2)}) collective-permute-start(bf16[256,896]{1,0:T(8,128)(2,1)S(1)} %collective-permute-done.6.refs_7_.refs_9_.refs_10_), channel_id=1, source_target_pairs={{0,4},{4,0},{8,12},{12,8},{16,20},{20,16},{24,28},{28,24},{1,5},{5... | collective-permute-start | bytes 1376264 | tf_op jit(solution)/shard_map/ppermute | solution.py:43
  38.7 4.9 %collective-permute-start.10 = (bf16[256,896]{1,0:T(8,128)(2,1)S(1)}, bf16[256,896]{1,0:T(8,128)(2,1)S(1)}, u32[]{:S(2)}, u32[]{:S(2)}) collective-permute-start(bf16[256,896]{1,0:T(8,128)(2,1)S(1)} %collective-permute-done.5.refs_6_.refs_8_.refs_9_), channel_id=1, source_target_pairs={{0,4},{4,0},{8,12},{12,8},{16,20},{20,16},{24,28},{28,24},{1,5},{5... | collective-permute-start | bytes 1376264 | tf_op jit(solution)/shard_map/ppermute | solution.py:43
  39.2 12.5 %copy-start.1 = (bf16[384,1792]{1,0:T(8,128)(2,1)}, bf16[384,1792]{1,0:T(8,128)(2,1)S(1)}, u32[]{:S(2)}) copy-start(bf16[384,1792]{1,0:T(8,128)(2,1)S(1)} %collective-permute-done.4.refs_1_) | copy-start | bytes 4128772
  39.2 5.9 %collective-permute-start.9 = (bf16[512,896]{1,0:T(8,128)(2,1)S(1)}, bf16[512,896]{1,0:T(8,128)(2,1)S(1)}, u32[]{:S(2)}, u32[]{:S(2)}) collective-permute-start(bf16[512,896]{1,0:T(8,128)(2,1)S(1)} %collective-permute-done.1.refs_5_.refs_7_.refs_8_), channel_id=1, source_target_pairs={{0,4},{4,0},{8,12},{12,8},{16,20},{20,16},{24,28},{28,24},{1,5},{5... | collective-permute-start | bytes 2752520 | tf_op jit(solution)/shard_map/ppermute | solution.py:43
  42.8 5.5 %collective-permute-start.8 = (bf16[512,896]{1,0:T(8,128)(2,1)S(1)}, bf16[512,896]{1,0:T(8,128)(2,1)S(1)}, u32[]{:S(2)}, u32[]{:S(2)}) collective-permute-start(bf16[512,896]{1,0:T(8,128)(2,1)S(1)} %collective-permute-done.refs_4_.refs_6_.refs_7_), channel_id=1, source_target_pairs={{0,4},{4,0},{8,12},{12,8},{16,20},{20,16},{24,28},{28,24},{1,5},{5... | collective-permute-start | bytes 2752520 | tf_op jit(solution)/shard_map/ppermute | solution.py:43
  42.8 5.6 %copy-start.11 = (bf16[256,896]{1,0:T(8,128)(2,1)}, bf16[256,896]{1,0:T(8,128)(2,1)S(1)}, u32[]{:S(2)}) copy-start(bf16[256,896]{1,0:T(8,128)(2,1)S(1)} %collective-permute-done.11.refs_12_.refs_14_.refs_15_) | copy-start | bytes 1376260
  42.8 23.1 %collective-permute-start.14 = (bf16[512,896]{1,0:T(8,128)(2,1)}, bf16[512,896]{1,0:T(8,128)(2,1)}, u32[]{:S(2)}, u32[]{:S(2)}) collective-permute-start(bf16[512,896]{1,0:T(8,128)(2,1)} %collective-permute-done.2.refs_15_.refs_16_), channel_id=1, source_target_pairs={{0,16},{4,20},{8,24},{12,28},{16,0},{20,4},{24,8},{28,12},{1,17},{... | collective-permute-start | bytes 2752520 | tf_op jit(solution)/shard_map/ppermute | solution.py:43
  43.6 4.8 %copy-start.12 = (bf16[256,896]{1,0:T(8,128)(2,1)}, bf16[256,896]{1,0:T(8,128)(2,1)S(1)}, u32[]{:S(2)}) copy-start(bf16[256,896]{1,0:T(8,128)(2,1)S(1)} %collective-permute-done.10.refs_11_.refs_13_.refs_14_) | copy-start | bytes 1376260
  43.6 22.7 %collective-permute-start.13 = (bf16[512,896]{1,0:T(8,128)(2,1)}, bf16[512,896]{1,0:T(8,128)(2,1)}, u32[]{:S(2)}, u32[]{:S(2)}) collective-permute-start(bf16[512,896]{1,0:T(8,128)(2,1)} %collective-permute-done.2.refs_15_.refs_16_), channel_id=1, source_target_pairs={{0,8},{4,12},{8,0},{12,4},{16,24},{20,28},{24,16},{28,20},{1,9},{5... | collective-permute-start | bytes 2752520 | tf_op jit(solution)/shard_map/ppermute | solution.py:43
  45.1 3.2 %copy-start.5 = (bf16[512,896]{1,0:T(8,128)(2,1)}, bf16[512,896]{1,0:T(8,128)(2,1)S(1)}, u32[]{:S(2)}) copy-start(bf16[512,896]{1,0:T(8,128)(2,1)S(1)} %collective-permute-done.7.refs_8_.refs_10_.refs_11_) | copy-start | bytes 2752516
  45.1 21.2 %collective-permute-start.15 = (bf16[384,896]{1,0:T(8,128)(2,1)}, bf16[384,896]{1,0:T(8,128)(2,1)}, u32[]{:S(2)}, u32[]{:S(2)}) collective-permute-start(bf16[384,896]{1,0:T(8,128)(2,1)} %collective-permute-done.3.refs_2_), channel_id=1, source_target_pairs={{0,4},{1,2},{2,1},{3,7},{4,0},{5,6},{6,5},{7,3},{8,12},{9,10},{10,... | collective-permute-start | bytes 2064392 | tf_op jit(solution)/shard_map/ppermute | solution.py:39
  45.1 3.3 %copy-start.6 = (bf16[512,896]{1,0:T(8,128)(2,1)}, bf16[512,896]{1,0:T(8,128)(2,1)S(1)}, u32[]{:S(2)}) copy-start(bf16[512,896]{1,0:T(8,128)(2,1)S(1)} %collective-permute-done.9.refs_10_.refs_12_.refs_13_) | copy-start | bytes 2752516
  45.1 21.7 %collective-permute-start.12 = (bf16[384,896]{1,0:T(8,128)(2,1)}, bf16[384,896]{1,0:T(8,128)(2,1)}, u32[]{:S(2)}, u32[]{:S(2)}) collective-permute-start(bf16[384,896]{1,0:T(8,128)(2,1)} %get-tuple-element.54), channel_id=1, source_target_pairs={{0,1},{1,0},{2,3},{3,2},{4,5},{5,4},{6,7},{7,6},{8,9},{9,8},{10,11... | collective-permute-start | bytes 2064392 | tf_op jit(solution)/shard_map/ppermute | solution.py:34
  48.3 0.9 copy-start.7
  48.3 20.8 %collective-permute-start.16 = (bf16[512,896]{1,0:T(8,128)(2,1)}, bf16[512,896]{1,0:T(8,128)(2,1)}, u32[]{:S(2)}, u32[]{:S(2)}) collective-permute-start(bf16[512,896]{1,0:T(8,128)(2,1)} %collective-permute-done.2.refs_15_.refs_16_), channel_id=1, source_target_pairs={{0,4},{4,0},{8,12},{12,8},{16,20},{20,16},{24,28},{28,24},{1,5},{5... | collective-permute-start | bytes 2752520 | tf_op jit(solution)/shard_map/ppermute | solution.py:43
  51.7 17.4 %copy-start.9 = (bf16[256,896]{1,0:T(8,128)(2,1)S(1)}, bf16[256,896]{1,0:T(8,128)(2,1)}, u32[]{:S(2)}) copy-start(bf16[256,896]{1,0:T(8,128)(2,1)} %copy-done.8) | copy-start | bytes 1376260
  66.3 5.9 %collective-permute-start.17 = (bf16[512,896]{1,0:T(8,128)(2,1)}, bf16[512,896]{1,0:T(8,128)(2,1)S(1)}, u32[]{:S(2)}, u32[]{:S(2)}) collective-permute-start(bf16[512,896]{1,0:T(8,128)(2,1)} %collective-permute-done.13.refs_16_.refs_17_), channel_id=1, source_target_pairs={{0,4},{4,0},{8,12},{12,8},{16,20},{20,16},{24,28},{28,24},{1,5},{5... | collective-permute-start | bytes 2752520 | tf_op jit(solution)/shard_map/ppermute | solution.py:43
  66.3 5.9 %collective-permute-start.18 = (bf16[512,896]{1,0:T(8,128)(2,1)}, bf16[512,896]{1,0:T(8,128)(2,1)S(1)}, u32[]{:S(2)}, u32[]{:S(2)}) collective-permute-start(bf16[512,896]{1,0:T(8,128)(2,1)} %collective-permute-done.14.refs_17_.refs_18_), channel_id=1, source_target_pairs={{0,4},{4,0},{8,12},{12,8},{16,20},{20,16},{24,28},{28,24},{1,5},{5... | collective-permute-start | bytes 2752520 | tf_op jit(solution)/shard_map/ppermute | solution.py:43
  66.9 17.9 %collective-permute-start.19 = (bf16[384,896]{1,0:T(8,128)(2,1)}, bf16[384,896]{1,0:T(8,128)(2,1)S(1)}, u32[]{:S(2)}, u32[]{:S(2)}) collective-permute-start(bf16[384,896]{1,0:T(8,128)(2,1)} %collective-permute-done.12.refs_3_), channel_id=1, source_target_pairs={{0,4},{1,2},{2,1},{3,7},{4,0},{5,6},{6,5},{7,3},{8,12},{9,10},{10,... | collective-permute-start | bytes 2064392 | tf_op jit(solution)/shard_map/ppermute | solution.py:39
  66.9 17.9 %collective-permute-start.21 = (bf16[256,896]{1,0:T(8,128)(2,1)}, bf16[256,896]{1,0:T(8,128)(2,1)S(1)}, u32[]{:S(2)}, u32[]{:S(2)}) collective-permute-start(bf16[256,896]{1,0:T(8,128)(2,1)} %slice.108), channel_id=1, source_target_pairs={{0,24},{4,28},{8,16},{12,20},{16,8},{20,12},{24,0},{28,4},{1,25},{... | collective-permute-start | bytes 1376264 | tf_op jit(solution)/shard_map/ppermute | solution.py:43
  69.1 15.7 %collective-permute-start.20 = (bf16[256,896]{1,0:T(8,128)(2,1)S(1)}, bf16[256,896]{1,0:T(8,128)(2,1)S(1)}, u32[]{:S(2)}, u32[]{:S(2)}) collective-permute-start(bf16[256,896]{1,0:T(8,128)(2,1)S(1)} %copy-done.9), channel_id=1, source_target_pairs={{0,1},{1,0},{2,3},{3,2},{4,5},{5,4},{6,7},{7,6},{8,9},{9,8},{10,11... | collective-permute-start | bytes 1376264 | tf_op jit(solution)/shard_map/ppermute | solution.py:34
  72.2 0.9 copy-start.13
  72.2 1.3 copy-start.14
  84.7 2.6 %copy-start.16 = (bf16[256,896]{1,0:T(8,128)(2,1)}, bf16[256,896]{1,0:T(8,128)(2,1)S(1)}, u32[]{:S(2)}) copy-start(bf16[256,896]{1,0:T(8,128)(2,1)S(1)} %collective-permute-done.21.refs_23_) | copy-start | bytes 1376260
  84.7 2.6 %copy-start.15 = (bf16[384,896]{1,0:T(8,128)(2,1)}, bf16[384,896]{1,0:T(8,128)(2,1)S(1)}, u32[]{:S(2)}) copy-start(bf16[384,896]{1,0:T(8,128)(2,1)S(1)} %collective-permute-done.19.refs_5_) | copy-start | bytes 2064388
  84.8 2.6 %copy-start.17 = (bf16[256,896]{1,0:T(8,128)(2,1)}, bf16[256,896]{1,0:T(8,128)(2,1)S(1)}, u32[]{:S(2)}) copy-start(bf16[256,896]{1,0:T(8,128)(2,1)S(1)} %collective-permute-done.20.refs_22_) | copy-start | bytes 1376260
  84.8 1.9 %collective-permute-start.22 = (bf16[256,896]{1,0:T(8,128)(2,1)S(1)}, bf16[256,896]{1,0:T(8,128)(2,1)S(1)}, u32[]{:S(2)}, u32[]{:S(2)}) collective-permute-start(bf16[256,896]{1,0:T(8,128)(2,1)S(1)} %collective-permute-done.20.refs_22_), channel_id=1, source_target_pairs={{0,4},{4,0},{8,12},{12,8},{16,20},{20,16},{24,28},{28,24},{1,5},{5... | collective-permute-start | bytes 1376264 | tf_op jit(solution)/shard_map/ppermute | solution.py:43
  84.9 2.5 %collective-permute-start.23 = (bf16[256,896]{1,0:T(8,128)(2,1)S(1)}, bf16[256,896]{1,0:T(8,128)(2,1)S(1)}, u32[]{:S(2)}, u32[]{:S(2)}) collective-permute-start(bf16[256,896]{1,0:T(8,128)(2,1)S(1)} %collective-permute-done.21.refs_23_), channel_id=1, source_target_pairs={{0,4},{4,0},{8,12},{12,8},{16,20},{20,16},{24,28},{28,24},{1,5},{5... | collective-permute-start | bytes 1376264 | tf_op jit(solution)/shard_map/ppermute | solution.py:43
  86.7 0.8 copy-start.18
  87.3 0.8 copy-start.19
  97.3 14.1 %copy-start = (f32[384,1024]{1,0:T(8,128)S(1)}, f32[384,1024]{1,0:T(8,128)}, u32[]{:S(2)}) copy-start(f32[384,1024]{1,0:T(8,128)} %get-tuple-element.71) | copy-start | bytes 4718596
  97.3 1.6 %collective-permute-start.24 = (f32[72,512]{1,0:T(8,128)}, f32[72,512]{1,0:T(8,128)S(1)}, u32[]{:S(2)}, u32[]{:S(2)}) collective-permute-start(f32[72,512]{1,0:T(8,128)} %get-tuple-element.70), channel_id=1, source_target_pairs={{0,4},{4,0},{8,12},{12,8},{16,20},{20,16},{24,28},{28,24},{1,5},{5... | collective-permute-start | bytes 442376 | tf_op jit(solution)/shard_map/ppermute | solution.py:43
  99.9 7.7 %collective-permute-start.27 = (f32[72,512]{1,0:T(8,128)S(1)}, f32[72,512]{1,0:T(8,128)S(1)}, u32[]{:S(2)}, u32[]{:S(2)}) collective-permute-start(f32[72,512]{1,0:T(8,128)S(1)} %add.111), channel_id=1, source_target_pairs={{0,24},{4,28},{8,16},{12,20},{16,8},{20,12},{24,0},{28,4},{1,25},{... | collective-permute-start | bytes 442376 | tf_op jit(solution)/shard_map/ppermute | solution.py:43
  100.9 8.8 %collective-permute-start.26 = (f32[72,512]{1,0:T(8,128)S(1)}, f32[72,512]{1,0:T(8,128)S(1)}, u32[]{:S(2)}, u32[]{:S(2)}) collective-permute-start(f32[72,512]{1,0:T(8,128)S(1)} %add.111), channel_id=1, source_target_pairs={{0,16},{4,20},{8,24},{12,28},{16,0},{20,4},{24,8},{28,12},{1,17},{... | collective-permute-start | bytes 442376 | tf_op jit(solution)/shard_map/ppermute | solution.py:43
  101.5 8.2 %collective-permute-start.25 = (f32[72,512]{1,0:T(8,128)S(1)}, f32[72,512]{1,0:T(8,128)S(1)}, u32[]{:S(2)}, u32[]{:S(2)}) collective-permute-start(f32[72,512]{1,0:T(8,128)S(1)} %add.111), channel_id=1, source_target_pairs={{0,8},{4,12},{8,0},{12,4},{16,24},{20,28},{24,16},{28,20},{1,9},{5... | collective-permute-start | bytes 442376 | tf_op jit(solution)/shard_map/ppermute | solution.py:43
  109.7 1.4 collective-permute-start.28
  113.0 1.4 collective-permute-start.29
  115.6 1.4 collective-permute-start.30
  117.1 7.7 %collective-permute-start.33 = (f32[72,512]{1,0:T(8,128)S(1)}, f32[72,512]{1,0:T(8,128)S(1)}, u32[]{:S(2)}, u32[]{:S(2)}) collective-permute-start(f32[72,512]{1,0:T(8,128)S(1)} %select_add_fusion.1), channel_id=1, source_target_pairs={{0,24},{4,28},{8,16},{12,20},{16,8},{20,12},{24,0},{28,4},{1,25},{... | collective-permute-start | bytes 442376 | tf_op jit(solution)/shard_map/ppermute | solution.py:43
  118.3 8.8 %collective-permute-start.32 = (f32[72,512]{1,0:T(8,128)S(1)}, f32[72,512]{1,0:T(8,128)S(1)}, u32[]{:S(2)}, u32[]{:S(2)}) collective-permute-start(f32[72,512]{1,0:T(8,128)S(1)} %select_add_fusion.1), channel_id=1, source_target_pairs={{0,16},{4,20},{8,24},{12,28},{16,0},{20,4},{24,8},{28,12},{1,17},{... | collective-permute-start | bytes 442376 | tf_op jit(solution)/shard_map/ppermute | solution.py:43
  119.0 8.2 %collective-permute-start.31 = (f32[72,512]{1,0:T(8,128)S(1)}, f32[72,512]{1,0:T(8,128)S(1)}, u32[]{:S(2)}, u32[]{:S(2)}) collective-permute-start(f32[72,512]{1,0:T(8,128)S(1)} %select_add_fusion.1), channel_id=1, source_target_pairs={{0,8},{4,12},{8,0},{12,4},{16,24},{20,28},{24,16},{28,20},{1,9},{5... | collective-permute-start | bytes 442376 | tf_op jit(solution)/shard_map/ppermute | solution.py:43
  127.2 1.4 collective-permute-start.34
  130.6 1.4 collective-permute-start.35
  133.4 1.4 collective-permute-start.37
  134.8 12.9 %collective-permute-start.40 = (f32[72,512]{1,0:T(8,128)S(1)}, f32[72,512]{1,0:T(8,128)S(1)}, u32[]{:S(2)}, u32[]{:S(2)}) collective-permute-start(f32[72,512]{1,0:T(8,128)S(1)} %select_add_fusion), channel_id=1, source_target_pairs={{0,24},{4,28},{8,16},{12,20},{16,8},{20,12},{24,0},{28,4},{1,25},{... | collective-permute-start | bytes 442376 | tf_op jit(solution)/shard_map/ppermute | solution.py:43
  136.1 11.6 %collective-permute-start.39 = (f32[72,512]{1,0:T(8,128)S(1)}, f32[72,512]{1,0:T(8,128)S(1)}, u32[]{:S(2)}, u32[]{:S(2)}) collective-permute-start(f32[72,512]{1,0:T(8,128)S(1)} %select_add_fusion), channel_id=1, source_target_pairs={{0,16},{4,20},{8,24},{12,28},{16,0},{20,4},{24,8},{28,12},{1,17},{... | collective-permute-start | bytes 442376 | tf_op jit(solution)/shard_map/ppermute | solution.py:43
  136.7 11.0 %collective-permute-start.38 = (f32[72,512]{1,0:T(8,128)S(1)}, f32[72,512]{1,0:T(8,128)S(1)}, u32[]{:S(2)}, u32[]{:S(2)}) collective-permute-start(f32[72,512]{1,0:T(8,128)S(1)} %select_add_fusion), channel_id=1, source_target_pairs={{0,8},{4,12},{8,0},{12,4},{16,24},{20,28},{24,16},{28,20},{1,9},{5... | collective-permute-start | bytes 442376 | tf_op jit(solution)/shard_map/ppermute | solution.py:43
  138.5 18.1 %collective-permute-start.36 = (f32[200,512]{1,0:T(8,128)S(1)}, f32[200,512]{1,0:T(8,128)S(1)}, u32[]{:S(2)}, u32[]{:S(2)}) collective-permute-start(f32[200,512]{1,0:T(8,128)S(1)} %slice.145), channel_id=1, source_target_pairs={{0,1},{1,0},{2,3},{3,2},{4,5},{5,4},{6,7},{7,6},{8,9},{9,8},{10,11... | collective-permute-start | bytes 1228808 | tf_op jit(solution)/shard_map/ppermute | solution.py:34
  147.8 1.4 collective-permute-start.41
  149.2 10.6 %collective-permute-start.42 = (f32[72,512]{1,0:T(8,128)S(1)}, f32[72,512]{1,0:T(8,128)S(1)}, u32[]{:S(2)}, u32[]{:S(2)}) collective-permute-start(f32[72,512]{1,0:T(8,128)S(1)} %broadcast_select_fusion), channel_id=1, source_target_pairs={{0,1},{1,0},{2,3},{3,2},{4,5},{5,4},{6,7},{7,6},{8,9},{9,8},{10,11... | collective-permute-start | bytes 442376 | tf_op jit(solution)/shard_map/ppermute | solution.py:34

commit v7 on v6

--- a/solution.py
+++ b/solution.py
@@ -418,7 +418,7 @@
         last = packed(times(image, kernel, (1, 0)), jnp.sum(image * image, axis=1))
         if settle is not None and iteration == ITERS - 1:
             state, finish = settle((coefficient, residual, direction), packed_twice((inner, lam * length), last.shape[1]))
-            sums = finish(sum_rows(last.at[count:].set(packed_twice((jnp.sum(image * image, axis=1),), last.shape[1]))))
+            sums = finish(last.at[count:].set(packed_twice((jnp.sum(image * image, axis=1),), last.shape[1])))
             coefficient, residual, direction = (state[i * count : (i + 1) * count] for i in range(3))
             inner, ridge = state[3 * count, :count], state[3 * count + 1, :count]
         else:
@@ -440,14 +440,24 @@
 def settled(state, vectors):
     z = lax.axis_index("landmark")
     middle = (z == 1) | (z == 2)
-    whole = jnp.concatenate([*state, vectors], axis=0)
-    half = whole.shape[1] // 2
-    taken = jnp.where(middle, whole[:, :half], handed(whole[:, half:]))
-
-    def finish(sums):
-        return jnp.where(middle, sums[:, :half], handed(sums[:, half:]))
-
-    return taken, finish
+    odd = lax.axis_index("proof") % 2 == 1
+    half = vectors.shape[1] // 2
+
+    def taken(*blocks):
+        whole = jnp.concatenate(blocks, axis=0)
+        return jnp.where(middle, whole[:, :half], handed(whole[:, half:]))
+
+    def finish(block):
+        low, high, end_low, end_high = (block[:, i * half // 2 : (i + 1) * half // 2] for i in range(4))
+        mine, other = jnp.where(odd, high, low), jnp.where(odd, low, high)
+        end_mine, end_other = jnp.where(odd, end_high, end_low), jnp.where(odd, end_low, end_high)
+        both = jnp.concatenate([mine, end_mine], axis=1) + flipped(jnp.concatenate([other, end_other], axis=1), 1)
+        work = jnp.where(middle, both[:, : half // 2], handed(both[:, half // 2 :]))
+        work = work + flipped(work, 2) + flipped(work, 4) + flipped(work, 6)
+        other = flipped(work, 1)
+        return jnp.concatenate([jnp.where(odd, other, work), jnp.where(odd, work, other)], axis=1)
+
+    return jnp.concatenate([taken(*state[:2]), taken(state[2], vectors)], axis=0), finish
 
 
 def folded(row_features, landmark_features, targets):

time: 161 us -> 156 us (0.969)
  starting transfers between devices: 48.6 us -> 42.2 us
    ppermute x32, waiting for transfers between devices: 40.1 us -> 59.3 us  [flipped(): return lax.ppermute(block, 'proof', [(i, i ^ bits) for i in range(8)])]
    ppermute x6 -> x7, waiting for transfers between devices: 23.1 us -> 6.48 us  [handed(): return lax.ppermute(block, 'landmark', NEIGHBOURS)]
    ppermute x6 -> x7, starting transfers between devices: 25.3 us -> 20.2 us  [handed(): return lax.ppermute(block, 'landmark', NEIGHBOURS)]
  transfers between devices with their start and end apart: 43 -> 44, of which waited for: 24 -> 26; matrix products, arithmetic and copies ran while one was open for 3% -> 4% of each run, Pallas kernels for 12% -> 13%
where the time goes in v7:
time: 156 us
  waiting for transfers between devices  67 us (43%)
  starting transfers between devices  42.2 us (27%)
  Pallas kernels  29.1 us (19%)
  local copies, waits for them, and re-layouts  7.21 us (5%)
  matrix products  5.35 us (3%)
  other arithmetic  3.75 us (2%)
    ppermute x32, waiting for transfers between devices, flipped(): return lax.ppermute(block, 'proof', [(i, i ^ bits) for i in range(8)])  59.3 us
    pallas_call x3, Pallas kernels, call(): pl.pallas_call(body, out_shape=tuple((jax.ShapeDtypeStruct(shape, jnp.flo...  29.1 us
    ppermute x32, starting transfers between devices, flipped(): return lax.ppermute(block, 'proof', [(i, i ^ bits) for i in range(8)])  21.6 us
    ppermute x7, starting transfers between devices, handed(): return lax.ppermute(block, 'landmark', NEIGHBOURS)  20.2 us
    ppermute x7, waiting for transfers between devices, handed(): return lax.ppermute(block, 'landmark', NEIGHBOURS)  6.48 us
    dot_general x4, matrix products, times(): lax.dot_general(left, right, ((contract[:1], contract[1:]), ((), ())), pr...  5.35 us
  transfers between devices with their start and end apart: 44, of which 26 were waited for; matrix products, arithmetic and copies ran while one was open for 4% of the time, Pallas kernels for 13%

profile of v7, /device:TPU:0, one launch (start us, length us, event | category | flops | bytes accessed | tf_op | source)
XLA Modules:
  0.0 155.8 jit_solution(4536334610623126153)
XLA Ops:
  0.6 3.0 %collective-permute-start = (bf16[512,896]{1,0:T(8,128)(2,1)}, bf16[512,896]{1,0:T(8,128)(2,1)S(1)}, u32[]{:S(2)}, u32[]{:S(2)}) collective-permute-start(bf16[512,896]{1,0:T(8,128)(2,1)} %refs_6_.1), channel_id=1, source_target_pairs={{0,8},{4,12},{8,0},{12,4},{16,24},{20,28},{24,16},{28,20},{1,9},{5... | collective-permute-start | bytes 2752520 | tf_op jit(solution)/shard_map/ppermute | solution.py:43
  3.6 1.5 collective-permute-start.1
  5.2 1.6 %collective-permute-start.2 = (bf16[512,896]{1,0:T(8,128)(2,1)}, bf16[512,896]{1,0:T(8,128)(2,1)}, u32[]{:S(2)}, u32[]{:S(2)}) collective-permute-start(bf16[512,896]{1,0:T(8,128)(2,1)} %refs_6_.1), channel_id=1, source_target_pairs={{0,1},{1,0},{2,3},{3,2},{4,5},{5,4},{6,7},{7,6},{8,9},{9,8},{10,11... | collective-permute-start | bytes 2752520 | tf_op jit(solution)/shard_map/ppermute | solution.py:34
  6.7 2.3 %fusion.26 = (bf16[384,896]{1,0:T(8,128)(2,1)}, bf16[384,896]{1,0:T(8,128)(2,1)S(1)}) fusion(bf16[384,1792]{1,0:T(8,128)(2,1)} %refs_0_.5), kind=kLoop, calls=%fused_computation.87 | loop fusion | bytes 2752512 | tf_op jit(solution)/shard_map/slice | solution.py:357
  9.0 15.2 %collective-permute-done.refs_4_.refs_6_.refs_7_ = bf16[512,896]{1,0:T(8,128)(2,1)S(1)} collective-permute-done((bf16[512,896]{1,0:T(8,128)(2,1)}, bf16[512,896]{1,0:T(8,128)(2,1)S(1)}, u32[]{:S(2)}, u32[]{:S(2)}) %collective-permute-start) | collective-permute-done | bytes 917536 | tf_op jit(solution)/shard_map/ppermute | solution.py:43
  24.2 1.5 collective-permute-done.1.refs_5_.refs_7_.refs_8_
  25.7 1.3 collective-permute-done.2.refs_15_.refs_16_
  27.0 1.6 %collective-permute-start.3 = (bf16[384,896]{1,0:T(8,128)(2,1)S(1)}, bf16[384,896]{1,0:T(8,128)(2,1)}, u32[]{:S(2)}, u32[]{:S(2)}) collective-permute-start(bf16[384,896]{1,0:T(8,128)(2,1)S(1)} %get-tuple-element.43), channel_id=1, source_target_pairs={{0,1},{1,0},{2,3},{3,2},{4,5},{5,4},{6,7},{7,6},{8,9},{9,8},{10,11... | collective-permute-start | bytes 2064392 | tf_op jit(solution)/shard_map/ppermute | solution.py:34
  28.6 0.6 collective-permute-start.5
  29.2 0.6 collective-permute-start.6
  29.8 9.3 %collective-permute-done.5.refs_6_.refs_8_.refs_9_ = bf16[256,896]{1,0:T(8,128)(2,1)S(1)} collective-permute-done((bf16[256,896]{1,0:T(8,128)(2,1)S(1)}, bf16[256,896]{1,0:T(8,128)(2,1)S(1)}, u32[]{:S(2)}, u32[]{:S(2)}) %collective-permute-start.5) | collective-permute-done | bytes 458784 | tf_op jit(solution)/shard_map/ppermute | solution.py:43
  39.2 0.4 collective-permute-done.6.refs_7_.refs_9_.refs_10_
  39.6 0.5 collective-permute-start.11
  40.2 2.6 %collective-permute-done.3.refs_2_ = bf16[384,896]{1,0:T(8,128)(2,1)} collective-permute-done((bf16[384,896]{1,0:T(8,128)(2,1)S(1)}, bf16[384,896]{1,0:T(8,128)(2,1)}, u32[]{:S(2)}, u32[]{:S(2)}) %collective-permute-start.3) | collective-permute-done | bytes 688160 | tf_op jit(solution)/shard_map/ppermute | solution.py:34
  42.8 0.6 collective-permute-start.13
  43.4 0.7 collective-permute-start.14
  44.2 3.1 %collective-permute-start.12 = (bf16[384,896]{1,0:T(8,128)(2,1)}, bf16[384,896]{1,0:T(8,128)(2,1)}, u32[]{:S(2)}, u32[]{:S(2)}) collective-permute-start(bf16[384,896]{1,0:T(8,128)(2,1)} %get-tuple-element.54), channel_id=1, source_target_pairs={{0,1},{1,0},{2,3},{3,2},{4,5},{5,4},{6,7},{7,6},{8,9},{9,8},{10,11... | collective-permute-start | bytes 2064392 | tf_op jit(solution)/shard_map/ppermute | solution.py:34
  47.4 0.9 copy-done.7
  48.3 0.7 pad_add_fusion.place_ref
  49.0 1.8 %slice.126 = bf16[256,896]{1,0:T(8,128)(2,1)} slice(bf16[512,896]{1,0:T(8,128)(2,1)} %collective-permute-done.2.refs_15_.refs_16_), slice={[256:512], [0:896]} | slice | bytes 917504 | tf_op jit(solution)/shard_map/slice | solution.py:368
  50.8 8.8 %own_block.1 = (f32[2,384,256]{2,1,0:T(8,128)}, f32[384,128]{1,0:T(8,128)}, f32[8,512]{1,0:T(8,128)}) custom-call(s32[2]{0:T(128)} %pad_add_fusion.place_ref, bf16[384,1792]{1,0:T(8,128)(2,1)} %refs_0_.5, bf16[384,1792]{1,0:T(8,128)(2,1)} %copy-done.1, bf16[384,896]{1,0:T(8,128)(2,1)} %collective-permute-done.3.refs_2_, bf16[512,896]{1,0:T(8,128)(2,1)} %refs_6_.1, ...), custom_call_target="tpu_custom_call" | custom-call | flops 1000 | bytes 1000 | tf_op jit(solution)/shard_map/own_block/pallas_call | solution.py:145
  59.6 6.3 %collective-permute-done.13.refs_16_.refs_17_ = bf16[512,896]{1,0:T(8,128)(2,1)} collective-permute-done((bf16[512,896]{1,0:T(8,128)(2,1)}, bf16[512,896]{1,0:T(8,128)(2,1)}, u32[]{:S(2)}, u32[]{:S(2)}) %collective-permute-start.13) | collective-permute-done | bytes 917536 | tf_op jit(solution)/shard_map/ppermute | solution.py:43
  66.1 0.5 collective-permute-start.18
  66.7 1.5 collective-permute-start.21
  68.2 3.2 %collective-permute-start.20 = (bf16[256,896]{1,0:T(8,128)(2,1)S(1)}, bf16[256,896]{1,0:T(8,128)(2,1)S(1)}, u32[]{:S(2)}, u32[]{:S(2)}) collective-permute-start(bf16[256,896]{1,0:T(8,128)(2,1)S(1)} %copy-done.9), channel_id=1, source_target_pairs={{0,1},{1,0},{2,3},{3,2},{4,5},{5,4},{6,7},{7,6},{8,9},{9,8},{10,11... | collective-permute-start | bytes 1376264 | tf_op jit(solution)/shard_map/ppermute | solution.py:34
  71.4 0.9 copy-done.13
  72.7 11.1 %end_block.1 = (f32[2,384,256]{2,1,0:T(8,128)}, f32[2,384,256]{2,1,0:T(8,128)}, f32[384,128]{1,0:T(8,128)}, f32[8,512]{1,0:T(8,128)}) custom-call(s32[2]{0:T(128)} %pad_add_fusion.place_ref, f32[2,384,256]{2,1,0:T(8,128)} %get-tuple-element.52.cross_in, f32[384,128]{1,0:T(8,128)} %get-tuple-element.53.norm_in, bf16[384,1792]{1,0:T(8,128)(2,1)} %refs_0_.5, ...), custom_call_target="tpu_custom_call" | custom-call | flops 1000 | bytes 1000 | tf_op jit(solution)/shard_map/end_block/pallas_call | solution.py:145
  84.0 0.5 collective-permute-start.22
  84.4 1.3 collective-permute-done.23.refs_25_
  85.7 0.7 collective-permute-done.22.refs_24_
  86.5 0.6 copy-done.19
  87.2 9.2 %last_block.1 = (f32[384,1024]{1,0:T(8,128)}, f32[72,512]{1,0:T(8,128)}, f32[72,512]{1,0:T(8,128)}) custom-call(s32[2]{0:T(128)} %pad_add_fusion.place_ref, f32[2,384,256]{2,1,0:T(8,128)} %get-tuple-element.60.cross_own_in, f32[2,384,256]{2,1,0:T(8,128)} %get-tuple-element.61.cross_end_in, f32[384,128]{1,0:T(8,128)} %get-tuple-element.62.row_norm_in, ...), custom_call_target="tpu_custom_call" | custom-call | flops 1000 | bytes 1000 | tf_op jit(solution)/shard_map/last_block/pallas_call | solution.py:145
  96.6 1.4 collective-permute-done.24
  98.1 0.9 add.110
  99.2 2.0 %collective-permute-start.26 = (f32[72,512]{1,0:T(8,128)S(1)}, f32[72,512]{1,0:T(8,128)S(1)}, u32[]{:S(2)}, u32[]{:S(2)}) collective-permute-start(f32[72,512]{1,0:T(8,128)S(1)} %add.110), channel_id=1, source_target_pairs={{0,16},{4,20},{8,24},{12,28},{16,0},{20,4},{24,8},{28,12},{1,17},{... | collective-permute-start | bytes 442376 | tf_op jit(solution)/shard_map/ppermute | solution.py:43
  101.2 1.3 collective-permute-start.27
  102.5 3.2 %collective-permute-done.25 = f32[72,512]{1,0:T(8,128)S(1)} collective-permute-done((f32[72,512]{1,0:T(8,128)S(1)}, f32[72,512]{1,0:T(8,128)S(1)}, u32[]{:S(2)}, u32[]{:S(2)}) %collective-permute-start.25) | collective-permute-done | bytes 147488 | tf_op jit(solution)/shard_map/ppermute | solution.py:43
  105.8 1.8 %collective-permute-done.26 = f32[72,512]{1,0:T(8,128)S(1)} collective-permute-done((f32[72,512]{1,0:T(8,128)S(1)}, f32[72,512]{1,0:T(8,128)S(1)}, u32[]{:S(2)}, u32[]{:S(2)}) %collective-permute-start.26) | collective-permute-done | bytes 147488 | tf_op jit(solution)/shard_map/ppermute | solution.py:43
  107.6 1.6 %collective-permute-done.27 = f32[72,512]{1,0:T(8,128)S(1)} collective-permute-done((f32[72,512]{1,0:T(8,128)S(1)}, f32[72,512]{1,0:T(8,128)S(1)}, u32[]{:S(2)}, u32[]{:S(2)}) %collective-permute-start.27) | collective-permute-done | bytes 147488 | tf_op jit(solution)/shard_map/ppermute | solution.py:43
  109.3 1.3 collective-permute-done.28
  110.9 1.6 %fusion.27 = f32[64,384]{1,0:T(8,128)S(1)} fusion(f32[64,1024]{1,0:T(8,128)S(1)} %get-tuple-element.80, f32[384,1024]{1,0:T(8,128)S(1)} %copy-done), kind=kOutput, calls=%fused_computation.88 | convolution fusion | flops 301989888 | bytes 1933312 | tf_op jit(solution)/shard_map/dot_general | solution.py:25
  112.7 1.2 collective-permute-done.29
  113.9 1.1 fusion.11
  115.4 1.2 collective-permute-done.30
  116.6 0.7 collective-permute-start.31
  117.4 1.7 %collective-permute-start.32 = (f32[72,512]{1,0:T(8,128)S(1)}, f32[72,512]{1,0:T(8,128)S(1)}, u32[]{:S(2)}, u32[]{:S(2)}) collective-permute-start(f32[72,512]{1,0:T(8,128)S(1)} %select_add_fusion), channel_id=1, source_target_pairs={{0,16},{4,20},{8,24},{12,28},{16,0},{20,4},{24,8},{28,12},{1,17},{... | collective-permute-start | bytes 442376 | tf_op jit(solution)/shard_map/ppermute | solution.py:43
  119.0 1.2 collective-permute-start.33
  120.2 3.2 %collective-permute-done.31 = f32[72,512]{1,0:T(8,128)S(1)} collective-permute-done((f32[72,512]{1,0:T(8,128)S(1)}, f32[72,512]{1,0:T(8,128)S(1)}, u32[]{:S(2)}, u32[]{:S(2)}) %collective-permute-start.31) | collective-permute-done | bytes 147488 | tf_op jit(solution)/shard_map/ppermute | solution.py:43
  123.4 2.8 %collective-permute-done.32 = f32[72,512]{1,0:T(8,128)S(1)} collective-permute-done((f32[72,512]{1,0:T(8,128)S(1)}, f32[72,512]{1,0:T(8,128)S(1)}, u32[]{:S(2)}, u32[]{:S(2)}) %collective-permute-start.32) | collective-permute-done | bytes 147488 | tf_op jit(solution)/shard_map/ppermute | solution.py:43
  126.3 1.3 collective-permute-done.34
  127.9 1.6 %fusion.24 = f32[64,384]{1,0:T(8,128)S(1)} fusion(f32[384,1024]{1,0:T(8,128)S(1)} %copy-done, f32[64,1024]{1,0:T(8,128)S(1)} %get-tuple-element.79, f32[1024]{0:T(1024)S(1)} %bitcast.27), kind=kOutput, calls=%fused_computation.86 | convolution fusion | flops 302055424 | bytes 1937408 | tf_op jit(solution)/shard_map/dot_general | solution.py:25
  129.8 7.4 %collective-permute-start.35 = (f32[128,512]{1,0:T(8,128)S(1)}, f32[128,512]{1,0:T(8,128)S(1)}, u32[]{:S(2)}, u32[]{:S(2)}) collective-permute-start(f32[128,512]{1,0:T(8,128)S(1)} %pad_maximum_fusion), channel_id=1, source_target_pairs={{0,1},{1,0},{2,3},{3,2},{4,5},{5,4},{6,7},{7,6},{8,9},{9,8},{10,11... | collective-permute-start | bytes 786440 | tf_op jit(solution)/shard_map/ppermute | solution.py:34
  137.2 1.1 fusion.14
  138.8 1.2 collective-permute-done.38
  140.1 3.3 %collective-permute-start.39 = (f32[72,256]{1,0:T(8,128)S(1)}, f32[72,256]{1,0:T(8,128)S(1)}, u32[]{:S(2)}, u32[]{:S(2)}) collective-permute-start(f32[72,256]{1,0:T(8,128)S(1)} %slice.180), channel_id=1, source_target_pairs={{0,1},{1,0},{2,3},{3,2},{4,5},{5,4},{6,7},{7,6},{8,9},{9,8},{10,11... | collective-permute-start | bytes 221192 | tf_op jit(solution)/shard_map/ppermute | solution.py:34
  143.6 2.5 %collective-permute-done.39 = f32[72,256]{1,0:T(8,128)S(1)} collective-permute-done((f32[72,256]{1,0:T(8,128)S(1)}, f32[72,256]{1,0:T(8,128)S(1)}, u32[]{:S(2)}, u32[]{:S(2)}) %collective-permute-start.39) | collective-permute-done | bytes 73760 | tf_op jit(solution)/shard_map/ppermute | solution.py:34
  146.1 1.6 collective-permute-start.40
  147.6 0.8 collective-permute-start.41
  148.4 1.2 collective-permute-start.42
  149.7 0.8 collective-permute-done.40
  150.5 2.1 %collective-permute-done.41 = f32[72,256]{1,0:T(8,128)S(1)} collective-permute-done((f32[72,256]{1,0:T(8,128)S(1)}, f32[72,256]{1,0:T(8,128)S(1)}, u32[]{:S(2)}, u32[]{:S(2)}) %collective-permute-start.41) | collective-permute-done | bytes 73760 | tf_op jit(solution)/shard_map/ppermute | solution.py:43
  152.6 1.0 collective-permute-done.42
  153.8 1.2 collective-permute-done.43
  155.0 0.8 fusion.9
  (116 shorter events, 4.0 us)
Async XLA Ops:
  0.6 23.6 %collective-permute-start = (bf16[512,896]{1,0:T(8,128)(2,1)}, bf16[512,896]{1,0:T(8,128)(2,1)S(1)}, u32[]{:S(2)}, u32[]{:S(2)}) collective-permute-start(bf16[512,896]{1,0:T(8,128)(2,1)} %refs_6_.1), channel_id=1, source_target_pairs={{0,8},{4,12},{8,0},{12,4},{16,24},{20,28},{24,16},{28,20},{1,9},{5... | collective-permute-start | bytes 2752520 | tf_op jit(solution)/shard_map/ppermute | solution.py:43
  3.6 22.0 %collective-permute-start.1 = (bf16[512,896]{1,0:T(8,128)(2,1)}, bf16[512,896]{1,0:T(8,128)(2,1)S(1)}, u32[]{:S(2)}, u32[]{:S(2)}) collective-permute-start(bf16[512,896]{1,0:T(8,128)(2,1)} %refs_6_.1), channel_id=1, source_target_pairs={{0,16},{4,20},{8,24},{12,28},{16,0},{20,4},{24,8},{28,12},{1,17},{... | collective-permute-start | bytes 2752520 | tf_op jit(solution)/shard_map/ppermute | solution.py:43
  5.2 21.8 %collective-permute-start.2 = (bf16[512,896]{1,0:T(8,128)(2,1)}, bf16[512,896]{1,0:T(8,128)(2,1)}, u32[]{:S(2)}, u32[]{:S(2)}) collective-permute-start(bf16[512,896]{1,0:T(8,128)(2,1)} %refs_6_.1), channel_id=1, source_target_pairs={{0,1},{1,0},{2,3},{3,2},{4,5},{5,4},{6,7},{7,6},{8,9},{9,8},{10,11... | collective-permute-start | bytes 2752520 | tf_op jit(solution)/shard_map/ppermute | solution.py:34
  6.7 33.4 %collective-permute-start.4 = (bf16[384,1792]{1,0:T(8,128)(2,1)}, bf16[384,1792]{1,0:T(8,128)(2,1)S(1)}, u32[]{:S(2)}, u32[]{:S(2)}) collective-permute-start(bf16[384,1792]{1,0:T(8,128)(2,1)} %refs_0_.5), channel_id=1, source_target_pairs={{0,4},{1,2},{2,1},{3,7},{4,0},{5,6},{6,5},{7,3},{8,12},{9,10},{10,... | collective-permute-start | bytes 4128776 | tf_op jit(solution)/shard_map/ppermute | solution.py:39
  9.0 20.8 %copy-start.4 = (bf16[512,896]{1,0:T(8,128)(2,1)S(1)}, bf16[512,896]{1,0:T(8,128)(2,1)}, u32[]{:S(2)}) copy-start(bf16[512,896]{1,0:T(8,128)(2,1)} %refs_6_.1) | copy-start | bytes 2752516
  24.2 26.6 %copy-start.2 = (bf16[512,896]{1,0:T(8,128)(2,1)}, bf16[512,896]{1,0:T(8,128)(2,1)S(1)}, u32[]{:S(2)}) copy-start(bf16[512,896]{1,0:T(8,128)(2,1)S(1)} %collective-permute-done.refs_4_.refs_6_.refs_7_) | copy-start | bytes 2752516
  25.7 25.1 %copy-start.3 = (bf16[512,896]{1,0:T(8,128)(2,1)}, bf16[512,896]{1,0:T(8,128)(2,1)S(1)}, u32[]{:S(2)}) copy-start(bf16[512,896]{1,0:T(8,128)(2,1)S(1)} %collective-permute-done.1.refs_5_.refs_7_.refs_8_) | copy-start | bytes 2752516
  27.0 15.8 %collective-permute-start.3 = (bf16[384,896]{1,0:T(8,128)(2,1)S(1)}, bf16[384,896]{1,0:T(8,128)(2,1)}, u32[]{:S(2)}, u32[]{:S(2)}) collective-permute-start(bf16[384,896]{1,0:T(8,128)(2,1)S(1)} %get-tuple-element.43), channel_id=1, source_target_pairs={{0,1},{1,0},{2,3},{3,2},{4,5},{5,4},{6,7},{7,6},{8,9},{9,8},{10,11... | collective-permute-start | bytes 2064392 | tf_op jit(solution)/shard_map/ppermute | solution.py:34
  28.6 10.6 %collective-permute-start.5 = (bf16[256,896]{1,0:T(8,128)(2,1)S(1)}, bf16[256,896]{1,0:T(8,128)(2,1)S(1)}, u32[]{:S(2)}, u32[]{:S(2)}) collective-permute-start(bf16[256,896]{1,0:T(8,128)(2,1)S(1)} %slice.124), channel_id=1, source_target_pairs={{0,16},{4,20},{8,24},{12,28},{16,0},{20,4},{24,8},{28,12},{1,17},{... | collective-permute-start | bytes 1376264 | tf_op jit(solution)/shard_map/ppermute | solution.py:43
  29.2 10.4 %collective-permute-start.6 = (bf16[256,896]{1,0:T(8,128)(2,1)S(1)}, bf16[256,896]{1,0:T(8,128)(2,1)S(1)}, u32[]{:S(2)}, u32[]{:S(2)}) collective-permute-start(bf16[256,896]{1,0:T(8,128)(2,1)S(1)} %slice.125), channel_id=1, source_target_pairs={{0,8},{4,12},{8,0},{12,4},{16,24},{20,28},{24,16},{28,20},{1,9},{5... | collective-permute-start | bytes 1376264 | tf_op jit(solution)/shard_map/ppermute | solution.py:43
  29.8 14.3 %collective-permute-start.7 = (bf16[512,896]{1,0:T(8,128)(2,1)S(1)}, bf16[512,896]{1,0:T(8,128)(2,1)S(1)}, u32[]{:S(2)}, u32[]{:S(2)}) collective-permute-start(bf16[512,896]{1,0:T(8,128)(2,1)S(1)} %copy-done.4), channel_id=1, source_target_pairs={{0,4},{4,0},{8,12},{12,8},{16,20},{20,16},{24,28},{28,24},{1,5},{5... | collective-permute-start | bytes 2752520 | tf_op jit(solution)/shard_map/ppermute | solution.py:43
  39.2 8.2 %copy-start.8 = (bf16[256,896]{1,0:T(8,128)(2,1)}, bf16[256,896]{1,0:T(8,128)(2,1)S(1)}, u32[]{:S(2)}) copy-start(bf16[256,896]{1,0:T(8,128)(2,1)S(1)} %collective-permute-done.5.refs_6_.refs_8_.refs_9_) | copy-start | bytes 1376260
  39.6 7.8 %copy-start.10 = (bf16[256,896]{1,0:T(8,128)(2,1)}, bf16[256,896]{1,0:T(8,128)(2,1)S(1)}, u32[]{:S(2)}) copy-start(bf16[256,896]{1,0:T(8,128)(2,1)S(1)} %collective-permute-done.6.refs_7_.refs_9_.refs_10_) | copy-start | bytes 1376260
  39.6 3.2 %collective-permute-start.10 = (bf16[256,896]{1,0:T(8,128)(2,1)S(1)}, bf16[256,896]{1,0:T(8,128)(2,1)S(1)}, u32[]{:S(2)}, u32[]{:S(2)}) collective-permute-start(bf16[256,896]{1,0:T(8,128)(2,1)S(1)} %collective-permute-done.5.refs_6_.refs_8_.refs_9_), channel_id=1, source_target_pairs={{0,4},{4,0},{8,12},{12,8},{16,20},{20,16},{24,28},{28,24},{1,5},{5... | collective-permute-start | bytes 1376264 | tf_op jit(solution)/shard_map/ppermute | solution.py:43
  39.6 3.8 %collective-permute-start.11 = (bf16[256,896]{1,0:T(8,128)(2,1)S(1)}, bf16[256,896]{1,0:T(8,128)(2,1)S(1)}, u32[]{:S(2)}, u32[]{:S(2)}) collective-permute-start(bf16[256,896]{1,0:T(8,128)(2,1)S(1)} %collective-permute-done.6.refs_7_.refs_9_.refs_10_), channel_id=1, source_target_pairs={{0,4},{4,0},{8,12},{12,8},{16,20},{20,16},{24,28},{28,24},{1,5},{5... | collective-permute-start | bytes 1376264 | tf_op jit(solution)/shard_map/ppermute | solution.py:43
  40.1 10.7 %copy-start.1 = (bf16[384,1792]{1,0:T(8,128)(2,1)}, bf16[384,1792]{1,0:T(8,128)(2,1)S(1)}, u32[]{:S(2)}) copy-start(bf16[384,1792]{1,0:T(8,128)(2,1)S(1)} %collective-permute-done.4.refs_1_) | copy-start | bytes 4128772
  40.1 4.0 %collective-permute-start.8 = (bf16[512,896]{1,0:T(8,128)(2,1)S(1)}, bf16[512,896]{1,0:T(8,128)(2,1)S(1)}, u32[]{:S(2)}, u32[]{:S(2)}) collective-permute-start(bf16[512,896]{1,0:T(8,128)(2,1)S(1)} %collective-permute-done.refs_4_.refs_6_.refs_7_), channel_id=1, source_target_pairs={{0,4},{4,0},{8,12},{12,8},{16,20},{20,16},{24,28},{28,24},{1,5},{5... | collective-permute-start | bytes 2752520 | tf_op jit(solution)/shard_map/ppermute | solution.py:43
  42.8 4.5 %collective-permute-start.9 = (bf16[512,896]{1,0:T(8,128)(2,1)S(1)}, bf16[512,896]{1,0:T(8,128)(2,1)S(1)}, u32[]{:S(2)}, u32[]{:S(2)}) collective-permute-start(bf16[512,896]{1,0:T(8,128)(2,1)S(1)} %collective-permute-done.1.refs_5_.refs_7_.refs_8_), channel_id=1, source_target_pairs={{0,4},{4,0},{8,12},{12,8},{16,20},{20,16},{24,28},{28,24},{1,5},{5... | collective-permute-start | bytes 2752520 | tf_op jit(solution)/shard_map/ppermute | solution.py:43
  42.8 4.6 %copy-start.11 = (bf16[256,896]{1,0:T(8,128)(2,1)}, bf16[256,896]{1,0:T(8,128)(2,1)S(1)}, u32[]{:S(2)}) copy-start(bf16[256,896]{1,0:T(8,128)(2,1)S(1)} %collective-permute-done.10.refs_11_.refs_13_.refs_14_) | copy-start | bytes 1376260
  42.8 23.1 %collective-permute-start.13 = (bf16[512,896]{1,0:T(8,128)(2,1)}, bf16[512,896]{1,0:T(8,128)(2,1)}, u32[]{:S(2)}, u32[]{:S(2)}) collective-permute-start(bf16[512,896]{1,0:T(8,128)(2,1)} %collective-permute-done.2.refs_15_.refs_16_), channel_id=1, source_target_pairs={{0,8},{4,12},{8,0},{12,4},{16,24},{20,28},{24,16},{28,20},{1,9},{5... | collective-permute-start | bytes 2752520 | tf_op jit(solution)/shard_map/ppermute | solution.py:43
  43.4 4.0 %copy-start.12 = (bf16[256,896]{1,0:T(8,128)(2,1)}, bf16[256,896]{1,0:T(8,128)(2,1)S(1)}, u32[]{:S(2)}) copy-start(bf16[256,896]{1,0:T(8,128)(2,1)S(1)} %collective-permute-done.11.refs_12_.refs_14_.refs_15_) | copy-start | bytes 1376260
  43.4 22.7 %collective-permute-start.14 = (bf16[512,896]{1,0:T(8,128)(2,1)}, bf16[512,896]{1,0:T(8,128)(2,1)}, u32[]{:S(2)}, u32[]{:S(2)}) collective-permute-start(bf16[512,896]{1,0:T(8,128)(2,1)} %collective-permute-done.2.refs_15_.refs_16_), channel_id=1, source_target_pairs={{0,16},{4,20},{8,24},{12,28},{16,0},{20,4},{24,8},{28,12},{1,17},{... | collective-permute-start | bytes 2752520 | tf_op jit(solution)/shard_map/ppermute | solution.py:43
  44.1 3.2 %copy-start.5 = (bf16[512,896]{1,0:T(8,128)(2,1)}, bf16[512,896]{1,0:T(8,128)(2,1)S(1)}, u32[]{:S(2)}) copy-start(bf16[512,896]{1,0:T(8,128)(2,1)S(1)} %collective-permute-done.7.refs_8_.refs_10_.refs_11_) | copy-start | bytes 2752516
  44.1 22.0 %collective-permute-start.15 = (bf16[384,896]{1,0:T(8,128)(2,1)}, bf16[384,896]{1,0:T(8,128)(2,1)}, u32[]{:S(2)}, u32[]{:S(2)}) collective-permute-start(bf16[384,896]{1,0:T(8,128)(2,1)} %collective-permute-done.3.refs_2_), channel_id=1, source_target_pairs={{0,4},{1,2},{2,1},{3,7},{4,0},{5,6},{6,5},{7,3},{8,12},{9,10},{10,... | collective-permute-start | bytes 2064392 | tf_op jit(solution)/shard_map/ppermute | solution.py:39
  44.2 3.3 %copy-start.6 = (bf16[512,896]{1,0:T(8,128)(2,1)}, bf16[512,896]{1,0:T(8,128)(2,1)S(1)}, u32[]{:S(2)}) copy-start(bf16[512,896]{1,0:T(8,128)(2,1)S(1)} %collective-permute-done.8.refs_9_.refs_11_.refs_12_) | copy-start | bytes 2752516
  44.2 22.5 %collective-permute-start.12 = (bf16[384,896]{1,0:T(8,128)(2,1)}, bf16[384,896]{1,0:T(8,128)(2,1)}, u32[]{:S(2)}, u32[]{:S(2)}) collective-permute-start(bf16[384,896]{1,0:T(8,128)(2,1)} %get-tuple-element.54), channel_id=1, source_target_pairs={{0,1},{1,0},{2,3},{3,2},{4,5},{5,4},{6,7},{7,6},{8,9},{9,8},{10,11... | collective-permute-start | bytes 2064392 | tf_op jit(solution)/shard_map/ppermute | solution.py:34
  47.3 1.0 copy-start.7
  47.3 20.9 %collective-permute-start.16 = (bf16[512,896]{1,0:T(8,128)(2,1)}, bf16[512,896]{1,0:T(8,128)(2,1)}, u32[]{:S(2)}, u32[]{:S(2)}) collective-permute-start(bf16[512,896]{1,0:T(8,128)(2,1)} %collective-permute-done.2.refs_15_.refs_16_), channel_id=1, source_target_pairs={{0,4},{4,0},{8,12},{12,8},{16,20},{20,16},{24,28},{28,24},{1,5},{5... | collective-permute-start | bytes 2752520 | tf_op jit(solution)/shard_map/ppermute | solution.py:43
  50.8 17.4 %copy-start.9 = (bf16[256,896]{1,0:T(8,128)(2,1)S(1)}, bf16[256,896]{1,0:T(8,128)(2,1)}, u32[]{:S(2)}) copy-start(bf16[256,896]{1,0:T(8,128)(2,1)} %copy-done.8) | copy-start | bytes 1376260
  66.1 5.2 %collective-permute-start.17 = (bf16[512,896]{1,0:T(8,128)(2,1)}, bf16[512,896]{1,0:T(8,128)(2,1)S(1)}, u32[]{:S(2)}, u32[]{:S(2)}) collective-permute-start(bf16[512,896]{1,0:T(8,128)(2,1)} %collective-permute-done.13.refs_16_.refs_17_), channel_id=1, source_target_pairs={{0,4},{4,0},{8,12},{12,8},{16,20},{20,16},{24,28},{28,24},{1,5},{5... | collective-permute-start | bytes 2752520 | tf_op jit(solution)/shard_map/ppermute | solution.py:43
  66.1 5.2 %collective-permute-start.18 = (bf16[512,896]{1,0:T(8,128)(2,1)}, bf16[512,896]{1,0:T(8,128)(2,1)S(1)}, u32[]{:S(2)}, u32[]{:S(2)}) collective-permute-start(bf16[512,896]{1,0:T(8,128)(2,1)} %collective-permute-done.14.refs_17_.refs_18_), channel_id=1, source_target_pairs={{0,4},{4,0},{8,12},{12,8},{16,20},{20,16},{24,28},{28,24},{1,5},{5... | collective-permute-start | bytes 2752520 | tf_op jit(solution)/shard_map/ppermute | solution.py:43
  66.7 17.2 %collective-permute-start.19 = (bf16[384,896]{1,0:T(8,128)(2,1)}, bf16[384,896]{1,0:T(8,128)(2,1)S(1)}, u32[]{:S(2)}, u32[]{:S(2)}) collective-permute-start(bf16[384,896]{1,0:T(8,128)(2,1)} %collective-permute-done.12.refs_3_), channel_id=1, source_target_pairs={{0,4},{1,2},{2,1},{3,7},{4,0},{5,6},{6,5},{7,3},{8,12},{9,10},{10,... | collective-permute-start | bytes 2064392 | tf_op jit(solution)/shard_map/ppermute | solution.py:39
  66.7 17.1 %collective-permute-start.21 = (bf16[256,896]{1,0:T(8,128)(2,1)}, bf16[256,896]{1,0:T(8,128)(2,1)S(1)}, u32[]{:S(2)}, u32[]{:S(2)}) collective-permute-start(bf16[256,896]{1,0:T(8,128)(2,1)} %slice.126), channel_id=1, source_target_pairs={{0,24},{4,28},{8,16},{12,20},{16,8},{20,12},{24,0},{28,4},{1,25},{... | collective-permute-start | bytes 1376264 | tf_op jit(solution)/shard_map/ppermute | solution.py:43
  68.2 15.8 %collective-permute-start.20 = (bf16[256,896]{1,0:T(8,128)(2,1)S(1)}, bf16[256,896]{1,0:T(8,128)(2,1)S(1)}, u32[]{:S(2)}, u32[]{:S(2)}) collective-permute-start(bf16[256,896]{1,0:T(8,128)(2,1)S(1)} %copy-done.9), channel_id=1, source_target_pairs={{0,1},{1,0},{2,3},{3,2},{4,5},{5,4},{6,7},{7,6},{8,9},{9,8},{10,11... | collective-permute-start | bytes 1376264 | tf_op jit(solution)/shard_map/ppermute | solution.py:34
  71.3 0.9 copy-start.13
  71.3 1.3 copy-start.14
  83.8 2.6 %copy-start.16 = (bf16[256,896]{1,0:T(8,128)(2,1)}, bf16[256,896]{1,0:T(8,128)(2,1)S(1)}, u32[]{:S(2)}) copy-start(bf16[256,896]{1,0:T(8,128)(2,1)S(1)} %collective-permute-done.21.refs_23_) | copy-start | bytes 1376260
  83.8 2.6 %copy-start.15 = (bf16[384,896]{1,0:T(8,128)(2,1)}, bf16[384,896]{1,0:T(8,128)(2,1)S(1)}, u32[]{:S(2)}) copy-start(bf16[384,896]{1,0:T(8,128)(2,1)S(1)} %collective-permute-done.19.refs_5_) | copy-start | bytes 2064388
  83.9 1.9 %collective-permute-start.23 = (bf16[256,896]{1,0:T(8,128)(2,1)S(1)}, bf16[256,896]{1,0:T(8,128)(2,1)S(1)}, u32[]{:S(2)}, u32[]{:S(2)}) collective-permute-start(bf16[256,896]{1,0:T(8,128)(2,1)S(1)} %collective-permute-done.21.refs_23_), channel_id=1, source_target_pairs={{0,4},{4,0},{8,12},{12,8},{16,20},{20,16},{24,28},{28,24},{1,5},{5... | collective-permute-start | bytes 1376264 | tf_op jit(solution)/shard_map/ppermute | solution.py:43
  83.9 2.5 %copy-start.17 = (bf16[256,896]{1,0:T(8,128)(2,1)}, bf16[256,896]{1,0:T(8,128)(2,1)S(1)}, u32[]{:S(2)}) copy-start(bf16[256,896]{1,0:T(8,128)(2,1)S(1)} %collective-permute-done.20.refs_22_) | copy-start | bytes 1376260
  84.0 2.4 %collective-permute-start.22 = (bf16[256,896]{1,0:T(8,128)(2,1)S(1)}, bf16[256,896]{1,0:T(8,128)(2,1)S(1)}, u32[]{:S(2)}, u32[]{:S(2)}) collective-permute-start(bf16[256,896]{1,0:T(8,128)(2,1)S(1)} %collective-permute-done.20.refs_22_), channel_id=1, source_target_pairs={{0,4},{4,0},{8,12},{12,8},{16,20},{20,16},{24,28},{28,24},{1,5},{5... | collective-permute-start | bytes 1376264 | tf_op jit(solution)/shard_map/ppermute | solution.py:43
  85.7 0.8 copy-start.18
  86.4 0.8 copy-start.19
  96.4 14.5 %copy-start = (f32[384,1024]{1,0:T(8,128)S(1)}, f32[384,1024]{1,0:T(8,128)}, u32[]{:S(2)}) copy-start(f32[384,1024]{1,0:T(8,128)} %get-tuple-element.71) | copy-start | bytes 4718596
  96.4 1.6 %collective-permute-start.24 = (f32[72,512]{1,0:T(8,128)}, f32[72,512]{1,0:T(8,128)S(1)}, u32[]{:S(2)}, u32[]{:S(2)}) collective-permute-start(f32[72,512]{1,0:T(8,128)} %get-tuple-element.70), channel_id=1, source_target_pairs={{0,4},{4,0},{8,12},{12,8},{16,20},{20,16},{24,28},{28,24},{1,5},{5... | collective-permute-start | bytes 442376 | tf_op jit(solution)/shard_map/ppermute | solution.py:43
  99.0 6.8 %collective-permute-start.25 = (f32[72,512]{1,0:T(8,128)S(1)}, f32[72,512]{1,0:T(8,128)S(1)}, u32[]{:S(2)}, u32[]{:S(2)}) collective-permute-start(f32[72,512]{1,0:T(8,128)S(1)} %add.110), channel_id=1, source_target_pairs={{0,8},{4,12},{8,0},{12,4},{16,24},{20,28},{24,16},{28,20},{1,9},{5... | collective-permute-start | bytes 442376 | tf_op jit(solution)/shard_map/ppermute | solution.py:43
  99.2 8.3 %collective-permute-start.26 = (f32[72,512]{1,0:T(8,128)S(1)}, f32[72,512]{1,0:T(8,128)S(1)}, u32[]{:S(2)}, u32[]{:S(2)}) collective-permute-start(f32[72,512]{1,0:T(8,128)S(1)} %add.110), channel_id=1, source_target_pairs={{0,16},{4,20},{8,24},{12,28},{16,0},{20,4},{24,8},{28,12},{1,17},{... | collective-permute-start | bytes 442376 | tf_op jit(solution)/shard_map/ppermute | solution.py:43
  101.2 8.0 %collective-permute-start.27 = (f32[72,512]{1,0:T(8,128)S(1)}, f32[72,512]{1,0:T(8,128)S(1)}, u32[]{:S(2)}, u32[]{:S(2)}) collective-permute-start(f32[72,512]{1,0:T(8,128)S(1)} %add.110), channel_id=1, source_target_pairs={{0,24},{4,28},{8,16},{12,20},{16,8},{20,12},{24,0},{28,4},{1,25},{... | collective-permute-start | bytes 442376 | tf_op jit(solution)/shard_map/ppermute | solution.py:43
  109.3 1.4 collective-permute-start.28
  112.5 1.4 collective-permute-start.29
  115.2 1.4 collective-permute-start.30
  116.6 6.8 %collective-permute-start.31 = (f32[72,512]{1,0:T(8,128)S(1)}, f32[72,512]{1,0:T(8,128)S(1)}, u32[]{:S(2)}, u32[]{:S(2)}) collective-permute-start(f32[72,512]{1,0:T(8,128)S(1)} %select_add_fusion), channel_id=1, source_target_pairs={{0,8},{4,12},{8,0},{12,4},{16,24},{20,28},{24,16},{28,20},{1,9},{5... | collective-permute-start | bytes 442376 | tf_op jit(solution)/shard_map/ppermute | solution.py:43
  117.4 8.8 %collective-permute-start.32 = (f32[72,512]{1,0:T(8,128)S(1)}, f32[72,512]{1,0:T(8,128)S(1)}, u32[]{:S(2)}, u32[]{:S(2)}) collective-permute-start(f32[72,512]{1,0:T(8,128)S(1)} %select_add_fusion), channel_id=1, source_target_pairs={{0,16},{4,20},{8,24},{12,28},{16,0},{20,4},{24,8},{28,12},{1,17},{... | collective-permute-start | bytes 442376 | tf_op jit(solution)/shard_map/ppermute | solution.py:43
  119.0 7.1 %collective-permute-start.33 = (f32[72,512]{1,0:T(8,128)S(1)}, f32[72,512]{1,0:T(8,128)S(1)}, u32[]{:S(2)}, u32[]{:S(2)}) collective-permute-start(f32[72,512]{1,0:T(8,128)S(1)} %select_add_fusion), channel_id=1, source_target_pairs={{0,24},{4,28},{8,16},{12,20},{16,8},{20,12},{24,0},{28,4},{1,25},{... | collective-permute-start | bytes 442376 | tf_op jit(solution)/shard_map/ppermute | solution.py:43
  126.2 1.4 collective-permute-start.34
  129.6 7.6 %collective-permute-start.36 = (f32[72,384]{1,0:T(8,128)S(1)}, f32[72,384]{1,0:T(8,128)S(1)}, u32[]{:S(2)}, u32[]{:S(2)}) collective-permute-start(f32[72,384]{1,0:T(8,128)S(1)} %pad_maximum_fusion.5), channel_id=1, source_target_pairs={{0,4},{1,2},{2,1},{3,7},{4,0},{5,6},{6,5},{7,3},{8,12},{9,10},{10,... | collective-permute-start | bytes 331784 | tf_op jit(solution)/shard_map/ppermute | solution.py:39
  129.8 23.9 %collective-permute-start.35 = (f32[128,512]{1,0:T(8,128)S(1)}, f32[128,512]{1,0:T(8,128)S(1)}, u32[]{:S(2)}, u32[]{:S(2)}) collective-permute-start(f32[128,512]{1,0:T(8,128)S(1)} %pad_maximum_fusion), channel_id=1, source_target_pairs={{0,1},{1,0},{2,3},{3,2},{4,5},{5,4},{6,7},{7,6},{8,9},{9,8},{10,11... | collective-permute-start | bytes 786440 | tf_op jit(solution)/shard_map/ppermute | solution.py:34
  138.6 1.4 collective-permute-start.38
  140.1 6.0 %collective-permute-start.39 = (f32[72,256]{1,0:T(8,128)S(1)}, f32[72,256]{1,0:T(8,128)S(1)}, u32[]{:S(2)}, u32[]{:S(2)}) collective-permute-start(f32[72,256]{1,0:T(8,128)S(1)} %slice.180), channel_id=1, source_target_pairs={{0,1},{1,0},{2,3},{3,2},{4,5},{5,4},{6,7},{7,6},{8,9},{9,8},{10,11... | collective-permute-start | bytes 221192 | tf_op jit(solution)/shard_map/ppermute | solution.py:34
  143.5 6.2 %collective-permute-start.37 = (f32[72,512]{1,0:T(8,128)S(1)}, f32[72,512]{1,0:T(8,128)S(1)}, u32[]{:S(2)}, u32[]{:S(2)}) collective-permute-start(f32[72,512]{1,0:T(8,128)S(1)} %slice.172), channel_id=1, source_target_pairs={{0,1},{1,0},{2,3},{3,2},{4,5},{5,4},{6,7},{7,6},{8,9},{9,8},{10,11... | collective-permute-start | bytes 442376 | tf_op jit(solution)/shard_map/ppermute | solution.py:34
  146.1 4.4 %collective-permute-start.40 = (f32[72,256]{1,0:T(8,128)S(1)}, f32[72,256]{1,0:T(8,128)S(1)}, u32[]{:S(2)}, u32[]{:S(2)}) collective-permute-start(f32[72,256]{1,0:T(8,128)S(1)} %slice_select_fusion.2), channel_id=1, source_target_pairs={{0,8},{4,12},{8,0},{12,4},{16,24},{20,28},{24,16},{28,20},{1,9},{5... | collective-permute-start | bytes 221192 | tf_op jit(solution)/shard_map/ppermute | solution.py:43
  147.6 5.0 %collective-permute-start.41 = (f32[72,256]{1,0:T(8,128)S(1)}, f32[72,256]{1,0:T(8,128)S(1)}, u32[]{:S(2)}, u32[]{:S(2)}) collective-permute-start(f32[72,256]{1,0:T(8,128)S(1)} %slice_select_fusion.2), channel_id=1, source_target_pairs={{0,16},{4,20},{8,24},{12,28},{16,0},{20,4},{24,8},{28,12},{1,17},{... | collective-permute-start | bytes 221192 | tf_op jit(solution)/shard_map/ppermute | solution.py:43
  148.4 5.3 %collective-permute-start.42 = (f32[72,256]{1,0:T(8,128)S(1)}, f32[72,256]{1,0:T(8,128)S(1)}, u32[]{:S(2)}, u32[]{:S(2)}) collective-permute-start(f32[72,256]{1,0:T(8,128)S(1)} %slice_select_fusion.2), channel_id=1, source_target_pairs={{0,24},{4,28},{8,16},{12,20},{16,8},{20,12},{24,0},{28,4},{1,25},{... | collective-permute-start | bytes 221192 | tf_op jit(solution)/shard_map/ppermute | solution.py:43
  153.7 1.3 collective-permute-start.43

commit v8 on v7

--- a/solution.py
+++ b/solution.py
@@ -358,8 +358,8 @@
     end = handed(own)
     own_x, own_y = flipped(own, 2), flipped(own, 4)
     middle_rows = across(row_features)
-    own_x, own_y, end, left = lax.optimization_barrier((own_x, own_y, end, left))
-    end_left = handed(left)
+    end_left = handed(after(left, end))
+    own_x, own_y = lax.optimization_barrier((own_x, own_y))
     own_low, own_high = flipped(own_x[:middle], 4), flipped(own_y[middle:], 2)
     other_own, other_x, other_y = flipped(after(own, own_x), 1), flipped(own_x, 1), flipped(own_y, 1)
     own_low, own_high, end = lax.optimization_barrier((own_low, own_high, end))
@@ -377,9 +377,9 @@
     cross_own, row_norm, norm_own = own_block(rows, own_parts, n, m, half)
     end_x, end_y, end_bottom, far_left, _ = lax.optimization_barrier((end_x, end_y, end_bottom, far_left, cross_own))
     end_high = flipped(end_bottom, 6)
-    end_right = after(end_right, end_x, end_y)
+    end_right = after(end_right, cross_own)
     far_right = across(end_right)
-    end_low = handed(after(own_low, end_right))
+    end_low = handed(after(own_low, end_right, end_x, end_y))
     end_parts = [(0, 0, end), (2, 0, end_x), (4, 0, end_y)]
     end_parts += [(bits + 1, row, flipped(block, 1)) for bits, row, block in end_parts]
     rows |= {(1, 1): end_right, (2, 0): far_left}

time: 156 us -> 155 us (level)
  waiting for transfers between devices: 67 us -> 63.1 us
  starting transfers between devices: 42.2 us -> 45.3 us
    ppermute x32, waiting for transfers between devices: 59.3 us -> 42.7 us  [flipped(): return lax.ppermute(block, 'proof', [(i, i ^ bits) for i in range(8)])]
    ppermute x7, waiting for transfers between devices: 6.48 us -> 19.2 us  [handed(): return lax.ppermute(block, 'landmark', NEIGHBOURS)]
    ppermute x7, starting transfers between devices: 20.2 us -> 22 us  [handed(): return lax.ppermute(block, 'landmark', NEIGHBOURS)]
  transfers between devices with their start and end apart: 44 -> 44, of which waited for: 26 -> 25; matrix products, arithmetic and copies ran while one was open for 4% -> 4% of each run, Pallas kernels for 13% -> 13%
where the time goes in v8:
time: 155 us
  waiting for transfers between devices  63.1 us (41%)
  starting transfers between devices  45.3 us (29%)
  Pallas kernels  29.1 us (19%)
  local copies, waits for them, and re-layouts  7.21 us (5%)
  matrix products  5.34 us (3%)
  other arithmetic  3.75 us (2%)
    ppermute x32, waiting for transfers between devices, flipped(): return lax.ppermute(block, 'proof', [(i, i ^ bits) for i in range(8)])  42.7 us
    pallas_call x3, Pallas kernels, call(): pl.pallas_call(body, out_shape=tuple((jax.ShapeDtypeStruct(shape, jnp.flo...  29.1 us
    ppermute x32, starting transfers between devices, flipped(): return lax.ppermute(block, 'proof', [(i, i ^ bits) for i in range(8)])  22.8 us
    ppermute x7, starting transfers between devices, handed(): return lax.ppermute(block, 'landmark', NEIGHBOURS)  22 us
    ppermute x7, waiting for transfers between devices, handed(): return lax.ppermute(block, 'landmark', NEIGHBOURS)  19.2 us
    dot_general x4, matrix products, times(): lax.dot_general(left, right, ((contract[:1], contract[1:]), ((), ())), pr...  5.34 us
  transfers between devices with their start and end apart: 44, of which 25 were waited for; matrix products, arithmetic and copies ran while one was open for 4% of the time, Pallas kernels for 13%

profile of v8, /device:TPU:0, one launch (start us, length us, event | category | flops | bytes accessed | tf_op | source)
XLA Modules:
  0.0 154.9 jit_solution(7112649844365397610)
XLA Ops:
  0.6 3.1 %collective-permute-start = (bf16[512,896]{1,0:T(8,128)(2,1)}, bf16[512,896]{1,0:T(8,128)(2,1)}, u32[]{:S(2)}, u32[]{:S(2)}) collective-permute-start(bf16[512,896]{1,0:T(8,128)(2,1)} %refs_6_.1), channel_id=1, source_target_pairs={{0,1},{1,0},{2,3},{3,2},{4,5},{5,4},{6,7},{7,6},{8,9},{9,8},{10,11... | collective-permute-start | bytes 2752520 | tf_op jit(solution)/shard_map/ppermute | solution.py:34
  3.7 1.5 collective-permute-start.3
  5.2 1.5 collective-permute-start.4
  6.7 2.3 %fusion.26 = (bf16[384,896]{1,0:T(8,128)(2,1)}, bf16[384,896]{1,0:T(8,128)(2,1)S(1)}) fusion(bf16[384,1792]{1,0:T(8,128)(2,1)} %refs_0_.5), kind=kLoop, calls=%fused_computation.87 | loop fusion | bytes 2752512 | tf_op jit(solution)/shard_map/slice | solution.py:357
  9.0 15.4 %collective-permute-done.refs_15_.refs_16_ = bf16[512,896]{1,0:T(8,128)(2,1)} collective-permute-done((bf16[512,896]{1,0:T(8,128)(2,1)}, bf16[512,896]{1,0:T(8,128)(2,1)}, u32[]{:S(2)}, u32[]{:S(2)}) %collective-permute-start) | collective-permute-done | bytes 917536 | tf_op jit(solution)/shard_map/ppermute | solution.py:34
  24.4 1.7 %collective-permute-start.1 = (bf16[384,896]{1,0:T(8,128)(2,1)S(1)}, bf16[384,896]{1,0:T(8,128)(2,1)}, u32[]{:S(2)}, u32[]{:S(2)}) collective-permute-start(bf16[384,896]{1,0:T(8,128)(2,1)S(1)} %get-tuple-element.42), channel_id=1, source_target_pairs={{0,1},{1,0},{2,3},{3,2},{4,5},{5,4},{6,7},{7,6},{8,9},{9,8},{10,11... | collective-permute-start | bytes 2064392 | tf_op jit(solution)/shard_map/ppermute | solution.py:34
  26.1 0.8 collective-permute-done.4.refs_5_.refs_7_.refs_8_
  27.0 1.6 %collective-permute-start.5 = (bf16[256,896]{1,0:T(8,128)(2,1)S(1)}, bf16[256,896]{1,0:T(8,128)(2,1)S(1)}, u32[]{:S(2)}, u32[]{:S(2)}) collective-permute-start(bf16[256,896]{1,0:T(8,128)(2,1)S(1)} %slice.124), channel_id=1, source_target_pairs={{0,16},{4,20},{8,24},{12,28},{16,0},{20,4},{24,8},{28,12},{1,17},{... | collective-permute-start | bytes 1376264 | tf_op jit(solution)/shard_map/ppermute | solution.py:43
  28.6 0.8 collective-permute-start.6
  29.4 8.5 %collective-permute-done.5.refs_6_.refs_8_.refs_9_ = bf16[256,896]{1,0:T(8,128)(2,1)S(1)} collective-permute-done((bf16[256,896]{1,0:T(8,128)(2,1)S(1)}, bf16[256,896]{1,0:T(8,128)(2,1)S(1)}, u32[]{:S(2)}, u32[]{:S(2)}) %collective-permute-start.5) | collective-permute-done | bytes 458784 | tf_op jit(solution)/shard_map/ppermute | solution.py:43
  37.8 1.3 collective-permute-done.6.refs_7_.refs_9_.refs_10_
  39.2 0.5 collective-permute-start.11
  39.8 1.3 collective-permute-done.1.refs_2_
  41.1 1.4 collective-permute-start.13
  42.5 1.5 collective-permute-start.14
  44.1 3.1 %collective-permute-start.12 = (bf16[384,896]{1,0:T(8,128)(2,1)}, bf16[384,896]{1,0:T(8,128)(2,1)}, u32[]{:S(2)}, u32[]{:S(2)}) collective-permute-start(bf16[384,896]{1,0:T(8,128)(2,1)} %get-tuple-element.52), channel_id=1, source_target_pairs={{0,1},{1,0},{2,3},{3,2},{4,5},{5,4},{6,7},{7,6},{8,9},{9,8},{10,11... | collective-permute-start | bytes 2064392 | tf_op jit(solution)/shard_map/ppermute | solution.py:34
  47.3 0.9 copy-done.7
  48.2 0.7 pad_add_fusion.place_ref
  48.9 1.8 %slice.126 = bf16[256,896]{1,0:T(8,128)(2,1)} slice(bf16[512,896]{1,0:T(8,128)(2,1)} %collective-permute-done.refs_15_.refs_16_), slice={[256:512], [0:896]} | slice | bytes 917504 | tf_op jit(solution)/shard_map/slice | solution.py:368
  50.7 8.8 %own_block.1 = (f32[2,384,256]{2,1,0:T(8,128)}, f32[384,128]{1,0:T(8,128)}, f32[8,512]{1,0:T(8,128)}) custom-call(s32[2]{0:T(128)} %pad_add_fusion.place_ref, bf16[384,1792]{1,0:T(8,128)(2,1)} %refs_0_.5, bf16[384,1792]{1,0:T(8,128)(2,1)} %copy-done.1, bf16[384,896]{1,0:T(8,128)(2,1)} %collective-permute-done.1.refs_2_, bf16[512,896]{1,0:T(8,128)(2,1)} %refs_6_.1, ...), custom_call_target="tpu_custom_call" | custom-call | flops 1000 | bytes 1000 | tf_op jit(solution)/shard_map/own_block/pallas_call | solution.py:145
  59.5 4.7 %collective-permute-done.13.refs_16_.refs_17_ = bf16[512,896]{1,0:T(8,128)(2,1)} collective-permute-done((bf16[512,896]{1,0:T(8,128)(2,1)}, bf16[512,896]{1,0:T(8,128)(2,1)}, u32[]{:S(2)}, u32[]{:S(2)}) %collective-permute-start.13) | collective-permute-done | bytes 917536 | tf_op jit(solution)/shard_map/ppermute | solution.py:43
  64.2 1.1 collective-permute-done.14.refs_17_.refs_18_
  65.3 0.5 collective-permute-start.18
  65.8 1.5 collective-permute-start.21
  67.3 3.2 %collective-permute-start.20 = (bf16[256,896]{1,0:T(8,128)(2,1)S(1)}, bf16[256,896]{1,0:T(8,128)(2,1)S(1)}, u32[]{:S(2)}, u32[]{:S(2)}) collective-permute-start(bf16[256,896]{1,0:T(8,128)(2,1)S(1)} %copy-done.9), channel_id=1, source_target_pairs={{0,1},{1,0},{2,3},{3,2},{4,5},{5,4},{6,7},{7,6},{8,9},{9,8},{10,11... | collective-permute-start | bytes 1376264 | tf_op jit(solution)/shard_map/ppermute | solution.py:34
  70.5 0.9 copy-done.13
  71.8 11.1 %end_block.1 = (f32[2,384,256]{2,1,0:T(8,128)}, f32[2,384,256]{2,1,0:T(8,128)}, f32[384,128]{1,0:T(8,128)}, f32[8,512]{1,0:T(8,128)}) custom-call(s32[2]{0:T(128)} %pad_add_fusion.place_ref, f32[2,384,256]{2,1,0:T(8,128)} %get-tuple-element.50.cross_in, f32[384,128]{1,0:T(8,128)} %get-tuple-element.51.norm_in, bf16[384,1792]{1,0:T(8,128)(2,1)} %refs_0_.5, ...), custom_call_target="tpu_custom_call" | custom-call | flops 1000 | bytes 1000 | tf_op jit(solution)/shard_map/end_block/pallas_call | solution.py:145
  83.5 1.3 collective-permute-done.23.refs_25_
  84.8 0.7 collective-permute-done.22.refs_24_
  85.6 0.6 copy-done.19
  86.2 9.2 %last_block.1 = (f32[384,1024]{1,0:T(8,128)}, f32[72,512]{1,0:T(8,128)}, f32[72,512]{1,0:T(8,128)}) custom-call(s32[2]{0:T(128)} %pad_add_fusion.place_ref, f32[2,384,256]{2,1,0:T(8,128)} %get-tuple-element.58.cross_own_in, f32[2,384,256]{2,1,0:T(8,128)} %get-tuple-element.59.cross_end_in, f32[384,128]{1,0:T(8,128)} %get-tuple-element.60.row_norm_in, ...), custom_call_target="tpu_custom_call" | custom-call | flops 1000 | bytes 1000 | tf_op jit(solution)/shard_map/last_block/pallas_call | solution.py:145
  95.7 1.4 collective-permute-done.24
  97.1 0.9 add.110
  98.1 1.1 collective-permute-start.25
  99.1 1.2 collective-permute-start.26
  100.3 1.3 collective-permute-start.27
  101.6 3.2 %collective-permute-done.25 = f32[72,512]{1,0:T(8,128)S(1)} collective-permute-done((f32[72,512]{1,0:T(8,128)S(1)}, f32[72,512]{1,0:T(8,128)S(1)}, u32[]{:S(2)}, u32[]{:S(2)}) %collective-permute-start.25) | collective-permute-done | bytes 147488 | tf_op jit(solution)/shard_map/ppermute | solution.py:43
  104.8 3.1 %collective-permute-done.26 = f32[72,512]{1,0:T(8,128)S(1)} collective-permute-done((f32[72,512]{1,0:T(8,128)S(1)}, f32[72,512]{1,0:T(8,128)S(1)}, u32[]{:S(2)}, u32[]{:S(2)}) %collective-permute-start.26) | collective-permute-done | bytes 147488 | tf_op jit(solution)/shard_map/ppermute | solution.py:43
  108.1 1.3 collective-permute-done.28
  109.6 1.6 %fusion.27 = f32[64,384]{1,0:T(8,128)S(1)} fusion(f32[64,1024]{1,0:T(8,128)S(1)} %get-tuple-element.78, f32[384,1024]{1,0:T(8,128)S(1)} %copy-done), kind=kOutput, calls=%fused_computation.88 | convolution fusion | flops 301989888 | bytes 1933312 | tf_op jit(solution)/shard_map/dot_general | solution.py:25
  111.5 1.2 collective-permute-done.29
  112.6 1.0 fusion.11
  114.1 1.2 collective-permute-done.30
  115.3 1.1 collective-permute-start.31
  116.4 0.8 collective-permute-start.32
  117.2 1.7 %collective-permute-start.33 = (f32[72,512]{1,0:T(8,128)S(1)}, f32[72,512]{1,0:T(8,128)S(1)}, u32[]{:S(2)}, u32[]{:S(2)}) collective-permute-start(f32[72,512]{1,0:T(8,128)S(1)} %select_add_fusion), channel_id=1, source_target_pairs={{0,24},{4,28},{8,16},{12,20},{16,8},{20,12},{24,0},{28,4},{1,25},{... | collective-permute-start | bytes 442376 | tf_op jit(solution)/shard_map/ppermute | solution.py:43
  118.9 3.2 %collective-permute-done.31 = f32[72,512]{1,0:T(8,128)S(1)} collective-permute-done((f32[72,512]{1,0:T(8,128)S(1)}, f32[72,512]{1,0:T(8,128)S(1)}, u32[]{:S(2)}, u32[]{:S(2)}) %collective-permute-start.31) | collective-permute-done | bytes 147488 | tf_op jit(solution)/shard_map/ppermute | solution.py:43
  122.1 0.7 collective-permute-done.32
  122.8 2.4 %collective-permute-done.33 = f32[72,512]{1,0:T(8,128)S(1)} collective-permute-done((f32[72,512]{1,0:T(8,128)S(1)}, f32[72,512]{1,0:T(8,128)S(1)}, u32[]{:S(2)}, u32[]{:S(2)}) %collective-permute-start.33) | collective-permute-done | bytes 147488 | tf_op jit(solution)/shard_map/ppermute | solution.py:43
  125.3 1.3 collective-permute-done.34
  127.0 1.6 %fusion.24 = f32[64,384]{1,0:T(8,128)S(1)} fusion(f32[384,1024]{1,0:T(8,128)S(1)} %copy-done, f32[64,1024]{1,0:T(8,128)S(1)} %get-tuple-element.77, f32[1024]{0:T(1024)S(1)} %bitcast.27), kind=kOutput, calls=%fused_computation.86 | convolution fusion | flops 302055424 | bytes 1937408 | tf_op jit(solution)/shard_map/dot_general | solution.py:25
  128.9 7.4 %collective-permute-start.35 = (f32[128,512]{1,0:T(8,128)S(1)}, f32[128,512]{1,0:T(8,128)S(1)}, u32[]{:S(2)}, u32[]{:S(2)}) collective-permute-start(f32[128,512]{1,0:T(8,128)S(1)} %pad_maximum_fusion), channel_id=1, source_target_pairs={{0,1},{1,0},{2,3},{3,2},{4,5},{5,4},{6,7},{7,6},{8,9},{9,8},{10,11... | collective-permute-start | bytes 786440 | tf_op jit(solution)/shard_map/ppermute | solution.py:34
  136.3 1.1 fusion.14
  137.9 1.2 collective-permute-done.38
  139.2 3.3 %collective-permute-start.39 = (f32[72,256]{1,0:T(8,128)S(1)}, f32[72,256]{1,0:T(8,128)S(1)}, u32[]{:S(2)}, u32[]{:S(2)}) collective-permute-start(f32[72,256]{1,0:T(8,128)S(1)} %slice.180), channel_id=1, source_target_pairs={{0,1},{1,0},{2,3},{3,2},{4,5},{5,4},{6,7},{7,6},{8,9},{9,8},{10,11... | collective-permute-start | bytes 221192 | tf_op jit(solution)/shard_map/ppermute | solution.py:34
  142.7 2.5 %collective-permute-done.39 = f32[72,256]{1,0:T(8,128)S(1)} collective-permute-done((f32[72,256]{1,0:T(8,128)S(1)}, f32[72,256]{1,0:T(8,128)S(1)}, u32[]{:S(2)}, u32[]{:S(2)}) %collective-permute-start.39) | collective-permute-done | bytes 73760 | tf_op jit(solution)/shard_map/ppermute | solution.py:34
  145.2 1.5 collective-permute-start.40
  146.7 0.8 collective-permute-start.41
  147.5 1.3 collective-permute-start.42
  148.8 0.8 collective-permute-done.40
  149.6 2.1 %collective-permute-done.41 = f32[72,256]{1,0:T(8,128)S(1)} collective-permute-done((f32[72,256]{1,0:T(8,128)S(1)}, f32[72,256]{1,0:T(8,128)S(1)}, u32[]{:S(2)}, u32[]{:S(2)}) %collective-permute-start.41) | collective-permute-done | bytes 73760 | tf_op jit(solution)/shard_map/ppermute | solution.py:43
  151.7 1.0 collective-permute-done.42
  152.9 1.2 collective-permute-done.43
  154.1 0.8 fusion.9
  (116 shorter events, 4.0 us)
Async XLA Ops:
  0.6 23.8 %collective-permute-start = (bf16[512,896]{1,0:T(8,128)(2,1)}, bf16[512,896]{1,0:T(8,128)(2,1)}, u32[]{:S(2)}, u32[]{:S(2)}) collective-permute-start(bf16[512,896]{1,0:T(8,128)(2,1)} %refs_6_.1), channel_id=1, source_target_pairs={{0,1},{1,0},{2,3},{3,2},{4,5},{5,4},{6,7},{7,6},{8,9},{9,8},{10,11... | collective-permute-start | bytes 2752520 | tf_op jit(solution)/shard_map/ppermute | solution.py:34
  3.7 22.4 %collective-permute-start.3 = (bf16[512,896]{1,0:T(8,128)(2,1)}, bf16[512,896]{1,0:T(8,128)(2,1)S(1)}, u32[]{:S(2)}, u32[]{:S(2)}) collective-permute-start(bf16[512,896]{1,0:T(8,128)(2,1)} %refs_6_.1), channel_id=1, source_target_pairs={{0,8},{4,12},{8,0},{12,4},{16,24},{20,28},{24,16},{28,20},{1,9},{5... | collective-permute-start | bytes 2752520 | tf_op jit(solution)/shard_map/ppermute | solution.py:43
  5.2 21.7 %collective-permute-start.4 = (bf16[512,896]{1,0:T(8,128)(2,1)}, bf16[512,896]{1,0:T(8,128)(2,1)S(1)}, u32[]{:S(2)}, u32[]{:S(2)}) collective-permute-start(bf16[512,896]{1,0:T(8,128)(2,1)} %refs_6_.1), channel_id=1, source_target_pairs={{0,16},{4,20},{8,24},{12,28},{16,0},{20,4},{24,8},{28,12},{1,17},{... | collective-permute-start | bytes 2752520 | tf_op jit(solution)/shard_map/ppermute | solution.py:43
  6.7 33.0 %collective-permute-start.2 = (bf16[384,1792]{1,0:T(8,128)(2,1)}, bf16[384,1792]{1,0:T(8,128)(2,1)S(1)}, u32[]{:S(2)}, u32[]{:S(2)}) collective-permute-start(bf16[384,1792]{1,0:T(8,128)(2,1)} %refs_0_.5), channel_id=1, source_target_pairs={{0,4},{1,2},{2,1},{3,7},{4,0},{5,6},{6,5},{7,3},{8,12},{9,10},{10,... | collective-permute-start | bytes 4128776 | tf_op jit(solution)/shard_map/ppermute | solution.py:39
  9.0 20.4 %copy-start.4 = (bf16[512,896]{1,0:T(8,128)(2,1)S(1)}, bf16[512,896]{1,0:T(8,128)(2,1)}, u32[]{:S(2)}) copy-start(bf16[512,896]{1,0:T(8,128)(2,1)} %refs_6_.1) | copy-start | bytes 2752516
  24.4 16.7 %collective-permute-start.1 = (bf16[384,896]{1,0:T(8,128)(2,1)S(1)}, bf16[384,896]{1,0:T(8,128)(2,1)}, u32[]{:S(2)}, u32[]{:S(2)}) collective-permute-start(bf16[384,896]{1,0:T(8,128)(2,1)S(1)} %get-tuple-element.42), channel_id=1, source_target_pairs={{0,1},{1,0},{2,3},{3,2},{4,5},{5,4},{6,7},{7,6},{8,9},{9,8},{10,11... | collective-permute-start | bytes 2064392 | tf_op jit(solution)/shard_map/ppermute | solution.py:34
  26.1 24.6 %copy-start.2 = (bf16[512,896]{1,0:T(8,128)(2,1)}, bf16[512,896]{1,0:T(8,128)(2,1)S(1)}, u32[]{:S(2)}) copy-start(bf16[512,896]{1,0:T(8,128)(2,1)S(1)} %collective-permute-done.3.refs_4_.refs_6_.refs_7_) | copy-start | bytes 2752516
  27.0 23.8 %copy-start.3 = (bf16[512,896]{1,0:T(8,128)(2,1)}, bf16[512,896]{1,0:T(8,128)(2,1)S(1)}, u32[]{:S(2)}) copy-start(bf16[512,896]{1,0:T(8,128)(2,1)S(1)} %collective-permute-done.4.refs_5_.refs_7_.refs_8_) | copy-start | bytes 2752516
  27.0 10.8 %collective-permute-start.5 = (bf16[256,896]{1,0:T(8,128)(2,1)S(1)}, bf16[256,896]{1,0:T(8,128)(2,1)S(1)}, u32[]{:S(2)}, u32[]{:S(2)}) collective-permute-start(bf16[256,896]{1,0:T(8,128)(2,1)S(1)} %slice.124), channel_id=1, source_target_pairs={{0,16},{4,20},{8,24},{12,28},{16,0},{20,4},{24,8},{28,12},{1,17},{... | collective-permute-start | bytes 1376264 | tf_op jit(solution)/shard_map/ppermute | solution.py:43
  28.6 10.6 %collective-permute-start.6 = (bf16[256,896]{1,0:T(8,128)(2,1)S(1)}, bf16[256,896]{1,0:T(8,128)(2,1)S(1)}, u32[]{:S(2)}, u32[]{:S(2)}) collective-permute-start(bf16[256,896]{1,0:T(8,128)(2,1)S(1)} %slice.125), channel_id=1, source_target_pairs={{0,8},{4,12},{8,0},{12,4},{16,24},{20,28},{24,16},{28,20},{1,9},{5... | collective-permute-start | bytes 1376264 | tf_op jit(solution)/shard_map/ppermute | solution.py:43
  29.4 14.7 %collective-permute-start.7 = (bf16[512,896]{1,0:T(8,128)(2,1)S(1)}, bf16[512,896]{1,0:T(8,128)(2,1)S(1)}, u32[]{:S(2)}, u32[]{:S(2)}) collective-permute-start(bf16[512,896]{1,0:T(8,128)(2,1)S(1)} %copy-done.4), channel_id=1, source_target_pairs={{0,4},{4,0},{8,12},{12,8},{16,20},{20,16},{24,28},{28,24},{1,5},{5... | collective-permute-start | bytes 2752520 | tf_op jit(solution)/shard_map/ppermute | solution.py:43
  37.8 9.5 %copy-start.8 = (bf16[256,896]{1,0:T(8,128)(2,1)}, bf16[256,896]{1,0:T(8,128)(2,1)S(1)}, u32[]{:S(2)}) copy-start(bf16[256,896]{1,0:T(8,128)(2,1)S(1)} %collective-permute-done.5.refs_6_.refs_8_.refs_9_) | copy-start | bytes 1376260
  39.2 8.1 %copy-start.10 = (bf16[256,896]{1,0:T(8,128)(2,1)}, bf16[256,896]{1,0:T(8,128)(2,1)S(1)}, u32[]{:S(2)}) copy-start(bf16[256,896]{1,0:T(8,128)(2,1)S(1)} %collective-permute-done.6.refs_7_.refs_9_.refs_10_) | copy-start | bytes 1376260
  39.2 1.9 %collective-permute-start.10 = (bf16[256,896]{1,0:T(8,128)(2,1)S(1)}, bf16[256,896]{1,0:T(8,128)(2,1)S(1)}, u32[]{:S(2)}, u32[]{:S(2)}) collective-permute-start(bf16[256,896]{1,0:T(8,128)(2,1)S(1)} %collective-permute-done.5.refs_6_.refs_8_.refs_9_), channel_id=1, source_target_pairs={{0,4},{4,0},{8,12},{12,8},{16,20},{20,16},{24,28},{28,24},{1,5},{5... | collective-permute-start | bytes 1376264 | tf_op jit(solution)/shard_map/ppermute | solution.py:43
  39.2 3.3 %collective-permute-start.11 = (bf16[256,896]{1,0:T(8,128)(2,1)S(1)}, bf16[256,896]{1,0:T(8,128)(2,1)S(1)}, u32[]{:S(2)}, u32[]{:S(2)}) collective-permute-start(bf16[256,896]{1,0:T(8,128)(2,1)S(1)} %collective-permute-done.6.refs_7_.refs_9_.refs_10_), channel_id=1, source_target_pairs={{0,4},{4,0},{8,12},{12,8},{16,20},{20,16},{24,28},{28,24},{1,5},{5... | collective-permute-start | bytes 1376264 | tf_op jit(solution)/shard_map/ppermute | solution.py:43
  39.7 11.0 %copy-start.1 = (bf16[384,1792]{1,0:T(8,128)(2,1)}, bf16[384,1792]{1,0:T(8,128)(2,1)S(1)}, u32[]{:S(2)}) copy-start(bf16[384,1792]{1,0:T(8,128)(2,1)S(1)} %collective-permute-done.2.refs_1_) | copy-start | bytes 4128772
  39.7 4.4 %collective-permute-start.8 = (bf16[512,896]{1,0:T(8,128)(2,1)S(1)}, bf16[512,896]{1,0:T(8,128)(2,1)S(1)}, u32[]{:S(2)}, u32[]{:S(2)}) collective-permute-start(bf16[512,896]{1,0:T(8,128)(2,1)S(1)} %collective-permute-done.3.refs_4_.refs_6_.refs_7_), channel_id=1, source_target_pairs={{0,4},{4,0},{8,12},{12,8},{16,20},{20,16},{24,28},{28,24},{1,5},{5... | collective-permute-start | bytes 2752520 | tf_op jit(solution)/shard_map/ppermute | solution.py:43
  41.1 6.1 %collective-permute-start.9 = (bf16[512,896]{1,0:T(8,128)(2,1)S(1)}, bf16[512,896]{1,0:T(8,128)(2,1)S(1)}, u32[]{:S(2)}, u32[]{:S(2)}) collective-permute-start(bf16[512,896]{1,0:T(8,128)(2,1)S(1)} %collective-permute-done.4.refs_5_.refs_7_.refs_8_), channel_id=1, source_target_pairs={{0,4},{4,0},{8,12},{12,8},{16,20},{20,16},{24,28},{28,24},{1,5},{5... | collective-permute-start | bytes 2752520 | tf_op jit(solution)/shard_map/ppermute | solution.py:43
  41.1 6.2 %copy-start.11 = (bf16[256,896]{1,0:T(8,128)(2,1)}, bf16[256,896]{1,0:T(8,128)(2,1)S(1)}, u32[]{:S(2)}) copy-start(bf16[256,896]{1,0:T(8,128)(2,1)S(1)} %collective-permute-done.10.refs_11_.refs_13_.refs_14_) | copy-start | bytes 1376260
  41.1 23.1 %collective-permute-start.13 = (bf16[512,896]{1,0:T(8,128)(2,1)}, bf16[512,896]{1,0:T(8,128)(2,1)}, u32[]{:S(2)}, u32[]{:S(2)}) collective-permute-start(bf16[512,896]{1,0:T(8,128)(2,1)} %collective-permute-done.refs_15_.refs_16_), channel_id=1, source_target_pairs={{0,8},{4,12},{8,0},{12,4},{16,24},{20,28},{24,16},{28,20},{1,9},{5... | collective-permute-start | bytes 2752520 | tf_op jit(solution)/shard_map/ppermute | solution.py:43
  42.5 4.8 %copy-start.12 = (bf16[256,896]{1,0:T(8,128)(2,1)}, bf16[256,896]{1,0:T(8,128)(2,1)S(1)}, u32[]{:S(2)}) copy-start(bf16[256,896]{1,0:T(8,128)(2,1)S(1)} %collective-permute-done.11.refs_12_.refs_14_.refs_15_) | copy-start | bytes 1376260
  42.5 22.7 %collective-permute-start.14 = (bf16[512,896]{1,0:T(8,128)(2,1)}, bf16[512,896]{1,0:T(8,128)(2,1)}, u32[]{:S(2)}, u32[]{:S(2)}) collective-permute-start(bf16[512,896]{1,0:T(8,128)(2,1)} %collective-permute-done.refs_15_.refs_16_), channel_id=1, source_target_pairs={{0,16},{4,20},{8,24},{12,28},{16,0},{20,4},{24,8},{28,12},{1,17},{... | collective-permute-start | bytes 2752520 | tf_op jit(solution)/shard_map/ppermute | solution.py:43
  44.1 3.2 %copy-start.5 = (bf16[512,896]{1,0:T(8,128)(2,1)}, bf16[512,896]{1,0:T(8,128)(2,1)S(1)}, u32[]{:S(2)}) copy-start(bf16[512,896]{1,0:T(8,128)(2,1)S(1)} %collective-permute-done.7.refs_8_.refs_10_.refs_11_) | copy-start | bytes 2752516
  44.1 21.2 %collective-permute-start.15 = (bf16[384,896]{1,0:T(8,128)(2,1)}, bf16[384,896]{1,0:T(8,128)(2,1)}, u32[]{:S(2)}, u32[]{:S(2)}) collective-permute-start(bf16[384,896]{1,0:T(8,128)(2,1)} %collective-permute-done.1.refs_2_), channel_id=1, source_target_pairs={{0,4},{1,2},{2,1},{3,7},{4,0},{5,6},{6,5},{7,3},{8,12},{9,10},{10,... | collective-permute-start | bytes 2064392 | tf_op jit(solution)/shard_map/ppermute | solution.py:39
  44.1 3.3 %copy-start.6 = (bf16[512,896]{1,0:T(8,128)(2,1)}, bf16[512,896]{1,0:T(8,128)(2,1)S(1)}, u32[]{:S(2)}) copy-start(bf16[512,896]{1,0:T(8,128)(2,1)S(1)} %collective-permute-done.8.refs_9_.refs_11_.refs_12_) | copy-start | bytes 2752516
  44.1 21.7 %collective-permute-start.12 = (bf16[384,896]{1,0:T(8,128)(2,1)}, bf16[384,896]{1,0:T(8,128)(2,1)}, u32[]{:S(2)}, u32[]{:S(2)}) collective-permute-start(bf16[384,896]{1,0:T(8,128)(2,1)} %get-tuple-element.52), channel_id=1, source_target_pairs={{0,1},{1,0},{2,3},{3,2},{4,5},{5,4},{6,7},{7,6},{8,9},{9,8},{10,11... | collective-permute-start | bytes 2064392 | tf_op jit(solution)/shard_map/ppermute | solution.py:34
  47.2 1.0 copy-start.7
  47.2 20.1 %collective-permute-start.16 = (bf16[512,896]{1,0:T(8,128)(2,1)}, bf16[512,896]{1,0:T(8,128)(2,1)}, u32[]{:S(2)}, u32[]{:S(2)}) collective-permute-start(bf16[512,896]{1,0:T(8,128)(2,1)} %collective-permute-done.refs_15_.refs_16_), channel_id=1, source_target_pairs={{0,4},{4,0},{8,12},{12,8},{16,20},{20,16},{24,28},{28,24},{1,5},{5... | collective-permute-start | bytes 2752520 | tf_op jit(solution)/shard_map/ppermute | solution.py:43
  50.7 16.6 %copy-start.9 = (bf16[256,896]{1,0:T(8,128)(2,1)S(1)}, bf16[256,896]{1,0:T(8,128)(2,1)}, u32[]{:S(2)}) copy-start(bf16[256,896]{1,0:T(8,128)(2,1)} %copy-done.8) | copy-start | bytes 1376260
  65.3 5.2 %collective-permute-start.17 = (bf16[512,896]{1,0:T(8,128)(2,1)}, bf16[512,896]{1,0:T(8,128)(2,1)S(1)}, u32[]{:S(2)}, u32[]{:S(2)}) collective-permute-start(bf16[512,896]{1,0:T(8,128)(2,1)} %collective-permute-done.13.refs_16_.refs_17_), channel_id=1, source_target_pairs={{0,4},{4,0},{8,12},{12,8},{16,20},{20,16},{24,28},{28,24},{1,5},{5... | collective-permute-start | bytes 2752520 | tf_op jit(solution)/shard_map/ppermute | solution.py:43
  65.3 5.2 %collective-permute-start.18 = (bf16[512,896]{1,0:T(8,128)(2,1)}, bf16[512,896]{1,0:T(8,128)(2,1)S(1)}, u32[]{:S(2)}, u32[]{:S(2)}) collective-permute-start(bf16[512,896]{1,0:T(8,128)(2,1)} %collective-permute-done.14.refs_17_.refs_18_), channel_id=1, source_target_pairs={{0,4},{4,0},{8,12},{12,8},{16,20},{20,16},{24,28},{28,24},{1,5},{5... | collective-permute-start | bytes 2752520 | tf_op jit(solution)/shard_map/ppermute | solution.py:43
  65.8 17.1 %collective-permute-start.19 = (bf16[384,896]{1,0:T(8,128)(2,1)}, bf16[384,896]{1,0:T(8,128)(2,1)S(1)}, u32[]{:S(2)}, u32[]{:S(2)}) collective-permute-start(bf16[384,896]{1,0:T(8,128)(2,1)} %collective-permute-done.12.refs_3_), channel_id=1, source_target_pairs={{0,4},{1,2},{2,1},{3,7},{4,0},{5,6},{6,5},{7,3},{8,12},{9,10},{10,... | collective-permute-start | bytes 2064392 | tf_op jit(solution)/shard_map/ppermute | solution.py:39
  65.8 17.1 %collective-permute-start.21 = (bf16[256,896]{1,0:T(8,128)(2,1)}, bf16[256,896]{1,0:T(8,128)(2,1)S(1)}, u32[]{:S(2)}, u32[]{:S(2)}) collective-permute-start(bf16[256,896]{1,0:T(8,128)(2,1)} %slice.126), channel_id=1, source_target_pairs={{0,24},{4,28},{8,16},{12,20},{16,8},{20,12},{24,0},{28,4},{1,25},{... | collective-permute-start | bytes 1376264 | tf_op jit(solution)/shard_map/ppermute | solution.py:43
  67.3 15.7 %collective-permute-start.20 = (bf16[256,896]{1,0:T(8,128)(2,1)S(1)}, bf16[256,896]{1,0:T(8,128)(2,1)S(1)}, u32[]{:S(2)}, u32[]{:S(2)}) collective-permute-start(bf16[256,896]{1,0:T(8,128)(2,1)S(1)} %copy-done.9), channel_id=1, source_target_pairs={{0,1},{1,0},{2,3},{3,2},{4,5},{5,4},{6,7},{7,6},{8,9},{9,8},{10,11... | collective-permute-start | bytes 1376264 | tf_op jit(solution)/shard_map/ppermute | solution.py:34
  70.4 0.9 copy-start.13
  70.4 1.3 copy-start.14
  82.9 2.6 %copy-start.16 = (bf16[256,896]{1,0:T(8,128)(2,1)}, bf16[256,896]{1,0:T(8,128)(2,1)S(1)}, u32[]{:S(2)}) copy-start(bf16[256,896]{1,0:T(8,128)(2,1)S(1)} %collective-permute-done.21.refs_23_) | copy-start | bytes 1376260
  82.9 2.6 %copy-start.15 = (bf16[384,896]{1,0:T(8,128)(2,1)}, bf16[384,896]{1,0:T(8,128)(2,1)S(1)}, u32[]{:S(2)}) copy-start(bf16[384,896]{1,0:T(8,128)(2,1)S(1)} %collective-permute-done.19.refs_5_) | copy-start | bytes 2064388
  82.9 1.9 %collective-permute-start.23 = (bf16[256,896]{1,0:T(8,128)(2,1)S(1)}, bf16[256,896]{1,0:T(8,128)(2,1)S(1)}, u32[]{:S(2)}, u32[]{:S(2)}) collective-permute-start(bf16[256,896]{1,0:T(8,128)(2,1)S(1)} %collective-permute-done.21.refs_23_), channel_id=1, source_target_pairs={{0,4},{4,0},{8,12},{12,8},{16,20},{20,16},{24,28},{28,24},{1,5},{5... | collective-permute-start | bytes 1376264 | tf_op jit(solution)/shard_map/ppermute | solution.py:43
  83.0 2.5 %copy-start.17 = (bf16[256,896]{1,0:T(8,128)(2,1)}, bf16[256,896]{1,0:T(8,128)(2,1)S(1)}, u32[]{:S(2)}) copy-start(bf16[256,896]{1,0:T(8,128)(2,1)S(1)} %collective-permute-done.20.refs_22_) | copy-start | bytes 1376260
  83.0 2.4 %collective-permute-start.22 = (bf16[256,896]{1,0:T(8,128)(2,1)S(1)}, bf16[256,896]{1,0:T(8,128)(2,1)S(1)}, u32[]{:S(2)}, u32[]{:S(2)}) collective-permute-start(bf16[256,896]{1,0:T(8,128)(2,1)S(1)} %collective-permute-done.20.refs_22_), channel_id=1, source_target_pairs={{0,4},{4,0},{8,12},{12,8},{16,20},{20,16},{24,28},{28,24},{1,5},{5... | collective-permute-start | bytes 1376264 | tf_op jit(solution)/shard_map/ppermute | solution.py:43
  84.8 0.8 copy-start.18
  85.4 0.8 copy-start.19
  95.5 14.1 %copy-start = (f32[384,1024]{1,0:T(8,128)S(1)}, f32[384,1024]{1,0:T(8,128)}, u32[]{:S(2)}) copy-start(f32[384,1024]{1,0:T(8,128)} %get-tuple-element.69) | copy-start | bytes 4718596
  95.5 1.6 %collective-permute-start.24 = (f32[72,512]{1,0:T(8,128)}, f32[72,512]{1,0:T(8,128)S(1)}, u32[]{:S(2)}, u32[]{:S(2)}) collective-permute-start(f32[72,512]{1,0:T(8,128)} %get-tuple-element.68), channel_id=1, source_target_pairs={{0,4},{4,0},{8,12},{12,8},{16,20},{20,16},{24,28},{28,24},{1,5},{5... | collective-permute-start | bytes 442376 | tf_op jit(solution)/shard_map/ppermute | solution.py:43
  98.1 6.8 %collective-permute-start.25 = (f32[72,512]{1,0:T(8,128)S(1)}, f32[72,512]{1,0:T(8,128)S(1)}, u32[]{:S(2)}, u32[]{:S(2)}) collective-permute-start(f32[72,512]{1,0:T(8,128)S(1)} %add.110), channel_id=1, source_target_pairs={{0,8},{4,12},{8,0},{12,4},{16,24},{20,28},{24,16},{28,20},{1,9},{5... | collective-permute-start | bytes 442376 | tf_op jit(solution)/shard_map/ppermute | solution.py:43
  99.1 8.8 %collective-permute-start.26 = (f32[72,512]{1,0:T(8,128)S(1)}, f32[72,512]{1,0:T(8,128)S(1)}, u32[]{:S(2)}, u32[]{:S(2)}) collective-permute-start(f32[72,512]{1,0:T(8,128)S(1)} %add.110), channel_id=1, source_target_pairs={{0,16},{4,20},{8,24},{12,28},{16,0},{20,4},{24,8},{28,12},{1,17},{... | collective-permute-start | bytes 442376 | tf_op jit(solution)/shard_map/ppermute | solution.py:43
  100.3 7.6 %collective-permute-start.27 = (f32[72,512]{1,0:T(8,128)S(1)}, f32[72,512]{1,0:T(8,128)S(1)}, u32[]{:S(2)}, u32[]{:S(2)}) collective-permute-start(f32[72,512]{1,0:T(8,128)S(1)} %add.110), channel_id=1, source_target_pairs={{0,24},{4,28},{8,16},{12,20},{16,8},{20,12},{24,0},{28,4},{1,25},{... | collective-permute-start | bytes 442376 | tf_op jit(solution)/shard_map/ppermute | solution.py:43
  108.0 1.4 collective-permute-start.28
  111.2 1.4 collective-permute-start.29
  113.9 1.4 collective-permute-start.30
  115.3 6.8 %collective-permute-start.31 = (f32[72,512]{1,0:T(8,128)S(1)}, f32[72,512]{1,0:T(8,128)S(1)}, u32[]{:S(2)}, u32[]{:S(2)}) collective-permute-start(f32[72,512]{1,0:T(8,128)S(1)} %select_add_fusion), channel_id=1, source_target_pairs={{0,8},{4,12},{8,0},{12,4},{16,24},{20,28},{24,16},{28,20},{1,9},{5... | collective-permute-start | bytes 442376 | tf_op jit(solution)/shard_map/ppermute | solution.py:43
  116.4 6.4 %collective-permute-start.32 = (f32[72,512]{1,0:T(8,128)S(1)}, f32[72,512]{1,0:T(8,128)S(1)}, u32[]{:S(2)}, u32[]{:S(2)}) collective-permute-start(f32[72,512]{1,0:T(8,128)S(1)} %select_add_fusion), channel_id=1, source_target_pairs={{0,16},{4,20},{8,24},{12,28},{16,0},{20,4},{24,8},{28,12},{1,17},{... | collective-permute-start | bytes 442376 | tf_op jit(solution)/shard_map/ppermute | solution.py:43
  117.2 8.0 %collective-permute-start.33 = (f32[72,512]{1,0:T(8,128)S(1)}, f32[72,512]{1,0:T(8,128)S(1)}, u32[]{:S(2)}, u32[]{:S(2)}) collective-permute-start(f32[72,512]{1,0:T(8,128)S(1)} %select_add_fusion), channel_id=1, source_target_pairs={{0,24},{4,28},{8,16},{12,20},{16,8},{20,12},{24,0},{28,4},{1,25},{... | collective-permute-start | bytes 442376 | tf_op jit(solution)/shard_map/ppermute | solution.py:43
  125.2 1.4 collective-permute-start.34
  128.6 7.7 %collective-permute-start.36 = (f32[72,384]{1,0:T(8,128)S(1)}, f32[72,384]{1,0:T(8,128)S(1)}, u32[]{:S(2)}, u32[]{:S(2)}) collective-permute-start(f32[72,384]{1,0:T(8,128)S(1)} %pad_maximum_fusion.5), channel_id=1, source_target_pairs={{0,4},{1,2},{2,1},{3,7},{4,0},{5,6},{6,5},{7,3},{8,12},{9,10},{10,... | collective-permute-start | bytes 331784 | tf_op jit(solution)/shard_map/ppermute | solution.py:39
  128.9 24.0 %collective-permute-start.35 = (f32[128,512]{1,0:T(8,128)S(1)}, f32[128,512]{1,0:T(8,128)S(1)}, u32[]{:S(2)}, u32[]{:S(2)}) collective-permute-start(f32[128,512]{1,0:T(8,128)S(1)} %pad_maximum_fusion), channel_id=1, source_target_pairs={{0,1},{1,0},{2,3},{3,2},{4,5},{5,4},{6,7},{7,6},{8,9},{9,8},{10,11... | collective-permute-start | bytes 786440 | tf_op jit(solution)/shard_map/ppermute | solution.py:34
  137.7 1.4 collective-permute-start.38
  139.2 6.0 %collective-permute-start.39 = (f32[72,256]{1,0:T(8,128)S(1)}, f32[72,256]{1,0:T(8,128)S(1)}, u32[]{:S(2)}, u32[]{:S(2)}) collective-permute-start(f32[72,256]{1,0:T(8,128)S(1)} %slice.180), channel_id=1, source_target_pairs={{0,1},{1,0},{2,3},{3,2},{4,5},{5,4},{6,7},{7,6},{8,9},{9,8},{10,11... | collective-permute-start | bytes 221192 | tf_op jit(solution)/shard_map/ppermute | solution.py:34
  142.6 6.2 %collective-permute-start.37 = (f32[72,512]{1,0:T(8,128)S(1)}, f32[72,512]{1,0:T(8,128)S(1)}, u32[]{:S(2)}, u32[]{:S(2)}) collective-permute-start(f32[72,512]{1,0:T(8,128)S(1)} %slice.172), channel_id=1, source_target_pairs={{0,1},{1,0},{2,3},{3,2},{4,5},{5,4},{6,7},{7,6},{8,9},{9,8},{10,11... | collective-permute-start | bytes 442376 | tf_op jit(solution)/shard_map/ppermute | solution.py:34
  145.2 4.4 %collective-permute-start.40 = (f32[72,256]{1,0:T(8,128)S(1)}, f32[72,256]{1,0:T(8,128)S(1)}, u32[]{:S(2)}, u32[]{:S(2)}) collective-permute-start(f32[72,256]{1,0:T(8,128)S(1)} %slice_select_fusion.2), channel_id=1, source_target_pairs={{0,8},{4,12},{8,0},{12,4},{16,24},{20,28},{24,16},{28,20},{1,9},{5... | collective-permute-start | bytes 221192 | tf_op jit(solution)/shard_map/ppermute | solution.py:43
  146.7 5.0 %collective-permute-start.41 = (f32[72,256]{1,0:T(8,128)S(1)}, f32[72,256]{1,0:T(8,128)S(1)}, u32[]{:S(2)}, u32[]{:S(2)}) collective-permute-start(f32[72,256]{1,0:T(8,128)S(1)} %slice_select_fusion.2), channel_id=1, source_target_pairs={{0,16},{4,20},{8,24},{12,28},{16,0},{20,4},{24,8},{28,12},{1,17},{... | collective-permute-start | bytes 221192 | tf_op jit(solution)/shard_map/ppermute | solution.py:43
  147.5 5.3 %collective-permute-start.42 = (f32[72,256]{1,0:T(8,128)S(1)}, f32[72,256]{1,0:T(8,128)S(1)}, u32[]{:S(2)}, u32[]{:S(2)}) collective-permute-start(f32[72,256]{1,0:T(8,128)S(1)} %slice_select_fusion.2), channel_id=1, source_target_pairs={{0,24},{4,28},{8,16},{12,20},{16,8},{20,12},{24,0},{28,4},{1,25},{... | collective-permute-start | bytes 221192 | tf_op jit(solution)/shard_map/ppermute | solution.py:43
  152.8 1.3 collective-permute-start.43
